TPU v7x, 256 devices: a whole 4x4x8 slice. The times are simulated.
256 devices in a mesh: pts: 32 (over x, z), cent: 8 (over y, core).
Axes of the slice: x: 4, y: 4, z: 8, core: 2. Of those that a mesh axis runs over, the one named last changes fastest.
Arguments:
- points: bfloat16 [16384, 1024], P('pts'), may hold values from -20 to 20
- centroids: bfloat16 [25600, 1024], P('cent'), may hold values from -0.7 to 0.7
Outputs:
- level_four_points: bfloat16 [25600, 1024], P('pts', 'cent')
All inputs are finite; a program needn't handle non-finite values.
Results may differ from a plain program's by a relative error of at most 0.0059.
Values may be sent and summed in bfloat16 or wider, within the bound.
No kernel may reach another device: no remote copies, remote signals or barrier semaphores. Data moves between devices by JAX's collectives and lax.ppermute only.
A program may use at most 64 MiB of HBM per device.

v0:
```python
import jax
import jax.numpy as jnp
from jax import lax
from jax.sharding import PartitionSpec as P


def body(points, centroids):
    half_norms = 0.5 * jnp.sum(jnp.square(centroids.astype(jnp.float32)), axis=1)
    logits = (
        lax.dot_general(
            points, centroids, (((1,), (1,)), ((), ())), preferred_element_type=jnp.float32
        )
        - half_norms[None, :]
    )
    row_top = lax.pmax(jnp.max(logits, axis=1), "cent")
    exponent = jnp.exp(logits - row_top[:, None])
    row_total = lax.psum(jnp.sum(exponent, axis=1), "cent")
    weights = (exponent / row_total[:, None]).astype(jnp.bfloat16)
    counts = jnp.sum(weights.astype(jnp.float32), axis=0)
    numerator = lax.dot_general(
        weights, points, (((0,), (0,)), ((), ())), preferred_element_type=jnp.float32
    )
    summed_numer, summed_counts = (
        lax.psum_scatter(numerator, "pts", scatter_dimension=0, tiled=True),
        lax.psum_scatter(counts[:, None], "pts", scatter_dimension=0, tiled=True),
    )
    finished = (summed_numer / (summed_counts + 1.0)).astype(jnp.bfloat16)
    return lax.all_to_all(finished, "cent", split_axis=1, concat_axis=0, tiled=True)


def solution(mesh):
    placed = (P("pts", None), P("cent", None))
    return jax.shard_map(
        body, mesh=mesh, in_specs=placed, out_specs=P("pts", "cent"), check_vma=False
    )
```

profile of v0, /device:TPU:1, one launch (start us, length us, event | category | flops | bytes accessed | tf_op | source)
XLA Modules:
  0.0 368.8 jit_solution(23285502681763115)
XLA Ops:
  0.0 0.0 copy-start
  0.0 0.0 copy-start.1
  0.0 4.4 %multiply_reduce_fusion = f32[3200]{0:T(1024)S(1)} fusion(bf16[3200,1024]{1,0:T(8,128)(2,1)} %param.3), kind=kLoop, calls=%fused_computation | loop fusion | flops 9827200 | bytes 6566400 | tf_op jit(solution)/shard_map/reduce_sum | solution.py:8
  4.4 0.0 copy-done
  4.4 0.7 copy-done.1
  5.1 5.9 %fusion.5 = (f32[512]{0:T(512)S(1)}, f32[512,3200]{1,0:T(8,128)}) fusion(f32[3200]{0:T(1024)S(1)} %broadcast_multiply_fusion, bf16[512,1024]{1,0:T(8,128)(2,1)S(1)} %copy-done, bf16[3200,1024]{1,0:T(8,128)(2,1)S(1)} %copy-done.1), kind=kOutput, calls=%fused_computation.12 | convolution fusion | flops 3358719488 | bytes 14170624 | tf_op jit(solution)/shard_map/dot_general | solution.py:10
  11.0 15.0 %pmax.7 = f32[512]{0:T(512)S(1)} all-reduce(f32[512]{0:T(512)S(1)} %get-tuple-element.9), channel_id=1, replica_groups=mesh['pts'=32,'cent'=8] {'cent'}, use_global_device_ids=true, to_apply=%region_2.0 | all-reduce | flops 512 | bytes 4096 | tf_op jit(solution)/shard_map/pmax | solution.py:15
  26.0 3.9 %fusion.1 = f32[512]{0:T(512)S(1)} fusion(f32[512,3200]{1,0:T(8,128)} %get-tuple-element.10, f32[512]{0:T(512)S(1)} %pmax.7), kind=kLoop, calls=%fused_computation.5 | loop fusion | flops 3276288 | bytes 6557696 | tf_op jit(solution)/shard_map/reduce_sum | solution.py:17
  29.8 13.1 %psum.7 = f32[512]{0:T(512)S(1)} all-reduce(f32[512]{0:T(512)S(1)} %fusion.1), channel_id=1, replica_groups=mesh['pts'=32,'cent'=8] {'cent'}, use_global_device_ids=true, to_apply=%region_4.0 | all-reduce | flops 512 | bytes 4096 | tf_op jit(solution)/shard_map/psum | solution.py:17
  43.0 3.7 convert_reduce_fusion
  46.6 6.6 %fusion.6 = f32[3200,1024]{1,0:T(8,128)} fusion(bf16[512,3200]{1,0:T(8,128)(2,1)S(1)} %get-tuple-element.6, bf16[512,1024]{1,0:T(8,128)(2,1)S(1)} %copy-done), kind=kOutput, calls=%fused_computation.13 | convolution fusion | flops 3355443200 | bytes 17432576 | tf_op jit(solution)/shard_map/dot_general | solution.py:20
  53.2 157.7 %fusion = f32[104,1024]{1,0:T(8,128)S(1)} fusion(f32[3200,1024]{1,0:T(8,128)} %fusion.6), kind=kCustom, calls=%all-reduce-scatter | all-reduce-scatter fusion | flops 3407873 | bytes 13534208
  211.0 1.8 collective-permute-start
  212.8 1.3 collective-permute-start.1
  214.1 0.0 copy-done.2
  214.1 0.7 fusion.4
  216.1 112.5 %all-reduce.1 = f32[3200,1]{0,1:T(1,128)S(1)} all-reduce(f32[3200,1]{0,1:T(1,128)S(1)} %broadcast_in_dim.2), channel_id=3, replica_groups=mesh['pts'=32,'cent'=8] {'pts'}, use_global_device_ids=true, to_apply=%region_7.0.clone | all-reduce | flops 3200 | bytes 25600
  328.6 0.1 fusion.3
  328.7 0.0 collective-permute-done.1
  328.7 0.0 collective-permute-done
  328.7 0.5 concatenate
  329.2 0.1 fusion.2
  329.4 38.7 %all_to_all.19 = bf16[100,8,128]{2,0,1:T(8,128)(2,1)S(1)} all-to-all(bf16[100,8,128]{2,0,1:T(8,128)(2,1)S(1)} %copy.5), channel_id=1, replica_groups=mesh['pts'=32,'cent'=8] {'cent'}, dimensions={1} | all-to-all | bytes 409600 | tf_op jit(solution)/shard_map/all_to_all | solution.py:28
  368.1 0.7 all_to_all.17
  (7 shorter events, 0.1 us)
Async XLA Ops:
  0.0 4.4 %copy-start = (bf16[512,1024]{1,0:T(8,128)(2,1)S(1)}, bf16[512,1024]{1,0:T(8,128)(2,1)}, u32[]{:S(2)}) copy-start(bf16[512,1024]{1,0:T(8,128)(2,1)} %param.2) | copy-start | bytes 3145732
  0.0 5.1 %copy-start.1 = (bf16[3200,1024]{1,0:T(8,128)(2,1)S(1)}, bf16[3200,1024]{1,0:T(8,128)(2,1)}, u32[]{:S(2)}) copy-start(bf16[3200,1024]{1,0:T(8,128)(2,1)} %param.3) | copy-start | bytes 19660804
  53.2 160.9 %copy-start.2 = (u32[256]{0:T(256)S(1)}, u32[256]{0:T(256)}, u32[]{:S(2)}) copy-start(u32[256]{0:T(256)} %constant.10) | copy-start | bytes 3076
  211.0 117.7 %collective-permute-start = (f32[104,1024]{1,0:T(8,128)S(1)}, f32[104,1024]{1,0:T(8,128)S(1)}, u32[]{:S(2)}, u32[]{:S(2)}) collective-permute-start(f32[104,1024]{1,0:T(8,128)S(1)} %fusion), channel_id=1, source_target_pairs={{0,8},{8,16},{16,24},{24,32},{32,40},{40,48},{48,56},{56,64},{64,7... | collective-permute-start | bytes 1277960
  212.8 115.9 %collective-permute-start.1 = (f32[20,1024]{1,0:T(8,128)S(1)}, f32[20,1024]{1,0:T(8,128)S(1)}, u32[]{:S(2)}, u32[]{:S(2)}) collective-permute-start(f32[20,1024]{1,0:T(8,128)S(1)} %slice), channel_id=1, source_target_pairs={{0,16},{8,24},{16,32},{24,40},{32,48},{40,56},{48,64},{56,72},{64,... | collective-permute-start | bytes 245768
where the time goes:
time: 369 us
  blocking collectives  337 us (91%)
  matrix products  12.5 us (3%)
  other arithmetic  12.1 us (3%)
    unnamed x2, blocking collectives  270 us
    all_to_all x1, blocking collectives, body(): lax.all_to_all(finished, 'cent', split_axis=1, concat_axis=0, tiled=True)  38.7 us
    pmax x1, blocking collectives, body(): row_top = lax.pmax(jnp.max(logits, axis=1), 'cent')  15 us
    psum x1, blocking collectives, body(): row_total = lax.psum(jnp.sum(exponent, axis=1), 'cent')  13.1 us
  transfers between devices with their start and end apart: 2, of which 0 were waited for; matrix products, arithmetic and copies ran while one was open for 0% of the time, Pallas kernels for 0%

commit v1 on v0

v1 whole, which is shorter than its diff:
```python
import jax
import jax.numpy as jnp
from jax import lax
from jax.sharding import Mesh, PartitionSpec as P

BF = jnp.bfloat16
F32 = jnp.float32


def dot_nt(a, b):
    return lax.dot_general(a, b, (((1,), (1,)), ((), ())), preferred_element_type=F32)


def share(a, axes, n):
    return lax.all_to_all(jnp.broadcast_to(a[None], (n, *a.shape)), axes, 0, 0)


def body(points, centroids):
    n_x, n_z, n_y, n_core = (lax.axis_size(a) for a in ("x", "z", "y", "core"))
    n_cent = n_y * n_core
    rows, dim = centroids.shape
    pts = points.shape[0]
    slot = rows // (n_x * n_z)
    cols = dim // n_cent
    me_z, me_core = lax.axis_index("z"), lax.axis_index("core")

    half = lax.dynamic_slice_in_dim(points, me_core * (pts // n_core), pts // n_core, 0)
    gathered = lax.all_gather(half, ("z", "core"), tiled=True)

    half_norms = 0.5 * jnp.sum(jnp.square(centroids.astype(F32)), axis=1)
    logits = dot_nt(points, centroids) - half_norms[None, :]
    top = jnp.max(logits, axis=1)
    total = jnp.sum(jnp.exp(logits - top[:, None]), axis=1)
    stats = share(jnp.stack([top, total]), ("y", "core"), n_cent)
    row_top = jnp.max(stats[:, 0], axis=0)
    lse = row_top + jnp.log(jnp.sum(stats[:, 1] * jnp.exp(stats[:, 0] - row_top[None]), axis=0))
    all_lse = share(lse, "z", n_z).reshape(-1)

    mine = lax.dynamic_index_in_dim(centroids.reshape(n_x, n_z, slot, dim), me_z, 1, keepdims=False)
    mine = mine.reshape(n_x * slot, dim)
    norms = lax.dynamic_index_in_dim(half_norms.reshape(n_x, n_z, slot), me_z, 1, keepdims=False).reshape(-1)

    logits2 = dot_nt(gathered, mine) - norms[None, :] - all_lse[:, None]
    weights = jnp.exp(logits2).astype(BF)
    counts = jnp.sum(weights.astype(F32), axis=0).reshape(n_x, 1, 1, slot)
    numer = lax.dot_general(weights, gathered, (((0,), (0,)), ((), ())), preferred_element_type=F32)
    numer = numer.astype(BF).reshape(n_x, slot, n_cent, cols).transpose(0, 2, 1, 3)
    high = counts.astype(BF)
    low = (counts - high.astype(F32)).astype(BF)
    tail = jnp.concatenate([high, low], axis=2)
    tail = jnp.pad(tail, ((0, 0), (0, 0), (0, 2), (0, cols - slot)))
    tail = jnp.broadcast_to(tail, (n_x, n_cent, 4, cols))
    send = jnp.concatenate([numer, tail], axis=2).reshape(n_x * n_cent, slot + 4, cols)
    got = lax.all_to_all(send, ("x", "y", "core"), 0, 0)
    got = jnp.sum(got.reshape(n_x, n_cent, slot + 4, cols).astype(F32), axis=0)
    count = got[:, slot, :slot] + got[:, slot + 1, :slot]
    out = got[:, :slot] / (count[:, :, None] + 1.0)
    return out.astype(BF).reshape(n_cent * slot, cols)


def solution(mesh):
    fine = Mesh(mesh.devices.reshape(4, 8, 4, 2), ("x", "z", "y", "core"))
    pts, cent = ("x", "z"), ("y", "core")
    return jax.shard_map(
        body, mesh=fine, in_specs=(P(pts, None), P(cent, None)), out_specs=P(pts, cent), check_vma=False
    )
```

time: 369 us -> 112 us (0.30)
  blocking collectives: 337 us -> 21.8 us
  waiting for transfers between devices: 0.01 us -> 25.9 us
  local copies, waits for them, and re-layouts: 2.68 us -> 14.8 us
  between operations: 1.47 us -> 13.5 us
  starting transfers between devices: 3.05 us -> 14.2 us
  other arithmetic: 12.1 us -> 5.9 us
    unnamed x2 -> x0, blocking collectives: 270 us -> none
    all_gather x0 -> x1, waiting for transfers between devices: none -> 20.6 us  [body(): gathered = lax.all_gather(half, ('z', 'core'), tiled=True)]
    all_to_all x1, blocking collectives: 38.7 us -> 21.8 us  [body(): got = lax.all_to_all(send, ('x', 'y', 'core'), 0, 0)]
    pmax x1 -> x0, blocking collectives: 15 us -> none  [body(): row_top = lax.pmax(jnp.max(logits, axis=1), 'cent')]
    all_to_all x0 -> x2, starting transfers between devices: none -> 14.2 us  [share(): return lax.all_to_all(jnp.broadcast_to(a[None], (n, *a.shape)), axes, 0, 0)]
    psum x1 -> x0, blocking collectives: 13.1 us -> none  [body(): row_total = lax.psum(jnp.sum(exponent, axis=1), 'cent')]
    reshape x0 -> x5, local copies, waits for them, and re-layouts: none -> 9.47 us  [the longest x1 8.38 us: body(): centroids.reshape(n_x, n_z, slot, dim)]
    reduce_sum x3 -> x4, other arithmetic: 11.9 us -> 5.54 us  [the longest x1 4.36 us: body(): half_norms = 0.5 * jnp.sum(jnp.square(centroids.astype(F32)), axis=1)]
  transfers between devices with their start and end apart: 2 -> 3, of which waited for: 0 -> 2; matrix products, arithmetic and copies ran while one was open for 0% -> 19% of each run, Pallas kernels for 0% -> 0%
where the time goes in v1:
time: 112 us; the launch traced here: 111 us
  waiting for transfers between devices  25.9 us (23%)
  blocking collectives  21.8 us (19%)
  matrix products  15.2 us (14%)
  local copies, waits for them, and re-layouts  14.8 us (13%)
  starting transfers between devices  14.2 us (13%)
  between operations  13.5 us (12%)
  other arithmetic  5.9 us (5%)
    all_to_all x1, blocking collectives, body(): got = lax.all_to_all(send, ('x', 'y', 'core'), 0, 0)  21.8 us
    all_gather x1, waiting for transfers between devices, body(): gathered = lax.all_gather(half, ('z', 'core'), tiled=True)  20.6 us
    all_to_all x2, starting transfers between devices, share(): return lax.all_to_all(jnp.broadcast_to(a[None], (n, *a.shape)), axes, 0, 0)  14.2 us
    dot_general x2, matrix products, dot_nt(): lax.dot_general(a, b, (((1,), (1,)), ((), ())), preferred_element_type=F32)  11.6 us
    reshape x1, local copies, waits for them, and re-layouts, body(): centroids.reshape(n_x, n_z, slot, dim)  8.38 us
    all_to_all x2, waiting for transfers between devices, share(): return lax.all_to_all(jnp.broadcast_to(a[None], (n, *a.shape)), axes, 0, 0)  5.21 us
    reduce_sum x1, other arithmetic, body(): half_norms = 0.5 * jnp.sum(jnp.square(centroids.astype(F32)), axis=1)  4.36 us
    dot_general x1, matrix products, body(): lax.dot_general(weights, gathered, (((0,), (0,)), ((), ())), preferred_el...  3.6 us
  transfers between devices with their start and end apart: 3, of which 2 were waited for; matrix products, arithmetic and copies ran while one was open for 19% of the time, Pallas kernels for 0%

profile of v1, /device:TPU:1, one launch (start us, length us, event | category | flops | bytes accessed | tf_op | source)
XLA Modules:
  0.0 111.3 jit_solution(11883174086701008138)
XLA Ops:
  6.5 1.2 %copy-done = bf16[512,1024]{1,0:T(8,128)(2,1)S(1)} copy-done((bf16[512,1024]{1,0:T(8,128)(2,1)S(1)}, bf16[512,1024]{1,0:T(8,128)(2,1)}, u32[]{:S(2)}) %copy-start) | copy-done | bytes 1048600
  7.8 0.8 constant_dynamic-slice_fusion.1
  8.6 4.4 %multiply_reduce_fusion = f32[3200]{0:T(1024)S(1)} fusion(bf16[3200,1024]{1,0:T(8,128)(2,1)} %param.3), kind=kLoop, calls=%fused_computation | loop fusion | flops 9827200 | bytes 6566400 | tf_op jit(solution)/shard_map/reduce_sum | solution.py:30
  13.0 0.4 copy-done.1
  13.4 3.9 %fusion.16 = (f32[512]{0:T(512)S(1)}, f32[512,3200]{1,0:T(8,128)S(1)}) fusion(f32[3200]{0:T(1024)S(1)} %broadcast_multiply_fusion, bf16[512,1024]{1,0:T(8,128)(2,1)S(1)} %copy-done, bf16[3200,1024]{1,0:T(8,128)(2,1)S(1)} %copy-done.1), kind=kOutput, calls=%fused_computation.38 | convolution fusion | flops 3358719488 | bytes 14170624 | tf_op jit(solution)/shard_map/dot_general | solution.py:11
  17.2 1.0 exponential_reduce_fusion
  18.3 0.6 broadcast_in_dim.8
  18.9 6.5 %all-to-all-start = ((f32[8,2,512]{2,1,0:T(2,128)}), f32[8,2,512]{2,1,0:T(2,128)S(1)}, u32[]{:S(2)}, u32[]{:S(2)}) async-start(f32[8,2,512]{2,1,0:T(2,128)} %broadcast_in_dim.8), calls=%async_computation | async-start | bytes 65536 | tf_op jit(solution)/shard_map/all_to_all | solution.py:15
  25.4 8.4 %reshape.98 = bf16[4,8,100,1024]{3,2,1,0:T(8,128)(2,1)} reshape(bf16[3200,1024]{1,0:T(8,128)(2,1)} %param.3) | data formatting | bytes 13107200 | tf_op jit(solution)/shard_map/reshape | solution.py:39
  33.9 0.6 broadcast_in_dim.9
  34.5 7.7 %all-to-all-start.1 = ((f32[8,1,512]{2,1,0:T(1,128)}), f32[8,1,512]{2,1,0:T(1,128)S(1)}, u32[]{:S(2)}, u32[]{:S(2)}) async-start(f32[8,1,512]{2,1,0:T(1,128)} %broadcast_in_dim.9), calls=%async_computation.1 | async-start | bytes 32768 | tf_op jit(solution)/shard_map/all_to_all | solution.py:15
  42.2 1.3 %constant_dynamic-slice_fusion = bf16[4,1,100,1024]{3,2,1,0:T(8,128)(2,1)S(1)} fusion(bf16[4,8,100,1024]{3,2,1,0:T(8,128)(2,1)} %reshape.98, s32[]{:T(128)S(6)} %select_n.10), kind=kLoop, calls=%fused_computation.33 | loop fusion | bytes 1638404 | tf_op jit(solution)/shard_map/jit(dynamic_index_in_dim)/dynamic_slice | solution.py:39
  43.5 0.1 mul.23
  43.7 0.2 reshape.99
  43.9 5.2 %all-to-all-done.1 = f32[8,1,512]{2,1,0:T(1,128)S(1)} async-done(((f32[8,1,512]{2,1,0:T(1,128)}), f32[8,1,512]{2,1,0:T(1,128)S(1)}, u32[]{:S(2)}, u32[]{:S(2)}) %all-to-all-start.1) | async-done | bytes 16416 | tf_op jit(solution)/shard_map/all_to_all | solution.py:15
  49.1 20.6 %all-gather.2.cloned.1.call-done = bf16[4096,1024]{1,0:T(8,128)(2,1)} async-done(((bf16[256,1024]{1,0:T(8,128)(2,1)}), bf16[4096,1024]{1,0:T(8,128)(2,1)}) %all-gather.2.cloned.1.call-update) | async-done | bytes 8388624 | tf_op jit(solution)/shard_map/all_gather | solution.py:28
  69.7 7.7 %convert_reduce_fusion = (f32[400]{0:T(512)S(1)}, bf16[4096,400]{0,1:T(8,128)(2,1)S(1)}) fusion(f32[4096]{0:T(1024)S(1)} %bitcast.39, f32[400]{0:T(512)S(1)} %sub.55, bf16[4096,1024]{1,0:T(8,128)(2,1)} %all-gather.2.cloned.1.call-done, bf16[400,1024]{1,0:T(8,128)(2,1)S(1)} %reshape.99), kind=kOutput, calls=%fused_computation.1 | convolution fusion | flops 3363634688 | bytes 12504192 | tf_op jit(solution)/shard_map/dot_general | solution.py:11
  77.5 3.6 %fusion = bf16[50,8,8,128]{3,1,2,0:T(8,128)(2,1)S(1)} fusion(bf16[4096,400]{0,1:T(8,128)(2,1)S(1)} %get-tuple-element.13, bf16[4096,1024]{1,0:T(8,128)(2,1)S(1)} %copy-done.2), kind=kOutput, calls=%fused_computation.7 | convolution fusion | flops 3355852800 | bytes 12484608 | tf_op jit(solution)/shard_map/dot_general | solution.py:46
  81.1 0.2 copy.12
  81.2 0.1 copy.24
  81.6 21.8 %all_to_all.16 = bf16[32,104,128]{2,1,0:T(8,128)(2,1)S(1)} all-to-all(bf16[32,104,128]{2,1,0:T(8,128)(2,1)S(1)} %bitcast.36), channel_id=1, replica_groups=mesh['x'=4,'z'=8,'y'=4,'core'=2] {'x','y','core'}, dimensions={0} | all-to-all | bytes 1703936 | tf_op jit(solution)/shard_map/all_to_all | solution.py:54
  103.4 0.1 convert_reduce_fusion.1
  103.5 0.2 fusion.1
  103.7 0.7 reshape.103
  (20 shorter events, 0.4 us)
Async XLA Ops:
  6.5 1.2 %copy-start = (bf16[512,1024]{1,0:T(8,128)(2,1)S(1)}, bf16[512,1024]{1,0:T(8,128)(2,1)}, u32[]{:S(2)}) copy-start(bf16[512,1024]{1,0:T(8,128)(2,1)} %param.2) | copy-start | bytes 3145732
  6.5 63.2 %all-gather.2.cloned.1.call-start = ((), (), s32[]{:S(2)}) async-start(), calls=%async_computation.3 | async-start | bytes 8912896 | tf_op jit(solution)/shard_map/all_gather | solution.py:28
  8.6 4.7 %copy-start.1 = (bf16[3200,1024]{1,0:T(8,128)(2,1)S(1)}, bf16[3200,1024]{1,0:T(8,128)(2,1)}, u32[]{:S(2)}) copy-start(bf16[3200,1024]{1,0:T(8,128)(2,1)} %param.3) | copy-start | bytes 19660804
  18.9 14.9 %all-to-all-start = ((f32[8,2,512]{2,1,0:T(2,128)}), f32[8,2,512]{2,1,0:T(2,128)S(1)}, u32[]{:S(2)}, u32[]{:S(2)}) async-start(f32[8,2,512]{2,1,0:T(2,128)} %broadcast_in_dim.8), calls=%async_computation | async-start | bytes 65536 | tf_op jit(solution)/shard_map/all_to_all | solution.py:15
  34.5 14.6 %all-to-all-start.1 = ((f32[8,1,512]{2,1,0:T(1,128)}), f32[8,1,512]{2,1,0:T(1,128)S(1)}, u32[]{:S(2)}, u32[]{:S(2)}) async-start(f32[8,1,512]{2,1,0:T(1,128)} %broadcast_in_dim.9), calls=%async_computation.1 | async-start | bytes 32768 | tf_op jit(solution)/shard_map/all_to_all | solution.py:15
  69.7 7.8 %copy-start.2 = (bf16[4096,1024]{1,0:T(8,128)(2,1)S(1)}, bf16[4096,1024]{1,0:T(8,128)(2,1)}, u32[]{:S(2)}) copy-start(bf16[4096,1024]{1,0:T(8,128)(2,1)} %all-gather.2.cloned.1.call-done) | copy-start | bytes 25165828
Sparse Core Ops, SparseCore 0:
  9.2 60.4 all-gather.1

commit v2 on v1

v2 whole, which is shorter than its diff:
```python
import jax
import jax.numpy as jnp
from jax import lax
from jax.sharding import Mesh, PartitionSpec as P

BF = jnp.bfloat16
F32 = jnp.float32
NX, NZ, NY, NC = 4, 8, 4, 2
Z = ("zq", "zp")
CENT = ("y", "core")
TAIL = 4


def dot_nt(a, b):
    return lax.dot_general(a, b, (((1,), (1,)), ((), ())), preferred_element_type=F32)


def share(a, axes, n):
    return lax.all_to_all(jnp.broadcast_to(a[None], (n, *a.shape)), axes, 0, 0)


def split(counts):
    high = counts.astype(BF)
    return high, (counts - high.astype(F32)).astype(BF)


def body(points, centroids):
    rows, dim = centroids.shape
    pts = points.shape[0]
    n_cent = NY * NC
    slot = rows // (NX * NZ)
    cols = dim // n_cent
    mine = rows // NX
    half = pts // NC
    x, parity, core = lax.axis_index("x"), lax.axis_index("zp"), lax.axis_index("core")

    own = lax.dynamic_slice_in_dim(points, core * half, half, 0)
    shards = {
        k: lax.ppermute(own, "x", [(i, (i + k) % NX) for i in range(NX)]) for k in (1, 3, 2)
    }
    other = {k: lax.ppermute(a, "core", [(0, 1), (1, 0)]) for k, a in shards.items()}

    half_norms = 0.5 * jnp.sum(jnp.square(centroids.astype(F32)), axis=1)
    logits = dot_nt(points, centroids) - half_norms[None, :]
    top = jnp.max(logits, axis=1)
    total = jnp.sum(jnp.exp(logits - top[:, None]), axis=1)
    stats = share(jnp.stack([top, total]), ("x", *CENT), NX * n_cent)
    stats = stats.reshape(NX, n_cent, 2, pts)
    row_top = jnp.max(stats[:, :, 0], axis=1)
    row_sum = jnp.sum(stats[:, :, 1] * jnp.exp(stats[:, :, 0] - row_top[:, None]), axis=1)
    lse = row_top + jnp.log(row_sum)

    blocks = lax.dynamic_slice_in_dim(centroids, x * mine, mine, 0).reshape(NZ // 2, 2, slot, dim)
    norms = lax.dynamic_slice_in_dim(half_norms, x * mine, mine, 0).reshape(NZ // 2, 2, slot)
    pad = ((0, 0), (0, TAIL), (0, 0))

    def pick(p):
        rows_p = jnp.pad(lax.dynamic_index_in_dim(blocks, p, 1, keepdims=False), pad)
        norms_p = jnp.pad(lax.dynamic_index_in_dim(norms, p, 1, keepdims=False), pad[:2])
        return rows_p.reshape(-1, dim), norms_p.reshape(-1)

    all_points = [points]
    all_lse = [lax.dynamic_index_in_dim(lse, x, 0, keepdims=False)]
    for k in (1, 3, 2):
        source = lax.dynamic_index_in_dim(lse, lax.rem(x + NX - k, NX), 0, keepdims=False)
        all_points += [shards[k], other[k]]
        all_lse += [
            lax.dynamic_slice_in_dim(source, core * half, half, 0),
            lax.dynamic_slice_in_dim(source, (1 - core) * half, half, 0),
        ]
    all_points = jnp.concatenate(all_points, axis=0)
    all_lse = jnp.concatenate(all_lse, axis=0)

    def partial(p):
        rows_p, norms_p = pick(p)
        weights = jnp.exp(dot_nt(rows_p, all_points) - norms_p[:, None] - all_lse[None, :]).astype(BF)
        counts = jnp.sum(weights.astype(F32), axis=1).reshape(NZ // 2, slot + TAIL)
        numer = jnp.dot(weights, all_points, preferred_element_type=F32)
        return numer.reshape(NZ // 2, slot + TAIL, dim), counts

    def tails(counts):
        high, low = split(counts)
        tail = jnp.stack([high[..., :slot], low[..., :slot]], axis=1)
        return jnp.pad(tail, ((0, 0), (0, TAIL - 2), (0, cols - slot)))

    def counts_of(a):
        return a[:, slot, :slot].astype(F32) + a[:, slot + 1, :slot].astype(F32)

    give, give_counts = partial(1 - parity)
    tail = jnp.tile(tails(give_counts), (1, 1, n_cent // 2))
    given = []
    for h in range(2):
        part = give[:, :slot, h * dim // 2 : (h + 1) * dim // 2].astype(BF)
        part = jnp.concatenate([part, tail], axis=1)
        pairs = [(i, i ^ 1) for i in range(NZ)] if h == 0 else [(i, (i + (1 if i % 2 else -1)) % NZ) for i in range(NZ)]
        given.append(lax.ppermute(part, Z, pairs))
    keep, keep_counts = partial(parity)
    merged = []
    for h in range(2):
        part = keep[:, :slot, h * dim // 2 : (h + 1) * dim // 2] + given[h][:, :slot].astype(F32)
        tail = jnp.tile(tails(keep_counts[:, :slot] + counts_of(given[h])), (1, 1, n_cent // 2))
        merged.append(jnp.concatenate([part.astype(BF), tail], axis=1))
    merged = jnp.concatenate(merged, axis=2)
    send = merged.reshape(NZ // 2, slot + TAIL, n_cent, cols).transpose(0, 2, 1, 3)
    got = lax.all_to_all(send.reshape(-1, slot + TAIL, cols), ("zq", *CENT), 0, 0)
    got = jnp.sum(got.reshape(NZ // 2, n_cent, slot + TAIL, cols).astype(F32), axis=0)
    out = got[:, :slot] / (counts_of(got)[:, :, None] + 1.0)
    return out.astype(BF).reshape(n_cent * slot, cols)


def solution(mesh):
    fine = Mesh(mesh.devices.reshape(NX, NZ // 2, 2, NY, NC), ("x", *Z, *CENT))
    pts = ("x", *Z)
    return jax.shard_map(
        body, mesh=fine, in_specs=(P(pts, None), P(CENT, None)), out_specs=P(pts, CENT), check_vma=False
    )
```

time: 112 us -> 103 us (0.920)
  the two profiles are of different devices: /device:TPU:1 before, /device:TPU:35 now
where the time goes in v2:
time: 103 us; the launch traced here: 102 us
  blocking collectives  31.1 us (30%)
  starting transfers between devices  18.6 us (18%)
  local copies, waits for them, and re-layouts  17.5 us (17%)
  matrix products  17.1 us (17%)
  other arithmetic  9.81 us (10%)
  waiting for transfers between devices  7.95 us (8%)
    all_to_all x1, blocking collectives, body(): lax.all_to_all(send.reshape(-1, slot + TAIL, cols), ('zq', *CENT), 0, 0)  31.1 us
    dot_general x3, matrix products, dot_nt(): lax.dot_general(a, b, (((1,), (1,)), ((), ())), preferred_element_type=F32)  13.2 us
    unnamed x23, local copies, waits for them, and re-layouts  10 us
    all_to_all x1, starting transfers between devices, share(): return lax.all_to_all(jnp.broadcast_to(a[None], (n, *a.shape)), axes, 0, 0)  8.37 us
    ppermute x2, starting transfers between devices, body(): given.append(lax.ppermute(part, Z, pairs))  5.49 us
    all_to_all x1, waiting for transfers between devices, share(): return lax.all_to_all(jnp.broadcast_to(a[None], (n, *a.shape)), axes, 0, 0)  4.44 us
    reduce_sum x1, other arithmetic, body(): half_norms = 0.5 * jnp.sum(jnp.square(centroids.astype(F32)), axis=1)  4.21 us
    dot_general x2, matrix products, partial(): numer = jnp.dot(weights, all_points, preferred_element_type=F32)  3.9 us
  transfers between devices with their start and end apart: 9, of which 2 were waited for; matrix products, arithmetic and copies ran while one was open for 29% of the time, Pallas kernels for 0%

profile of v2, /device:TPU:35, one launch (start us, length us, event | category | flops | bytes accessed | tf_op | source)
XLA Modules:
  0.0 102.5 jit_solution(15781917689036815644)
XLA Ops:
  0.0 2.0 %constant_dynamic-slice_fusion.3 = bf16[256,1024]{1,0:T(8,128)(2,1)} fusion(bf16[512,1024]{1,0:T(8,128)(2,1)} %param.2, s32[]{:T(128)S(6)} %select_n.50), kind=kLoop, calls=%fused_computation.72 | loop fusion | bytes 1048580 | tf_op jit(solution)/shard_map/dynamic_slice | solution.py:37
  2.0 1.2 %collective-permute-start = (bf16[256,1024]{1,0:T(8,128)(2,1)}, bf16[256,1024]{1,0:T(8,128)(2,1)}, u32[]{:S(2)}, u32[]{:S(2)}) collective-permute-start(bf16[256,1024]{1,0:T(8,128)(2,1)} %constant_dynamic-slice_fusion.3), channel_id=1, source_target_pairs={{0,64},{64,128},{128,192},{192,0},{1,65},{65,129},{129,193},{193,1... | collective-permute-start | bytes 1572872 | tf_op jit(solution)/shard_map/ppermute | solution.py:39
  3.5 1.8 %collective-permute-start.4 = (bf16[256,1024]{1,0:T(8,128)(2,1)}, bf16[256,1024]{1,0:T(8,128)(2,1)}, u32[]{:S(2)}, u32[]{:S(2)}) collective-permute-start(bf16[256,1024]{1,0:T(8,128)(2,1)} %constant_dynamic-slice_fusion.3), channel_id=1, source_target_pairs={{0,128},{64,192},{128,0},{192,64},{1,129},{65,193},{129,1},{193,65... | collective-permute-start | bytes 1572872 | tf_op jit(solution)/shard_map/ppermute | solution.py:39
  5.3 4.2 %multiply_reduce_fusion = f32[3200]{0:T(1024)S(1)} fusion(bf16[3200,1024]{1,0:T(8,128)(2,1)} %param.3), kind=kLoop, calls=%fused_computation | loop fusion | flops 9827200 | bytes 6566400 | tf_op jit(solution)/shard_map/reduce_sum | solution.py:43
  9.6 3.9 %fusion.28 = (f32[512]{0:T(512)S(1)}, f32[512,3200]{1,0:T(8,128)S(1)}) fusion(f32[3200]{0:T(1024)S(1)} %broadcast_multiply_fusion, bf16[512,1024]{1,0:T(8,128)(2,1)S(1)} %copy-done.1, bf16[3200,1024]{1,0:T(8,128)(2,1)S(1)} %copy-done), kind=kOutput, calls=%fused_computation.86 | convolution fusion | flops 3358719488 | bytes 14170624 | tf_op jit(solution)/shard_map/dot_general | solution.py:15
  13.4 1.0 %exponential_reduce_fusion = f32[512]{0:T(512)S(1)} fusion(f32[512,3200]{1,0:T(8,128)S(1)} %get-tuple-element.31, f32[512]{0:T(512)S(1)} %get-tuple-element.30), kind=kLoop, calls=%fused_computation.1 | loop fusion | flops 3276288 | bytes 6557696 | tf_op jit(solution)/shard_map/reduce_sum | solution.py:46
  15.2 8.4 %all-to-all-start = ((f32[32,2,512]{2,1,0:T(2,128)}), f32[32,2,512]{2,1,0:T(2,128)S(1)}, u32[]{:S(2)}, u32[]{:S(2)}) async-start(f32[32,2,512]{2,1,0:T(2,128)} %broadcast_in_dim.2), calls=%async_computation | async-start | bytes 262144 | tf_op jit(solution)/shard_map/all_to_all | solution.py:19
  23.7 1.6 %constant_dynamic-slice_fusion.4 = bf16[800,1024]{1,0:T(8,128)(2,1)S(1)} fusion(bf16[3200,1024]{1,0:T(8,128)(2,1)} %param.3, s32[]{:T(128)S(6)} %select_n.48), kind=kLoop, calls=%fused_computation.73 | loop fusion | bytes 3276804 | tf_op jit(solution)/shard_map/dynamic_slice | solution.py:53
  26.3 2.3 %constant_dynamic-update-slice_fusion.6 = bf16[2048,1024]{1,0:T(8,128)(2,1)} fusion(bf16[512,1024]{1,0:T(8,128)(2,1)} %param.2), kind=kLoop, calls=%fused_computation.34 | loop fusion | bytes 2097152
  28.5 4.4 %all-to-all-done = f32[32,2,512]{2,1,0:T(2,128)S(1)} async-done(((f32[32,2,512]{2,1,0:T(2,128)}), f32[32,2,512]{2,1,0:T(2,128)S(1)}, u32[]{:S(2)}, u32[]{:S(2)}) %all-to-all-start) | async-done | bytes 131104 | tf_op jit(solution)/shard_map/all_to_all | solution.py:19
  34.8 1.9 %constant_dynamic-update-slice_fusion.5 = bf16[2048,1024]{1,0:T(8,128)(2,1)} fusion(bf16[2048,1024]{1,0:T(8,128)(2,1)} %constant_dynamic-update-slice_fusion.6, bf16[256,1024]{1,0:T(8,128)(2,1)} %collective-permute-done), kind=kLoop, calls=%fused_computation.33 | loop fusion | bytes 1048576
  37.5 1.9 %constant_dynamic-update-slice_fusion.3 = bf16[2048,1024]{1,0:T(8,128)(2,1)} fusion(bf16[2048,1024]{1,0:T(8,128)(2,1)} %constant_dynamic-update-slice_fusion.4, bf16[256,1024]{1,0:T(8,128)(2,1)} %collective-permute-done.2), kind=kLoop, calls=%fused_computation.31 | loop fusion | bytes 1048576
  39.3 0.8 constant_dynamic-update-slice_fusion.2
  40.2 1.9 %constant_dynamic-update-slice_fusion.1 = bf16[2048,1024]{1,0:T(8,128)(2,1)} fusion(bf16[2048,1024]{1,0:T(8,128)(2,1)} %constant_dynamic-update-slice_fusion.2, bf16[256,1024]{1,0:T(8,128)(2,1)} %collective-permute-done.4), kind=kLoop, calls=%fused_computation.29 | loop fusion | bytes 1048576
  42.9 4.7 %convert_reduce_fusion.1 = (f32[416]{0:T(512)S(1)}, bf16[416,2048]{1,0:T(8,128)(2,1)S(1)}) fusion(f32[2048]{0:T(1024)S(1)} %constant_dynamic-update-slice_fusion.8, f32[416]{0:T(512)S(1)} %sub.100, bf16[416,1024]{1,0:T(8,128)(2,1)S(1)} %bitcast.85, bf16[2048,1024]{1,0:T(8,128)(2,1)} %constant_dynamic-update-slice_fusion), kind=kOutput, calls=%fused_computation.4 | convolution fusion | flops 1749089920 | bytes 6761728 | tf_op jit(solution)/shard_map/dot_general | solution.py:15
  47.5 2.0 %convolution_convert_fusion = bf16[416,1024]{1,0:T(8,128)(2,1)S(1)} fusion(bf16[416,2048]{1,0:T(8,128)(2,1)S(1)} %get-tuple-element.33, bf16[2048,1024]{1,0:T(8,128)(2,1)S(1)} %copy-done.2), kind=kOutput, calls=%fused_computation.8 | convolution fusion | flops 1745256448 | bytes 6750208 | tf_op jit(solution)/shard_map/dot_general | solution.py:78
  49.8 1.7 %collective-permute-start.7 = (bf16[4,104,512]{2,1,0:T(8,128)(2,1)S(1)}, bf16[4,104,512]{2,1,0:T(8,128)(2,1)S(1)}, u32[]{:S(2)}, u32[]{:S(2)}) collective-permute-start(bf16[4,104,512]{2,1,0:T(8,128)(2,1)S(1)} %pad_maximum_fusion.2), channel_id=1, source_target_pairs={{0,56},{8,16},{16,8},{24,32},{32,24},{40,48},{48,40},{56,0},{1,57}... | collective-permute-start | bytes 1277960 | tf_op jit(solution)/shard_map/ppermute | solution.py:96
  51.7 1.0 %pad_maximum_fusion = bf16[4,104,512]{2,0,1:T(4,128)(2,1)} fusion(bf16[4,4,512]{2,0,1:T(4,128)(2,1)S(1)} %tile.13, bf16[4,100,512]{2,0,1:T(4,128)(2,1)S(1)} %copy.39), kind=kLoop, calls=%fused_computation.19 | loop fusion | flops 212992 | bytes 851968 | tf_op jit(solution)/shard_map/concatenate | solution.py:94
  52.8 3.8 %collective-permute-start.6 = (bf16[4,104,512]{2,0,1:T(4,128)(2,1)}, bf16[4,104,512]{2,0,1:T(4,128)(2,1)}, u32[]{:S(2)}, u32[]{:S(2)}) collective-permute-start(bf16[4,104,512]{2,0,1:T(4,128)(2,1)} %pad_maximum_fusion), channel_id=1, source_target_pairs={{0,8},{8,0},{16,24},{24,16},{32,40},{40,32},{48,56},{56,48},{1,9},... | collective-permute-start | bytes 1277960 | tf_op jit(solution)/shard_map/ppermute | solution.py:96
  56.5 4.7 %convert_reduce_fusion = (f32[416]{0:T(512)S(1)}, bf16[416,2048]{1,0:T(8,128)(2,1)S(1)}) fusion(f32[2048]{0:T(1024)S(1)} %constant_dynamic-update-slice_fusion.8, f32[416]{0:T(512)S(1)} %sub.84, bf16[416,1024]{1,0:T(8,128)(2,1)S(1)} %bitcast.84, bf16[2048,1024]{1,0:T(8,128)(2,1)} %constant_dynamic-update-slice_fusion), kind=kOutput, calls=%fused_computation.3 | convolution fusion | flops 1749089920 | bytes 6761728 | tf_op jit(solution)/shard_map/dot_general | solution.py:15
  61.2 1.9 %fusion.29 = f32[416,1024]{1,0:T(8,128)S(1)} fusion(bf16[416,2048]{1,0:T(8,128)(2,1)S(1)} %get-tuple-element.35, bf16[2048,1024]{1,0:T(8,128)(2,1)S(1)} %copy-done.3), kind=kOutput, calls=%fused_computation.87 | convolution fusion | flops 1744830464 | bytes 7602176 | tf_op jit(solution)/shard_map/dot_general | solution.py:78
  63.3 3.5 %collective-permute-done.6 = bf16[4,104,512]{2,0,1:T(4,128)(2,1)} collective-permute-done((bf16[4,104,512]{2,0,1:T(4,128)(2,1)}, bf16[4,104,512]{2,0,1:T(4,128)(2,1)}, u32[]{:S(2)}, u32[]{:S(2)}) %collective-permute-start.6) | collective-permute-done | bytes 426016 | tf_op jit(solution)/shard_map/ppermute | solution.py:96
  67.7 1.6 %fusion.1 = bf16[4,100,512]{2,0,1:T(4,128)(2,1)S(1)} fusion(f32[4,100,512]{2,1,0:T(8,128)S(1)} %get-tuple-element.7, bf16[4,104,512]{2,0,1:T(4,128)(2,1)} %collective-permute-done.6), kind=kLoop, calls=%fused_computation.16 | loop fusion | flops 614400 | bytes 1638400 | tf_op jit(solution)/shard_map/convert_element_type | solution.py:102
  70.3 31.1 %all_to_all.10 = bf16[32,104,128]{2,1,0:T(8,128)(2,1)S(1)} all-to-all(bf16[32,104,128]{2,1,0:T(8,128)(2,1)S(1)} %bitcast.82), channel_id=1, replica_groups=mesh['x'=4,'zq'=4,'zp'=2,'y'=4,'core'=2] {'zq','y','core'}, dimensions={0} | all-to-all | bytes 1703936 | tf_op jit(solution)/shard_map/all_to_all | solution.py:105
  (80 shorter events, 8.8 us)
Async XLA Ops:
  0.0 9.6 %copy-start.1 = (bf16[512,1024]{1,0:T(8,128)(2,1)S(1)}, bf16[512,1024]{1,0:T(8,128)(2,1)}, u32[]{:S(2)}) copy-start(bf16[512,1024]{1,0:T(8,128)(2,1)} %param.2) | copy-start | bytes 3145732
  0.0 9.6 %copy-start = (bf16[3200,1024]{1,0:T(8,128)(2,1)S(1)}, bf16[3200,1024]{1,0:T(8,128)(2,1)}, u32[]{:S(2)}) copy-start(bf16[3200,1024]{1,0:T(8,128)(2,1)} %param.3) | copy-start | bytes 19660804
  2.0 31.3 %collective-permute-start = (bf16[256,1024]{1,0:T(8,128)(2,1)}, bf16[256,1024]{1,0:T(8,128)(2,1)}, u32[]{:S(2)}, u32[]{:S(2)}) collective-permute-start(bf16[256,1024]{1,0:T(8,128)(2,1)} %constant_dynamic-slice_fusion.3), channel_id=1, source_target_pairs={{0,64},{64,128},{128,192},{192,0},{1,65},{65,129},{129,193},{193,1... | collective-permute-start | bytes 1572872 | tf_op jit(solution)/shard_map/ppermute | solution.py:39
  3.2 30.6 %collective-permute-start.2 = (bf16[256,1024]{1,0:T(8,128)(2,1)}, bf16[256,1024]{1,0:T(8,128)(2,1)}, u32[]{:S(2)}, u32[]{:S(2)}) collective-permute-start(bf16[256,1024]{1,0:T(8,128)(2,1)} %constant_dynamic-slice_fusion.3), channel_id=1, source_target_pairs={{0,192},{64,0},{128,64},{192,128},{1,193},{65,1},{129,65},{193,129... | collective-permute-start | bytes 1572872 | tf_op jit(solution)/shard_map/ppermute | solution.py:39
  3.5 30.5 %collective-permute-start.4 = (bf16[256,1024]{1,0:T(8,128)(2,1)}, bf16[256,1024]{1,0:T(8,128)(2,1)}, u32[]{:S(2)}, u32[]{:S(2)}) collective-permute-start(bf16[256,1024]{1,0:T(8,128)(2,1)} %constant_dynamic-slice_fusion.3), channel_id=1, source_target_pairs={{0,128},{64,192},{128,0},{192,64},{1,129},{65,193},{129,1},{193,65... | collective-permute-start | bytes 1572872 | tf_op jit(solution)/shard_map/ppermute | solution.py:39
  15.2 17.8 %all-to-all-start = ((f32[32,2,512]{2,1,0:T(2,128)}), f32[32,2,512]{2,1,0:T(2,128)S(1)}, u32[]{:S(2)}, u32[]{:S(2)}) async-start(f32[32,2,512]{2,1,0:T(2,128)} %broadcast_in_dim.2), calls=%async_computation | async-start | bytes 262144 | tf_op jit(solution)/shard_map/all_to_all | solution.py:19
  33.3 3.3 %collective-permute-start.1 = (bf16[256,1024]{1,0:T(8,128)(2,1)}, bf16[256,1024]{1,0:T(8,128)(2,1)S(1)}, u32[]{:S(2)}, u32[]{:S(2)}) collective-permute-start(bf16[256,1024]{1,0:T(8,128)(2,1)} %collective-permute-done), channel_id=1, source_target_pairs={{0,1},{1,0},{2,3},{3,2},{4,5},{5,4},{6,7},{7,6},{8,9},{9,8},{10,11... | collective-permute-start | bytes 1572872 | tf_op jit(solution)/shard_map/ppermute | solution.py:41
  33.9 5.5 %collective-permute-start.3 = (bf16[256,1024]{1,0:T(8,128)(2,1)}, bf16[256,1024]{1,0:T(8,128)(2,1)S(1)}, u32[]{:S(2)}, u32[]{:S(2)}) collective-permute-start(bf16[256,1024]{1,0:T(8,128)(2,1)} %collective-permute-done.2), channel_id=1, source_target_pairs={{0,1},{1,0},{2,3},{3,2},{4,5},{5,4},{6,7},{7,6},{8,9},{9,8},{10,11... | collective-permute-start | bytes 1572872 | tf_op jit(solution)/shard_map/ppermute | solution.py:41
  34.0 8.0 %collective-permute-start.5 = (bf16[256,1024]{1,0:T(8,128)(2,1)}, bf16[256,1024]{1,0:T(8,128)(2,1)S(1)}, u32[]{:S(2)}, u32[]{:S(2)}) collective-permute-start(bf16[256,1024]{1,0:T(8,128)(2,1)} %collective-permute-done.4), channel_id=1, source_target_pairs={{0,1},{1,0},{2,3},{3,2},{4,5},{5,4},{6,7},{7,6},{8,9},{9,8},{10,11... | collective-permute-start | bytes 1572872 | tf_op jit(solution)/shard_map/ppermute | solution.py:41
  42.9 4.7 %copy-start.2 = (bf16[2048,1024]{1,0:T(8,128)(2,1)S(1)}, bf16[2048,1024]{1,0:T(8,128)(2,1)}, u32[]{:S(2)}) copy-start(bf16[2048,1024]{1,0:T(8,128)(2,1)} %constant_dynamic-update-slice_fusion) | copy-start | bytes 12582916
  49.8 13.5 %collective-permute-start.7 = (bf16[4,104,512]{2,1,0:T(8,128)(2,1)S(1)}, bf16[4,104,512]{2,1,0:T(8,128)(2,1)S(1)}, u32[]{:S(2)}, u32[]{:S(2)}) collective-permute-start(bf16[4,104,512]{2,1,0:T(8,128)(2,1)S(1)} %pad_maximum_fusion.2), channel_id=1, source_target_pairs={{0,56},{8,16},{16,8},{24,32},{32,24},{40,48},{48,40},{56,0},{1,57}... | collective-permute-start | bytes 1277960 | tf_op jit(solution)/shard_map/ppermute | solution.py:96
  52.8 14.0 %collective-permute-start.6 = (bf16[4,104,512]{2,0,1:T(4,128)(2,1)}, bf16[4,104,512]{2,0,1:T(4,128)(2,1)}, u32[]{:S(2)}, u32[]{:S(2)}) collective-permute-start(bf16[4,104,512]{2,0,1:T(4,128)(2,1)} %pad_maximum_fusion), channel_id=1, source_target_pairs={{0,8},{8,0},{16,24},{24,16},{32,40},{40,32},{48,56},{56,48},{1,9},... | collective-permute-start | bytes 1277960 | tf_op jit(solution)/shard_map/ppermute | solution.py:96
  56.5 4.7 %copy-start.3 = (bf16[2048,1024]{1,0:T(8,128)(2,1)S(1)}, bf16[2048,1024]{1,0:T(8,128)(2,1)}, u32[]{:S(2)}) copy-start(bf16[2048,1024]{1,0:T(8,128)(2,1)} %constant_dynamic-update-slice_fusion) | copy-start | bytes 12582916

commit v3 on v0

v3 whole, which is shorter than its diff:
```python
import functools

import jax
import jax.numpy as jnp
from jax import lax
from jax.experimental import pallas as pl
from jax.experimental.pallas import tpu as pltpu
from jax.sharding import Mesh, PartitionSpec as P

BF = jnp.bfloat16
F32 = jnp.float32
NX, NZ, NY, NC = 4, 8, 4, 2
Z = ("zq", "zp")
CENT = ("y", "core")
N_CENT = NY * NC
LANES = 128
TAIL = 4
VMEM = pl.BlockSpec(memory_space=pltpu.VMEM)
SMEM = pl.BlockSpec(memory_space=pltpu.SMEM)
ANY = pl.BlockSpec(memory_space=pl.ANY)
LIMIT = 40 * 2**20


def dot_nt(a, b):
    return lax.dot_general(a, b, (((1,), (1,)), ((), ())), preferred_element_type=F32)


def params():
    return pltpu.CompilerParams(vmem_limit_bytes=LIMIT)


def cost(flops, read):
    return pl.CostEstimate(flops=flops, bytes_accessed=read, transcendentals=0)


def cut_kernel(place, points, half_out, eighth_out, sem):
    half, eighth = half_out.shape[0], eighth_out.shape[0]
    a = pltpu.make_async_copy(points.at[pl.ds(pl.multiple_of(place[0] * half, half), half)], half_out, sem.at[0])
    b = pltpu.make_async_copy(
        points.at[pl.ds(pl.multiple_of(place[1] * eighth, eighth), eighth)], eighth_out, sem.at[1]
    )
    a.start()
    b.start()
    a.wait()
    b.wait()


def stats_kernel(points, cents, out, top, total):
    step = pl.program_id(0)
    rows = cents[...]
    wide = rows.astype(F32)
    norms = 0.5 * jnp.sum(wide * wide, axis=1, keepdims=True)
    logits = dot_nt(rows, points[...]) - norms
    tile_top = jnp.max(logits, axis=0, keepdims=True)

    @pl.when(step == 0)
    def _():
        top[...] = tile_top
        total[...] = jnp.zeros_like(total)

    old = top[...]
    new = jnp.maximum(old, tile_top)
    total[...] = total[...] * jnp.exp(old - new) + jnp.sum(jnp.exp(logits - new), axis=0, keepdims=True)
    top[...] = new

    @pl.when(step == pl.num_programs(0) - 1)
    def _():
        groups = top.shape[1] // LANES
        tile = jnp.concatenate(
            [r[:, g * LANES : (g + 1) * LANES] for r in (top[...], total[...]) for g in range(groups)], axis=0
        )
        out[...] = jnp.broadcast_to(tile[None], out.shape)


def weighted(place, stats, own, near, cents, norms, weights):
    x, core = place[2], place[0]
    groups = stats.shape[1] // 2

    def lse_of(source):
        part = stats[pl.ds(source * N_CENT, N_CENT)]
        m, s = part[:, :groups], part[:, groups:]
        high = jnp.max(m, axis=0)
        return high + jnp.log(jnp.sum(s * jnp.exp(m - high[None]), axis=0))

    pieces = []
    lse = lse_of(x)
    pieces.append((own, [lse[g : g + 1] for g in range(groups)]))
    for k, mine, other in near:
        lse = lse_of(lax.rem(x + NX - k, NX))
        low, high = lse[: groups // 2], lse[groups // 2 :]
        first = core == 0
        for ref, part in ((mine, jnp.where(first, low, high)), (other, jnp.where(first, high, low))):
            pieces.append((ref, [part[g : g + 1] for g in range(groups // 2)]))
    rows = cents[...]
    shift = norms[...]
    counts = jnp.zeros((rows.shape[0], LANES), F32)
    at = 0
    numer = None
    for ref, parts in pieces:
        block = ref[...]
        logits = dot_nt(rows, block)
        chunk = []
        for g, part in enumerate(parts):
            w = jnp.exp(logits[:, g * LANES : (g + 1) * LANES] - shift - part).astype(BF)
            counts += w.astype(F32)
            chunk.append(w)
        term = jnp.dot(jnp.concatenate(chunk, axis=1), block, preferred_element_type=F32)
        numer = term if numer is None else numer + term
    return numer, counts


def row_counts(counts, block, height):
    part = counts[block * height : (block + 1) * height]
    part = jnp.concatenate([part, jnp.zeros((LANES - height, LANES), F32)], axis=0)
    return jnp.sum(part.T, axis=0, keepdims=True)


def close(values, first, second):
    height, width = values.shape
    first = jnp.concatenate([first] * (width // LANES), axis=1)
    second = jnp.concatenate([second] * (width // LANES), axis=1)
    last = values[height - 8 :]
    row = lax.broadcasted_iota(jnp.int32, last.shape, 0)
    last = jnp.where(row == 8 - TAIL, first, jnp.where(row == 9 - TAIL, second, jnp.where(row > 9 - TAIL, 0.0, last)))
    return jnp.concatenate([values[: height - 8], last], axis=0)


def split(counts):
    high = counts.astype(BF).astype(F32)
    return high, counts - high


def give_kernel(place, stats, own, a1, a3, a2, b1, b3, b2, cents, norms, left, right, weights):
    numer, counts = weighted(place, stats, own, ((1, a1, b1), (3, a3, b3), (2, a2, b2)), cents, norms, weights)
    blocks, height, width = left.shape
    for b in range(blocks):
        high, low = split(row_counts(counts, b, height))
        values = close(numer[b * height : (b + 1) * height], high, low).astype(BF)
        left[b] = values[:, :width]
        right[b] = values[:, width:]


def keep_kernel(place, stats, own, a1, a3, a2, b1, b3, b2, cents, norms, kept, weights):
    numer, counts = weighted(place, stats, own, ((1, a1, b1), (3, a3, b3), (2, a2, b2)), cents, norms, weights)
    blocks, height, width = kept.shape
    for b in range(blocks):
        total = row_counts(counts, b, height)
        kept[b] = close(numer[b * height : (b + 1) * height], total, jnp.zeros_like(total))


def merge_kernel(kept, left, right, send):
    blocks, height, width = kept.shape
    at = height - TAIL
    for b in range(blocks):
        for h, got in ((0, left), (1, right)):
            half = width // 2
            mine = kept[b, :, h * half : (h + 1) * half]
            theirs = got[b].astype(F32)
            values = mine + theirs
            tail = values[height - 8 :]
            counts = tail[8 - TAIL : 9 - TAIL, :LANES] + tail[9 - TAIL : 10 - TAIL, :LANES]
            high, low = split(counts)
            values = close(values, high, low).astype(BF)
            for c in range(half // LANES):
                send[b * N_CENT + h * (half // LANES) + c] = values[:, c * LANES : (c + 1) * LANES]


def final_kernel(got, out, scratch):
    n, height, _ = got.shape
    slot = height - TAIL
    for c in range(N_CENT):
        values = got[c].astype(F32)
        for i in range(1, n // N_CENT):
            values += got[i * N_CENT + c].astype(F32)
        tail = values[height - 8 :]
        counts = tail[8 - TAIL : 9 - TAIL] + tail[9 - TAIL : 10 - TAIL] + 1.0
        column = jnp.broadcast_to(counts, (LANES, LANES)).T
        scratch[c * slot : (c + 1) * slot] = (values / column[:height])[:slot]
    out[...] = scratch[...].astype(BF)


def body(points, centroids):
    rows, dim = centroids.shape
    pts = points.shape[0]
    slot = rows // (NX * NZ)
    height = slot + TAIL
    mine = rows // NX
    half, eighth = pts // NC, pts // N_CENT
    x, y, parity, core = (lax.axis_index(a) for a in ("x", "y", "zp", "core"))
    place = jnp.stack([core, core * NY + y, x]).astype(jnp.int32)
    shape = jax.ShapeDtypeStruct

    own_half, own_eighth = pl.pallas_call(
        cut_kernel,
        out_shape=(shape((half, dim), BF), shape((eighth, dim), BF)),
        in_specs=[SMEM, ANY],
        out_specs=(VMEM, VMEM),
        scratch_shapes=[pltpu.SemaphoreType.DMA((2,))],
        compiler_params=params(),
        cost_estimate=cost(0, 2 * half * dim * 2),
        name="cut",
    )(place, points)

    def ring(a, k):
        return lax.ppermute(a, "x", [(i, (i + k) % NX) for i in range(NX)])

    far = ring(own_eighth, 2)
    shards = {1: ring(own_half, 1), 3: ring(own_half, 3)}

    tile = 640
    send_stats = pl.pallas_call(
        stats_kernel,
        grid=(rows // tile,),
        out_shape=shape((NX * N_CENT, 2 * pts // LANES, LANES), F32),
        in_specs=[pl.BlockSpec((pts, dim), lambda i: (0, 0)), pl.BlockSpec((tile, dim), lambda i: (i, 0))],
        out_specs=pl.BlockSpec((NX * N_CENT, 2 * pts // LANES, LANES), lambda i: (0, 0, 0)),
        scratch_shapes=[pltpu.VMEM((1, pts), F32), pltpu.VMEM((1, pts), F32)],
        compiler_params=params(),
        cost_estimate=cost(2 * pts * rows * dim, rows * dim * 2),
        name="stats",
    )(points, centroids)
    far, centroids, send_stats = lax.optimization_barrier((far, centroids, send_stats))
    stats = lax.all_to_all(send_stats, ("x", *CENT), 0, 0)

    slices = [far] + [lax.ppermute(far, "y", [(i, i ^ k) for i in range(NY)]) for k in range(1, NY)]
    order = jnp.stack(slices)
    shards[2] = jnp.concatenate([lax.dynamic_index_in_dim(order, y ^ k, 0, keepdims=False) for k in range(NY)], axis=0)
    shards, stats = lax.optimization_barrier((shards, stats))
    other = {k: lax.ppermute(a, "core", [(0, 1), (1, 0)]) for k, a in shards.items()}

    blocks = lax.dynamic_slice_in_dim(centroids, x * mine, mine, 0).reshape(NZ // 2, 2, slot, dim)

    def pick(p):
        part = jnp.pad(lax.dynamic_index_in_dim(blocks, p, 1, keepdims=False), ((0, 0), (0, TAIL), (0, 0)))
        part = part.reshape(-1, dim)
        return part, 0.5 * jnp.sum(jnp.square(part.astype(F32)), axis=1, keepdims=True)

    pieces = (points, shards[1], shards[3], shards[2], other[1], other[3], other[2])
    work = NZ // 2 * height
    total = NX * pts

    def call(kernel, p, out_shape):
        return pl.pallas_call(
            kernel,
            out_shape=out_shape,
            in_specs=[SMEM] + [VMEM] * 10,
            out_specs=jax.tree.map(lambda _: VMEM, out_shape),
            scratch_shapes=[pltpu.VMEM((8, LANES), BF)],
            compiler_params=params(),
            cost_estimate=cost(4 * work * total * dim, total * dim * 2),
            name=kernel.__name__,
        )(place, stats, *pieces, *pick(p))

    n_blocks = NZ // 2
    part = shape((n_blocks, height, dim // 2), BF)
    left, right = call(give_kernel, 1 - parity, (part, part))
    got_left = lax.ppermute(left, Z, [(i, i ^ 1) for i in range(NZ)])
    got_right = lax.ppermute(right, Z, [(i, (i + (1 if i % 2 else -1)) % NZ) for i in range(NZ)])
    kept = call(keep_kernel, parity, shape((n_blocks, height, dim), F32))
    send = pl.pallas_call(
        merge_kernel,
        out_shape=shape((n_blocks * N_CENT, height, LANES), BF),
        in_specs=[VMEM] * 3,
        out_specs=VMEM,
        compiler_params=params(),
        name="merge",
    )(kept, got_left, got_right)
    got = lax.all_to_all(send, ("zq", *CENT), 0, 0)
    return pl.pallas_call(
        final_kernel,
        out_shape=shape((N_CENT * slot, LANES), BF),
        in_specs=[VMEM],
        out_specs=VMEM,
        scratch_shapes=[pltpu.VMEM((N_CENT * slot, LANES), F32)],
        compiler_params=params(),
        name="final",
    )(got)


def solution(mesh):
    fine = Mesh(mesh.devices.reshape(NX, NZ // 2, 2, NY, NC), ("x", *Z, *CENT))
    pts = ("x", *Z)
    return jax.shard_map(
        body, mesh=fine, in_specs=(P(pts, None), P(CENT, None)), out_specs=P(pts, CENT), check_vma=False
    )
```

time: 369 us -> 107 us (0.29)
  blocking collectives: 337 us -> 30.5 us
  Pallas kernels: 0 us -> 21.7 us
  starting transfers between devices: 3.05 us -> 23.6 us
  local copies, waits for them, and re-layouts: 2.68 us -> 17.4 us
  matrix products: 12.5 us -> 0 us
  waiting for transfers between devices: 0.01 us -> 12.5 us
  other arithmetic: 12.1 us -> 0.61 us
    unnamed x2 -> x0, blocking collectives: 270 us -> none
    pallas_call x0 -> x6, Pallas kernels: none -> 21.7 us  [the longest x2 13.5 us: call(): pl.pallas_call(kernel, out_shape=out_shape, in_specs=[SMEM] + [VMEM] * 10...]
    ppermute x0 -> x11, starting transfers between devices: none -> 15.6 us  [the longest x1 5.61 us: body(): lax.ppermute(right, Z, [(i, (i + (1 if i % 2 else -1)) % NZ) for i in ran...]
    pmax x1 -> x0, blocking collectives: 15 us -> none  [body(): row_top = lax.pmax(jnp.max(logits, axis=1), 'cent')]
    psum x1 -> x0, blocking collectives: 13.1 us -> none  [body(): row_total = lax.psum(jnp.sum(exponent, axis=1), 'cent')]
    dot_general x2 -> x0, matrix products: 12.5 us -> none  [the longest x1 6.6 us: body(): lax.dot_general(weights, points, (((0,), (0,)), ((), ())), preferred_elem...]
    reduce_sum x3 -> x1, other arithmetic: 11.9 us -> 0.42 us  [pick(): jnp.sum(jnp.square(part.astype(F32)), axis=1, keepdims=True)]
    all_to_all x1, blocking collectives: 38.7 us -> 30.5 us  [body(): got = lax.all_to_all(send, ('zq', *CENT), 0, 0)]
  transfers between devices with their start and end apart: 2 -> 12, of which waited for: 0 -> 3; matrix products, arithmetic and copies ran while one was open for 0% -> 8% of each run, Pallas kernels for 0% -> 12%
where the time goes in v3:
time: 107 us
  blocking collectives  30.5 us (29%)
  starting transfers between devices  23.6 us (22%)
  Pallas kernels  21.7 us (20%)
  local copies, waits for them, and re-layouts  17.4 us (16%)
  waiting for transfers between devices  12.5 us (12%)
    all_to_all x1, blocking collectives, body(): got = lax.all_to_all(send, ('zq', *CENT), 0, 0)  30.5 us
    pallas_call x2, Pallas kernels, call(): pl.pallas_call(kernel, out_shape=out_shape, in_specs=[SMEM] + [VMEM] * 10...  13.5 us
    unnamed x28, local copies, waits for them, and re-layouts  8.9 us
    all_to_all x1, starting transfers between devices, body(): stats = lax.all_to_all(send_stats, ('x', *CENT), 0, 0)  8 us
    all_to_all x1, waiting for transfers between devices, body(): stats = lax.all_to_all(send_stats, ('x', *CENT), 0, 0)  7.49 us
    pallas_call x1, Pallas kernels, body(): pl.pallas_call(stats_kernel, grid=(rows // tile,), out_shape=shape((NX *...  6.39 us
    ppermute x1, starting transfers between devices, body(): lax.ppermute(right, Z, [(i, (i + (1 if i % 2 else -1)) % NZ) for i in ran...  5.61 us
    ppermute x3, starting transfers between devices, ring(): return lax.ppermute(a, 'x', [(i, (i + k) % NX) for i in range(NX)])  5.12 us
  transfers between devices with their start and end apart: 12, of which 3 were waited for; matrix products, arithmetic and copies ran while one was open for 8% of the time, Pallas kernels for 12%

profile of v3, /device:TPU:1, one launch (start us, length us, event | category | flops | bytes accessed | tf_op | source)
XLA Modules:
  0.0 106.6 jit_solution(8569742409920726265)
XLA Ops:
  0.1 1.2 %copy-done = bf16[512,1024]{1,0:T(8,128)(2,1)S(1)} copy-done((bf16[512,1024]{1,0:T(8,128)(2,1)S(1)}, bf16[512,1024]{1,0:T(8,128)(2,1)}, u32[]{:S(2)}) %copy-start) | copy-done | bytes 1048600
  2.1 2.1 %collective-permute-start = (bf16[256,1024]{1,0:T(8,128)(2,1)S(1)}, bf16[256,1024]{1,0:T(8,128)(2,1)S(1)}, u32[]{:S(2)}, u32[]{:S(2)}) collective-permute-start(bf16[256,1024]{1,0:T(8,128)(2,1)S(1)} %get-tuple-element.16), channel_id=1, source_target_pairs={{0,64},{64,128},{128,192},{192,0},{1,65},{65,129},{129,193},{193,1... | collective-permute-start | bytes 1572872 | tf_op jit(solution)/shard_map/ppermute | solution.py:205
  4.2 1.4 %collective-permute-start.5 = (bf16[256,1024]{1,0:T(8,128)(2,1)S(1)}, bf16[256,1024]{1,0:T(8,128)(2,1)S(1)}, u32[]{:S(2)}, u32[]{:S(2)}) collective-permute-start(bf16[256,1024]{1,0:T(8,128)(2,1)S(1)} %get-tuple-element.16), channel_id=1, source_target_pairs={{0,192},{64,0},{128,64},{192,128},{1,193},{65,1},{129,65},{193,129... | collective-permute-start | bytes 1572872 | tf_op jit(solution)/shard_map/ppermute | solution.py:205
  5.6 1.6 %collective-permute-start.1 = (bf16[64,1024]{1,0:T(8,128)(2,1)S(1)}, bf16[64,1024]{1,0:T(8,128)(2,1)S(1)}, u32[]{:S(2)}, u32[]{:S(2)}) collective-permute-start(bf16[64,1024]{1,0:T(8,128)(2,1)S(1)} %get-tuple-element.17), channel_id=1, source_target_pairs={{0,128},{64,192},{128,0},{192,64},{1,129},{65,193},{129,1},{193,65... | collective-permute-start | bytes 393224 | tf_op jit(solution)/shard_map/ppermute | solution.py:205
  7.2 2.9 %copy-done.2 = bf16[3200,1024]{1,0:T(8,128)(2,1)S(1)} copy-done((bf16[3200,1024]{1,0:T(8,128)(2,1)S(1)}, bf16[3200,1024]{1,0:T(8,128)(2,1)}, u32[]{:S(2)}) %copy-start.2) | copy-done | bytes 6553624
  10.1 6.4 %stats.1 = f32[32,8,128]{2,1,0:T(8,128)} custom-call(bf16[512,1024]{1,0:T(8,128)(2,1)S(1)} %copy-done, bf16[3200,1024]{1,0:T(8,128)(2,1)S(1)} %copy-done.2), custom_call_target="tpu_custom_call" | custom-call | flops 3355443200 | bytes 6553600 | tf_op jit(solution)/shard_map/stats/pallas_call | solution.py:211
  16.5 4.3 %collective-permute-done.1 = bf16[64,1024]{1,0:T(8,128)(2,1)S(1)} collective-permute-done((bf16[64,1024]{1,0:T(8,128)(2,1)S(1)}, bf16[64,1024]{1,0:T(8,128)(2,1)S(1)}, u32[]{:S(2)}, u32[]{:S(2)}) %collective-permute-start.1) | collective-permute-done | bytes 131104 | tf_op jit(solution)/shard_map/ppermute | solution.py:205
  20.8 1.3 %collective-permute-start.2 = (bf16[64,1024]{1,0:T(8,128)(2,1)S(1)}, bf16[64,1024]{1,0:T(8,128)(2,1)S(1)}, u32[]{:S(2)}, u32[]{:S(2)}) collective-permute-start(bf16[64,1024]{1,0:T(8,128)(2,1)S(1)} %collective-permute-done.1), channel_id=1, source_target_pairs={{0,2},{2,0},{4,6},{6,4},{1,3},{3,1},{5,7},{7,5},{8,10},{10,8},{12,... | collective-permute-start | bytes 393224 | tf_op jit(solution)/shard_map/ppermute | solution.py:225
  22.1 2.6 %collective-permute-start.3 = (bf16[64,1024]{1,0:T(8,128)(2,1)S(1)}, bf16[64,1024]{1,0:T(8,128)(2,1)S(1)}, u32[]{:S(2)}, u32[]{:S(2)}) collective-permute-start(bf16[64,1024]{1,0:T(8,128)(2,1)S(1)} %collective-permute-done.1), channel_id=1, source_target_pairs={{0,4},{2,6},{4,0},{6,2},{1,5},{3,7},{5,1},{7,3},{8,12},{10,14},{12... | collective-permute-start | bytes 393224 | tf_op jit(solution)/shard_map/ppermute | solution.py:225
  24.7 8.0 %all-to-all-start = ((f32[32,8,128]{2,1,0:T(8,128)}), f32[32,8,128]{2,1,0:T(8,128)S(1)}, u32[]{:S(2)}, u32[]{:S(2)}) async-start(f32[32,8,128]{2,1,0:T(8,128)} %stats.1), calls=%async_computation | async-start | bytes 262144 | tf_op jit(solution)/shard_map/all_to_all | solution.py:223
  32.9 7.5 %all-to-all-done.stats = f32[32,8,128]{2,1,0:T(8,128)S(1)} async-done(((f32[32,8,128]{2,1,0:T(8,128)}), f32[32,8,128]{2,1,0:T(8,128)S(1)}, u32[]{:S(2)}, u32[]{:S(2)}) %all-to-all-start) | async-done | bytes 131104 | tf_op jit(solution)/shard_map/all_to_all | solution.py:223
  41.4 2.7 %constant_dynamic-slice_fusion = bf16[800,1024]{1,0:T(8,128)(2,1)} fusion(bf16[3200,1024]{1,0:T(8,128)(2,1)} %cents.1, s32[]{:T(128)S(6)} %select_n.27), kind=kLoop, calls=%fused_computation.10 | loop fusion | bytes 3276804 | tf_op jit(solution)/shard_map/dynamic_slice | solution.py:231
  44.2 2.5 %reshape.39 = bf16[4,2,100,1024]{3,2,1,0:T(8,128)(2,1)} reshape(bf16[800,1024]{1,0:T(8,128)(2,1)} %constant_dynamic-slice_fusion) | data formatting | bytes 3276800 | tf_op jit(solution)/shard_map/reshape | solution.py:231
  46.7 1.6 %dynamic-slice_bitcast_fusion = (bf16[4,100,1024]{2,1,0:T(8,128)(2,1)S(1)}, bf16[4,100,1024]{2,1,0:T(8,128)(2,1)S(1)}) fusion(bf16[4,2,100,1024]{3,2,1,0:T(8,128)(2,1)} %reshape.39, s32[]{:T(128)S(6)} %select_n.29, s32[]{:T(128)S(6)} %select_n.28), kind=kLoop, calls=%fused_computation.2 | loop fusion | bytes 3276808 | tf_op jit(solution)/shard_map/jit(dynamic_index_in_dim)/squeeze | solution.py:234
  49.7 1.2 %pad.8 = bf16[4,104,1024]{2,1,0:T(8,128)(2,1)S(1)} pad(bf16[4,100,1024]{2,1,0:T(8,128)(2,1)} %copy-done.13, bf16[]{:T(256)} %constant.49.clone.1), padding=0_0x0_4x0_0 | pad | bytes 1671170 | tf_op jit(solution)/shard_map/jit(_pad)/pad | solution.py:234
  51.0 7.2 %give_kernel.1 = (bf16[4,104,512]{2,1,0:T(8,128)(2,1)}, bf16[4,104,512]{2,1,0:T(8,128)(2,1)}) custom-call(s32[3]{0:T(128)S(1)} %pad_add_fusion.place, f32[32,8,128]{2,1,0:T(8,128)S(1)} %all-to-all-done.stats, bf16[512,1024]{1,0:T(8,128)(2,1)S(1)} %copy-done.1, bf16[256,1024]{1,0:T(8,128)(2,1)S(1)} %collective-permute-done.a1, ...), custom_call_target="tpu_custom_call" | custom-call | flops 3489660928 | bytes 4194304 | tf_op jit(solution)/shard_map/give_kernel/pallas_call | solution.py:243
  58.2 5.6 %collective-permute-start.10 = (bf16[4,104,512]{2,1,0:T(8,128)(2,1)}, bf16[4,104,512]{2,1,0:T(8,128)(2,1)S(1)}, u32[]{:S(2)}, u32[]{:S(2)}) collective-permute-start(bf16[4,104,512]{2,1,0:T(8,128)(2,1)} %get-tuple-element.26), channel_id=1, source_target_pairs={{0,56},{8,16},{16,8},{24,32},{32,24},{40,48},{48,40},{56,0},{1,57}... | collective-permute-start | bytes 1277960 | tf_op jit(solution)/shard_map/ppermute | solution.py:258
  64.1 0.9 copy-done.4
  65.0 1.0 copy-done.6
  66.0 1.0 copy-done.8
  67.1 1.0 copy-done.10
  68.1 6.3 %keep_kernel.1.kept = f32[4,104,1024]{2,1,0:T(8,128)S(1)} custom-call(s32[3]{0:T(128)S(1)} %pad_add_fusion.place, f32[32,8,128]{2,1,0:T(8,128)S(1)} %copy-done.4, bf16[512,1024]{1,0:T(8,128)(2,1)S(1)} %copy-done.1, bf16[256,1024]{1,0:T(8,128)(2,1)S(1)} %copy-done.6, bf16[256,1024]{1,0:T(8,128)(2,1)S(1)} %copy-done.8, ...), custom_call_target="tpu_custom_call" | custom-call | flops 3489660928 | bytes 4194304 | tf_op jit(solution)/shard_map/keep_kernel/pallas_call | solution.py:243
  75.2 30.5 %all_to_all.10.got = bf16[32,104,128]{2,1,0:T(8,128)(2,1)S(1)} all-to-all(bf16[32,104,128]{2,1,0:T(8,128)(2,1)S(1)} %merge.1), channel_id=1, replica_groups=mesh['x'=4,'zq'=4,'zp'=2,'y'=4,'core'=2] {'zq','y','core'}, dimensions={0} | all-to-all | bytes 1703936 | tf_op jit(solution)/shard_map/all_to_all | solution.py:268
  105.7 0.9 final.1
  (49 shorter events, 4.5 us)
Async XLA Ops:
  0.1 1.2 %copy-start = (bf16[512,1024]{1,0:T(8,128)(2,1)S(1)}, bf16[512,1024]{1,0:T(8,128)(2,1)}, u32[]{:S(2)}) copy-start(bf16[512,1024]{1,0:T(8,128)(2,1)} %own.3) | copy-start | bytes 3145732
  2.1 38.3 %collective-permute-start = (bf16[256,1024]{1,0:T(8,128)(2,1)S(1)}, bf16[256,1024]{1,0:T(8,128)(2,1)S(1)}, u32[]{:S(2)}, u32[]{:S(2)}) collective-permute-start(bf16[256,1024]{1,0:T(8,128)(2,1)S(1)} %get-tuple-element.16), channel_id=1, source_target_pairs={{0,64},{64,128},{128,192},{192,0},{1,65},{65,129},{129,193},{193,1... | collective-permute-start | bytes 1572872 | tf_op jit(solution)/shard_map/ppermute | solution.py:205
  4.2 36.2 %collective-permute-start.5 = (bf16[256,1024]{1,0:T(8,128)(2,1)S(1)}, bf16[256,1024]{1,0:T(8,128)(2,1)S(1)}, u32[]{:S(2)}, u32[]{:S(2)}) collective-permute-start(bf16[256,1024]{1,0:T(8,128)(2,1)S(1)} %get-tuple-element.16), channel_id=1, source_target_pairs={{0,192},{64,0},{128,64},{192,128},{1,193},{65,1},{129,65},{193,129... | collective-permute-start | bytes 1572872 | tf_op jit(solution)/shard_map/ppermute | solution.py:205
  5.6 15.2 %collective-permute-start.1 = (bf16[64,1024]{1,0:T(8,128)(2,1)S(1)}, bf16[64,1024]{1,0:T(8,128)(2,1)S(1)}, u32[]{:S(2)}, u32[]{:S(2)}) collective-permute-start(bf16[64,1024]{1,0:T(8,128)(2,1)S(1)} %get-tuple-element.17), channel_id=1, source_target_pairs={{0,128},{64,192},{128,0},{192,64},{1,129},{65,193},{129,1},{193,65... | collective-permute-start | bytes 393224 | tf_op jit(solution)/shard_map/ppermute | solution.py:205
  7.2 2.9 %copy-start.2 = (bf16[3200,1024]{1,0:T(8,128)(2,1)S(1)}, bf16[3200,1024]{1,0:T(8,128)(2,1)}, u32[]{:S(2)}) copy-start(bf16[3200,1024]{1,0:T(8,128)(2,1)} %cents.1) | copy-start | bytes 19660804
  20.8 11.9 %collective-permute-start.2 = (bf16[64,1024]{1,0:T(8,128)(2,1)S(1)}, bf16[64,1024]{1,0:T(8,128)(2,1)S(1)}, u32[]{:S(2)}, u32[]{:S(2)}) collective-permute-start(bf16[64,1024]{1,0:T(8,128)(2,1)S(1)} %collective-permute-done.1), channel_id=1, source_target_pairs={{0,2},{2,0},{4,6},{6,4},{1,3},{3,1},{5,7},{7,5},{8,10},{10,8},{12,... | collective-permute-start | bytes 393224 | tf_op jit(solution)/shard_map/ppermute | solution.py:225
  22.1 10.6 %collective-permute-start.3 = (bf16[64,1024]{1,0:T(8,128)(2,1)S(1)}, bf16[64,1024]{1,0:T(8,128)(2,1)S(1)}, u32[]{:S(2)}, u32[]{:S(2)}) collective-permute-start(bf16[64,1024]{1,0:T(8,128)(2,1)S(1)} %collective-permute-done.1), channel_id=1, source_target_pairs={{0,4},{2,6},{4,0},{6,2},{1,5},{3,7},{5,1},{7,3},{8,12},{10,14},{12... | collective-permute-start | bytes 393224 | tf_op jit(solution)/shard_map/ppermute | solution.py:225
  24.7 8.0 %collective-permute-start.4 = (bf16[64,1024]{1,0:T(8,128)(2,1)S(1)}, bf16[64,1024]{1,0:T(8,128)(2,1)S(1)}, u32[]{:S(2)}, u32[]{:S(2)}) collective-permute-start(bf16[64,1024]{1,0:T(8,128)(2,1)S(1)} %collective-permute-done.1), channel_id=1, source_target_pairs={{0,6},{2,4},{4,2},{6,0},{1,7},{3,5},{5,3},{7,1},{8,14},{10,12},{12... | collective-permute-start | bytes 393224 | tf_op jit(solution)/shard_map/ppermute | solution.py:225
  24.7 15.7 %all-to-all-start = ((f32[32,8,128]{2,1,0:T(8,128)}), f32[32,8,128]{2,1,0:T(8,128)S(1)}, u32[]{:S(2)}, u32[]{:S(2)}) async-start(f32[32,8,128]{2,1,0:T(8,128)} %stats.1), calls=%async_computation | async-start | bytes 262144 | tf_op jit(solution)/shard_map/all_to_all | solution.py:223
  40.4 10.5 %copy-start.3 = (f32[32,8,128]{2,1,0:T(8,128)}, f32[32,8,128]{2,1,0:T(8,128)S(1)}, u32[]{:S(2)}) copy-start(f32[32,8,128]{2,1,0:T(8,128)S(1)} %all-to-all-done.stats) | copy-start | bytes 393220
  40.4 10.5 %copy-start.5 = (bf16[256,1024]{1,0:T(8,128)(2,1)}, bf16[256,1024]{1,0:T(8,128)(2,1)S(1)}, u32[]{:S(2)}) copy-start(bf16[256,1024]{1,0:T(8,128)(2,1)S(1)} %collective-permute-done.a1) | copy-start | bytes 1572868
  40.4 10.5 %copy-start.7 = (bf16[256,1024]{1,0:T(8,128)(2,1)}, bf16[256,1024]{1,0:T(8,128)(2,1)S(1)}, u32[]{:S(2)}) copy-start(bf16[256,1024]{1,0:T(8,128)(2,1)S(1)} %collective-permute-done.5.a3) | copy-start | bytes 1572868
  40.4 10.5 %collective-permute-start.6 = (bf16[256,1024]{1,0:T(8,128)(2,1)S(1)}, bf16[256,1024]{1,0:T(8,128)(2,1)S(1)}, u32[]{:S(2)}, u32[]{:S(2)}) collective-permute-start(bf16[256,1024]{1,0:T(8,128)(2,1)S(1)} %collective-permute-done.a1), channel_id=1, source_target_pairs={{0,1},{1,0},{2,3},{3,2},{4,5},{5,4},{6,7},{7,6},{8,9},{9,8},{10,11... | collective-permute-start | bytes 1572872 | tf_op jit(solution)/shard_map/ppermute | solution.py:229
  40.9 10.0 %collective-permute-start.7 = (bf16[256,1024]{1,0:T(8,128)(2,1)S(1)}, bf16[256,1024]{1,0:T(8,128)(2,1)}, u32[]{:S(2)}, u32[]{:S(2)}) collective-permute-start(bf16[256,1024]{1,0:T(8,128)(2,1)S(1)} %collective-permute-done.5.a3), channel_id=1, source_target_pairs={{0,1},{1,0},{2,3},{3,2},{4,5},{5,4},{6,7},{7,6},{8,9},{9,8},{10,11... | collective-permute-start | bytes 1572872 | tf_op jit(solution)/shard_map/ppermute | solution.py:229
  41.0 9.9 %collective-permute-start.8 = (bf16[256,1024]{1,0:T(8,128)(2,1)S(1)}, bf16[256,1024]{1,0:T(8,128)(2,1)}, u32[]{:S(2)}, u32[]{:S(2)}) collective-permute-start(bf16[256,1024]{1,0:T(8,128)(2,1)S(1)} %pad_maximum_fusion.1.a2), channel_id=1, source_target_pairs={{0,1},{1,0},{2,3},{3,2},{4,5},{5,4},{6,7},{7,6},{8,9},{9,8},{10,11... | collective-permute-start | bytes 1572872 | tf_op jit(solution)/shard_map/ppermute | solution.py:229
  48.3 1.2 %copy-start.13 = (bf16[4,100,1024]{2,1,0:T(8,128)(2,1)}, bf16[4,100,1024]{2,1,0:T(8,128)(2,1)S(1)}, u32[]{:S(2)}) copy-start(bf16[4,100,1024]{2,1,0:T(8,128)(2,1)S(1)} %get-tuple-element.27) | copy-start | bytes 2457604
  48.3 2.7 %copy-start.1 = (bf16[512,1024]{1,0:T(8,128)(2,1)S(1)}, bf16[512,1024]{1,0:T(8,128)(2,1)}, u32[]{:S(2)}) copy-start(bf16[512,1024]{1,0:T(8,128)(2,1)} %own.3) | copy-start | bytes 3145732
  50.9 7.3 %copy-start.9 = (bf16[256,1024]{1,0:T(8,128)(2,1)}, bf16[256,1024]{1,0:T(8,128)(2,1)S(1)}, u32[]{:S(2)}) copy-start(bf16[256,1024]{1,0:T(8,128)(2,1)S(1)} %collective-permute-done.6.b1) | copy-start | bytes 1572868
  51.0 12.8 %copy-start.12 = (bf16[4,100,1024]{2,1,0:T(8,128)(2,1)S(1)}, bf16[4,100,1024]{2,1,0:T(8,128)(2,1)}, u32[]{:S(2)}) copy-start(bf16[4,100,1024]{2,1,0:T(8,128)(2,1)} %copy-done.11) | copy-start | bytes 2457604
  58.2 16.2 %collective-permute-start.10 = (bf16[4,104,512]{2,1,0:T(8,128)(2,1)}, bf16[4,104,512]{2,1,0:T(8,128)(2,1)S(1)}, u32[]{:S(2)}, u32[]{:S(2)}) collective-permute-start(bf16[4,104,512]{2,1,0:T(8,128)(2,1)} %get-tuple-element.26), channel_id=1, source_target_pairs={{0,56},{8,16},{16,8},{24,32},{32,24},{40,48},{48,40},{56,0},{1,57}... | collective-permute-start | bytes 1277960 | tf_op jit(solution)/shard_map/ppermute | solution.py:258
  63.8 11.3 %collective-permute-start.9 = (bf16[4,104,512]{2,1,0:T(8,128)(2,1)}, bf16[4,104,512]{2,1,0:T(8,128)(2,1)S(1)}, u32[]{:S(2)}, u32[]{:S(2)}) collective-permute-start(bf16[4,104,512]{2,1,0:T(8,128)(2,1)} %get-tuple-element.25), channel_id=1, source_target_pairs={{0,8},{8,0},{16,24},{24,16},{32,40},{40,32},{48,56},{56,48},{1,9},... | collective-permute-start | bytes 1277960 | tf_op jit(solution)/shard_map/ppermute | solution.py:257
  65.0 1.0 copy-start.6
  66.0 1.0 copy-start.8
  67.1 1.0 copy-start.10
  (2 other events, 1.8 us)

commit v4 on v3

v4 whole, which is shorter than its diff:
```python
import functools

import jax
import jax.numpy as jnp
from jax import lax
from jax.experimental import pallas as pl
from jax.experimental.pallas import tpu as pltpu
from jax.sharding import Mesh, PartitionSpec as P

BF = jnp.bfloat16
F32 = jnp.float32
NX, NZ, NY, NC = 4, 8, 4, 2
Z = ("zq", "zp")
CENT = ("y", "core")
N_CENT = NY * NC
LANES = 128
TAIL = 4
VMEM = pl.BlockSpec(memory_space=pltpu.VMEM)
SMEM = pl.BlockSpec(memory_space=pltpu.SMEM)
ANY = pl.BlockSpec(memory_space=pl.ANY)
WIDE = 58 * 2**20
WIDEST = 125 * 2**19
CHUNKS = 10
CUT = 256


def dot_nt(a, b):
    return lax.dot_general(a, b, (((1,), (1,)), ((), ())), preferred_element_type=F32)


def params(limit=24 * 2**20):
    return pltpu.CompilerParams(vmem_limit_bytes=limit)


def cost(flops, read):
    return pl.CostEstimate(flops=flops, bytes_accessed=read, transcendentals=0)


def cut_kernel(place, points, half_out, eighth_out, sem):
    half, eighth = half_out.shape[0], eighth_out.shape[0]
    a = pltpu.make_async_copy(points.at[pl.ds(pl.multiple_of(place[0] * half, half), half)], half_out, sem.at[0])
    b = pltpu.make_async_copy(
        points.at[pl.ds(pl.multiple_of(place[1] * eighth, eighth), eighth)], eighth_out, sem.at[1]
    )
    a.start()
    b.start()
    a.wait()
    b.wait()


def stats_kernel(points, cents, out, held, sems):
    chunk = held.shape[0] // CHUNKS
    copies = [
        pltpu.make_async_copy(cents.at[pl.ds(i * chunk, chunk)], held.at[pl.ds(i * chunk, chunk)], sems.at[i])
        for i in range(CHUNKS)
    ]
    for copy in copies:
        copy.start()
    pts = points[...]
    tops, totals = [], []
    for i, copy in enumerate(copies):
        copy.wait()
        rows = held[i * chunk : (i + 1) * chunk]
        wide = rows.astype(F32)
        norms = 0.5 * jnp.sum(wide * wide, axis=1, keepdims=True)
        logits = dot_nt(rows, pts) - norms
        top = jnp.max(logits, axis=0, keepdims=True)
        tops.append(top)
        totals.append(jnp.sum(jnp.exp(logits - top), axis=0, keepdims=True))
    top = functools.reduce(jnp.maximum, tops)
    total = sum(s * jnp.exp(t - top) for s, t in zip(totals, tops))
    groups = top.shape[1] // LANES
    tile = jnp.concatenate([r[:, g * LANES : (g + 1) * LANES] for r in (top, total) for g in range(groups)], axis=0)
    out[...] = jnp.broadcast_to(tile[None], out.shape)


def prep_kernel(place, cents, after, rows_out, norms_out, held, sems):
    _, n_rows, _ = rows_out.shape
    n_blocks, window, dim = held.shape
    height = 2 * n_rows // n_blocks
    slot = height - TAIL
    base = place[2] * (n_blocks * slot)
    copies = []
    for b in range(n_blocks):
        at = pl.multiple_of(base + b * slot // 16 * 16, 16)
        copies.append(pltpu.make_async_copy(cents.at[pl.ds(at, window)], held.at[b], sems.at[b]))
    for copy in copies:
        copy.start()
    for q in range(2):
        parts, norms = [], []
        for b in range(q, n_blocks, 2):
            copies[b].wait()
            wide = held[b].astype(F32)[b * slot % 16 :][:slot]
            parts += [wide, jnp.zeros((TAIL, dim), F32)]
            norms += [0.5 * jnp.sum(wide * wide, axis=1, keepdims=True), jnp.full((TAIL, 1), 1e30, F32)]
        rows_out[q] = jnp.concatenate(parts, axis=0).astype(BF)
        norms_out[q] = jnp.concatenate(norms, axis=0)


def lse_of(stats, source):
    groups = stats.shape[1] // 2
    part = stats[pl.ds(source * N_CENT, N_CENT)]
    m, s = part[:, :groups], part[:, groups:]
    high = jnp.max(m, axis=0)
    return high + jnp.log(jnp.sum(s * jnp.exp(m - high[None]), axis=0))


def lse_halves(place, stats, k):
    lse = lse_of(stats, lax.rem(place[2] + NX - k, NX))
    half = lse.shape[0] // 2
    first = place[0] == 0
    return jnp.where(first, lse[:half], lse[half:]), jnp.where(first, lse[half:], lse[:half])


def weighted(pieces, rows, shift, weights):
    counts = jnp.zeros((rows.shape[0], LANES), F32)
    at = 0
    for ref, lse in pieces:
        n = ref.shape[0]
        for c in range(0, n, CUT):
            logits = dot_nt(rows, ref[c : c + CUT])
            for g in range(CUT // LANES):
                row = c // LANES + g
                w = jnp.exp(logits[:, g * LANES : (g + 1) * LANES] - shift - lse[row : row + 1]).astype(BF)
                counts += w.astype(F32)
                weights[:, at + c + g * LANES : at + c + (g + 1) * LANES] = w
        at += n
    numer = None
    at = 0
    for ref, _ in pieces:
        n = ref.shape[0]
        term = jnp.dot(weights[:, at : at + n], ref[...], preferred_element_type=F32)
        numer = term if numer is None else numer + term
        at += n
    return numer, counts


def row_counts(counts, block, height):
    part = counts[block * height : (block + 1) * height]
    part = jnp.concatenate([part, jnp.zeros((LANES - height, LANES), F32)], axis=0)
    return jnp.sum(part.T, axis=0, keepdims=True)


def close(values, first, second):
    height, width = values.shape
    first = jnp.concatenate([first] * (width // LANES), axis=1)
    second = jnp.concatenate([second] * (width // LANES), axis=1)
    last = values[height - 8 :]
    row = lax.broadcasted_iota(jnp.int32, last.shape, 0)
    last = jnp.where(row == 8 - TAIL, first, jnp.where(row == 9 - TAIL, second, jnp.where(row > 9 - TAIL, 0.0, last)))
    return jnp.concatenate([values[: height - 8], last], axis=0)


def split(counts):
    high = counts.astype(BF).astype(F32)
    return high, counts - high


def near_pieces(place, stats, own, a1, a3, b1, b3):
    pieces = [(own, lse_of(stats, place[2]))]
    for k, a, b in ((1, a1, b1), (3, a3, b3)):
        mine, other = lse_halves(place, stats, k)
        pieces += [(a, mine), (b, other)]
    return pieces


def near_kernel(place, stats, rows, norms, own, a1, a3, b1, b3, numer_out, counts_out, weights):
    q = 1 - place[3]
    pieces = near_pieces(place, stats, own, a1, a3, b1, b3)
    numer_out[...], counts_out[...] = weighted(pieces, rows[q], norms[q], weights)


def give_kernel(place, stats, rows, norms, a2, b2, numer, counts, left, right, weights):
    q = 1 - place[3]
    mine, other = lse_halves(place, stats, 2)
    more, more_counts = weighted([(a2, mine), (b2, other)], rows[q], norms[q], weights)
    total, counts = numer[...] + more, counts[...] + more_counts
    blocks, height, width = left.shape
    for b in range(blocks):
        high, low = split(row_counts(counts, b, height))
        values = close(total[b * height : (b + 1) * height], high, low).astype(BF)
        left[b] = values[:, :width]
        right[b] = values[:, width:]


def keep_kernel(place, stats, rows, norms, own, a1, a3, b1, b3, a2, b2, kept, weights):
    q = place[3]
    pieces = near_pieces(place, stats, own, a1, a3, b1, b3)
    mine, other = lse_halves(place, stats, 2)
    numer, counts = weighted(pieces + [(a2, mine), (b2, other)], rows[q], norms[q], weights)
    blocks, height, width = kept.shape
    for b in range(blocks):
        total = row_counts(counts, b, height)
        kept[b] = close(numer[b * height : (b + 1) * height], total, jnp.zeros_like(total))


def merge_kernel(kept, left, right, send):
    blocks, height, width = kept.shape
    at = height - TAIL
    for b in range(blocks):
        for h, got in ((0, left), (1, right)):
            half = width // 2
            mine = kept[b, :, h * half : (h + 1) * half]
            theirs = got[b].astype(F32)
            values = mine + theirs
            tail = values[height - 8 :]
            counts = tail[8 - TAIL : 9 - TAIL, :LANES] + tail[9 - TAIL : 10 - TAIL, :LANES]
            high, low = split(counts)
            values = close(values, high, low).astype(BF)
            for c in range(half // LANES):
                send[b * N_CENT + h * (half // LANES) + c] = values[:, c * LANES : (c + 1) * LANES]


def final_kernel(got, out, scratch):
    n, height, _ = got.shape
    slot = height - TAIL
    for c in range(N_CENT):
        values = got[c].astype(F32)
        for i in range(1, n // N_CENT):
            values += got[i * N_CENT + c].astype(F32)
        tail = values[height - 8 :]
        counts = tail[8 - TAIL : 9 - TAIL] + tail[9 - TAIL : 10 - TAIL] + 1.0
        column = jnp.broadcast_to(counts, (LANES, LANES)).T
        scratch[c * slot : (c + 1) * slot] = (values / column[:height])[:slot]
    out[...] = scratch[...].astype(BF)


def body(points, centroids):
    rows, dim = centroids.shape
    pts = points.shape[0]
    slot = rows // (NX * NZ)
    height = slot + TAIL
    half, eighth = pts // NC, pts // N_CENT
    x, y, parity, core = (lax.axis_index(a) for a in ("x", "y", "zp", "core"))
    place = jnp.stack([core, core * NY + y, x, parity]).astype(jnp.int32)
    shape = jax.ShapeDtypeStruct

    own_half, own_eighth = pl.pallas_call(
        cut_kernel,
        out_shape=(shape((half, dim), BF), shape((eighth, dim), BF)),
        in_specs=[SMEM, ANY],
        out_specs=(VMEM, VMEM),
        scratch_shapes=[pltpu.SemaphoreType.DMA((2,))],
        compiler_params=params(WIDEST),
        cost_estimate=cost(0, 2 * half * dim * 2),
        name="cut",
    )(place, points)

    def ring(a, k):
        return lax.ppermute(a, "x", [(i, (i + k) % NX) for i in range(NX)])

    far = ring(own_eighth, 2)
    near = {1: ring(own_half, 1), 3: ring(own_half, 3)}

    stats_shape = (NX * N_CENT, 2 * pts // LANES, LANES)
    send_stats = pl.pallas_call(
        stats_kernel,
        out_shape=shape(stats_shape, F32),
        in_specs=[VMEM, ANY],
        out_specs=VMEM,
        scratch_shapes=[pltpu.VMEM((rows, dim), BF), pltpu.SemaphoreType.DMA((CHUNKS,))],
        compiler_params=params(WIDE),
        cost_estimate=cost(2 * pts * rows * dim, rows * dim * 2),
        name="stats",
    )(points, centroids)
    stats = lax.all_to_all(send_stats, ("x", *CENT), 0, 0)

    work = NZ // 2 * height
    by_parity, norms = pl.pallas_call(
        prep_kernel,
        out_shape=(shape((2, work, dim), BF), shape((2, work, 1), F32)),
        in_specs=[SMEM, ANY, ANY],
        out_specs=(VMEM, VMEM),
        scratch_shapes=[pltpu.VMEM((NZ, slot + 12, dim), BF), pltpu.SemaphoreType.DMA((NZ,))],
        compiler_params=params(WIDE),
        cost_estimate=cost(0, rows // NX * dim * 2),
        name="prep",
    )(place, centroids, send_stats)

    far, by_parity, norms, stats = lax.optimization_barrier((far, by_parity, norms, stats))
    slices = [far] + [lax.ppermute(far, "y", [(i, i ^ k) for i in range(NY)]) for k in range(1, NY)]
    near, stats = lax.optimization_barrier((near, stats))
    swap = [(0, 1), (1, 0)]
    near_other = {k: lax.ppermute(a, "core", swap) for k, a in near.items()}
    def call(kernel, out_shape, n_points, *args):
        return pl.pallas_call(
            kernel,
            out_shape=out_shape,
            in_specs=[SMEM] + [VMEM] * (3 + len(args)),
            out_specs=jax.tree.map(lambda _: VMEM, out_shape),
            scratch_shapes=[pltpu.VMEM((work, n_points), BF)],
            compiler_params=params(),
            cost_estimate=cost(4 * work * n_points * dim, n_points * dim * 2),
            name=kernel.__name__,
        )(place, stats, by_parity, norms, *args)

    early = (points, near[1], near[3], near_other[1], near_other[3])
    numer = call(near_kernel, (shape((work, dim), F32), shape((work, LANES), F32)), (NX - 1) * pts, *early)
    slices, numer = lax.optimization_barrier((slices, numer))
    slices = jnp.stack(slices)
    a2 = jnp.concatenate([lax.dynamic_index_in_dim(slices, y ^ k, 0, keepdims=False) for k in range(NY)], axis=0)
    b2 = lax.ppermute(a2, "core", swap)
    n_blocks = NZ // 2
    part = shape((n_blocks, height, dim // 2), BF)
    left, right = call(give_kernel, (part, part), pts, a2, b2, *numer)
    got_left = lax.ppermute(left, Z, [(i, i ^ 1) for i in range(NZ)])
    got_right = lax.ppermute(right, Z, [(i, (i + (1 if i % 2 else -1)) % NZ) for i in range(NZ)])
    kept = call(keep_kernel, shape((n_blocks, height, dim), F32), NX * pts, *early, a2, b2)
    send = pl.pallas_call(
        merge_kernel,
        out_shape=shape((n_blocks * N_CENT, height, LANES), BF),
        in_specs=[VMEM] * 3,
        out_specs=VMEM,
        compiler_params=params(),
        name="merge",
    )(kept, got_left, got_right)
    got = lax.all_to_all(send, ("zq", *CENT), 0, 0)
    return pl.pallas_call(
        final_kernel,
        out_shape=shape((N_CENT * slot, LANES), BF),
        in_specs=[VMEM],
        out_specs=VMEM,
        scratch_shapes=[pltpu.VMEM((N_CENT * slot, LANES), F32)],
        compiler_params=params(),
        name="final",
    )(got)


def solution(mesh):
    fine = Mesh(mesh.devices.reshape(NX, NZ // 2, 2, NY, NC), ("x", *Z, *CENT))
    pts = ("x", *Z)
    return jax.shard_map(
        body, mesh=fine, in_specs=(P(pts, None), P(CENT, None)), out_specs=P(pts, CENT), check_vma=False
    )
```

time: 107 us -> 97.4 us (0.910)
  local copies, waits for them, and re-layouts: 17.4 us -> 2.51 us
  Pallas kernels: 21.7 us -> 28.2 us
  waiting for transfers between devices: 12.5 us -> 9.62 us
  blocking collectives: 30.5 us -> 31.7 us
    unnamed x28 -> x10, local copies, waits for them, and re-layouts: 8.9 us -> 2.47 us
    pallas_call x3 -> x5, Pallas kernels: 19.8 us -> 24.5 us  [the longest x3 10.2 us: call(): pl.pallas_call(kernel, out_shape=out_shape, in_specs=[SMEM] + [VMEM] * (3...]
    ppermute x1, waiting for transfers between devices: 0.01 us -> 4.49 us  [body(): lax.ppermute(right, Z, [(i, (i + (1 if i % 2 else -1)) % NZ) for i in ran...]
    all_to_all x1, waiting for transfers between devices: 7.49 us -> 3.16 us  [body(): stats = lax.all_to_all(send_stats, ('x', *CENT), 0, 0)]
    ppermute x3, waiting for transfers between devices: 4.34 us -> 0.01 us  [ring(): return lax.ppermute(a, 'x', [(i, (i + k) % NX) for i in range(NX)])]
    dynamic_slice x1 -> x0, local copies, waits for them, and re-layouts: 2.73 us -> none  [body(): lax.dynamic_slice_in_dim(centroids, x * mine, mine, 0)]
    reshape x1 -> x0, local copies, waits for them, and re-layouts: 2.52 us -> none  [body(): lax.dynamic_slice_in_dim(centroids, x * mine, mine, 0)]
    pallas_call x1, Pallas kernels: 0.77 us -> 2.6 us  [body(): pl.pallas_call(cut_kernel, out_shape=(shape((half, dim), BF), shape((eigh...]
  transfers between devices with their start and end apart: 12 -> 12, of which waited for: 3 -> 4; matrix products, arithmetic and copies ran while one was open for 8% -> 0% of each run, Pallas kernels for 12% -> 23%
where the time goes in v4:
time: 97.4 us; the launch traced here: 97 us
  blocking collectives  31.7 us (33%)
  Pallas kernels  28.2 us (29%)
  starting transfers between devices  24.1 us (25%)
  waiting for transfers between devices  9.62 us (10%)
  local copies, waits for them, and re-layouts  2.51 us (3%)
    all_to_all x1, blocking collectives, body(): got = lax.all_to_all(send, ('zq', *CENT), 0, 0)  31.7 us
    pallas_call x3, Pallas kernels, call(): pl.pallas_call(kernel, out_shape=out_shape, in_specs=[SMEM] + [VMEM] * (3...  10.2 us
    pallas_call x1, Pallas kernels, body(): pl.pallas_call(stats_kernel, out_shape=shape(stats_shape, F32), in_specs=...  9.88 us
    all_to_all x1, starting transfers between devices, body(): stats = lax.all_to_all(send_stats, ('x', *CENT), 0, 0)  7.4 us
    ppermute x3, starting transfers between devices, ring(): return lax.ppermute(a, 'x', [(i, (i + k) % NX) for i in range(NX)])  5.12 us
    ppermute x1, starting transfers between devices, body(): lax.ppermute(right, Z, [(i, (i + (1 if i % 2 else -1)) % NZ) for i in ran...  4.67 us
    pallas_call x1, Pallas kernels, body(): pl.pallas_call(prep_kernel, out_shape=(shape((2, work, dim), BF), shape((...  4.51 us
    ppermute x1, waiting for transfers between devices, body(): lax.ppermute(right, Z, [(i, (i + (1 if i % 2 else -1)) % NZ) for i in ran...  4.49 us
  transfers between devices with their start and end apart: 12, of which 4 were waited for; matrix products, arithmetic and copies ran while one was open for 0% of the time, Pallas kernels for 23%

profile of v4, /device:TPU:1, one launch (start us, length us, event | category | flops | bytes accessed | tf_op | source)
XLA Modules:
  0.0 97.0 jit_solution(12689153320974408949)
XLA Ops:
  0.0 0.6 pad_add_fusion.place
  0.6 2.6 %cut.1 = (bf16[256,1024]{1,0:T(8,128)(2,1)}, bf16[64,1024]{1,0:T(8,128)(2,1)}) custom-call(s32[4]{0:T(128)} %pad_add_fusion.place, bf16[512,1024]{1,0:T(8,128)(2,1)} %own.3), custom_call_target="tpu_custom_call" | custom-call | bytes 1048576 | tf_op jit(solution)/shard_map/cut/pallas_call | solution.py:238
  3.2 3.4 %collective-permute-start.1 = (bf16[256,1024]{1,0:T(8,128)(2,1)}, bf16[256,1024]{1,0:T(8,128)(2,1)S(1)}, u32[]{:S(2)}, u32[]{:S(2)}) collective-permute-start(bf16[256,1024]{1,0:T(8,128)(2,1)} %get-tuple-element.26), channel_id=1, source_target_pairs={{0,192},{64,0},{128,64},{192,128},{1,193},{65,1},{129,65},{193,129... | collective-permute-start | bytes 1572872 | tf_op jit(solution)/shard_map/ppermute | solution.py:250
  6.6 1.7 %collective-permute-start.2 = (bf16[64,1024]{1,0:T(8,128)(2,1)}, bf16[64,1024]{1,0:T(8,128)(2,1)S(1)}, u32[]{:S(2)}, u32[]{:S(2)}) collective-permute-start(bf16[64,1024]{1,0:T(8,128)(2,1)} %get-tuple-element.27), channel_id=1, source_target_pairs={{0,128},{64,192},{128,0},{192,64},{1,129},{65,193},{129,1},{193,65... | collective-permute-start | bytes 393224 | tf_op jit(solution)/shard_map/ppermute | solution.py:250
  8.3 9.9 %stats.1.after = f32[32,8,128]{2,1,0:T(8,128)} custom-call(bf16[512,1024]{1,0:T(8,128)(2,1)} %own.3, bf16[3200,1024]{1,0:T(8,128)(2,1)} %cents.3), custom_call_target="tpu_custom_call" | custom-call | flops 3355443200 | bytes 6553600 | tf_op jit(solution)/shard_map/stats/pallas_call | solution.py:256
  18.2 7.4 %all-to-all-start = ((f32[32,8,128]{2,1,0:T(8,128)}), f32[32,8,128]{2,1,0:T(8,128)S(1)}, u32[]{:S(2)}, u32[]{:S(2)}) async-start(f32[32,8,128]{2,1,0:T(8,128)} %stats.1.after), calls=%async_computation | async-start | bytes 262144 | tf_op jit(solution)/shard_map/all_to_all | solution.py:266
  25.6 4.5 %prep.1 = (bf16[2,416,1024]{2,1,0:T(8,128)(2,1)}, f32[2,416,1]{2,1,0:T(8,128)}) custom-call(s32[4]{0:T(128)} %pad_add_fusion.place, bf16[3200,1024]{1,0:T(8,128)(2,1)} %cents.3, f32[32,8,128]{2,1,0:T(8,128)} %stats.1.after), custom_call_target="tpu_custom_call" | custom-call | bytes 1638400 | tf_op jit(solution)/shard_map/prep/pallas_call | solution.py:269
  30.2 3.2 %all-to-all-done.stats = f32[32,8,128]{2,1,0:T(8,128)S(1)} async-done(((f32[32,8,128]{2,1,0:T(8,128)}), f32[32,8,128]{2,1,0:T(8,128)S(1)}, u32[]{:S(2)}, u32[]{:S(2)}) %all-to-all-start) | async-done | bytes 131104 | tf_op jit(solution)/shard_map/all_to_all | solution.py:266
  33.3 0.5 collective-permute-start.3
  33.9 0.9 collective-permute-start.7
  34.9 1.1 %collective-permute-start.6 = (bf16[64,1024]{1,0:T(8,128)(2,1)S(1)}, bf16[64,1024]{1,0:T(8,128)(2,1)S(1)}, u32[]{:S(2)}, u32[]{:S(2)}) collective-permute-start(bf16[64,1024]{1,0:T(8,128)(2,1)S(1)} %collective-permute-done.2), channel_id=1, source_target_pairs={{0,4},{2,6},{4,0},{6,2},{1,5},{3,7},{5,1},{7,3},{8,12},{10,14},{12... | collective-permute-start | bytes 393224 | tf_op jit(solution)/shard_map/ppermute | solution.py:281
  36.0 1.2 %collective-permute-start.5 = (bf16[64,1024]{1,0:T(8,128)(2,1)S(1)}, bf16[64,1024]{1,0:T(8,128)(2,1)S(1)}, u32[]{:S(2)}, u32[]{:S(2)}) collective-permute-start(bf16[64,1024]{1,0:T(8,128)(2,1)S(1)} %collective-permute-done.2), channel_id=1, source_target_pairs={{0,2},{2,0},{4,6},{6,4},{1,3},{3,1},{5,7},{7,5},{8,10},{10,8},{12,... | collective-permute-start | bytes 393224 | tf_op jit(solution)/shard_map/ppermute | solution.py:281
  37.2 1.4 %copy-done = bf16[2,416,1024]{2,1,0:T(8,128)(2,1)S(1)} copy-done((bf16[2,416,1024]{2,1,0:T(8,128)(2,1)S(1)}, bf16[2,416,1024]{2,1,0:T(8,128)(2,1)}, u32[]{:S(2)}) %copy-start) | copy-done | bytes 1703960
  38.7 1.0 %copy-done.3 = f32[2,416,1]{2,1,0:T(8,128)S(1)} copy-done((f32[2,416,1]{2,1,0:T(8,128)S(1)}, f32[2,416,1]{2,1,0:T(8,128)}, u32[]{:S(2)}) %copy-start.3) | copy-done | bytes 3352
  39.7 3.7 %near_kernel.1 = (f32[416,1024]{1,0:T(8,128)S(1)}, f32[416,128]{1,0:T(8,128)S(1)}) custom-call(s32[4]{0:T(128)S(1)} %copy-done.4, f32[32,8,128]{2,1,0:T(8,128)S(1)} %all-to-all-done.stats, bf16[2,416,1024]{2,1,0:T(8,128)(2,1)S(1)} %copy-done, f32[2,416,1]{2,1,0:T(8,128)S(1)} %copy-done.3, bf16[512,1024]{1,0:T(8,128)(2,1)S(1)} %copy-done.2, ...), custom_call_target="tpu_custom_call" | custom-call | flops 2617245696 | bytes 3145728 | tf_op jit(solution)/shard_map/near_kernel/pallas_call | solution.py:286
  43.6 1.3 %collective-permute-start.8 = (bf16[256,1024]{1,0:T(8,128)(2,1)S(1)}, bf16[256,1024]{1,0:T(8,128)(2,1)S(1)}, u32[]{:S(2)}, u32[]{:S(2)}) collective-permute-start(bf16[256,1024]{1,0:T(8,128)(2,1)S(1)} %pad_maximum_fusion.1.a2), channel_id=1, source_target_pairs={{0,1},{1,0},{2,3},{3,2},{4,5},{5,4},{6,7},{7,6},{8,9},{9,8},{10,11... | collective-permute-start | bytes 1572872 | tf_op jit(solution)/shard_map/ppermute | solution.py:302
  44.9 1.5 %collective-permute-done.8.b2 = bf16[256,1024]{1,0:T(8,128)(2,1)S(1)} collective-permute-done((bf16[256,1024]{1,0:T(8,128)(2,1)S(1)}, bf16[256,1024]{1,0:T(8,128)(2,1)S(1)}, u32[]{:S(2)}, u32[]{:S(2)}) %collective-permute-start.8) | collective-permute-done | bytes 524320 | tf_op jit(solution)/shard_map/ppermute | solution.py:302
  46.5 1.8 %give_kernel.1 = (bf16[4,104,512]{2,1,0:T(8,128)(2,1)S(1)}, bf16[4,104,512]{2,1,0:T(8,128)(2,1)S(1)}) custom-call(s32[4]{0:T(128)S(1)} %copy-done.4, f32[32,8,128]{2,1,0:T(8,128)S(1)} %all-to-all-done.stats, bf16[2,416,1024]{2,1,0:T(8,128)(2,1)S(1)} %copy-done.1, f32[2,416,1]{2,1,0:T(8,128)S(1)} %copy-done.3, bf16[256,1024]{1,0:T(8,128)(2,1)S(1)} %pad_maximum_fusion.1.a2, ...), custom_call_target="tpu_custom_call" | custom-call | flops 872415232 | bytes 1048576 | tf_op jit(solution)/shard_map/give_kernel/pallas_call | solution.py:286
  48.3 1.7 %collective-permute-start.9 = (bf16[4,104,512]{2,1,0:T(8,128)(2,1)S(1)}, bf16[4,104,512]{2,1,0:T(8,128)(2,1)S(1)}, u32[]{:S(2)}, u32[]{:S(2)}) collective-permute-start(bf16[4,104,512]{2,1,0:T(8,128)(2,1)S(1)} %get-tuple-element.45), channel_id=1, source_target_pairs={{0,8},{8,0},{16,24},{24,16},{32,40},{40,32},{48,56},{56,48},{1,9},... | collective-permute-start | bytes 1277960 | tf_op jit(solution)/shard_map/ppermute | solution.py:306
  50.0 4.7 %collective-permute-start.10 = (bf16[4,104,512]{2,1,0:T(8,128)(2,1)S(1)}, bf16[4,104,512]{2,1,0:T(8,128)(2,1)S(1)}, u32[]{:S(2)}, u32[]{:S(2)}) collective-permute-start(bf16[4,104,512]{2,1,0:T(8,128)(2,1)S(1)} %get-tuple-element.46), channel_id=1, source_target_pairs={{0,56},{8,16},{16,8},{24,32},{32,24},{40,48},{48,40},{56,0},{1,57}... | collective-permute-start | bytes 1277960 | tf_op jit(solution)/shard_map/ppermute | solution.py:307
  54.7 4.7 %keep_kernel.1.kept = f32[4,104,1024]{2,1,0:T(8,128)S(1)} custom-call(s32[4]{0:T(128)S(1)} %copy-done.4, f32[32,8,128]{2,1,0:T(8,128)S(1)} %all-to-all-done.stats, bf16[2,416,1024]{2,1,0:T(8,128)(2,1)S(1)} %copy-done.1, f32[2,416,1]{2,1,0:T(8,128)S(1)} %copy-done.3, bf16[512,1024]{1,0:T(8,128)(2,1)S(1)} %copy-done.2, ...), custom_call_target="tpu_custom_call" | custom-call | flops 3489660928 | bytes 4194304 | tf_op jit(solution)/shard_map/keep_kernel/pallas_call | solution.py:286
  59.7 4.5 %collective-permute-done.10.right = bf16[4,104,512]{2,1,0:T(8,128)(2,1)S(1)} collective-permute-done((bf16[4,104,512]{2,1,0:T(8,128)(2,1)S(1)}, bf16[4,104,512]{2,1,0:T(8,128)(2,1)S(1)}, u32[]{:S(2)}, u32[]{:S(2)}) %collective-permute-start.10) | collective-permute-done | bytes 426016 | tf_op jit(solution)/shard_map/ppermute | solution.py:307
  64.4 31.7 %all_to_all.10.got = bf16[32,104,128]{2,1,0:T(8,128)(2,1)S(1)} all-to-all(bf16[32,104,128]{2,1,0:T(8,128)(2,1)S(1)} %merge.1), channel_id=1, replica_groups=mesh['x'=4,'zq'=4,'zp'=2,'y'=4,'core'=2] {'zq','y','core'}, dimensions={0} | all-to-all | bytes 1703936 | tf_op jit(solution)/shard_map/all_to_all | solution.py:317
  96.1 0.9 final.1
  (23 shorter events, 0.9 us)
Async XLA Ops:
  3.2 30.1 %collective-permute-start.1 = (bf16[256,1024]{1,0:T(8,128)(2,1)}, bf16[256,1024]{1,0:T(8,128)(2,1)S(1)}, u32[]{:S(2)}, u32[]{:S(2)}) collective-permute-start(bf16[256,1024]{1,0:T(8,128)(2,1)} %get-tuple-element.26), channel_id=1, source_target_pairs={{0,192},{64,0},{128,64},{192,128},{1,193},{65,1},{129,65},{193,129... | collective-permute-start | bytes 1572872 | tf_op jit(solution)/shard_map/ppermute | solution.py:250
  6.6 26.7 %collective-permute-start = (bf16[256,1024]{1,0:T(8,128)(2,1)}, bf16[256,1024]{1,0:T(8,128)(2,1)S(1)}, u32[]{:S(2)}, u32[]{:S(2)}) collective-permute-start(bf16[256,1024]{1,0:T(8,128)(2,1)} %get-tuple-element.26), channel_id=1, source_target_pairs={{0,64},{64,128},{128,192},{192,0},{1,65},{65,129},{129,193},{193,1... | collective-permute-start | bytes 1572872 | tf_op jit(solution)/shard_map/ppermute | solution.py:250
  6.6 26.7 %collective-permute-start.2 = (bf16[64,1024]{1,0:T(8,128)(2,1)}, bf16[64,1024]{1,0:T(8,128)(2,1)S(1)}, u32[]{:S(2)}, u32[]{:S(2)}) collective-permute-start(bf16[64,1024]{1,0:T(8,128)(2,1)} %get-tuple-element.27), channel_id=1, source_target_pairs={{0,128},{64,192},{128,0},{192,64},{1,129},{65,193},{129,1},{193,65... | collective-permute-start | bytes 393224 | tf_op jit(solution)/shard_map/ppermute | solution.py:250
  18.2 15.1 %all-to-all-start = ((f32[32,8,128]{2,1,0:T(8,128)}), f32[32,8,128]{2,1,0:T(8,128)S(1)}, u32[]{:S(2)}, u32[]{:S(2)}) async-start(f32[32,8,128]{2,1,0:T(8,128)} %stats.1.after), calls=%async_computation | async-start | bytes 262144 | tf_op jit(solution)/shard_map/all_to_all | solution.py:266
  25.6 11.6 %copy-start.2 = (bf16[512,1024]{1,0:T(8,128)(2,1)S(1)}, bf16[512,1024]{1,0:T(8,128)(2,1)}, u32[]{:S(2)}) copy-start(bf16[512,1024]{1,0:T(8,128)(2,1)} %own.3) | copy-start | bytes 3145732
  25.6 11.6 %copy-start.4 = (s32[4]{0:T(128)S(1)}, s32[4]{0:T(128)}, u32[]{:S(2)}) copy-start(s32[4]{0:T(128)} %pad_add_fusion.place) | copy-start | bytes 52
  33.3 3.9 %collective-permute-start.3 = (bf16[256,1024]{1,0:T(8,128)(2,1)S(1)}, bf16[256,1024]{1,0:T(8,128)(2,1)S(1)}, u32[]{:S(2)}, u32[]{:S(2)}) collective-permute-start(bf16[256,1024]{1,0:T(8,128)(2,1)S(1)} %collective-permute-done.a1), channel_id=1, source_target_pairs={{0,1},{1,0},{2,3},{3,2},{4,5},{5,4},{6,7},{7,6},{8,9},{9,8},{10,11... | collective-permute-start | bytes 1572872 | tf_op jit(solution)/shard_map/ppermute | solution.py:284
  33.8 3.4 %collective-permute-start.4 = (bf16[256,1024]{1,0:T(8,128)(2,1)S(1)}, bf16[256,1024]{1,0:T(8,128)(2,1)S(1)}, u32[]{:S(2)}, u32[]{:S(2)}) collective-permute-start(bf16[256,1024]{1,0:T(8,128)(2,1)S(1)} %collective-permute-done.1.a3), channel_id=1, source_target_pairs={{0,1},{1,0},{2,3},{3,2},{4,5},{5,4},{6,7},{7,6},{8,9},{9,8},{10,11... | collective-permute-start | bytes 1572872 | tf_op jit(solution)/shard_map/ppermute | solution.py:284
  33.9 9.5 %collective-permute-start.7 = (bf16[64,1024]{1,0:T(8,128)(2,1)S(1)}, bf16[64,1024]{1,0:T(8,128)(2,1)S(1)}, u32[]{:S(2)}, u32[]{:S(2)}) collective-permute-start(bf16[64,1024]{1,0:T(8,128)(2,1)S(1)} %collective-permute-done.2), channel_id=1, source_target_pairs={{0,6},{2,4},{4,2},{6,0},{1,7},{3,5},{5,3},{7,1},{8,14},{10,12},{12... | collective-permute-start | bytes 393224 | tf_op jit(solution)/shard_map/ppermute | solution.py:281
  34.9 8.5 %collective-permute-start.6 = (bf16[64,1024]{1,0:T(8,128)(2,1)S(1)}, bf16[64,1024]{1,0:T(8,128)(2,1)S(1)}, u32[]{:S(2)}, u32[]{:S(2)}) collective-permute-start(bf16[64,1024]{1,0:T(8,128)(2,1)S(1)} %collective-permute-done.2), channel_id=1, source_target_pairs={{0,4},{2,6},{4,0},{6,2},{1,5},{3,7},{5,1},{7,3},{8,12},{10,14},{12... | collective-permute-start | bytes 393224 | tf_op jit(solution)/shard_map/ppermute | solution.py:281
  36.0 7.4 %collective-permute-start.5 = (bf16[64,1024]{1,0:T(8,128)(2,1)S(1)}, bf16[64,1024]{1,0:T(8,128)(2,1)S(1)}, u32[]{:S(2)}, u32[]{:S(2)}) collective-permute-start(bf16[64,1024]{1,0:T(8,128)(2,1)S(1)} %collective-permute-done.2), channel_id=1, source_target_pairs={{0,2},{2,0},{4,6},{6,4},{1,3},{3,1},{5,7},{7,5},{8,10},{10,8},{12,... | collective-permute-start | bytes 393224 | tf_op jit(solution)/shard_map/ppermute | solution.py:281
  37.2 1.5 %copy-start = (bf16[2,416,1024]{2,1,0:T(8,128)(2,1)S(1)}, bf16[2,416,1024]{2,1,0:T(8,128)(2,1)}, u32[]{:S(2)}) copy-start(bf16[2,416,1024]{2,1,0:T(8,128)(2,1)} %get-tuple-element.32.rows) | copy-start | bytes 5111812
  38.7 1.0 %copy-start.3 = (f32[2,416,1]{2,1,0:T(8,128)S(1)}, f32[2,416,1]{2,1,0:T(8,128)}, u32[]{:S(2)}) copy-start(f32[2,416,1]{2,1,0:T(8,128)} %get-tuple-element.33.norms) | copy-start | bytes 9988
  43.4 3.1 %copy-start.1 = (bf16[2,416,1024]{2,1,0:T(8,128)(2,1)S(1)}, bf16[2,416,1024]{2,1,0:T(8,128)(2,1)}, u32[]{:S(2)}) copy-start(bf16[2,416,1024]{2,1,0:T(8,128)(2,1)} %get-tuple-element.32.rows) | copy-start | bytes 5111812
  43.6 2.9 %collective-permute-start.8 = (bf16[256,1024]{1,0:T(8,128)(2,1)S(1)}, bf16[256,1024]{1,0:T(8,128)(2,1)S(1)}, u32[]{:S(2)}, u32[]{:S(2)}) collective-permute-start(bf16[256,1024]{1,0:T(8,128)(2,1)S(1)} %pad_maximum_fusion.1.a2), channel_id=1, source_target_pairs={{0,1},{1,0},{2,3},{3,2},{4,5},{5,4},{6,7},{7,6},{8,9},{9,8},{10,11... | collective-permute-start | bytes 1572872 | tf_op jit(solution)/shard_map/ppermute | solution.py:302
  48.3 11.4 %collective-permute-start.9 = (bf16[4,104,512]{2,1,0:T(8,128)(2,1)S(1)}, bf16[4,104,512]{2,1,0:T(8,128)(2,1)S(1)}, u32[]{:S(2)}, u32[]{:S(2)}) collective-permute-start(bf16[4,104,512]{2,1,0:T(8,128)(2,1)S(1)} %get-tuple-element.45), channel_id=1, source_target_pairs={{0,8},{8,0},{16,24},{24,16},{32,40},{40,32},{48,56},{56,48},{1,9},... | collective-permute-start | bytes 1277960 | tf_op jit(solution)/shard_map/ppermute | solution.py:306
  50.0 14.2 %collective-permute-start.10 = (bf16[4,104,512]{2,1,0:T(8,128)(2,1)S(1)}, bf16[4,104,512]{2,1,0:T(8,128)(2,1)S(1)}, u32[]{:S(2)}, u32[]{:S(2)}) collective-permute-start(bf16[4,104,512]{2,1,0:T(8,128)(2,1)S(1)} %get-tuple-element.46), channel_id=1, source_target_pairs={{0,56},{8,16},{16,8},{24,32},{32,24},{40,48},{48,40},{56,0},{1,57}... | collective-permute-start | bytes 1277960 | tf_op jit(solution)/shard_map/ppermute | solution.py:307

commit v5 on v4

v5 whole, which is shorter than its diff:
```python
import functools

import jax
import jax.numpy as jnp
from jax import lax
from jax.experimental import pallas as pl
from jax.experimental.pallas import tpu as pltpu
from jax.sharding import Mesh, PartitionSpec as P

BF = jnp.bfloat16
F32 = jnp.float32
NX, NQ, NP, NY, NC = 4, 4, 2, 4, 2
CENT = ("y", "core")
N_CENT = NY * NC
LANES = 128
TAIL = 4
VMEM = pl.BlockSpec(memory_space=pltpu.VMEM)
SMEM = pl.BlockSpec(memory_space=pltpu.SMEM)
ANY = pl.BlockSpec(memory_space=pl.ANY)
MIB = 2**20
CHEAP = pl.CostEstimate(flops=1, bytes_accessed=1, transcendentals=0)
CHUNKS = 5
CUT = 256


def dot_nt(a, b):
    return lax.dot_general(a, b, (((1,), (1,)), ((), ())), preferred_element_type=F32)


def params(mib):
    return pltpu.CompilerParams(vmem_limit_bytes=mib * MIB)


def cut_kernel(place, points, half_out, eighth_out, sem):
    half, eighth = half_out.shape[0], eighth_out.shape[0]
    a = pltpu.make_async_copy(points.at[pl.ds(pl.multiple_of(place[0] * half, half), half)], half_out, sem.at[0])
    b = pltpu.make_async_copy(
        points.at[pl.ds(pl.multiple_of(place[1] * eighth, eighth), eighth)], eighth_out, sem.at[1]
    )
    a.start()
    b.start()
    a.wait()
    b.wait()


def stats_kernel(points, cents, out):
    chunk = cents.shape[0] // CHUNKS
    pts = points[...]
    tops, totals = [], []
    for i in range(CHUNKS):
        rows = cents[i * chunk : (i + 1) * chunk]
        wide = rows.astype(F32)
        norms = 0.5 * jnp.sum(wide * wide, axis=1, keepdims=True)
        logits = dot_nt(rows, pts) - norms
        top = jnp.max(logits, axis=0, keepdims=True)
        tops.append(top)
        totals.append(jnp.sum(jnp.exp(logits - top), axis=0, keepdims=True))
    top = functools.reduce(jnp.maximum, tops)
    total = sum(s * jnp.exp(t - top) for s, t in zip(totals, tops))
    groups = top.shape[1] // LANES
    tile = jnp.concatenate([r[:, g * LANES : (g + 1) * LANES] for r in (top, total) for g in range(groups)], axis=0)
    out[...] = jnp.broadcast_to(tile[None], out.shape)


def prep_kernel(place, cents, after, rows_out, norms_out, held, sems):
    n_blocks, window, dim = held.shape
    slot = rows_out.shape[0] // n_blocks - TAIL
    zq = place[2]
    odd = lax.rem(zq, 2) == 1
    copies = []
    for b in range(n_blocks):
        at = b // NP * (NQ * NP * slot) + (zq * NP + b % NP) * slot
        at = pl.multiple_of(at // 16 * 16, 16)
        copies.append(pltpu.make_async_copy(cents.at[pl.ds(at, window)], held.at[b], sems.at[b]))
    for copy in copies:
        copy.start()
    parts, norms = [], []
    for b in range(n_blocks):
        copies[b].wait()
        wide = held[b].astype(F32)
        even_at, odd_at = b % NP * slot % 16, (NP + b % NP) * slot % 16
        wide = jnp.where(odd, wide[odd_at : odd_at + slot], wide[even_at : even_at + slot])
        parts += [wide, jnp.zeros((TAIL, dim), F32)]
        norms += [0.5 * jnp.sum(wide * wide, axis=1, keepdims=True), jnp.full((TAIL, 1), 1e30, F32)]
    rows_out[...] = jnp.concatenate(parts, axis=0).astype(BF)
    norms_out[...] = jnp.concatenate(norms, axis=0)


def lse_of(stats, source):
    groups = stats.shape[1] // 2
    part = stats[pl.ds(source * N_CENT, N_CENT)]
    m, s = part[:, :groups], part[:, groups:]
    high = jnp.max(m, axis=0)
    return high + jnp.log(jnp.sum(s * jnp.exp(m - high[None]), axis=0))


def lse_halves(place, stats, k):
    lse = lse_of(stats, lax.rem(place[2] + NQ - k, NQ))
    half = lse.shape[0] // 2
    first = place[0] == 0
    return jnp.where(first, lse[:half], lse[half:]), jnp.where(first, lse[half:], lse[:half])


def weighted(pieces, rows, shift, weights):
    counts = jnp.zeros((rows.shape[0], LANES), F32)
    at = 0
    for ref, lse in pieces:
        n = ref.shape[0]
        for c in range(0, n, CUT):
            logits = dot_nt(rows, ref[c : c + CUT])
            for g in range(CUT // LANES):
                row = c // LANES + g
                w = jnp.exp(logits[:, g * LANES : (g + 1) * LANES] - shift - lse[row : row + 1]).astype(BF)
                counts += w.astype(F32)
                weights[:, at + c + g * LANES : at + c + (g + 1) * LANES] = w
        at += n
    numer = None
    at = 0
    for ref, _ in pieces:
        n = ref.shape[0]
        term = jnp.dot(weights[:, at : at + n], ref[...], preferred_element_type=F32)
        numer = term if numer is None else numer + term
        at += n
    return numer, counts


def row_counts(counts, block, height):
    part = counts[block * height : (block + 1) * height]
    part = jnp.concatenate([part, jnp.zeros((LANES - height, LANES), F32)], axis=0)
    return jnp.sum(part.T, axis=0, keepdims=True)


def close(values, first, second):
    height, width = values.shape
    first = jnp.concatenate([first] * (width // LANES), axis=1)
    second = jnp.concatenate([second] * (width // LANES), axis=1)
    last = values[height - 8 :]
    row = lax.broadcasted_iota(jnp.int32, last.shape, 0)
    last = jnp.where(row == 8 - TAIL, first, jnp.where(row == 9 - TAIL, second, jnp.where(row > 9 - TAIL, 0.0, last)))
    return jnp.concatenate([values[: height - 8], last], axis=0)


def split(counts):
    high = counts.astype(BF).astype(F32)
    return high, counts - high


def own_kernel(place, stats, rows, norms, own, numer, counts, weights):
    pieces = [(own, lse_of(stats, place[2]))]
    numer[...], counts[...] = weighted(pieces, rows[...], norms[...], weights)


def far_kernel(place, stats, rows, norms, a, b, numer_in, counts_in, numer, counts, weights):
    mine, other = lse_halves(place, stats, 2)
    more, more_counts = weighted([(a, mine), (b, other)], rows[...], norms[...], weights)
    numer[...], counts[...] = numer_in[...] + more, counts_in[...] + more_counts


def near_pieces(place, stats, up, down, which):
    return [(ref, lse_halves(place, stats, k)[which]) for k, ref in ((1, up), (NQ - 1, down))]


def near_kernel(place, stats, rows, norms, up, down, numer_in, counts_in, numer, counts, weights):
    pieces = near_pieces(place, stats, up, down, 0)
    more, more_counts = weighted(pieces, rows[...], norms[...], weights)
    numer[...], counts[...] = numer_in[...] + more, counts_in[...] + more_counts


def last_kernel(place, stats, rows, norms, up, down, numer_in, counts_in, send, weights):
    pieces = near_pieces(place, stats, up, down, 1)
    more, more_counts = weighted(pieces, rows[...], norms[...], weights)
    numer, counts = numer_in[...] + more, counts_in[...] + more_counts
    n, height, _ = send.shape
    for b in range(n // N_CENT):
        high, low = split(row_counts(counts, b, height))
        values = close(numer[b * height : (b + 1) * height], high, low).astype(BF)
        for c in range(N_CENT):
            send[b * N_CENT + c] = values[:, c * LANES : (c + 1) * LANES]


def final_kernel(got, out, scratch):
    n, height, _ = got.shape
    slot = height - TAIL
    for c in range(N_CENT):
        values = got[c].astype(F32)
        for i in range(1, n // N_CENT):
            values += got[i * N_CENT + c].astype(F32)
        tail = values[height - 8 :]
        counts = tail[8 - TAIL : 9 - TAIL] + tail[9 - TAIL : 10 - TAIL] + 1.0
        column = jnp.broadcast_to(counts, (LANES, LANES)).T
        scratch[c * slot : (c + 1) * slot] = (values / column[:height])[:slot]
    out[...] = scratch[...].astype(BF)


def body(points, centroids):
    rows, dim = centroids.shape
    pts = points.shape[0]
    n_blocks = NX * NP
    slot = rows // (n_blocks * NQ)
    height = slot + TAIL
    half, eighth = pts // NC, pts // N_CENT
    zq, y, core = (lax.axis_index(a) for a in ("zq", "y", "core"))
    place = jnp.stack([core, core * NY + y, zq]).astype(jnp.int32)
    shape = jax.ShapeDtypeStruct

    own_half, own_eighth = pl.pallas_call(
        cut_kernel,
        out_shape=(shape((half, dim), BF), shape((eighth, dim), BF)),
        in_specs=[SMEM, ANY],
        out_specs=(VMEM, VMEM),
        scratch_shapes=[pltpu.SemaphoreType.DMA((2,))],
        compiler_params=params(4),
        cost_estimate=CHEAP,
        name="cut",
    )(place, points)

    def ring(a, k):
        return lax.ppermute(a, "zq", [(i, (i + k) % NQ) for i in range(NQ)])

    far = ring(own_eighth, 2)
    up, down = ring(own_half, 1), ring(own_half, NQ - 1)

    points, own_half, own_eighth = lax.optimization_barrier((points, own_half, own_eighth))
    send_stats = pl.pallas_call(
        stats_kernel,
        out_shape=shape((NQ * N_CENT, 2 * pts // LANES, LANES), F32),
        in_specs=[VMEM, VMEM],
        out_specs=VMEM,
        compiler_params=params(16),
        cost_estimate=CHEAP,
        name="stats",
    )(points, centroids)
    far, _ = lax.optimization_barrier((far, send_stats))
    stats = lax.all_to_all(send_stats, ("zq", *CENT), 0, 0)

    work = n_blocks * height
    mine, norms = pl.pallas_call(
        prep_kernel,
        out_shape=(shape((work, dim), BF), shape((work, 1), F32)),
        in_specs=[SMEM, ANY, ANY],
        out_specs=(VMEM, VMEM),
        scratch_shapes=[pltpu.VMEM((n_blocks, slot + 12, dim), BF), pltpu.SemaphoreType.DMA((n_blocks,))],
        compiler_params=params(16),
        cost_estimate=CHEAP,
        name="prep",
    )(place, centroids, send_stats)

    def call(kernel, out_shape, *args):
        return pl.pallas_call(
            kernel,
            out_shape=out_shape,
            in_specs=[SMEM] + [VMEM] * (3 + len(args)),
            out_specs=jax.tree.map(lambda _: VMEM, out_shape),
            scratch_shapes=[pltpu.VMEM((work, pts), BF)],
            compiler_params=params(24),
            cost_estimate=CHEAP,
            name=kernel.__name__,
        )(place, stats, mine, norms, *args)

    sums = (shape((work, dim), F32), shape((work, LANES), F32))
    swap = [(0, 1), (1, 0)]

    slices = [far] + [lax.ppermute(far, "y", [(i, i ^ k) for i in range(NY)]) for k in range(1, NY)]
    up, down, stats = lax.optimization_barrier((up, down, stats))
    other_up, other_down = (lax.ppermute(a, "core", swap) for a in (up, down))
    numer = call(own_kernel, sums, points)
    slices, numer = lax.optimization_barrier((slices, numer))
    slices = jnp.stack(slices)
    far = jnp.concatenate([lax.dynamic_index_in_dim(slices, y ^ k, 0, keepdims=False) for k in range(NY)], axis=0)
    other_far = lax.ppermute(far, "core", swap)
    numer = call(near_kernel, sums, up, down, *numer)
    numer = call(far_kernel, sums, far, other_far, *numer)
    send = call(last_kernel, shape((n_blocks * N_CENT, height, LANES), BF), other_up, other_down, *numer)
    got = lax.all_to_all(send, ("x", "zp", *CENT), 0, 0)
    return pl.pallas_call(
        final_kernel,
        out_shape=shape((N_CENT * slot, LANES), BF),
        in_specs=[VMEM],
        out_specs=VMEM,
        scratch_shapes=[pltpu.VMEM((N_CENT * slot, LANES), F32)],
        compiler_params=params(16),
        name="final",
    )(got)


def solution(mesh):
    fine = Mesh(mesh.devices.reshape(NX, NQ, NP, NY, NC), ("x", "zq", "zp", *CENT))
    pts = ("x", "zq", "zp")
    return jax.shard_map(
        body, mesh=fine, in_specs=(P(pts, None), P(CENT, None)), out_specs=P(pts, CENT), check_vma=False
    )
```

time: 97.4 us -> 105 us (1.078)
  blocking collectives: 31.7 us -> 43.5 us
  local copies, waits for them, and re-layouts: 2.51 us -> 8.22 us
  waiting for transfers between devices: 9.62 us -> 4.63 us
  Pallas kernels: 28.2 us -> 24.1 us
  starting transfers between devices: 24.1 us -> 22.8 us
    all_to_all x1, blocking collectives: 31.7 us -> 43.5 us  [body(): got = lax.all_to_all(send, ('x', 'zp', *CENT), 0, 0)]
    unnamed x10, local copies, waits for them, and re-layouts: 2.47 us -> 8.17 us
    ppermute x8 -> x6, waiting for transfers between devices: 6.45 us -> 0.95 us  [the longest x3 0.94 us: ring(): return lax.ppermute(a, 'zq', [(i, (i + k) % NQ) for i in range(NQ)])]
    pallas_call x3 -> x2, Pallas kernels: 14.6 us -> 10.1 us  [the longest x1 5.7 us: body(): pl.pallas_call(stats_kernel, out_shape=shape((NQ * N_CENT, 2 * pts // LAN...]
    pallas_call x3 -> x4, Pallas kernels: 10.2 us -> 11.5 us  [call(): pl.pallas_call(kernel, out_shape=out_shape, in_specs=[SMEM] + [VMEM] * (3...]
    ppermute x8 -> x6, starting transfers between devices: 13.4 us -> 12.3 us  [the longest x3 11.4 us: ring(): return lax.ppermute(a, 'zq', [(i, (i + k) % NQ) for i in range(NQ)])]
  transfers between devices with their start and end apart: 12 -> 10, of which waited for: 4 -> 2; matrix products, arithmetic and copies ran while one was open for 0% -> 0% of each run, Pallas kernels for 23% -> 18%
where the time goes in v5:
time: 105 us
  blocking collectives  43.5 us (41%)
  Pallas kernels  24.1 us (23%)
  starting transfers between devices  22.8 us (22%)
  local copies, waits for them, and re-layouts  8.22 us (8%)
  waiting for transfers between devices  4.63 us (4%)
  other arithmetic  1.21 us (1%)
    all_to_all x1, blocking collectives, body(): got = lax.all_to_all(send, ('x', 'zp', *CENT), 0, 0)  43.5 us
    pallas_call x4, Pallas kernels, call(): pl.pallas_call(kernel, out_shape=out_shape, in_specs=[SMEM] + [VMEM] * (3...  11.5 us
    ppermute x3, starting transfers between devices, ring(): return lax.ppermute(a, 'zq', [(i, (i + k) % NQ) for i in range(NQ)])  11.4 us
    unnamed x10, local copies, waits for them, and re-layouts  8.17 us
    all_to_all x1, starting transfers between devices, body(): stats = lax.all_to_all(send_stats, ('zq', *CENT), 0, 0)  6.58 us
    pallas_call x1, Pallas kernels, body(): pl.pallas_call(stats_kernel, out_shape=shape((NQ * N_CENT, 2 * pts // LAN...  5.7 us
    pallas_call x1, Pallas kernels, body(): pl.pallas_call(prep_kernel, out_shape=(shape((work, dim), BF), shape((wor...  4.38 us
    ppermute x3, starting transfers between devices, body(): lax.ppermute(far, 'y', [(i, i ^ k) for i in range(NY)])  3.97 us
  transfers between devices with their start and end apart: 10, of which 2 were waited for; matrix products, arithmetic and copies ran while one was open for 0% of the time, Pallas kernels for 18%

profile of v5, /device:TPU:1, one launch (start us, length us, event | category | flops | bytes accessed | tf_op | source)
XLA Modules:
  0.0 104.7 jit_solution(17160829453451055100)
XLA Ops:
  0.1 1.2 %copy-done.2 = bf16[512,1024]{1,0:T(8,128)(2,1)S(1)} copy-done((bf16[512,1024]{1,0:T(8,128)(2,1)S(1)}, bf16[512,1024]{1,0:T(8,128)(2,1)}, u32[]{:S(2)}) %copy-start.2) | copy-done | bytes 1048600
  1.3 1.6 %cut.1 = (bf16[256,1024]{1,0:T(8,128)(2,1)}, bf16[64,1024]{1,0:T(8,128)(2,1)S(1)}) custom-call(s32[3]{0:T(128)S(1)} %pad_add_fusion.place, bf16[512,1024]{1,0:T(8,128)(2,1)S(1)} %copy-done.2), custom_call_target="tpu_custom_call" | custom-call | flops 1 | bytes 1 | tf_op jit(solution)/shard_map/cut/pallas_call | solution.py:206
  2.9 3.9 %collective-permute-start = (bf16[256,1024]{1,0:T(8,128)(2,1)}, bf16[256,1024]{1,0:T(8,128)(2,1)}, u32[]{:S(2)}, u32[]{:S(2)}) collective-permute-start(bf16[256,1024]{1,0:T(8,128)(2,1)} %get-tuple-element.26), channel_id=1, source_target_pairs={{0,16},{16,32},{32,48},{48,0},{1,17},{17,33},{33,49},{49,1},{2,18}... | collective-permute-start | bytes 1572872 | tf_op jit(solution)/shard_map/ppermute | solution.py:218
  6.8 3.1 %collective-permute-start.1 = (bf16[256,1024]{1,0:T(8,128)(2,1)}, bf16[256,1024]{1,0:T(8,128)(2,1)}, u32[]{:S(2)}, u32[]{:S(2)}) collective-permute-start(bf16[256,1024]{1,0:T(8,128)(2,1)} %get-tuple-element.26), channel_id=1, source_target_pairs={{0,48},{16,0},{32,16},{48,32},{1,49},{17,1},{33,17},{49,33},{2,50}... | collective-permute-start | bytes 1572872 | tf_op jit(solution)/shard_map/ppermute | solution.py:218
  9.9 4.4 %collective-permute-start.4 = (bf16[64,1024]{1,0:T(8,128)(2,1)S(1)}, bf16[64,1024]{1,0:T(8,128)(2,1)S(1)}, u32[]{:S(2)}, u32[]{:S(2)}) collective-permute-start(bf16[64,1024]{1,0:T(8,128)(2,1)S(1)} %get-tuple-element.27), channel_id=1, source_target_pairs={{0,32},{16,48},{32,0},{48,16},{1,33},{17,49},{33,1},{49,17},{2,34}... | collective-permute-start | bytes 393224 | tf_op jit(solution)/shard_map/ppermute | solution.py:218
  14.3 2.9 %copy-done = bf16[3200,1024]{1,0:T(8,128)(2,1)S(1)} copy-done((bf16[3200,1024]{1,0:T(8,128)(2,1)S(1)}, bf16[3200,1024]{1,0:T(8,128)(2,1)}, u32[]{:S(2)}) %copy-start) | copy-done | bytes 6553624
  17.1 1.2 %copy-done.3 = bf16[512,1024]{1,0:T(8,128)(2,1)S(1)} copy-done((bf16[512,1024]{1,0:T(8,128)(2,1)S(1)}, bf16[512,1024]{1,0:T(8,128)(2,1)}, u32[]{:S(2)}) %copy-start.3) | copy-done | bytes 1048600
  18.4 5.7 %stats.1.after = f32[32,8,128]{2,1,0:T(8,128)} custom-call(bf16[512,1024]{1,0:T(8,128)(2,1)S(1)} %copy-done.3, bf16[3200,1024]{1,0:T(8,128)(2,1)S(1)} %copy-done), custom_call_target="tpu_custom_call" | custom-call | flops 1 | bytes 1 | tf_op jit(solution)/shard_map/stats/pallas_call | solution.py:224
  24.1 6.6 %all-to-all-start = ((f32[32,8,128]{2,1,0:T(8,128)}), f32[32,8,128]{2,1,0:T(8,128)S(1)}, u32[]{:S(2)}, u32[]{:S(2)}) async-start(f32[32,8,128]{2,1,0:T(8,128)} %stats.1.after), calls=%async_computation | async-start | bytes 262144 | tf_op jit(solution)/shard_map/all_to_all | solution.py:234
  30.6 0.9 collective-permute-done.4
  31.6 1.3 %collective-permute-start.5 = (bf16[64,1024]{1,0:T(8,128)(2,1)S(1)}, bf16[64,1024]{1,0:T(8,128)(2,1)}, u32[]{:S(2)}, u32[]{:S(2)}) collective-permute-start(bf16[64,1024]{1,0:T(8,128)(2,1)S(1)} %collective-permute-done.4), channel_id=1, source_target_pairs={{0,2},{2,0},{4,6},{6,4},{1,3},{3,1},{5,7},{7,5},{8,10},{10,8},{12,... | collective-permute-start | bytes 393224 | tf_op jit(solution)/shard_map/ppermute | solution.py:263
  32.9 2.7 %collective-permute-start.6 = (bf16[64,1024]{1,0:T(8,128)(2,1)S(1)}, bf16[64,1024]{1,0:T(8,128)(2,1)}, u32[]{:S(2)}, u32[]{:S(2)}) collective-permute-start(bf16[64,1024]{1,0:T(8,128)(2,1)S(1)} %collective-permute-done.4), channel_id=1, source_target_pairs={{0,4},{2,6},{4,0},{6,2},{1,5},{3,7},{5,1},{7,3},{8,12},{10,14},{12... | collective-permute-start | bytes 393224 | tf_op jit(solution)/shard_map/ppermute | solution.py:263
  35.5 2.9 %copy-done.1 = bf16[3200,1024]{1,0:T(8,128)(2,1)S(1)} copy-done((bf16[3200,1024]{1,0:T(8,128)(2,1)S(1)}, bf16[3200,1024]{1,0:T(8,128)(2,1)}, u32[]{:S(2)}) %copy-start.1) | copy-done | bytes 6553624
  38.4 4.4 %prep.1 = (bf16[832,1024]{1,0:T(8,128)(2,1)S(1)}, f32[832,1]{1,0:T(8,128)S(1)}) custom-call(s32[3]{0:T(128)S(1)} %pad_add_fusion.place, bf16[3200,1024]{1,0:T(8,128)(2,1)S(1)} %copy-done.1, f32[32,8,128]{2,1,0:T(8,128)} %stats.1.after), custom_call_target="tpu_custom_call" | custom-call | flops 1 | bytes 1 | tf_op jit(solution)/shard_map/prep/pallas_call | solution.py:237
  42.8 3.7 %all-to-all-done.stats = f32[32,8,128]{2,1,0:T(8,128)S(1)} async-done(((f32[32,8,128]{2,1,0:T(8,128)}), f32[32,8,128]{2,1,0:T(8,128)S(1)}, u32[]{:S(2)}, u32[]{:S(2)}) %all-to-all-start) | async-done | bytes 131104 | tf_op jit(solution)/shard_map/all_to_all | solution.py:234
  46.5 2.6 %own_kernel.1 = (f32[832,1024]{1,0:T(8,128)S(1)}, f32[832,128]{1,0:T(8,128)S(1)}) custom-call(s32[3]{0:T(128)S(1)} %pad_add_fusion.place, f32[32,8,128]{2,1,0:T(8,128)S(1)} %all-to-all-done.stats, bf16[832,1024]{1,0:T(8,128)(2,1)S(1)} %get-tuple-element.30.rows, f32[832,1]{1,0:T(8,128)S(1)} %get-tuple-element.31.norms, bf16[512,1024]{1,0:T(8,128)(2,1)S(1)} %copy-done.4), custom_call_target="tpu_custom_call" | custom-call | flops 1 | bytes 1 | tf_op jit(solution)/shard_map/own_kernel/pallas_call | solution.py:249
  49.2 1.1 %pad_maximum_fusion = bf16[4,64,1024]{2,1,0:T(8,128)(2,1)S(1)} fusion(bf16[1,64,1024]{2,1,0:T(8,128)(2,1)} %bitcast.6, bf16[1,64,1024]{2,1,0:T(8,128)(2,1)} %bitcast.5, bf16[1,64,1024]{2,1,0:T(8,128)(2,1)} %bitcast.4, bf16[1,64,1024]{2,1,0:T(8,128)(2,1)S(1)} %bitcast.15), kind=kLoop, calls=%fused_computation | loop fusion | flops 786432 | bytes 1048576 | tf_op jit(solution)/shard_map/stack | solution.py:268
  50.4 0.3 collective-permute-start.8
  50.6 0.5 collective-permute-start.2
  51.2 3.4 %near_kernel.1 = (f32[832,1024]{1,0:T(8,128)S(1)}, f32[832,128]{1,0:T(8,128)S(1)}) custom-call(s32[3]{0:T(128)S(1)} %pad_add_fusion.place, f32[32,8,128]{2,1,0:T(8,128)S(1)} %all-to-all-done.stats, bf16[832,1024]{1,0:T(8,128)(2,1)S(1)} %get-tuple-element.30.rows, f32[832,1]{1,0:T(8,128)S(1)} %get-tuple-element.31.norms, ...), custom_call_target="tpu_custom_call" | custom-call | flops 1 | bytes 1 | tf_op jit(solution)/shard_map/near_kernel/pallas_call | solution.py:249
  54.6 2.7 %far_kernel.1 = (f32[832,1024]{1,0:T(8,128)S(1)}, f32[832,128]{1,0:T(8,128)S(1)}) custom-call(s32[3]{0:T(128)S(1)} %pad_add_fusion.place, f32[32,8,128]{2,1,0:T(8,128)S(1)} %all-to-all-done.stats, bf16[832,1024]{1,0:T(8,128)(2,1)S(1)} %get-tuple-element.30.rows, f32[832,1]{1,0:T(8,128)S(1)} %get-tuple-element.31.norms, ...), custom_call_target="tpu_custom_call" | custom-call | flops 1 | bytes 1 | tf_op jit(solution)/shard_map/far_kernel/pallas_call | solution.py:249
  57.4 2.8 %last_kernel.1 = bf16[64,104,128]{2,1,0:T(8,128)(2,1)S(1)} custom-call(s32[3]{0:T(128)S(1)} %pad_add_fusion.place, f32[32,8,128]{2,1,0:T(8,128)S(1)} %all-to-all-done.stats, bf16[832,1024]{1,0:T(8,128)(2,1)S(1)} %get-tuple-element.30.rows, f32[832,1]{1,0:T(8,128)S(1)} %get-tuple-element.31.norms, bf16[256,1024]{1,0:T(8,128)(2,1)S(1)} %collective-permute-done.2.up, ...), custom_call_target="tpu_custom_call" | custom-call | flops 1 | bytes 1 | tf_op jit(solution)/shard_map/last_kernel/pallas_call | solution.py:249
  60.2 43.5 %all_to_all.10.got = bf16[64,104,128]{2,1,0:T(8,128)(2,1)S(1)} all-to-all(bf16[64,104,128]{2,1,0:T(8,128)(2,1)S(1)} %last_kernel.1), channel_id=1, replica_groups=mesh['x'=4,'zq'=4,'zp'=2,'y'=4,'core'=2] {'x','zp','y','core'}, dimensions={0} | all-to-all | bytes 3407872 | tf_op jit(solution)/shard_map/all_to_all | solution.py:274
  103.7 1.0 final.1
  (19 shorter events, 0.3 us)
Async XLA Ops:
  0.1 1.2 %copy-start.2 = (bf16[512,1024]{1,0:T(8,128)(2,1)S(1)}, bf16[512,1024]{1,0:T(8,128)(2,1)}, u32[]{:S(2)}) copy-start(bf16[512,1024]{1,0:T(8,128)(2,1)} %own) | copy-start | bytes 3145732
  2.9 43.6 %collective-permute-start = (bf16[256,1024]{1,0:T(8,128)(2,1)}, bf16[256,1024]{1,0:T(8,128)(2,1)}, u32[]{:S(2)}, u32[]{:S(2)}) collective-permute-start(bf16[256,1024]{1,0:T(8,128)(2,1)} %get-tuple-element.26), channel_id=1, source_target_pairs={{0,16},{16,32},{32,48},{48,0},{1,17},{17,33},{33,49},{49,1},{2,18}... | collective-permute-start | bytes 1572872 | tf_op jit(solution)/shard_map/ppermute | solution.py:218
  6.8 39.7 %collective-permute-start.1 = (bf16[256,1024]{1,0:T(8,128)(2,1)}, bf16[256,1024]{1,0:T(8,128)(2,1)}, u32[]{:S(2)}, u32[]{:S(2)}) collective-permute-start(bf16[256,1024]{1,0:T(8,128)(2,1)} %get-tuple-element.26), channel_id=1, source_target_pairs={{0,48},{16,0},{32,16},{48,32},{1,49},{17,1},{33,17},{49,33},{2,50}... | collective-permute-start | bytes 1572872 | tf_op jit(solution)/shard_map/ppermute | solution.py:218
  9.9 21.7 %collective-permute-start.4 = (bf16[64,1024]{1,0:T(8,128)(2,1)S(1)}, bf16[64,1024]{1,0:T(8,128)(2,1)S(1)}, u32[]{:S(2)}, u32[]{:S(2)}) collective-permute-start(bf16[64,1024]{1,0:T(8,128)(2,1)S(1)} %get-tuple-element.27), channel_id=1, source_target_pairs={{0,32},{16,48},{32,0},{48,16},{1,33},{17,49},{33,1},{49,17},{2,34}... | collective-permute-start | bytes 393224 | tf_op jit(solution)/shard_map/ppermute | solution.py:218
  14.3 2.9 %copy-start = (bf16[3200,1024]{1,0:T(8,128)(2,1)S(1)}, bf16[3200,1024]{1,0:T(8,128)(2,1)}, u32[]{:S(2)}) copy-start(bf16[3200,1024]{1,0:T(8,128)(2,1)} %cents.3) | copy-start | bytes 19660804
  17.1 1.2 %copy-start.3 = (bf16[512,1024]{1,0:T(8,128)(2,1)S(1)}, bf16[512,1024]{1,0:T(8,128)(2,1)}, u32[]{:S(2)}) copy-start(bf16[512,1024]{1,0:T(8,128)(2,1)} %own) | copy-start | bytes 3145732
  18.4 28.1 %copy-start.4 = (bf16[512,1024]{1,0:T(8,128)(2,1)S(1)}, bf16[512,1024]{1,0:T(8,128)(2,1)}, u32[]{:S(2)}) copy-start(bf16[512,1024]{1,0:T(8,128)(2,1)} %own) | copy-start | bytes 3145732
  24.1 22.4 %all-to-all-start = ((f32[32,8,128]{2,1,0:T(8,128)}), f32[32,8,128]{2,1,0:T(8,128)S(1)}, u32[]{:S(2)}, u32[]{:S(2)}) async-start(f32[32,8,128]{2,1,0:T(8,128)} %stats.1.after), calls=%async_computation | async-start | bytes 262144 | tf_op jit(solution)/shard_map/all_to_all | solution.py:234
  31.6 17.6 %collective-permute-start.5 = (bf16[64,1024]{1,0:T(8,128)(2,1)S(1)}, bf16[64,1024]{1,0:T(8,128)(2,1)}, u32[]{:S(2)}, u32[]{:S(2)}) collective-permute-start(bf16[64,1024]{1,0:T(8,128)(2,1)S(1)} %collective-permute-done.4), channel_id=1, source_target_pairs={{0,2},{2,0},{4,6},{6,4},{1,3},{3,1},{5,7},{7,5},{8,10},{10,8},{12,... | collective-permute-start | bytes 393224 | tf_op jit(solution)/shard_map/ppermute | solution.py:263
  32.9 16.3 %collective-permute-start.6 = (bf16[64,1024]{1,0:T(8,128)(2,1)S(1)}, bf16[64,1024]{1,0:T(8,128)(2,1)}, u32[]{:S(2)}, u32[]{:S(2)}) collective-permute-start(bf16[64,1024]{1,0:T(8,128)(2,1)S(1)} %collective-permute-done.4), channel_id=1, source_target_pairs={{0,4},{2,6},{4,0},{6,2},{1,5},{3,7},{5,1},{7,3},{8,12},{10,14},{12... | collective-permute-start | bytes 393224 | tf_op jit(solution)/shard_map/ppermute | solution.py:263
  35.5 13.6 %collective-permute-start.7 = (bf16[64,1024]{1,0:T(8,128)(2,1)S(1)}, bf16[64,1024]{1,0:T(8,128)(2,1)}, u32[]{:S(2)}, u32[]{:S(2)}) collective-permute-start(bf16[64,1024]{1,0:T(8,128)(2,1)S(1)} %collective-permute-done.4), channel_id=1, source_target_pairs={{0,6},{2,4},{4,2},{6,0},{1,7},{3,5},{5,3},{7,1},{8,14},{10,12},{12... | collective-permute-start | bytes 393224 | tf_op jit(solution)/shard_map/ppermute | solution.py:263
  35.5 2.9 %copy-start.1 = (bf16[3200,1024]{1,0:T(8,128)(2,1)S(1)}, bf16[3200,1024]{1,0:T(8,128)(2,1)}, u32[]{:S(2)}) copy-start(bf16[3200,1024]{1,0:T(8,128)(2,1)} %cents.3) | copy-start | bytes 19660804
  50.4 4.3 %collective-permute-start.8 = (bf16[256,1024]{1,0:T(8,128)(2,1)S(1)}, bf16[256,1024]{1,0:T(8,128)(2,1)S(1)}, u32[]{:S(2)}, u32[]{:S(2)}) collective-permute-start(bf16[256,1024]{1,0:T(8,128)(2,1)S(1)} %pad_maximum_fusion.1.a), channel_id=1, source_target_pairs={{0,1},{1,0},{2,3},{3,2},{4,5},{5,4},{6,7},{7,6},{8,9},{9,8},{10,11... | collective-permute-start | bytes 1572872 | tf_op jit(solution)/shard_map/ppermute | solution.py:270
  50.6 6.7 %collective-permute-start.2 = (bf16[256,1024]{1,0:T(8,128)(2,1)}, bf16[256,1024]{1,0:T(8,128)(2,1)S(1)}, u32[]{:S(2)}, u32[]{:S(2)}) collective-permute-start(bf16[256,1024]{1,0:T(8,128)(2,1)} %collective-permute-done.up), channel_id=1, source_target_pairs={{0,1},{1,0},{2,3},{3,2},{4,5},{5,4},{6,7},{7,6},{8,9},{9,8},{10,11... | collective-permute-start | bytes 1572872 | tf_op jit(solution)/shard_map/ppermute | solution.py:265
  51.1 6.3 %collective-permute-start.3 = (bf16[256,1024]{1,0:T(8,128)(2,1)}, bf16[256,1024]{1,0:T(8,128)(2,1)S(1)}, u32[]{:S(2)}, u32[]{:S(2)}) collective-permute-start(bf16[256,1024]{1,0:T(8,128)(2,1)} %collective-permute-done.1.down), channel_id=1, source_target_pairs={{0,1},{1,0},{2,3},{3,2},{4,5},{5,4},{6,7},{7,6},{8,9},{9,8},{10,11... | collective-permute-start | bytes 1572872 | tf_op jit(solution)/shard_map/ppermute | solution.py:265

commit v6 on v5

v6 whole, which is shorter than its diff:
```python
import functools

import jax
import jax.numpy as jnp
from jax import lax
from jax.experimental import pallas as pl
from jax.experimental.pallas import tpu as pltpu
from jax.sharding import Mesh, PartitionSpec as P

BF = jnp.bfloat16
F32 = jnp.float32
NX, NQ, NP, NY, NC = 4, 4, 2, 4, 2
CENT = ("y", "core")
N_CENT = NY * NC
LANES = 128
TAIL = 4
VMEM = pl.BlockSpec(memory_space=pltpu.VMEM)
SMEM = pl.BlockSpec(memory_space=pltpu.SMEM)
ANY = pl.BlockSpec(memory_space=pl.ANY)
MIB = 2**20
CHEAP = pl.CostEstimate(flops=1, bytes_accessed=1, transcendentals=0)
TILE = 640
CUT = 256


def dot_nt(a, b):
    return lax.dot_general(a, b, (((1,), (1,)), ((), ())), preferred_element_type=F32)


def params(mib):
    return pltpu.CompilerParams(vmem_limit_bytes=mib * MIB)


def cut_kernel(place, points, half_out, eighth_out, sem):
    half, eighth = half_out.shape[0], eighth_out.shape[0]
    a = pltpu.make_async_copy(points.at[pl.ds(pl.multiple_of(place[0] * half, half), half)], half_out, sem.at[0])
    b = pltpu.make_async_copy(
        points.at[pl.ds(pl.multiple_of(place[1] * eighth, eighth), eighth)], eighth_out, sem.at[1]
    )
    a.start()
    b.start()
    a.wait()
    b.wait()


def stats_kernel(place, points, cents, table, out, mine, top, total, sems):
    step = pl.program_id(0)
    count = NX
    window = mine.shape[0] // count
    stride = table.shape[0] // count
    start = pl.multiple_of(place[2] * (stride // NQ) // 16 * 16, 16)
    copies = [
        pltpu.make_async_copy(table.at[pl.ds(i * stride + start, window)], mine.at[pl.ds(i * window, window)], sems.at[i])
        for i in range(count)
    ]

    @pl.when(step == 0)
    def _():
        for copy in copies:
            copy.start()
        top[...] = jnp.full_like(top, -jnp.inf)
        total[...] = jnp.zeros_like(total)

    rows = cents[...]
    chunk = rows.shape[0] // 2
    pts = points[...]
    tops, totals = [top[...]], [total[...]]
    for i in range(2):
        part = rows[i * chunk : (i + 1) * chunk]
        wide = part.astype(F32)
        logits = dot_nt(part, pts) - 0.5 * jnp.sum(wide * wide, axis=1, keepdims=True)
        high = jnp.max(logits, axis=0, keepdims=True)
        tops.append(high)
        totals.append(jnp.sum(jnp.exp(logits - high), axis=0, keepdims=True))
    new = functools.reduce(jnp.maximum, tops)
    top[...] = new
    total[...] = sum(s * jnp.exp(t - new) for s, t in zip(totals, tops))

    @pl.when(step == pl.num_programs(0) - 1)
    def _():
        groups = top.shape[1] // LANES
        both = [r[:, g * LANES : (g + 1) * LANES] for r in (top[...], total[...]) for g in range(groups)]
        out[...] = jnp.broadcast_to(jnp.concatenate(both, axis=0)[None], out.shape)
        for copy in copies:
            copy.wait()


def lse_of(stats, source):
    groups = stats.shape[1] // 2
    part = stats[pl.ds(source * N_CENT, N_CENT)]
    m, s = part[:, :groups], part[:, groups:]
    high = jnp.max(m, axis=0)
    return high + jnp.log(jnp.sum(s * jnp.exp(m - high[None]), axis=0))


def lse_halves(place, stats, k):
    lse = lse_of(stats, lax.rem(place[2] + NQ - k, NQ))
    half = lse.shape[0] // 2
    first = place[0] == 0
    return jnp.where(first, lse[:half], lse[half:]), jnp.where(first, lse[half:], lse[:half])


def weighted(pieces, rows, shift, weights):
    counts = jnp.zeros((rows.shape[0], LANES), F32)
    at = 0
    for ref, lse in pieces:
        n = ref.shape[0]
        for c in range(0, n, CUT):
            logits = dot_nt(rows, ref[c : c + CUT])
            for g in range(CUT // LANES):
                row = c // LANES + g
                w = jnp.exp(logits[:, g * LANES : (g + 1) * LANES] - shift - lse[row : row + 1]).astype(BF)
                counts += w.astype(F32)
                weights[:, at + c + g * LANES : at + c + (g + 1) * LANES] = w
        at += n
    numer = None
    at = 0
    for ref, _ in pieces:
        n = ref.shape[0]
        term = jnp.dot(weights[:, at : at + n], ref[...], preferred_element_type=F32)
        numer = term if numer is None else numer + term
        at += n
    return numer, counts


def row_counts(part):
    part = jnp.concatenate([part, jnp.zeros((LANES - part.shape[0], LANES), F32)], axis=0)
    return jnp.sum(part.T, axis=0, keepdims=True)


def close(values, first, second):
    height, width = values.shape
    first = jnp.concatenate([first] * (width // LANES), axis=1)
    second = jnp.concatenate([second] * (width // LANES), axis=1)
    last = values[height - 8 :]
    row = lax.broadcasted_iota(jnp.int32, last.shape, 0)
    last = jnp.where(row == 8 - TAIL, first, jnp.where(row == 9 - TAIL, second, jnp.where(row > 9 - TAIL, 0.0, last)))
    return jnp.concatenate([values[: height - 8], last], axis=0)


def split(counts):
    high = counts.astype(BF).astype(F32)
    return high, counts - high


def own_kernel(place, stats, rows, own, numer, counts, norms, weights):
    values = rows[...]
    wide = values.astype(F32)
    shift = 0.5 * jnp.sum(wide * wide, axis=1, keepdims=True)
    norms[...] = shift
    numer[...], counts[...] = weighted([(own, lse_of(stats, place[2]))], values, shift, weights)


def half_pieces(place, stats, up, down, far, which):
    lse = lse_halves(place, stats, 2)[which]
    y = place[3]
    lse = jnp.where(lax.rem(y, 2) == 1, jnp.concatenate([lse[:, LANES // 2 :], lse[:, : LANES // 2]], axis=1), lse)
    lse = jnp.where(y >= 2, jnp.concatenate([lse[1:], lse[:1]], axis=0), lse)
    pieces = [(ref, lse_halves(place, stats, k)[which]) for k, ref in ((1, up), (NQ - 1, down))]
    return [(far, lse)] + pieces


def first_kernel(place, stats, rows, norms, up, down, far, numer_in, counts_in, numer, counts, weights):
    pieces = half_pieces(place, stats, up, down, far, 0)
    more, more_counts = weighted(pieces, rows[...], norms[...], weights)
    numer[...], counts[...] = numer_in[...] + more, counts_in[...] + more_counts


def second_kernel(place, stats, rows, norms, up, down, far, numer_in, counts_in, send, weights, numer, counts):
    pieces = half_pieces(place, stats, up, down, far, 1)
    more, more_counts = weighted(pieces, rows[...], norms[...], weights)
    numer[...], counts[...] = numer_in[...] + more, counts_in[...] + more_counts
    n, height, _ = send.shape
    slot = height - TAIL
    window = rows.shape[0] // NX
    skip = lax.rem(place[2], 2) * 8
    for b in range(n // N_CENT):
        at = b % NP * slot
        start = pl.multiple_of(b // NP * window + skip + at // 8 * 8, 8)
        off = at % 8
        values = numer[pl.ds(start, height)]
        some = counts[pl.ds(start, height)]
        if off:
            values = jnp.concatenate([values[off:], values[:off]], axis=0)
            some = jnp.concatenate([some[off:], some[:off]], axis=0)
        high, low = split(row_counts(some))
        values = close(values, high, low).astype(BF)
        for c in range(N_CENT):
            send[b * N_CENT + c] = values[:, c * LANES : (c + 1) * LANES]


def final_kernel(got, out, scratch):
    n, height, _ = got.shape
    slot = height - TAIL
    for c in range(N_CENT):
        values = got[c].astype(F32)
        for i in range(1, n // N_CENT):
            values += got[i * N_CENT + c].astype(F32)
        tail = values[height - 8 :]
        counts = tail[8 - TAIL : 9 - TAIL] + tail[9 - TAIL : 10 - TAIL] + 1.0
        column = jnp.broadcast_to(counts, (LANES, LANES)).T
        scratch[c * slot : (c + 1) * slot] = (values / column[:height])[:slot]
    out[...] = scratch[...].astype(BF)


def body(points, centroids):
    rows, dim = centroids.shape
    pts = points.shape[0]
    n_blocks = NX * NP
    slot = rows // (n_blocks * NQ)
    height = slot + TAIL
    half, eighth = pts // NC, pts // N_CENT
    zq, y, core = (lax.axis_index(a) for a in ("zq", "y", "core"))
    place = jnp.stack([core, core * NY + y, zq, y]).astype(jnp.int32)
    shape = jax.ShapeDtypeStruct

    own_half, own_eighth = pl.pallas_call(
        cut_kernel,
        out_shape=(shape((half, dim), BF), shape((eighth, dim), BF)),
        in_specs=[SMEM, ANY],
        out_specs=(ANY, ANY),
        scratch_shapes=[pltpu.SemaphoreType.DMA((2,))],
        compiler_params=params(62),
        cost_estimate=CHEAP,
        name="cut",
    )(place, points)

    def ring(a, k):
        return lax.ppermute(a, "zq", [(i, (i + k) % NQ) for i in range(NQ)])

    far = ring(own_eighth, 2)
    up, down = ring(own_half, 1), ring(own_half, NQ - 1)

    points, own_half, own_eighth = lax.optimization_barrier((points, own_half, own_eighth))
    window = -(-(rows // (NX * NQ)) // 16) * 16
    work = NX * window
    stats_shape = (NQ * N_CENT, 2 * pts // LANES, LANES)
    send_stats, mine = pl.pallas_call(
        stats_kernel,
        grid=(rows // TILE,),
        out_shape=(shape(stats_shape, F32), shape((work, dim), BF)),
        in_specs=[
            SMEM,
            pl.BlockSpec((pts, dim), lambda i: (0, 0)),
            pl.BlockSpec((TILE, dim), lambda i: (i, 0)),
            ANY,
        ],
        out_specs=(pl.BlockSpec(stats_shape, lambda i: (0, 0, 0)), ANY),
        scratch_shapes=[pltpu.VMEM((1, pts), F32), pltpu.VMEM((1, pts), F32), pltpu.SemaphoreType.DMA((NX,))],
        compiler_params=params(57),
        cost_estimate=CHEAP,
        name="stats",
    )(place, points, centroids, centroids)
    far, _ = lax.optimization_barrier((far, send_stats))
    stats = lax.all_to_all(send_stats, ("zq", *CENT), 0, 0)

    def call(kernel, out_shape, n_points, *args, scratch=()):
        return pl.pallas_call(
            kernel,
            out_shape=out_shape,
            in_specs=[SMEM] + [VMEM] * (2 + len(args)),
            out_specs=jax.tree.map(lambda _: VMEM, out_shape),
            scratch_shapes=[pltpu.VMEM((work, n_points), BF), *scratch],
            compiler_params=params(28),
            cost_estimate=CHEAP,
            name=kernel.__name__,
        )(place, stats, mine, *args)

    swap = [(0, 1), (1, 0)]
    slices = [far] + [lax.ppermute(far, "y", [(i, i ^ k) for i in range(NY)]) for k in range(1, NY)]
    up, down, stats = lax.optimization_barrier((up, down, stats))
    others = [lax.ppermute(a, "core", swap) for a in (up, down)]
    sums = (shape((work, dim), F32), shape((work, LANES), F32))
    *numer, norms = call(own_kernel, (*sums, shape((work, 1), F32)), pts, points)
    slices, numer = lax.optimization_barrier((slices, numer))
    far = jnp.concatenate(slices, axis=0)
    others.append(lax.ppermute(far, "core", swap))
    more = (NQ - 1) * half
    numer = call(first_kernel, sums, more, norms, up, down, far, *numer)
    send = call(
        second_kernel,
        shape((n_blocks * N_CENT, height, LANES), BF),
        more,
        norms,
        *others,
        *numer,
        scratch=[pltpu.VMEM(s.shape, F32) for s in sums],
    )
    got = lax.all_to_all(send, ("x", "zp", *CENT), 0, 0)
    return pl.pallas_call(
        final_kernel,
        out_shape=shape((N_CENT * slot, LANES), BF),
        in_specs=[VMEM],
        out_specs=VMEM,
        scratch_shapes=[pltpu.VMEM((N_CENT * slot, LANES), F32)],
        compiler_params=params(16),
        name="final",
    )(got)


def solution(mesh):
    fine = Mesh(mesh.devices.reshape(NX, NQ, NP, NY, NC), ("x", "zq", "zp", *CENT))
    pts = ("x", "zq", "zp")
    return jax.shard_map(
        body, mesh=fine, in_specs=(P(pts, None), P(CENT, None)), out_specs=P(pts, CENT), check_vma=False
    )
```

time: 105 us -> 155 us (1.48)
  Pallas kernels: 24.1 us -> 91.8 us
  blocking collectives: 43.5 us -> 30.8 us
  local copies, waits for them, and re-layouts: 8.22 us -> 1.5 us
  waiting for transfers between devices: 4.63 us -> 7.11 us
    pallas_call x6 -> x4, Pallas kernels: 21.6 us -> 69.2 us  [the longest x1 55 us: body(): pl.pallas_call(stats_kernel, grid=(rows // TILE,), out_shape=(shape(stats...]
    pallas_call x1, Pallas kernels: 1.57 us -> 21.6 us  [body(): pl.pallas_call(cut_kernel, out_shape=(shape((half, dim), BF), shape((eigh...]
    all_to_all x1, blocking collectives: 43.5 us -> 30.8 us  [body(): got = lax.all_to_all(send, ('x', 'zp', *CENT), 0, 0)]
    unnamed x10 -> x11, local copies, waits for them, and re-layouts: 8.17 us -> 1.49 us
    all_to_all x1, waiting for transfers between devices: 3.67 us -> 7.09 us  [body(): stats = lax.all_to_all(send_stats, ('zq', *CENT), 0, 0)]
  transfers between devices with their start and end apart: 10 -> 10, of which waited for: 2 -> 1; matrix products, arithmetic and copies ran while one was open for 0% -> 0% of each run, Pallas kernels for 18% -> 41%
where the time goes in v6:
time: 155 us
  Pallas kernels  91.8 us (59%)
  blocking collectives  30.8 us (20%)
  starting transfers between devices  22.9 us (15%)
  waiting for transfers between devices  7.11 us (5%)
    pallas_call x1, Pallas kernels, body(): pl.pallas_call(stats_kernel, grid=(rows // TILE,), out_shape=(shape(stats...  55 us
    all_to_all x1, blocking collectives, body(): got = lax.all_to_all(send, ('x', 'zp', *CENT), 0, 0)  30.8 us
    pallas_call x1, Pallas kernels, body(): pl.pallas_call(cut_kernel, out_shape=(shape((half, dim), BF), shape((eigh...  21.6 us
    pallas_call x3, Pallas kernels, call(): pl.pallas_call(kernel, out_shape=out_shape, in_specs=[SMEM] + [VMEM] * (2...  14.2 us
    ppermute x3, starting transfers between devices, ring(): return lax.ppermute(a, 'zq', [(i, (i + k) % NQ) for i in range(NQ)])  11.4 us
    all_to_all x1, waiting for transfers between devices, body(): stats = lax.all_to_all(send_stats, ('zq', *CENT), 0, 0)  7.09 us
    all_to_all x1, starting transfers between devices, body(): stats = lax.all_to_all(send_stats, ('zq', *CENT), 0, 0)  6.77 us
    ppermute x3, starting transfers between devices, body(): lax.ppermute(far, 'y', [(i, i ^ k) for i in range(NY)])  3.96 us
  transfers between devices with their start and end apart: 10, of which 1 were waited for; matrix products, arithmetic and copies ran while one was open for 0% of the time, Pallas kernels for 41%

profile of v6, /device:TPU:1, one launch (start us, length us, event | category | flops | bytes accessed | tf_op | source)
XLA Modules:
  0.0 155.0 jit_solution(6978703414577702402)
XLA Ops:
  0.0 0.6 pad_add_fusion.place
  0.6 21.6 %cut.1 = (bf16[256,1024]{1,0:T(8,128)(2,1)}, bf16[64,1024]{1,0:T(8,128)(2,1)}) custom-call(s32[4]{0:T(128)} %pad_add_fusion.place, bf16[512,1024]{1,0:T(8,128)(2,1)} %own), custom_call_target="tpu_custom_call" | custom-call | flops 1 | bytes 1 | tf_op jit(solution)/shard_map/cut/pallas_call | solution.py:217
  22.3 3.9 %collective-permute-start = (bf16[256,1024]{1,0:T(8,128)(2,1)}, bf16[256,1024]{1,0:T(8,128)(2,1)S(1)}, u32[]{:S(2)}, u32[]{:S(2)}) collective-permute-start(bf16[256,1024]{1,0:T(8,128)(2,1)} %get-tuple-element.25), channel_id=1, source_target_pairs={{0,16},{16,32},{32,48},{48,0},{1,17},{17,33},{33,49},{49,1},{2,18}... | collective-permute-start | bytes 1572872 | tf_op jit(solution)/shard_map/ppermute | solution.py:229
  26.2 3.1 %collective-permute-start.1 = (bf16[256,1024]{1,0:T(8,128)(2,1)}, bf16[256,1024]{1,0:T(8,128)(2,1)S(1)}, u32[]{:S(2)}, u32[]{:S(2)}) collective-permute-start(bf16[256,1024]{1,0:T(8,128)(2,1)} %get-tuple-element.25), channel_id=1, source_target_pairs={{0,48},{16,0},{32,16},{48,32},{1,49},{17,1},{33,17},{49,33},{2,50}... | collective-permute-start | bytes 1572872 | tf_op jit(solution)/shard_map/ppermute | solution.py:229
  29.3 4.4 %collective-permute-start.4 = (bf16[64,1024]{1,0:T(8,128)(2,1)}, bf16[64,1024]{1,0:T(8,128)(2,1)S(1)}, u32[]{:S(2)}, u32[]{:S(2)}) collective-permute-start(bf16[64,1024]{1,0:T(8,128)(2,1)} %get-tuple-element.26), channel_id=1, source_target_pairs={{0,32},{16,48},{32,0},{48,16},{1,33},{17,49},{33,1},{49,17},{2,34}... | collective-permute-start | bytes 393224 | tf_op jit(solution)/shard_map/ppermute | solution.py:229
  33.7 55.0 %stats.1 = (f32[32,8,128]{2,1,0:T(8,128)}, bf16[832,1024]{1,0:T(8,128)(2,1)}) custom-call(s32[4]{0:T(128)} %pad_add_fusion.place, bf16[512,1024]{1,0:T(8,128)(2,1)} %own, bf16[3200,1024]{1,0:T(8,128)(2,1)} %table.1, bf16[3200,1024]{1,0:T(8,128)(2,1)} %table.1), custom_call_target="tpu_custom_call" | custom-call | flops 1 | bytes 1 | tf_op jit(solution)/shard_map/stats/pallas_call | solution.py:238
  88.7 6.8 %all-to-all-start = ((f32[32,8,128]{2,1,0:T(8,128)}), f32[32,8,128]{2,1,0:T(8,128)S(1)}, u32[]{:S(2)}, u32[]{:S(2)}) async-start(f32[32,8,128]{2,1,0:T(8,128)} %get-tuple-element.28), calls=%async_computation | async-start | bytes 262144 | tf_op jit(solution)/shard_map/all_to_all | solution.py:255
  95.5 0.0 collective-permute-done.4
  95.5 1.5 collective-permute-start.5
  97.0 2.4 %collective-permute-start.6 = (bf16[64,1024]{1,0:T(8,128)(2,1)S(1)}, bf16[64,1024]{1,0:T(8,128)(2,1)S(1)}, u32[]{:S(2)}, u32[]{:S(2)}) collective-permute-start(bf16[64,1024]{1,0:T(8,128)(2,1)S(1)} %collective-permute-done.4), channel_id=1, source_target_pairs={{0,4},{2,6},{4,0},{6,2},{1,5},{3,7},{5,1},{7,3},{8,12},{10,14},{12... | collective-permute-start | bytes 393224 | tf_op jit(solution)/shard_map/ppermute | solution.py:270
  99.4 0.1 collective-permute-start.7
  99.5 7.1 %all-to-all-done.stats = f32[32,8,128]{2,1,0:T(8,128)S(1)} async-done(((f32[32,8,128]{2,1,0:T(8,128)}), f32[32,8,128]{2,1,0:T(8,128)S(1)}, u32[]{:S(2)}, u32[]{:S(2)}) %all-to-all-start) | async-done | bytes 131104 | tf_op jit(solution)/shard_map/all_to_all | solution.py:255
  106.6 0.0 collective-permute-done.1.down
  106.6 1.4 copy-done
  108.1 2.9 %own_kernel.1 = (f32[832,1024]{1,0:T(8,128)S(1)}, f32[832,128]{1,0:T(8,128)S(1)}, f32[832,1]{1,0:T(8,128)S(1)}) custom-call(s32[4]{0:T(128)S(1)} %copy-done.3, f32[32,8,128]{2,1,0:T(8,128)S(1)} %all-to-all-done.stats, bf16[832,1024]{1,0:T(8,128)(2,1)S(1)} %copy-done, bf16[512,1024]{1,0:T(8,128)(2,1)S(1)} %copy-done.2), custom_call_target="tpu_custom_call" | custom-call | flops 1 | bytes 1 | tf_op jit(solution)/shard_map/own_kernel/pallas_call | solution.py:258
  111.0 0.0 collective-permute-done.6
  111.0 0.0 collective-permute-done.7
  111.1 0.3 collective-permute-start.8
  111.4 0.3 collective-permute-start.2
  111.7 0.2 collective-permute-start.3
  111.9 5.2 %first_kernel.1 = (f32[832,1024]{1,0:T(8,128)S(1)}, f32[832,128]{1,0:T(8,128)S(1)}) custom-call(s32[4]{0:T(128)S(1)} %copy-done.3, f32[32,8,128]{2,1,0:T(8,128)S(1)} %all-to-all-done.stats, bf16[832,1024]{1,0:T(8,128)(2,1)S(1)} %copy-done.1, f32[832,1]{1,0:T(8,128)S(1)} %get-tuple-element.31.norms, bf16[256,1024]{1,0:T(8,128)(2,1)S(1)} %collective-permute-done.up, ...), custom_call_target="tpu_custom_call" | custom-call | flops 1 | bytes 1 | tf_op jit(solution)/shard_map/first_kernel/pallas_call | solution.py:258
  117.1 6.1 %second_kernel.1 = bf16[64,104,128]{2,1,0:T(8,128)(2,1)S(1)} custom-call(s32[4]{0:T(128)S(1)} %copy-done.3, f32[32,8,128]{2,1,0:T(8,128)S(1)} %all-to-all-done.stats, bf16[832,1024]{1,0:T(8,128)(2,1)S(1)} %copy-done.1, f32[832,1]{1,0:T(8,128)S(1)} %get-tuple-element.31.norms, bf16[256,1024]{1,0:T(8,128)(2,1)S(1)} %collective-permute-done.2.up, ...), custom_call_target="tpu_custom_call" | custom-call | flops 1 | bytes 1 | tf_op jit(solution)/shard_map/second_kernel/pallas_call | solution.py:258
  123.2 30.8 %all_to_all.10.got = bf16[64,104,128]{2,1,0:T(8,128)(2,1)S(1)} all-to-all(bf16[64,104,128]{2,1,0:T(8,128)(2,1)S(1)} %second_kernel.1), channel_id=1, replica_groups=mesh['x'=4,'zq'=4,'zp'=2,'y'=4,'core'=2] {'x','zp','y','core'}, dimensions={0} | all-to-all | bytes 3407872 | tf_op jit(solution)/shard_map/all_to_all | solution.py:289
  154.0 1.0 final.1
  (16 shorter events, 0.1 us)
Async XLA Ops:
  22.3 84.3 %collective-permute-start = (bf16[256,1024]{1,0:T(8,128)(2,1)}, bf16[256,1024]{1,0:T(8,128)(2,1)S(1)}, u32[]{:S(2)}, u32[]{:S(2)}) collective-permute-start(bf16[256,1024]{1,0:T(8,128)(2,1)} %get-tuple-element.25), channel_id=1, source_target_pairs={{0,16},{16,32},{32,48},{48,0},{1,17},{17,33},{33,49},{49,1},{2,18}... | collective-permute-start | bytes 1572872 | tf_op jit(solution)/shard_map/ppermute | solution.py:229
  26.2 80.4 %collective-permute-start.1 = (bf16[256,1024]{1,0:T(8,128)(2,1)}, bf16[256,1024]{1,0:T(8,128)(2,1)S(1)}, u32[]{:S(2)}, u32[]{:S(2)}) collective-permute-start(bf16[256,1024]{1,0:T(8,128)(2,1)} %get-tuple-element.25), channel_id=1, source_target_pairs={{0,48},{16,0},{32,16},{48,32},{1,49},{17,1},{33,17},{49,33},{2,50}... | collective-permute-start | bytes 1572872 | tf_op jit(solution)/shard_map/ppermute | solution.py:229
  29.3 77.3 %copy-start.2 = (bf16[512,1024]{1,0:T(8,128)(2,1)S(1)}, bf16[512,1024]{1,0:T(8,128)(2,1)}, u32[]{:S(2)}) copy-start(bf16[512,1024]{1,0:T(8,128)(2,1)} %own) | copy-start | bytes 3145732
  29.3 77.3 %copy-start.3 = (s32[4]{0:T(128)S(1)}, s32[4]{0:T(128)}, u32[]{:S(2)}) copy-start(s32[4]{0:T(128)} %pad_add_fusion.place) | copy-start | bytes 52
  29.3 66.2 %collective-permute-start.4 = (bf16[64,1024]{1,0:T(8,128)(2,1)}, bf16[64,1024]{1,0:T(8,128)(2,1)S(1)}, u32[]{:S(2)}, u32[]{:S(2)}) collective-permute-start(bf16[64,1024]{1,0:T(8,128)(2,1)} %get-tuple-element.26), channel_id=1, source_target_pairs={{0,32},{16,48},{32,0},{48,16},{1,33},{17,49},{33,1},{49,17},{2,34}... | collective-permute-start | bytes 393224 | tf_op jit(solution)/shard_map/ppermute | solution.py:229
  88.7 17.8 %all-to-all-start = ((f32[32,8,128]{2,1,0:T(8,128)}), f32[32,8,128]{2,1,0:T(8,128)S(1)}, u32[]{:S(2)}, u32[]{:S(2)}) async-start(f32[32,8,128]{2,1,0:T(8,128)} %get-tuple-element.28), calls=%async_computation | async-start | bytes 262144 | tf_op jit(solution)/shard_map/all_to_all | solution.py:255
  95.5 15.4 %collective-permute-start.5 = (bf16[64,1024]{1,0:T(8,128)(2,1)S(1)}, bf16[64,1024]{1,0:T(8,128)(2,1)S(1)}, u32[]{:S(2)}, u32[]{:S(2)}) collective-permute-start(bf16[64,1024]{1,0:T(8,128)(2,1)S(1)} %collective-permute-done.4), channel_id=1, source_target_pairs={{0,2},{2,0},{4,6},{6,4},{1,3},{3,1},{5,7},{7,5},{8,10},{10,8},{12,... | collective-permute-start | bytes 393224 | tf_op jit(solution)/shard_map/ppermute | solution.py:270
  97.0 14.0 %collective-permute-start.6 = (bf16[64,1024]{1,0:T(8,128)(2,1)S(1)}, bf16[64,1024]{1,0:T(8,128)(2,1)S(1)}, u32[]{:S(2)}, u32[]{:S(2)}) collective-permute-start(bf16[64,1024]{1,0:T(8,128)(2,1)S(1)} %collective-permute-done.4), channel_id=1, source_target_pairs={{0,4},{2,6},{4,0},{6,2},{1,5},{3,7},{5,1},{7,3},{8,12},{10,14},{12... | collective-permute-start | bytes 393224 | tf_op jit(solution)/shard_map/ppermute | solution.py:270
  99.4 11.6 %collective-permute-start.7 = (bf16[64,1024]{1,0:T(8,128)(2,1)S(1)}, bf16[64,1024]{1,0:T(8,128)(2,1)S(1)}, u32[]{:S(2)}, u32[]{:S(2)}) collective-permute-start(bf16[64,1024]{1,0:T(8,128)(2,1)S(1)} %collective-permute-done.4), channel_id=1, source_target_pairs={{0,6},{2,4},{4,2},{6,0},{1,7},{3,5},{5,3},{7,1},{8,14},{10,12},{12... | collective-permute-start | bytes 393224 | tf_op jit(solution)/shard_map/ppermute | solution.py:270
  106.6 1.5 copy-start
  108.1 3.8 %copy-start.1 = (bf16[832,1024]{1,0:T(8,128)(2,1)S(1)}, bf16[832,1024]{1,0:T(8,128)(2,1)}, u32[]{:S(2)}) copy-start(bf16[832,1024]{1,0:T(8,128)(2,1)} %get-tuple-element.30.rows) | copy-start | bytes 5111812
  111.1 6.1 %collective-permute-start.8 = (bf16[256,1024]{1,0:T(8,128)(2,1)S(1)}, bf16[256,1024]{1,0:T(8,128)(2,1)S(1)}, u32[]{:S(2)}, u32[]{:S(2)}) collective-permute-start(bf16[256,1024]{1,0:T(8,128)(2,1)S(1)} %constant_dynamic-update-slice_fusion.far), channel_id=1, source_target_pairs={{0,1},{1,0},{2,3},{3,2},{4,5},{5,4},{6,7},{7,6},{8,9},{9,8},{10,11... | collective-permute-start | bytes 1572872 | tf_op jit(solution)/shard_map/ppermute | solution.py:277
  111.4 5.8 %collective-permute-start.2 = (bf16[256,1024]{1,0:T(8,128)(2,1)S(1)}, bf16[256,1024]{1,0:T(8,128)(2,1)S(1)}, u32[]{:S(2)}, u32[]{:S(2)}) collective-permute-start(bf16[256,1024]{1,0:T(8,128)(2,1)S(1)} %collective-permute-done.up), channel_id=1, source_target_pairs={{0,1},{1,0},{2,3},{3,2},{4,5},{5,4},{6,7},{7,6},{8,9},{9,8},{10,11... | collective-permute-start | bytes 1572872 | tf_op jit(solution)/shard_map/ppermute | solution.py:272
  111.7 5.5 %collective-permute-start.3 = (bf16[256,1024]{1,0:T(8,128)(2,1)S(1)}, bf16[256,1024]{1,0:T(8,128)(2,1)S(1)}, u32[]{:S(2)}, u32[]{:S(2)}) collective-permute-start(bf16[256,1024]{1,0:T(8,128)(2,1)S(1)} %collective-permute-done.1.down), channel_id=1, source_target_pairs={{0,1},{1,0},{2,3},{3,2},{4,5},{5,4},{6,7},{7,6},{8,9},{9,8},{10,11... | collective-permute-start | bytes 1572872 | tf_op jit(solution)/shard_map/ppermute | solution.py:272

commit v7 on v6

--- a/solution.py
+++ b/solution.py
@@ -31,33 +31,17 @@
     return pltpu.CompilerParams(vmem_limit_bytes=mib * MIB)
 
 
-def cut_kernel(place, points, half_out, eighth_out, sem):
+def cut_kernel(place, points, half_out, eighth_out):
     half, eighth = half_out.shape[0], eighth_out.shape[0]
-    a = pltpu.make_async_copy(points.at[pl.ds(pl.multiple_of(place[0] * half, half), half)], half_out, sem.at[0])
-    b = pltpu.make_async_copy(
-        points.at[pl.ds(pl.multiple_of(place[1] * eighth, eighth), eighth)], eighth_out, sem.at[1]
-    )
-    a.start()
-    b.start()
-    a.wait()
-    b.wait()
-
-
-def stats_kernel(place, points, cents, table, out, mine, top, total, sems):
+    half_out[...] = points[pl.ds(pl.multiple_of(place[0] * half, half), half)]
+    eighth_out[...] = points[pl.ds(pl.multiple_of(place[1] * eighth, eighth), eighth)]
+
+
+def stats_kernel(points, cents, out, top, total):
     step = pl.program_id(0)
-    count = NX
-    window = mine.shape[0] // count
-    stride = table.shape[0] // count
-    start = pl.multiple_of(place[2] * (stride // NQ) // 16 * 16, 16)
-    copies = [
-        pltpu.make_async_copy(table.at[pl.ds(i * stride + start, window)], mine.at[pl.ds(i * window, window)], sems.at[i])
-        for i in range(count)
-    ]
 
     @pl.when(step == 0)
     def _():
-        for copy in copies:
-            copy.start()
         top[...] = jnp.full_like(top, -jnp.inf)
         total[...] = jnp.zeros_like(total)
 
@@ -81,8 +65,22 @@
         groups = top.shape[1] // LANES
         both = [r[:, g * LANES : (g + 1) * LANES] for r in (top[...], total[...]) for g in range(groups)]
         out[...] = jnp.broadcast_to(jnp.concatenate(both, axis=0)[None], out.shape)
-        for copy in copies:
-            copy.wait()
+
+
+def window_kernel(place, table, after, mine, norms, sems):
+    window = mine.shape[0] // NX
+    stride = table.shape[0] // NX
+    start = pl.multiple_of(place[2] * (stride // NQ) // 16 * 16, 16)
+    copies = [
+        pltpu.make_async_copy(table.at[pl.ds(i * stride + start, window)], mine.at[pl.ds(i * window, window)], sems.at[i])
+        for i in range(NX)
+    ]
+    for copy in copies:
+        copy.start()
+    for i, copy in enumerate(copies):
+        copy.wait()
+        wide = mine[i * window : (i + 1) * window].astype(F32)
+        norms[i * window : (i + 1) * window] = 0.5 * jnp.sum(wide * wide, axis=1, keepdims=True)
 
 
 def lse_of(stats, source):
@@ -100,27 +98,24 @@
     return jnp.where(first, lse[:half], lse[half:]), jnp.where(first, lse[half:], lse[:half])
 
 
-def weighted(pieces, rows, shift, weights):
+def weighted(pieces, rows, shift, weights, held):
     counts = jnp.zeros((rows.shape[0], LANES), F32)
     at = 0
     for ref, lse in pieces:
         n = ref.shape[0]
         for c in range(0, n, CUT):
-            logits = dot_nt(rows, ref[c : c + CUT])
+            block = ref[c : c + CUT]
+            if held is not None:
+                held[at + c : at + c + CUT] = block
+            logits = dot_nt(rows, block)
             for g in range(CUT // LANES):
                 row = c // LANES + g
                 w = jnp.exp(logits[:, g * LANES : (g + 1) * LANES] - shift - lse[row : row + 1]).astype(BF)
                 counts += w.astype(F32)
                 weights[:, at + c + g * LANES : at + c + (g + 1) * LANES] = w
         at += n
-    numer = None
-    at = 0
-    for ref, _ in pieces:
-        n = ref.shape[0]
-        term = jnp.dot(weights[:, at : at + n], ref[...], preferred_element_type=F32)
-        numer = term if numer is None else numer + term
-        at += n
-    return numer, counts
+    source = pieces[0][0] if held is None else held
+    return jnp.dot(weights[...], source[...], preferred_element_type=F32), counts
 
 
 def row_counts(part):
@@ -143,12 +138,9 @@
     return high, counts - high
 
 
-def own_kernel(place, stats, rows, own, numer, counts, norms, weights):
-    values = rows[...]
-    wide = values.astype(F32)
-    shift = 0.5 * jnp.sum(wide * wide, axis=1, keepdims=True)
-    norms[...] = shift
-    numer[...], counts[...] = weighted([(own, lse_of(stats, place[2]))], values, shift, weights)
+def own_kernel(place, stats, rows, norms, own, numer, counts, weights):
+    pieces = [(own, lse_of(stats, place[2]))]
+    numer[...], counts[...] = weighted(pieces, rows[...], norms[...], weights, None)
 
 
 def half_pieces(place, stats, up, down, far, which):
@@ -160,15 +152,15 @@
     return [(far, lse)] + pieces
 
 
-def first_kernel(place, stats, rows, norms, up, down, far, numer_in, counts_in, numer, counts, weights):
+def first_kernel(place, stats, rows, norms, up, down, far, numer_in, counts_in, numer, counts, weights, held):
     pieces = half_pieces(place, stats, up, down, far, 0)
-    more, more_counts = weighted(pieces, rows[...], norms[...], weights)
+    more, more_counts = weighted(pieces, rows[...], norms[...], weights, held)
     numer[...], counts[...] = numer_in[...] + more, counts_in[...] + more_counts
 
 
-def second_kernel(place, stats, rows, norms, up, down, far, numer_in, counts_in, send, weights, numer, counts):
+def second_kernel(place, stats, rows, norms, up, down, far, numer_in, counts_in, send, weights, held, numer, counts):
     pieces = half_pieces(place, stats, up, down, far, 1)
-    more, more_counts = weighted(pieces, rows[...], norms[...], weights)
+    more, more_counts = weighted(pieces, rows[...], norms[...], weights, held)
     numer[...], counts[...] = numer_in[...] + more, counts_in[...] + more_counts
     n, height, _ = send.shape
     slot = height - TAIL
@@ -217,10 +209,9 @@
     own_half, own_eighth = pl.pallas_call(
         cut_kernel,
         out_shape=(shape((half, dim), BF), shape((eighth, dim), BF)),
-        in_specs=[SMEM, ANY],
-        out_specs=(ANY, ANY),
-        scratch_shapes=[pltpu.SemaphoreType.DMA((2,))],
-        compiler_params=params(62),
+        in_specs=[SMEM, VMEM],
+        out_specs=(VMEM, VMEM),
+        compiler_params=params(4),
         cost_estimate=CHEAP,
         name="cut",
     )(place, points)
@@ -235,56 +226,61 @@
     window = -(-(rows // (NX * NQ)) // 16) * 16
     work = NX * window
     stats_shape = (NQ * N_CENT, 2 * pts // LANES, LANES)
-    send_stats, mine = pl.pallas_call(
+    send_stats = pl.pallas_call(
         stats_kernel,
         grid=(rows // TILE,),
-        out_shape=(shape(stats_shape, F32), shape((work, dim), BF)),
-        in_specs=[
-            SMEM,
-            pl.BlockSpec((pts, dim), lambda i: (0, 0)),
-            pl.BlockSpec((TILE, dim), lambda i: (i, 0)),
-            ANY,
-        ],
-        out_specs=(pl.BlockSpec(stats_shape, lambda i: (0, 0, 0)), ANY),
-        scratch_shapes=[pltpu.VMEM((1, pts), F32), pltpu.VMEM((1, pts), F32), pltpu.SemaphoreType.DMA((NX,))],
-        compiler_params=params(57),
+        out_shape=shape(stats_shape, F32),
+        in_specs=[pl.BlockSpec((pts, dim), lambda i: (0, 0)), pl.BlockSpec((TILE, dim), lambda i: (i, 0))],
+        out_specs=pl.BlockSpec(stats_shape, lambda i: (0, 0, 0)),
+        scratch_shapes=[pltpu.VMEM((1, pts), F32), pltpu.VMEM((1, pts), F32)],
+        compiler_params=params(54),
         cost_estimate=CHEAP,
         name="stats",
-    )(place, points, centroids, centroids)
+    )(points, centroids)
     far, _ = lax.optimization_barrier((far, send_stats))
     stats = lax.all_to_all(send_stats, ("zq", *CENT), 0, 0)
+    mine, norms = pl.pallas_call(
+        window_kernel,
+        out_shape=(shape((work, dim), BF), shape((work, 1), F32)),
+        in_specs=[SMEM, ANY, ANY],
+        out_specs=(VMEM, VMEM),
+        scratch_shapes=[pltpu.SemaphoreType.DMA((NX,))],
+        compiler_params=params(50),
+        cost_estimate=CHEAP,
+        name="window",
+    )(place, centroids, send_stats)
 
     def call(kernel, out_shape, n_points, *args, scratch=()):
         return pl.pallas_call(
             kernel,
             out_shape=out_shape,
-            in_specs=[SMEM] + [VMEM] * (2 + len(args)),
+            in_specs=[SMEM] + [VMEM] * (3 + len(args)),
             out_specs=jax.tree.map(lambda _: VMEM, out_shape),
             scratch_shapes=[pltpu.VMEM((work, n_points), BF), *scratch],
             compiler_params=params(28),
             cost_estimate=CHEAP,
             name=kernel.__name__,
-        )(place, stats, mine, *args)
+        )(place, stats, mine, norms, *args)
 
     swap = [(0, 1), (1, 0)]
     slices = [far] + [lax.ppermute(far, "y", [(i, i ^ k) for i in range(NY)]) for k in range(1, NY)]
     up, down, stats = lax.optimization_barrier((up, down, stats))
     others = [lax.ppermute(a, "core", swap) for a in (up, down)]
     sums = (shape((work, dim), F32), shape((work, LANES), F32))
-    *numer, norms = call(own_kernel, (*sums, shape((work, 1), F32)), pts, points)
+    numer = call(own_kernel, sums, pts, points)
     slices, numer = lax.optimization_barrier((slices, numer))
     far = jnp.concatenate(slices, axis=0)
     others.append(lax.ppermute(far, "core", swap))
     more = (NQ - 1) * half
-    numer = call(first_kernel, sums, more, norms, up, down, far, *numer)
+    held = pltpu.VMEM((more, dim), BF)
+    numer = call(first_kernel, sums, more, up, down, far, *numer, scratch=[held])
     send = call(
         second_kernel,
         shape((n_blocks * N_CENT, height, LANES), BF),
         more,
-        norms,
         *others,
         *numer,
-        scratch=[pltpu.VMEM(s.shape, F32) for s in sums],
+        scratch=[held, *(pltpu.VMEM(s.shape, F32) for s in sums)],
     )
     got = lax.all_to_all(send, ("x", "zp", *CENT), 0, 0)
     return pl.pallas_call(

time: 155 us -> 102 us (0.66)
  Pallas kernels: 91.8 us -> 26 us
  blocking collectives: 30.8 us -> 39.2 us
  local copies, waits for them, and re-layouts: 1.5 us -> 4.89 us
  waiting for transfers between devices: 7.11 us -> 8.95 us
    pallas_call x4 -> x5, Pallas kernels: 69.2 us -> 23.6 us  [the longest x3 12.9 us: call(): pl.pallas_call(kernel, out_shape=out_shape, in_specs=[SMEM] + [VMEM] * (3...]
    pallas_call x1, Pallas kernels: 21.6 us -> 1.41 us  [body(): pl.pallas_call(cut_kernel, out_shape=(shape((half, dim), BF), shape((eigh...]
    all_to_all x1, blocking collectives: 30.8 us -> 39.2 us  [body(): got = lax.all_to_all(send, ('x', 'zp', *CENT), 0, 0)]
    unnamed x11 -> x9, local copies, waits for them, and re-layouts: 1.49 us -> 3.98 us
    ppermute x3, waiting for transfers between devices: 0.01 us -> 2.29 us  [ring(): return lax.ppermute(a, 'zq', [(i, (i + k) % NQ) for i in range(NQ)])]
  transfers between devices with their start and end apart: 10 -> 10, of which waited for: 1 -> 2; matrix products, arithmetic and copies ran while one was open for 0% -> 0% of each run, Pallas kernels for 41% -> 18%
where the time goes in v7:
time: 102 us
  blocking collectives  39.2 us (38%)
  Pallas kernels  26 us (25%)
  starting transfers between devices  22.4 us (22%)
  waiting for transfers between devices  8.95 us (9%)
  local copies, waits for them, and re-layouts  4.89 us (5%)
    all_to_all x1, blocking collectives, body(): got = lax.all_to_all(send, ('x', 'zp', *CENT), 0, 0)  39.2 us
    pallas_call x3, Pallas kernels, call(): pl.pallas_call(kernel, out_shape=out_shape, in_specs=[SMEM] + [VMEM] * (3...  12.9 us
    ppermute x3, starting transfers between devices, ring(): return lax.ppermute(a, 'zq', [(i, (i + k) % NQ) for i in range(NQ)])  11.3 us
    pallas_call x1, Pallas kernels, body(): pl.pallas_call(stats_kernel, grid=(rows // TILE,), out_shape=shape(stats_...  8.5 us
    all_to_all x1, waiting for transfers between devices, body(): stats = lax.all_to_all(send_stats, ('zq', *CENT), 0, 0)  6.64 us
    all_to_all x1, starting transfers between devices, body(): stats = lax.all_to_all(send_stats, ('zq', *CENT), 0, 0)  6.47 us
    unnamed x9, local copies, waits for them, and re-layouts  3.98 us
    ppermute x3, starting transfers between devices, body(): lax.ppermute(far, 'y', [(i, i ^ k) for i in range(NY)])  3.92 us
  transfers between devices with their start and end apart: 10, of which 2 were waited for; matrix products, arithmetic and copies ran while one was open for 0% of the time, Pallas kernels for 18%

profile of v7, /device:TPU:1, one launch (start us, length us, event | category | flops | bytes accessed | tf_op | source)
XLA Modules:
  0.0 101.7 jit_solution(3236025105440028365)
XLA Ops:
  0.1 1.2 %copy-done = bf16[512,1024]{1,0:T(8,128)(2,1)S(1)} copy-done((bf16[512,1024]{1,0:T(8,128)(2,1)S(1)}, bf16[512,1024]{1,0:T(8,128)(2,1)}, u32[]{:S(2)}) %copy-start) | copy-done | bytes 1048600
  1.3 1.4 %cut.1 = (bf16[256,1024]{1,0:T(8,128)(2,1)}, bf16[64,1024]{1,0:T(8,128)(2,1)S(1)}) custom-call(s32[4]{0:T(128)S(1)} %pad_add_fusion.place, bf16[512,1024]{1,0:T(8,128)(2,1)S(1)} %copy-done), custom_call_target="tpu_custom_call" | custom-call | flops 1 | bytes 1 | tf_op jit(solution)/shard_map/cut/pallas_call | solution.py:209
  2.7 3.8 %collective-permute-start = (bf16[256,1024]{1,0:T(8,128)(2,1)}, bf16[256,1024]{1,0:T(8,128)(2,1)}, u32[]{:S(2)}, u32[]{:S(2)}) collective-permute-start(bf16[256,1024]{1,0:T(8,128)(2,1)} %get-tuple-element.24), channel_id=1, source_target_pairs={{0,16},{16,32},{32,48},{48,0},{1,17},{17,33},{33,49},{49,1},{2,18}... | collective-permute-start | bytes 1572872 | tf_op jit(solution)/shard_map/ppermute | solution.py:220
  6.5 3.0 %collective-permute-start.1 = (bf16[256,1024]{1,0:T(8,128)(2,1)}, bf16[256,1024]{1,0:T(8,128)(2,1)}, u32[]{:S(2)}, u32[]{:S(2)}) collective-permute-start(bf16[256,1024]{1,0:T(8,128)(2,1)} %get-tuple-element.24), channel_id=1, source_target_pairs={{0,48},{16,0},{32,16},{48,32},{1,49},{17,1},{33,17},{49,33},{2,50}... | collective-permute-start | bytes 1572872 | tf_op jit(solution)/shard_map/ppermute | solution.py:220
  9.6 4.5 %collective-permute-start.4 = (bf16[64,1024]{1,0:T(8,128)(2,1)S(1)}, bf16[64,1024]{1,0:T(8,128)(2,1)S(1)}, u32[]{:S(2)}, u32[]{:S(2)}) collective-permute-start(bf16[64,1024]{1,0:T(8,128)(2,1)S(1)} %get-tuple-element.25), channel_id=1, source_target_pairs={{0,32},{16,48},{32,0},{48,16},{1,33},{17,49},{33,1},{49,17},{2,34}... | collective-permute-start | bytes 393224 | tf_op jit(solution)/shard_map/ppermute | solution.py:220
  14.0 8.5 %stats.1.after = f32[32,8,128]{2,1,0:T(8,128)} custom-call(bf16[512,1024]{1,0:T(8,128)(2,1)} %own, bf16[3200,1024]{1,0:T(8,128)(2,1)} %table.1), custom_call_target="tpu_custom_call" | custom-call | flops 1 | bytes 1 | tf_op jit(solution)/shard_map/stats/pallas_call | solution.py:229
  22.5 6.5 %all-to-all-start = ((f32[32,8,128]{2,1,0:T(8,128)}), f32[32,8,128]{2,1,0:T(8,128)S(1)}, u32[]{:S(2)}, u32[]{:S(2)}) async-start(f32[32,8,128]{2,1,0:T(8,128)} %stats.1.after), calls=%async_computation | async-start | bytes 262144 | tf_op jit(solution)/shard_map/all_to_all | solution.py:241
  29.0 2.3 %collective-permute-done.4 = bf16[64,1024]{1,0:T(8,128)(2,1)S(1)} collective-permute-done((bf16[64,1024]{1,0:T(8,128)(2,1)S(1)}, bf16[64,1024]{1,0:T(8,128)(2,1)S(1)}, u32[]{:S(2)}, u32[]{:S(2)}) %collective-permute-start.4) | collective-permute-done | bytes 131104 | tf_op jit(solution)/shard_map/ppermute | solution.py:220
  31.3 1.3 %collective-permute-start.5 = (bf16[64,1024]{1,0:T(8,128)(2,1)S(1)}, bf16[64,1024]{1,0:T(8,128)(2,1)}, u32[]{:S(2)}, u32[]{:S(2)}) collective-permute-start(bf16[64,1024]{1,0:T(8,128)(2,1)S(1)} %collective-permute-done.4), channel_id=1, source_target_pairs={{0,2},{2,0},{4,6},{6,4},{1,3},{3,1},{5,7},{7,5},{8,10},{10,8},{12,... | collective-permute-start | bytes 393224 | tf_op jit(solution)/shard_map/ppermute | solution.py:266
  32.6 2.6 %collective-permute-start.6 = (bf16[64,1024]{1,0:T(8,128)(2,1)S(1)}, bf16[64,1024]{1,0:T(8,128)(2,1)}, u32[]{:S(2)}, u32[]{:S(2)}) collective-permute-start(bf16[64,1024]{1,0:T(8,128)(2,1)S(1)} %collective-permute-done.4), channel_id=1, source_target_pairs={{0,4},{2,6},{4,0},{6,2},{1,5},{3,7},{5,1},{7,3},{8,12},{10,14},{12... | collective-permute-start | bytes 393224 | tf_op jit(solution)/shard_map/ppermute | solution.py:266
  35.2 0.9 copy-done.2
  36.1 2.2 %window.1 = (bf16[832,1024]{1,0:T(8,128)(2,1)S(1)}, f32[832,1]{1,0:T(8,128)S(1)}) custom-call(s32[4]{0:T(128)S(1)} %pad_add_fusion.place, bf16[3200,1024]{1,0:T(8,128)(2,1)} %table.1, f32[32,8,128]{2,1,0:T(8,128)S(1)} %copy-done.2), custom_call_target="tpu_custom_call" | custom-call | flops 1 | bytes 1 | tf_op jit(solution)/shard_map/window/pallas_call | solution.py:242
  38.4 6.6 %all-to-all-done.stats = f32[32,8,128]{2,1,0:T(8,128)S(1)} async-done(((f32[32,8,128]{2,1,0:T(8,128)}), f32[32,8,128]{2,1,0:T(8,128)S(1)}, u32[]{:S(2)}, u32[]{:S(2)}) %all-to-all-start) | async-done | bytes 131104 | tf_op jit(solution)/shard_map/all_to_all | solution.py:241
  45.0 2.6 %own_kernel.1 = (f32[832,1024]{1,0:T(8,128)S(1)}, f32[832,128]{1,0:T(8,128)S(1)}) custom-call(s32[4]{0:T(128)S(1)} %pad_add_fusion.place, f32[32,8,128]{2,1,0:T(8,128)S(1)} %all-to-all-done.stats, bf16[832,1024]{1,0:T(8,128)(2,1)S(1)} %get-tuple-element.28.rows, f32[832,1]{1,0:T(8,128)S(1)} %get-tuple-element.29.norms, bf16[512,1024]{1,0:T(8,128)(2,1)S(1)} %copy-done.1), custom_call_target="tpu_custom_call" | custom-call | flops 1 | bytes 1 | tf_op jit(solution)/shard_map/own_kernel/pallas_call | solution.py:254
  47.7 0.9 constant_dynamic-update-slice_fusion.2
  48.6 0.9 constant_dynamic-update-slice_fusion.1
  49.6 0.9 constant_dynamic-update-slice_fusion.far
  50.5 0.1 collective-permute-start.8
  50.6 0.5 collective-permute-start.2
  51.1 0.1 collective-permute-start.3
  51.2 5.1 %first_kernel.1 = (f32[832,1024]{1,0:T(8,128)S(1)}, f32[832,128]{1,0:T(8,128)S(1)}) custom-call(s32[4]{0:T(128)S(1)} %pad_add_fusion.place, f32[32,8,128]{2,1,0:T(8,128)S(1)} %all-to-all-done.stats, bf16[832,1024]{1,0:T(8,128)(2,1)S(1)} %get-tuple-element.28.rows, f32[832,1]{1,0:T(8,128)S(1)} %get-tuple-element.29.norms, ...), custom_call_target="tpu_custom_call" | custom-call | flops 1 | bytes 1 | tf_op jit(solution)/shard_map/first_kernel/pallas_call | solution.py:254
  56.3 5.2 %second_kernel.1 = bf16[64,104,128]{2,1,0:T(8,128)(2,1)S(1)} custom-call(s32[4]{0:T(128)S(1)} %pad_add_fusion.place, f32[32,8,128]{2,1,0:T(8,128)S(1)} %all-to-all-done.stats, bf16[832,1024]{1,0:T(8,128)(2,1)S(1)} %get-tuple-element.28.rows, f32[832,1]{1,0:T(8,128)S(1)} %get-tuple-element.29.norms, bf16[256,1024]{1,0:T(8,128)(2,1)S(1)} %collective-permute-done.2.up, ...), custom_call_target="tpu_custom_call" | custom-call | flops 1 | bytes 1 | tf_op jit(solution)/shard_map/second_kernel/pallas_call | solution.py:254
  61.5 39.2 %all_to_all.10.got = bf16[64,104,128]{2,1,0:T(8,128)(2,1)S(1)} all-to-all(bf16[64,104,128]{2,1,0:T(8,128)(2,1)S(1)} %second_kernel.1), channel_id=1, replica_groups=mesh['x'=4,'zq'=4,'zp'=2,'y'=4,'core'=2] {'x','zp','y','core'}, dimensions={0} | all-to-all | bytes 3407872 | tf_op jit(solution)/shard_map/all_to_all | solution.py:285
  100.7 1.0 final.1
  (15 shorter events, 0.1 us)
Async XLA Ops:
  0.1 1.2 %copy-start = (bf16[512,1024]{1,0:T(8,128)(2,1)S(1)}, bf16[512,1024]{1,0:T(8,128)(2,1)}, u32[]{:S(2)}) copy-start(bf16[512,1024]{1,0:T(8,128)(2,1)} %own) | copy-start | bytes 3145732
  2.7 42.3 %collective-permute-start = (bf16[256,1024]{1,0:T(8,128)(2,1)}, bf16[256,1024]{1,0:T(8,128)(2,1)}, u32[]{:S(2)}, u32[]{:S(2)}) collective-permute-start(bf16[256,1024]{1,0:T(8,128)(2,1)} %get-tuple-element.24), channel_id=1, source_target_pairs={{0,16},{16,32},{32,48},{48,0},{1,17},{17,33},{33,49},{49,1},{2,18}... | collective-permute-start | bytes 1572872 | tf_op jit(solution)/shard_map/ppermute | solution.py:220
  6.5 38.5 %collective-permute-start.1 = (bf16[256,1024]{1,0:T(8,128)(2,1)}, bf16[256,1024]{1,0:T(8,128)(2,1)}, u32[]{:S(2)}, u32[]{:S(2)}) collective-permute-start(bf16[256,1024]{1,0:T(8,128)(2,1)} %get-tuple-element.24), channel_id=1, source_target_pairs={{0,48},{16,0},{32,16},{48,32},{1,49},{17,1},{33,17},{49,33},{2,50}... | collective-permute-start | bytes 1572872 | tf_op jit(solution)/shard_map/ppermute | solution.py:220
  9.6 21.7 %collective-permute-start.4 = (bf16[64,1024]{1,0:T(8,128)(2,1)S(1)}, bf16[64,1024]{1,0:T(8,128)(2,1)S(1)}, u32[]{:S(2)}, u32[]{:S(2)}) collective-permute-start(bf16[64,1024]{1,0:T(8,128)(2,1)S(1)} %get-tuple-element.25), channel_id=1, source_target_pairs={{0,32},{16,48},{32,0},{48,16},{1,33},{17,49},{33,1},{49,17},{2,34}... | collective-permute-start | bytes 393224 | tf_op jit(solution)/shard_map/ppermute | solution.py:220
  22.5 22.5 %all-to-all-start = ((f32[32,8,128]{2,1,0:T(8,128)}), f32[32,8,128]{2,1,0:T(8,128)S(1)}, u32[]{:S(2)}, u32[]{:S(2)}) async-start(f32[32,8,128]{2,1,0:T(8,128)} %stats.1.after), calls=%async_computation | async-start | bytes 262144 | tf_op jit(solution)/shard_map/all_to_all | solution.py:241
  29.0 16.0 %copy-start.1 = (bf16[512,1024]{1,0:T(8,128)(2,1)S(1)}, bf16[512,1024]{1,0:T(8,128)(2,1)}, u32[]{:S(2)}) copy-start(bf16[512,1024]{1,0:T(8,128)(2,1)} %own) | copy-start | bytes 3145732
  31.3 16.4 %collective-permute-start.5 = (bf16[64,1024]{1,0:T(8,128)(2,1)S(1)}, bf16[64,1024]{1,0:T(8,128)(2,1)}, u32[]{:S(2)}, u32[]{:S(2)}) collective-permute-start(bf16[64,1024]{1,0:T(8,128)(2,1)S(1)} %collective-permute-done.4), channel_id=1, source_target_pairs={{0,2},{2,0},{4,6},{6,4},{1,3},{3,1},{5,7},{7,5},{8,10},{10,8},{12,... | collective-permute-start | bytes 393224 | tf_op jit(solution)/shard_map/ppermute | solution.py:266
  32.6 15.1 %collective-permute-start.6 = (bf16[64,1024]{1,0:T(8,128)(2,1)S(1)}, bf16[64,1024]{1,0:T(8,128)(2,1)}, u32[]{:S(2)}, u32[]{:S(2)}) collective-permute-start(bf16[64,1024]{1,0:T(8,128)(2,1)S(1)} %collective-permute-done.4), channel_id=1, source_target_pairs={{0,4},{2,6},{4,0},{6,2},{1,5},{3,7},{5,1},{7,3},{8,12},{10,14},{12... | collective-permute-start | bytes 393224 | tf_op jit(solution)/shard_map/ppermute | solution.py:266
  35.2 12.5 %collective-permute-start.7 = (bf16[64,1024]{1,0:T(8,128)(2,1)S(1)}, bf16[64,1024]{1,0:T(8,128)(2,1)}, u32[]{:S(2)}, u32[]{:S(2)}) collective-permute-start(bf16[64,1024]{1,0:T(8,128)(2,1)S(1)} %collective-permute-done.4), channel_id=1, source_target_pairs={{0,6},{2,4},{4,2},{6,0},{1,7},{3,5},{5,3},{7,1},{8,14},{10,12},{12... | collective-permute-start | bytes 393224 | tf_op jit(solution)/shard_map/ppermute | solution.py:266
  35.2 0.9 copy-start.2
  50.5 5.8 %collective-permute-start.8 = (bf16[256,1024]{1,0:T(8,128)(2,1)S(1)}, bf16[256,1024]{1,0:T(8,128)(2,1)S(1)}, u32[]{:S(2)}, u32[]{:S(2)}) collective-permute-start(bf16[256,1024]{1,0:T(8,128)(2,1)S(1)} %constant_dynamic-update-slice_fusion.far), channel_id=1, source_target_pairs={{0,1},{1,0},{2,3},{3,2},{4,5},{5,4},{6,7},{7,6},{8,9},{9,8},{10,11... | collective-permute-start | bytes 1572872 | tf_op jit(solution)/shard_map/ppermute | solution.py:273
  50.6 5.7 %collective-permute-start.2 = (bf16[256,1024]{1,0:T(8,128)(2,1)}, bf16[256,1024]{1,0:T(8,128)(2,1)S(1)}, u32[]{:S(2)}, u32[]{:S(2)}) collective-permute-start(bf16[256,1024]{1,0:T(8,128)(2,1)} %collective-permute-done.up), channel_id=1, source_target_pairs={{0,1},{1,0},{2,3},{3,2},{4,5},{5,4},{6,7},{7,6},{8,9},{9,8},{10,11... | collective-permute-start | bytes 1572872 | tf_op jit(solution)/shard_map/ppermute | solution.py:268
  51.1 5.2 %collective-permute-start.3 = (bf16[256,1024]{1,0:T(8,128)(2,1)}, bf16[256,1024]{1,0:T(8,128)(2,1)S(1)}, u32[]{:S(2)}, u32[]{:S(2)}) collective-permute-start(bf16[256,1024]{1,0:T(8,128)(2,1)} %collective-permute-done.1.down), channel_id=1, source_target_pairs={{0,1},{1,0},{2,3},{3,2},{4,5},{5,4},{6,7},{7,6},{8,9},{9,8},{10,11... | collective-permute-start | bytes 1572872 | tf_op jit(solution)/shard_map/ppermute | solution.py:268

commit v8 on v7

v8 whole, which is shorter than its diff:
```python
import functools

import jax
import jax.numpy as jnp
from jax import lax
from jax.experimental import pallas as pl
from jax.experimental.pallas import tpu as pltpu
from jax.sharding import Mesh, PartitionSpec as P

BF = jnp.bfloat16
F32 = jnp.float32
NX, NZ, NY, NC = 4, 8, 4, 2
Z = ("zq", "zp")
CENT = ("y", "core")
N_CENT = NY * NC
LANES = 128
TAIL = 4
VMEM = pl.BlockSpec(memory_space=pltpu.VMEM)
SMEM = pl.BlockSpec(memory_space=pltpu.SMEM)
ANY = pl.BlockSpec(memory_space=pl.ANY)
MIB = 2**20
CHEAP = pl.CostEstimate(flops=1, bytes_accessed=1, transcendentals=0)
TILE = 640


def dot_nt(a, b):
    return lax.dot_general(a, b, (((1,), (1,)), ((), ())), preferred_element_type=F32)


def params(mib):
    return pltpu.CompilerParams(vmem_limit_bytes=mib * MIB)


def cut_kernel(place, points, half_out, part_out):
    half, part = half_out.shape[0], part_out.shape[0]
    half_out[...] = points[pl.ds(pl.multiple_of(place[0] * half, half), half)]
    part_out[...] = points[pl.ds(pl.multiple_of(place[1] * part, part), part)]


def stats_kernel(points, cents, out, top, total):
    step = pl.program_id(0)

    @pl.when(step == 0)
    def _():
        top[...] = jnp.full_like(top, -jnp.inf)
        total[...] = jnp.zeros_like(total)

    rows = cents[...]
    chunk = rows.shape[0] // 2
    pts = points[...]
    tops, totals = [top[...]], [total[...]]
    for i in range(2):
        part = rows[i * chunk : (i + 1) * chunk]
        wide = part.astype(F32)
        logits = dot_nt(part, pts) - 0.5 * jnp.sum(wide * wide, axis=1, keepdims=True)
        high = jnp.max(logits, axis=0, keepdims=True)
        tops.append(high)
        totals.append(jnp.sum(jnp.exp(logits - high), axis=0, keepdims=True))
    new = functools.reduce(jnp.maximum, tops)
    top[...] = new
    total[...] = sum(s * jnp.exp(t - new) for s, t in zip(totals, tops))

    @pl.when(step == pl.num_programs(0) - 1)
    def _():
        groups = top.shape[1] // LANES
        both = [r[:, g * LANES : (g + 1) * LANES] for r in (top[...], total[...]) for g in range(groups)]
        out[...] = jnp.broadcast_to(jnp.concatenate(both, axis=0)[None], out.shape)


def window_kernel(place, table, after, mine, norms, sems):
    _, work, _ = mine.shape
    count = NZ // 2
    window = work // count
    stride = table.shape[0] // NX
    slot = stride // NZ
    copies = {}
    for q in range(2):
        for i in range(count):
            at = pl.multiple_of(place[2] * stride + (2 * i + q) * slot // 16 * 16, 16)
            to = mine.at[q, pl.ds(i * window, window)]
            copies[q, i] = pltpu.make_async_copy(table.at[pl.ds(at, window)], to, sems.at[q * count + i])
    for copy in copies.values():
        copy.start()
    for (q, i), copy in copies.items():
        copy.wait()
        here = slice(i * window, (i + 1) * window)
        wide = mine[q, here].astype(F32)
        norms[q, here] = 0.5 * jnp.sum(wide * wide, axis=1, keepdims=True)


def lse_of(stats, source):
    groups = stats.shape[1] // 2
    part = stats[pl.ds(source * N_CENT, N_CENT)]
    m, s = part[:, :groups], part[:, groups:]
    high = jnp.max(m, axis=0)
    return high + jnp.log(jnp.sum(s * jnp.exp(m - high[None]), axis=0))


def lse_halves(place, stats, k):
    lse = lse_of(stats, lax.rem(place[2] + NX - k, NX))
    half = lse.shape[0] // 2
    first = place[0] == 0
    return jnp.where(first, lse[:half], lse[half:]), jnp.where(first, lse[half:], lse[:half])


def weighted(pieces, rows, norms, q, held, numer, counts, before=None):
    at = 0
    lse = []
    for ref, part in pieces:
        held[at : at + ref.shape[0]] = ref[...]
        lse += [part[g : g + 1] for g in range(part.shape[0])]
        at += ref.shape[0]
    logits = dot_nt(rows[q], held[...])
    shift = norms[q]
    some = jnp.zeros(counts.shape, F32)
    weights = []
    for g, part in enumerate(lse):
        w = jnp.exp(logits[:, g * LANES : (g + 1) * LANES] - shift - part).astype(BF)
        some += w.astype(F32)
        weights.append(w)
    more = jnp.dot(jnp.concatenate(weights, axis=1), held[...], preferred_element_type=F32)
    if before is not None:
        more, some = before[0][...] + more, before[1][...] + some
    numer[...] = more
    counts[...] = some


def block_of(numer, counts, i, q, height):
    start = i * (numer.shape[0] * 2 // NZ) + 8 * (i % 2)
    found = []
    for ref in (numer, counts):
        v = ref[start : start + height]
        found.append(jnp.where(q == 1, jnp.concatenate([v[4:], v[:4]], axis=0), v))
    return found[0], row_counts(found[1])


def row_counts(part):
    part = jnp.concatenate([part, jnp.zeros((LANES - part.shape[0], LANES), F32)], axis=0)
    return jnp.sum(part.T, axis=0, keepdims=True)


def close(values, first, second):
    height, width = values.shape
    first = jnp.concatenate([first] * (width // LANES), axis=1)
    second = jnp.concatenate([second] * (width // LANES), axis=1)
    last = values[height - 8 :]
    row = lax.broadcasted_iota(jnp.int32, last.shape, 0)
    last = jnp.where(row == 8 - TAIL, first, jnp.where(row == 9 - TAIL, second, jnp.where(row > 9 - TAIL, 0.0, last)))
    return jnp.concatenate([values[: height - 8], last], axis=0)


def split(counts):
    high = counts.astype(BF).astype(F32)
    return high, counts - high


def own_kernel(place, stats, rows, norms, own, numer, counts, held):
    weighted([(own, lse_of(stats, place[2]))], rows, norms, 1 - place[3], held, numer, counts)


def near_pieces(place, stats, up, down, other_up, other_down):
    pieces = []
    for k, a, b in ((1, up, other_up), (NX - 1, down, other_down)):
        mine, other = lse_halves(place, stats, k)
        pieces += [(a, mine), (b, other)]
    return pieces


def far_pieces(place, stats, slices):
    lse = lse_of(stats, lax.rem(place[2] + 2, NX))
    y = place[1]
    pieces = []
    for k, ref in enumerate(slices):
        pair = jnp.where((y < 2) == (k < 2), lse[:2], lse[2:])
        pieces.append((ref, jnp.where(lax.rem(y + k, 2) == 1, pair[1:2], pair[0:1])))
    return pieces


def give_kernel(
    place, stats, rows, norms, up, down, other_up, other_down, f0, f1, f2, f3, numer_in, counts_in, left, right, held, numer, counts
):
    q = 1 - place[3]
    pieces = near_pieces(place, stats, up, down, other_up, other_down) + far_pieces(place, stats, (f0, f1, f2, f3))
    weighted(pieces, rows, norms, q, held, numer, counts, (numer_in, counts_in))
    blocks, height, width = left.shape
    for b in range(blocks):
        values, total = block_of(numer, counts, b, q, height)
        high, low = split(total)
        values = close(values, high, low).astype(BF)
        left[b] = values[:, :width]
        right[b] = values[:, width:]


def keep_kernel(
    place, stats, rows, norms, own, up, down, other_up, other_down, f0, f1, f2, f3, kept, held, numer, counts
):
    q = place[3]
    pieces = [(own, lse_of(stats, place[2]))] + near_pieces(place, stats, up, down, other_up, other_down)
    pieces += far_pieces(place, stats, (f0, f1, f2, f3))
    weighted(pieces, rows, norms, q, held, numer, counts)
    blocks, height, _ = kept.shape
    for b in range(blocks):
        values, total = block_of(numer, counts, b, q, height)
        kept[b] = close(values, total, jnp.zeros_like(total))


def merge_kernel(kept, left, right, send):
    blocks, height, width = kept.shape
    at = height - TAIL
    for b in range(blocks):
        for h, got in ((0, left), (1, right)):
            half = width // 2
            mine = kept[b, :, h * half : (h + 1) * half]
            theirs = got[b].astype(F32)
            values = mine + theirs
            tail = values[height - 8 :]
            counts = tail[8 - TAIL : 9 - TAIL, :LANES] + tail[9 - TAIL : 10 - TAIL, :LANES]
            high, low = split(counts)
            values = close(values, high, low).astype(BF)
            for c in range(half // LANES):
                send[b * N_CENT + h * (half // LANES) + c] = values[:, c * LANES : (c + 1) * LANES]


def final_kernel(got, out, scratch):
    n, height, _ = got.shape
    slot = height - TAIL
    for c in range(N_CENT):
        values = got[c].astype(F32)
        for i in range(1, n // N_CENT):
            values += got[i * N_CENT + c].astype(F32)
        tail = values[height - 8 :]
        counts = tail[8 - TAIL : 9 - TAIL] + tail[9 - TAIL : 10 - TAIL] + 1.0
        column = jnp.broadcast_to(counts, (LANES, LANES)).T
        scratch[c * slot : (c + 1) * slot] = (values / column[:height])[:slot]
    out[...] = scratch[...].astype(BF)


def body(points, centroids):
    rows, dim = centroids.shape
    pts = points.shape[0]
    n_blocks = NZ // 2
    slot = rows // (NX * NZ)
    height = slot + TAIL
    half, quarter = pts // NC, pts // NY
    x, y, core, parity = (lax.axis_index(a) for a in ("x", "y", "core", "zp"))
    place = jnp.stack([core, y, x, parity]).astype(jnp.int32)
    shape = jax.ShapeDtypeStruct

    own_half, own_quarter = pl.pallas_call(
        cut_kernel,
        out_shape=(shape((half, dim), BF), shape((quarter, dim), BF)),
        in_specs=[SMEM, VMEM],
        out_specs=(VMEM, VMEM),
        compiler_params=params(4),
        cost_estimate=CHEAP,
        name="cut",
    )(place, points)

    def ring(a, k):
        return lax.ppermute(a, "x", [(i, (i + k) % NX) for i in range(NX)])

    far = ring(own_quarter, 2)
    up, down = ring(own_half, 1), ring(own_half, NX - 1)

    points, own_half, own_quarter = lax.optimization_barrier((points, own_half, own_quarter))
    stats_shape = (NX * N_CENT, 2 * pts // LANES, LANES)
    send_stats = pl.pallas_call(
        stats_kernel,
        grid=(rows // TILE,),
        out_shape=shape(stats_shape, F32),
        in_specs=[pl.BlockSpec((pts, dim), lambda i: (0, 0)), pl.BlockSpec((TILE, dim), lambda i: (i, 0))],
        out_specs=pl.BlockSpec(stats_shape, lambda i: (0, 0, 0)),
        scratch_shapes=[pltpu.VMEM((1, pts), F32), pltpu.VMEM((1, pts), F32)],
        compiler_params=params(54),
        cost_estimate=CHEAP,
        name="stats",
    )(points, centroids)
    far, _ = lax.optimization_barrier((far, send_stats))
    stats = lax.all_to_all(send_stats, ("x", *CENT), 0, 0)
    work = n_blocks * (-(-(slot + 12) // 16) * 16)
    mine, norms = pl.pallas_call(
        window_kernel,
        out_shape=(shape((2, work, dim), BF), shape((2, work, 1), F32)),
        in_specs=[SMEM, ANY, ANY],
        out_specs=(VMEM, VMEM),
        scratch_shapes=[pltpu.SemaphoreType.DMA((NZ,))],
        compiler_params=params(50),
        cost_estimate=CHEAP,
        name="window",
    )(place, centroids, send_stats)

    def call(kernel, out_shape, n_points, *args, scratch=()):
        return pl.pallas_call(
            kernel,
            out_shape=out_shape,
            in_specs=[SMEM] + [VMEM] * (3 + len(args)),
            out_specs=jax.tree.map(lambda _: VMEM, out_shape),
            scratch_shapes=[pltpu.VMEM((n_points, dim), BF), *scratch],
            compiler_params=params(28),
            cost_estimate=CHEAP,
            name=kernel.__name__,
        )(place, stats, mine, norms, *args)

    swap = [(0, 1), (1, 0)]
    slices = [far] + [lax.ppermute(far, "y", [(i, i ^ k) for i in range(NY)]) for k in range(1, NY)]
    up, down, stats, _ = lax.optimization_barrier((up, down, stats, far))
    others = [lax.ppermute(a, "core", swap) for a in (up, down)]
    sums = (shape((work, dim), F32), shape((work, LANES), F32))
    spare = [pltpu.VMEM(s.shape, F32) for s in sums]
    numer = call(own_kernel, sums, pts, points)
    rest = (up, down, *others, *slices)
    part = shape((n_blocks, height, dim // 2), BF)
    left, right = call(give_kernel, (part, part), (NX - 1) * pts, *rest, *numer, scratch=spare)

    got_left = lax.ppermute(left, Z, [(i, i ^ 1) for i in range(NZ)])
    got_right = lax.ppermute(right, Z, [(i, (i + (1 if i % 2 else -1)) % NZ) for i in range(NZ)])
    kept = call(keep_kernel, shape((n_blocks, height, dim), F32), NX * pts, points, *rest, scratch=spare)
    send = pl.pallas_call(
        merge_kernel,
        out_shape=shape((n_blocks * N_CENT, height, LANES), BF),
        in_specs=[VMEM] * 3,
        out_specs=VMEM,
        compiler_params=params(16),
        name="merge",
    )(kept, got_left, got_right)
    got = lax.all_to_all(send, ("zq", *CENT), 0, 0)
    return pl.pallas_call(
        final_kernel,
        out_shape=shape((N_CENT * slot, LANES), BF),
        in_specs=[VMEM],
        out_specs=VMEM,
        scratch_shapes=[pltpu.VMEM((N_CENT * slot, LANES), F32)],
        compiler_params=params(16),
        name="final",
    )(got)


def solution(mesh):
    fine = Mesh(mesh.devices.reshape(NX, NZ // 2, 2, NY, NC), ("x", *Z, *CENT))
    pts = ("x", *Z)
    return jax.shard_map(
        body, mesh=fine, in_specs=(P(pts, None), P(CENT, None)), out_specs=P(pts, CENT), check_vma=False
    )
```

time: 102 us -> 100 us (0.980)
  waiting for transfers between devices: 8.95 us -> 17.8 us
  blocking collectives: 39.2 us -> 34.1 us
  Pallas kernels: 26 us -> 22.8 us
  local copies, waits for them, and re-layouts: 4.89 us -> 2.14 us
    ppermute x3, waiting for transfers between devices: 0.01 us -> 6.7 us  [body(): lax.ppermute(far, 'y', [(i, i ^ k) for i in range(NY)])]
    all_to_all x1, blocking collectives: 39.2 us -> 34.1 us  [body(): got = lax.all_to_all(send, ('zq', *CENT), 0, 0)]
    pallas_call x3, Pallas kernels: 12.9 us -> 10 us  [call(): pl.pallas_call(kernel, out_shape=out_shape, in_specs=[SMEM] + [VMEM] * (3...]
    unnamed x9 -> x6, local copies, waits for them, and re-layouts: 3.98 us -> 2.14 us
    ppermute x4 -> x5, waiting for transfers between devices: 2.3 us -> 3.95 us  [the longest x1 3.36 us: body(): lax.ppermute(right, Z, [(i, (i + (1 if i % 2 else -1)) % NZ) for i in ran...]
    pallas_call x2 -> x3, Pallas kernels: 3.64 us -> 3.34 us  [the longest x1 2.55 us: body(): pl.pallas_call(window_kernel, out_shape=(shape((2, work, dim), BF), shape...]
    ppermute x4 -> x5, starting transfers between devices: 11.4 us -> 11.5 us  [the longest x3 5.12 us: ring(): return lax.ppermute(a, 'x', [(i, (i + k) % NX) for i in range(NX)])]
  transfers between devices with their start and end apart: 10 -> 11, of which waited for: 2 -> 5; matrix products, arithmetic and copies ran while one was open for 0% -> 0% of each run, Pallas kernels for 18% -> 17%
where the time goes in v8:
time: 100 us
  blocking collectives  34.1 us (34%)
  starting transfers between devices  23.2 us (23%)
  Pallas kernels  22.8 us (23%)
  waiting for transfers between devices  17.8 us (18%)
  local copies, waits for them, and re-layouts  2.14 us (2%)
    all_to_all x1, blocking collectives, body(): got = lax.all_to_all(send, ('zq', *CENT), 0, 0)  34.1 us
    pallas_call x3, Pallas kernels, call(): pl.pallas_call(kernel, out_shape=out_shape, in_specs=[SMEM] + [VMEM] * (3...  10 us
    pallas_call x1, Pallas kernels, body(): pl.pallas_call(stats_kernel, grid=(rows // TILE,), out_shape=shape(stats_...  8.49 us
    all_to_all x1, starting transfers between devices, body(): stats = lax.all_to_all(send_stats, ('x', *CENT), 0, 0)  7.29 us
    all_to_all x1, waiting for transfers between devices, body(): stats = lax.all_to_all(send_stats, ('x', *CENT), 0, 0)  7.1 us
    ppermute x3, waiting for transfers between devices, body(): lax.ppermute(far, 'y', [(i, i ^ k) for i in range(NY)])  6.7 us
    ppermute x3, starting transfers between devices, ring(): return lax.ppermute(a, 'x', [(i, (i + k) % NX) for i in range(NX)])  5.12 us
    ppermute x1, starting transfers between devices, body(): lax.ppermute(right, Z, [(i, (i + (1 if i % 2 else -1)) % NZ) for i in ran...  4.67 us
  transfers between devices with their start and end apart: 11, of which 5 were waited for; matrix products, arithmetic and copies ran while one was open for 0% of the time, Pallas kernels for 17%

profile of v8, /device:TPU:1, one launch (start us, length us, event | category | flops | bytes accessed | tf_op | source)
XLA Modules:
  0.0 100.2 jit_solution(5657286613127529392)
XLA Ops:
  0.1 1.2 %copy-done = bf16[512,1024]{1,0:T(8,128)(2,1)S(1)} copy-done((bf16[512,1024]{1,0:T(8,128)(2,1)S(1)}, bf16[512,1024]{1,0:T(8,128)(2,1)}, u32[]{:S(2)}) %copy-start) | copy-done | bytes 1048600
  1.3 0.6 cut.1
  1.9 2.1 %collective-permute-start = (bf16[256,1024]{1,0:T(8,128)(2,1)S(1)}, bf16[256,1024]{1,0:T(8,128)(2,1)S(1)}, u32[]{:S(2)}, u32[]{:S(2)}) collective-permute-start(bf16[256,1024]{1,0:T(8,128)(2,1)S(1)} %get-tuple-element.18), channel_id=1, source_target_pairs={{0,64},{64,128},{128,192},{192,0},{1,65},{65,129},{129,193},{193,1... | collective-permute-start | bytes 1572872 | tf_op jit(solution)/shard_map/ppermute | solution.py:260
  4.0 1.4 %collective-permute-start.1 = (bf16[256,1024]{1,0:T(8,128)(2,1)S(1)}, bf16[256,1024]{1,0:T(8,128)(2,1)S(1)}, u32[]{:S(2)}, u32[]{:S(2)}) collective-permute-start(bf16[256,1024]{1,0:T(8,128)(2,1)S(1)} %get-tuple-element.18), channel_id=1, source_target_pairs={{0,192},{64,0},{128,64},{192,128},{1,193},{65,1},{129,65},{193,129... | collective-permute-start | bytes 1572872 | tf_op jit(solution)/shard_map/ppermute | solution.py:260
  5.4 1.6 %collective-permute-start.2 = (bf16[128,1024]{1,0:T(8,128)(2,1)S(1)}, bf16[128,1024]{1,0:T(8,128)(2,1)S(1)}, u32[]{:S(2)}, u32[]{:S(2)}) collective-permute-start(bf16[128,1024]{1,0:T(8,128)(2,1)S(1)} %get-tuple-element.19), channel_id=1, source_target_pairs={{0,128},{64,192},{128,0},{192,64},{1,129},{65,193},{129,1},{193,65... | collective-permute-start | bytes 786440 | tf_op jit(solution)/shard_map/ppermute | solution.py:260
  7.0 8.5 %stats.1.after = f32[32,8,128]{2,1,0:T(8,128)} custom-call(bf16[512,1024]{1,0:T(8,128)(2,1)} %own.1, bf16[3200,1024]{1,0:T(8,128)(2,1)} %table.1), custom_call_target="tpu_custom_call" | custom-call | flops 1 | bytes 1 | tf_op jit(solution)/shard_map/stats/pallas_call | solution.py:267
  15.5 7.3 %all-to-all-start = ((f32[32,8,128]{2,1,0:T(8,128)}), f32[32,8,128]{2,1,0:T(8,128)S(1)}, u32[]{:S(2)}, u32[]{:S(2)}) async-start(f32[32,8,128]{2,1,0:T(8,128)} %stats.1.after), calls=%async_computation | async-start | bytes 262144 | tf_op jit(solution)/shard_map/all_to_all | solution.py:279
  22.8 0.6 collective-permute-done.2.f0
  23.4 7.1 %all-to-all-done.stats = f32[32,8,128]{2,1,0:T(8,128)S(1)} async-done(((f32[32,8,128]{2,1,0:T(8,128)}), f32[32,8,128]{2,1,0:T(8,128)S(1)}, u32[]{:S(2)}, u32[]{:S(2)}) %all-to-all-start) | async-done | bytes 131104 | tf_op jit(solution)/shard_map/all_to_all | solution.py:279
  30.5 0.4 collective-permute-start.3
  31.3 1.9 %collective-permute-start.6 = (bf16[128,1024]{1,0:T(8,128)(2,1)S(1)}, bf16[128,1024]{1,0:T(8,128)(2,1)S(1)}, u32[]{:S(2)}, u32[]{:S(2)}) collective-permute-start(bf16[128,1024]{1,0:T(8,128)(2,1)S(1)} %collective-permute-done.2.f0), channel_id=1, source_target_pairs={{0,4},{2,6},{4,0},{6,2},{1,5},{3,7},{5,1},{7,3},{8,12},{10,14},{12... | collective-permute-start | bytes 786440 | tf_op jit(solution)/shard_map/ppermute | solution.py:305
  33.2 1.8 %collective-permute-start.7 = (bf16[128,1024]{1,0:T(8,128)(2,1)S(1)}, bf16[128,1024]{1,0:T(8,128)(2,1)S(1)}, u32[]{:S(2)}, u32[]{:S(2)}) collective-permute-start(bf16[128,1024]{1,0:T(8,128)(2,1)S(1)} %collective-permute-done.2.f0), channel_id=1, source_target_pairs={{0,6},{2,4},{4,2},{6,0},{1,7},{3,5},{5,3},{7,1},{8,14},{10,12},{12... | collective-permute-start | bytes 786440 | tf_op jit(solution)/shard_map/ppermute | solution.py:305
  34.9 0.9 copy-done.2
  35.8 2.6 %window.1 = (bf16[2,448,1024]{2,1,0:T(8,128)(2,1)S(1)}, f32[2,448,1]{2,1,0:T(8,128)S(1)}) custom-call(s32[4]{0:T(128)S(1)} %pad_add_fusion.place, bf16[3200,1024]{1,0:T(8,128)(2,1)} %table.1, f32[32,8,128]{2,1,0:T(8,128)S(1)} %copy-done.2), custom_call_target="tpu_custom_call" | custom-call | flops 1 | bytes 1 | tf_op jit(solution)/shard_map/window/pallas_call | solution.py:281
  38.4 1.7 %own_kernel.1 = (f32[448,1024]{1,0:T(8,128)S(1)}, f32[448,128]{1,0:T(8,128)S(1)}) custom-call(s32[4]{0:T(128)S(1)} %pad_add_fusion.place, f32[32,8,128]{2,1,0:T(8,128)S(1)} %all-to-all-done.stats, bf16[2,448,1024]{2,1,0:T(8,128)(2,1)S(1)} %get-tuple-element.23.rows, f32[2,448,1]{2,1,0:T(8,128)S(1)} %get-tuple-element.24.norms, bf16[512,1024]{1,0:T(8,128)(2,1)S(1)} %copy-done.1), custom_call_target="tpu_custom_call" | custom-call | flops 1 | bytes 1 | tf_op jit(solution)/shard_map/own_kernel/pallas_call | solution.py:293
  40.1 4.7 %collective-permute-done.6.f2 = bf16[128,1024]{1,0:T(8,128)(2,1)S(1)} collective-permute-done((bf16[128,1024]{1,0:T(8,128)(2,1)S(1)}, bf16[128,1024]{1,0:T(8,128)(2,1)S(1)}, u32[]{:S(2)}, u32[]{:S(2)}) %collective-permute-start.6) | collective-permute-done | bytes 262176 | tf_op jit(solution)/shard_map/ppermute | solution.py:305
  44.8 2.0 %collective-permute-done.7.f3 = bf16[128,1024]{1,0:T(8,128)(2,1)S(1)} collective-permute-done((bf16[128,1024]{1,0:T(8,128)(2,1)S(1)}, bf16[128,1024]{1,0:T(8,128)(2,1)S(1)}, u32[]{:S(2)}, u32[]{:S(2)}) %collective-permute-start.7) | collective-permute-done | bytes 262176 | tf_op jit(solution)/shard_map/ppermute | solution.py:305
  46.8 3.7 %give_kernel.1 = (bf16[4,104,512]{2,1,0:T(8,128)(2,1)S(1)}, bf16[4,104,512]{2,1,0:T(8,128)(2,1)S(1)}) custom-call(s32[4]{0:T(128)S(1)} %pad_add_fusion.place, f32[32,8,128]{2,1,0:T(8,128)S(1)} %all-to-all-done.stats, bf16[2,448,1024]{2,1,0:T(8,128)(2,1)S(1)} %get-tuple-element.23.rows, f32[2,448,1]{2,1,0:T(8,128)S(1)} %get-tuple-element.24.norms, ...), custom_call_target="tpu_custom_call" | custom-call | flops 1 | bytes 1 | tf_op jit(solution)/shard_map/give_kernel/pallas_call | solution.py:293
  50.5 1.7 %collective-permute-start.8 = (bf16[4,104,512]{2,1,0:T(8,128)(2,1)S(1)}, bf16[4,104,512]{2,1,0:T(8,128)(2,1)S(1)}, u32[]{:S(2)}, u32[]{:S(2)}) collective-permute-start(bf16[4,104,512]{2,1,0:T(8,128)(2,1)S(1)} %get-tuple-element.29), channel_id=1, source_target_pairs={{0,8},{8,0},{16,24},{24,16},{32,40},{40,32},{48,56},{56,48},{1,9},... | collective-permute-start | bytes 1277960 | tf_op jit(solution)/shard_map/ppermute | solution.py:315
  52.2 4.7 %collective-permute-start.9 = (bf16[4,104,512]{2,1,0:T(8,128)(2,1)S(1)}, bf16[4,104,512]{2,1,0:T(8,128)(2,1)S(1)}, u32[]{:S(2)}, u32[]{:S(2)}) collective-permute-start(bf16[4,104,512]{2,1,0:T(8,128)(2,1)S(1)} %get-tuple-element.30), channel_id=1, source_target_pairs={{0,56},{8,16},{16,8},{24,32},{32,24},{40,48},{48,40},{56,0},{1,57}... | collective-permute-start | bytes 1277960 | tf_op jit(solution)/shard_map/ppermute | solution.py:316
  56.9 4.6 %keep_kernel.1.kept = f32[4,104,1024]{2,1,0:T(8,128)S(1)} custom-call(s32[4]{0:T(128)S(1)} %pad_add_fusion.place, f32[32,8,128]{2,1,0:T(8,128)S(1)} %all-to-all-done.stats, bf16[2,448,1024]{2,1,0:T(8,128)(2,1)S(1)} %get-tuple-element.23.rows, f32[2,448,1]{2,1,0:T(8,128)S(1)} %get-tuple-element.24.norms, bf16[512,1024]{1,0:T(8,128)(2,1)S(1)} %copy-done.1, ...), custom_call_target="tpu_custom_call" | custom-call | flops 1 | bytes 1 | tf_op jit(solution)/shard_map/keep_kernel/pallas_call | solution.py:293
  61.5 3.4 %collective-permute-done.9.right = bf16[4,104,512]{2,1,0:T(8,128)(2,1)S(1)} collective-permute-done((bf16[4,104,512]{2,1,0:T(8,128)(2,1)S(1)}, bf16[4,104,512]{2,1,0:T(8,128)(2,1)S(1)}, u32[]{:S(2)}, u32[]{:S(2)}) %collective-permute-start.9) | collective-permute-done | bytes 426016 | tf_op jit(solution)/shard_map/ppermute | solution.py:316
  65.1 34.1 %all_to_all.10.got = bf16[32,104,128]{2,1,0:T(8,128)(2,1)S(1)} all-to-all(bf16[32,104,128]{2,1,0:T(8,128)(2,1)S(1)} %merge.1), channel_id=1, replica_groups=mesh['x'=4,'zq'=4,'zp'=2,'y'=4,'core'=2] {'zq','y','core'}, dimensions={0} | all-to-all | bytes 1703936 | tf_op jit(solution)/shard_map/all_to_all | solution.py:326
  99.2 0.9 final.1
  (14 shorter events, 0.7 us)
Async XLA Ops:
  0.1 1.2 %copy-start = (bf16[512,1024]{1,0:T(8,128)(2,1)S(1)}, bf16[512,1024]{1,0:T(8,128)(2,1)}, u32[]{:S(2)}) copy-start(bf16[512,1024]{1,0:T(8,128)(2,1)} %own.1) | copy-start | bytes 3145732
  1.9 28.6 %collective-permute-start = (bf16[256,1024]{1,0:T(8,128)(2,1)S(1)}, bf16[256,1024]{1,0:T(8,128)(2,1)S(1)}, u32[]{:S(2)}, u32[]{:S(2)}) collective-permute-start(bf16[256,1024]{1,0:T(8,128)(2,1)S(1)} %get-tuple-element.18), channel_id=1, source_target_pairs={{0,64},{64,128},{128,192},{192,0},{1,65},{65,129},{129,193},{193,1... | collective-permute-start | bytes 1572872 | tf_op jit(solution)/shard_map/ppermute | solution.py:260
  4.0 26.5 %collective-permute-start.1 = (bf16[256,1024]{1,0:T(8,128)(2,1)S(1)}, bf16[256,1024]{1,0:T(8,128)(2,1)S(1)}, u32[]{:S(2)}, u32[]{:S(2)}) collective-permute-start(bf16[256,1024]{1,0:T(8,128)(2,1)S(1)} %get-tuple-element.18), channel_id=1, source_target_pairs={{0,192},{64,0},{128,64},{192,128},{1,193},{65,1},{129,65},{193,129... | collective-permute-start | bytes 1572872 | tf_op jit(solution)/shard_map/ppermute | solution.py:260
  5.4 18.0 %collective-permute-start.2 = (bf16[128,1024]{1,0:T(8,128)(2,1)S(1)}, bf16[128,1024]{1,0:T(8,128)(2,1)S(1)}, u32[]{:S(2)}, u32[]{:S(2)}) collective-permute-start(bf16[128,1024]{1,0:T(8,128)(2,1)S(1)} %get-tuple-element.19), channel_id=1, source_target_pairs={{0,128},{64,192},{128,0},{192,64},{1,129},{65,193},{129,1},{193,65... | collective-permute-start | bytes 786440 | tf_op jit(solution)/shard_map/ppermute | solution.py:260
  15.5 15.0 %all-to-all-start = ((f32[32,8,128]{2,1,0:T(8,128)}), f32[32,8,128]{2,1,0:T(8,128)S(1)}, u32[]{:S(2)}, u32[]{:S(2)}) async-start(f32[32,8,128]{2,1,0:T(8,128)} %stats.1.after), calls=%async_computation | async-start | bytes 262144 | tf_op jit(solution)/shard_map/all_to_all | solution.py:279
  22.8 15.6 %copy-start.1 = (bf16[512,1024]{1,0:T(8,128)(2,1)S(1)}, bf16[512,1024]{1,0:T(8,128)(2,1)}, u32[]{:S(2)}) copy-start(bf16[512,1024]{1,0:T(8,128)(2,1)} %own.1) | copy-start | bytes 3145732
  30.5 16.3 %collective-permute-start.3 = (bf16[256,1024]{1,0:T(8,128)(2,1)S(1)}, bf16[256,1024]{1,0:T(8,128)(2,1)S(1)}, u32[]{:S(2)}, u32[]{:S(2)}) collective-permute-start(bf16[256,1024]{1,0:T(8,128)(2,1)S(1)} %collective-permute-done.up), channel_id=1, source_target_pairs={{0,1},{1,0},{2,3},{3,2},{4,5},{5,4},{6,7},{7,6},{8,9},{9,8},{10,11... | collective-permute-start | bytes 1572872 | tf_op jit(solution)/shard_map/ppermute | solution.py:307
  30.9 15.9 %collective-permute-start.4 = (bf16[256,1024]{1,0:T(8,128)(2,1)S(1)}, bf16[256,1024]{1,0:T(8,128)(2,1)S(1)}, u32[]{:S(2)}, u32[]{:S(2)}) collective-permute-start(bf16[256,1024]{1,0:T(8,128)(2,1)S(1)} %collective-permute-done.1.down), channel_id=1, source_target_pairs={{0,1},{1,0},{2,3},{3,2},{4,5},{5,4},{6,7},{7,6},{8,9},{9,8},{10,11... | collective-permute-start | bytes 1572872 | tf_op jit(solution)/shard_map/ppermute | solution.py:307
  31.0 9.1 %collective-permute-start.5 = (bf16[128,1024]{1,0:T(8,128)(2,1)S(1)}, bf16[128,1024]{1,0:T(8,128)(2,1)S(1)}, u32[]{:S(2)}, u32[]{:S(2)}) collective-permute-start(bf16[128,1024]{1,0:T(8,128)(2,1)S(1)} %collective-permute-done.2.f0), channel_id=1, source_target_pairs={{0,2},{2,0},{4,6},{6,4},{1,3},{3,1},{5,7},{7,5},{8,10},{10,8},{12,... | collective-permute-start | bytes 786440 | tf_op jit(solution)/shard_map/ppermute | solution.py:305
  31.3 13.5 %collective-permute-start.6 = (bf16[128,1024]{1,0:T(8,128)(2,1)S(1)}, bf16[128,1024]{1,0:T(8,128)(2,1)S(1)}, u32[]{:S(2)}, u32[]{:S(2)}) collective-permute-start(bf16[128,1024]{1,0:T(8,128)(2,1)S(1)} %collective-permute-done.2.f0), channel_id=1, source_target_pairs={{0,4},{2,6},{4,0},{6,2},{1,5},{3,7},{5,1},{7,3},{8,12},{10,14},{12... | collective-permute-start | bytes 786440 | tf_op jit(solution)/shard_map/ppermute | solution.py:305
  33.2 13.7 %collective-permute-start.7 = (bf16[128,1024]{1,0:T(8,128)(2,1)S(1)}, bf16[128,1024]{1,0:T(8,128)(2,1)S(1)}, u32[]{:S(2)}, u32[]{:S(2)}) collective-permute-start(bf16[128,1024]{1,0:T(8,128)(2,1)S(1)} %collective-permute-done.2.f0), channel_id=1, source_target_pairs={{0,6},{2,4},{4,2},{6,0},{1,7},{3,5},{5,3},{7,1},{8,14},{10,12},{12... | collective-permute-start | bytes 786440 | tf_op jit(solution)/shard_map/ppermute | solution.py:305
  34.9 0.9 copy-start.2
  50.5 11.0 %collective-permute-start.8 = (bf16[4,104,512]{2,1,0:T(8,128)(2,1)S(1)}, bf16[4,104,512]{2,1,0:T(8,128)(2,1)S(1)}, u32[]{:S(2)}, u32[]{:S(2)}) collective-permute-start(bf16[4,104,512]{2,1,0:T(8,128)(2,1)S(1)} %get-tuple-element.29), channel_id=1, source_target_pairs={{0,8},{8,0},{16,24},{24,16},{32,40},{40,32},{48,56},{56,48},{1,9},... | collective-permute-start | bytes 1277960 | tf_op jit(solution)/shard_map/ppermute | solution.py:315
  52.2 12.7 %collective-permute-start.9 = (bf16[4,104,512]{2,1,0:T(8,128)(2,1)S(1)}, bf16[4,104,512]{2,1,0:T(8,128)(2,1)S(1)}, u32[]{:S(2)}, u32[]{:S(2)}) collective-permute-start(bf16[4,104,512]{2,1,0:T(8,128)(2,1)S(1)} %get-tuple-element.30), channel_id=1, source_target_pairs={{0,56},{8,16},{16,8},{24,32},{32,24},{40,48},{48,40},{56,0},{1,57}... | collective-permute-start | bytes 1277960 | tf_op jit(solution)/shard_map/ppermute | solution.py:316

commit v9 on v8

--- a/solution.py
+++ b/solution.py
@@ -21,6 +21,7 @@
 MIB = 2**20
 CHEAP = pl.CostEstimate(flops=1, bytes_accessed=1, transcendentals=0)
 TILE = 640
+SHIFTS = (1, NX - 1, 2)
 
 
 def dot_nt(a, b):
@@ -31,13 +32,12 @@
     return pltpu.CompilerParams(vmem_limit_bytes=mib * MIB)
 
 
-def cut_kernel(place, points, half_out, part_out):
-    half, part = half_out.shape[0], part_out.shape[0]
+def cut_kernel(place, points, half_out):
+    half = half_out.shape[0]
     half_out[...] = points[pl.ds(pl.multiple_of(place[0] * half, half), half)]
-    part_out[...] = points[pl.ds(pl.multiple_of(place[1] * part, part), part)]
-
-
-def stats_kernel(points, cents, out, top, total):
+
+
+def stats_kernel(points, cents, after, out, top, total):
     step = pl.program_id(0)
 
     @pl.when(step == 0)
@@ -154,33 +154,22 @@
     return high, counts - high
 
 
+def half_pieces(place, stats, refs, which):
+    return [(ref, lse_halves(place, stats, k)[which]) for k, ref in zip(SHIFTS, refs)]
+
+
 def own_kernel(place, stats, rows, norms, own, numer, counts, held):
-    weighted([(own, lse_of(stats, place[2]))], rows, norms, 1 - place[3], held, numer, counts)
-
-
-def near_pieces(place, stats, up, down, other_up, other_down):
-    pieces = []
-    for k, a, b in ((1, up, other_up), (NX - 1, down, other_down)):
-        mine, other = lse_halves(place, stats, k)
-        pieces += [(a, mine), (b, other)]
-    return pieces
-
-
-def far_pieces(place, stats, slices):
-    lse = lse_of(stats, lax.rem(place[2] + 2, NX))
-    y = place[1]
-    pieces = []
-    for k, ref in enumerate(slices):
-        pair = jnp.where((y < 2) == (k < 2), lse[:2], lse[2:])
-        pieces.append((ref, jnp.where(lax.rem(y + k, 2) == 1, pair[1:2], pair[0:1])))
-    return pieces
-
-
-def give_kernel(
-    place, stats, rows, norms, up, down, other_up, other_down, f0, f1, f2, f3, numer_in, counts_in, left, right, held, numer, counts
-):
-    q = 1 - place[3]
-    pieces = near_pieces(place, stats, up, down, other_up, other_down) + far_pieces(place, stats, (f0, f1, f2, f3))
+    weighted([(own, lse_of(stats, place[2]))], rows, norms, 1 - place[1], held, numer, counts)
+
+
+def first_kernel(place, stats, rows, norms, up, down, far, numer_in, counts_in, numer, counts, held):
+    pieces = half_pieces(place, stats, (up, down, far), 0)
+    weighted(pieces, rows, norms, 1 - place[1], held, numer, counts, (numer_in, counts_in))
+
+
+def give_kernel(place, stats, rows, norms, up, down, far, numer_in, counts_in, left, right, held, numer, counts):
+    q = 1 - place[1]
+    pieces = half_pieces(place, stats, (up, down, far), 1)
     weighted(pieces, rows, norms, q, held, numer, counts, (numer_in, counts_in))
     blocks, height, width = left.shape
     for b in range(blocks):
@@ -191,12 +180,10 @@
         right[b] = values[:, width:]
 
 
-def keep_kernel(
-    place, stats, rows, norms, own, up, down, other_up, other_down, f0, f1, f2, f3, kept, held, numer, counts
-):
-    q = place[3]
-    pieces = [(own, lse_of(stats, place[2]))] + near_pieces(place, stats, up, down, other_up, other_down)
-    pieces += far_pieces(place, stats, (f0, f1, f2, f3))
+def keep_kernel(place, stats, rows, norms, own, up, down, far, up2, down2, far2, kept, held, numer, counts):
+    q = place[1]
+    pieces = [(own, lse_of(stats, place[2]))] + half_pieces(place, stats, (up, down, far), 0)
+    pieces += half_pieces(place, stats, (up2, down2, far2), 1)
     weighted(pieces, rows, norms, q, held, numer, counts)
     blocks, height, _ = kept.shape
     for b in range(blocks):
@@ -241,41 +228,34 @@
     n_blocks = NZ // 2
     slot = rows // (NX * NZ)
     height = slot + TAIL
-    half, quarter = pts // NC, pts // NY
-    x, y, core, parity = (lax.axis_index(a) for a in ("x", "y", "core", "zp"))
-    place = jnp.stack([core, y, x, parity]).astype(jnp.int32)
+    half = pts // NC
+    x, core, parity = (lax.axis_index(a) for a in ("x", "core", "zp"))
+    place = jnp.stack([core, parity, x]).astype(jnp.int32)
     shape = jax.ShapeDtypeStruct
 
-    own_half, own_quarter = pl.pallas_call(
+    own_half = pl.pallas_call(
         cut_kernel,
-        out_shape=(shape((half, dim), BF), shape((quarter, dim), BF)),
+        out_shape=shape((half, dim), BF),
         in_specs=[SMEM, VMEM],
-        out_specs=(VMEM, VMEM),
+        out_specs=VMEM,
         compiler_params=params(4),
         cost_estimate=CHEAP,
         name="cut",
     )(place, points)
-
-    def ring(a, k):
-        return lax.ppermute(a, "x", [(i, (i + k) % NX) for i in range(NX)])
-
-    far = ring(own_quarter, 2)
-    up, down = ring(own_half, 1), ring(own_half, NX - 1)
-
-    points, own_half, own_quarter = lax.optimization_barrier((points, own_half, own_quarter))
+    near = [lax.ppermute(own_half, "x", [(i, (i + k) % NX) for i in range(NX)]) for k in SHIFTS]
+
     stats_shape = (NX * N_CENT, 2 * pts // LANES, LANES)
     send_stats = pl.pallas_call(
         stats_kernel,
         grid=(rows // TILE,),
         out_shape=shape(stats_shape, F32),
-        in_specs=[pl.BlockSpec((pts, dim), lambda i: (0, 0)), pl.BlockSpec((TILE, dim), lambda i: (i, 0))],
+        in_specs=[pl.BlockSpec((pts, dim), lambda i: (0, 0)), pl.BlockSpec((TILE, dim), lambda i: (i, 0)), ANY],
         out_specs=pl.BlockSpec(stats_shape, lambda i: (0, 0, 0)),
         scratch_shapes=[pltpu.VMEM((1, pts), F32), pltpu.VMEM((1, pts), F32)],
         compiler_params=params(54),
         cost_estimate=CHEAP,
         name="stats",
-    )(points, centroids)
-    far, _ = lax.optimization_barrier((far, send_stats))
+    )(points, centroids, own_half)
     stats = lax.all_to_all(send_stats, ("x", *CENT), 0, 0)
     work = n_blocks * (-(-(slot + 12) // 16) * 16)
     mine, norms = pl.pallas_call(
@@ -301,20 +281,19 @@
             name=kernel.__name__,
         )(place, stats, mine, norms, *args)
 
-    swap = [(0, 1), (1, 0)]
-    slices = [far] + [lax.ppermute(far, "y", [(i, i ^ k) for i in range(NY)]) for k in range(1, NY)]
-    up, down, stats, _ = lax.optimization_barrier((up, down, stats, far))
-    others = [lax.ppermute(a, "core", swap) for a in (up, down)]
     sums = (shape((work, dim), F32), shape((work, LANES), F32))
     spare = [pltpu.VMEM(s.shape, F32) for s in sums]
     numer = call(own_kernel, sums, pts, points)
-    rest = (up, down, *others, *slices)
+    near, numer = lax.optimization_barrier((near, numer))
+    others = [lax.ppermute(a, "core", [(0, 1), (1, 0)]) for a in near]
+    numer = call(first_kernel, sums, 3 * half, *near, *numer)
+    others, numer = lax.optimization_barrier((others, numer))
     part = shape((n_blocks, height, dim // 2), BF)
-    left, right = call(give_kernel, (part, part), (NX - 1) * pts, *rest, *numer, scratch=spare)
+    left, right = call(give_kernel, (part, part), 3 * half, *others, *numer, scratch=spare)
 
     got_left = lax.ppermute(left, Z, [(i, i ^ 1) for i in range(NZ)])
     got_right = lax.ppermute(right, Z, [(i, (i + (1 if i % 2 else -1)) % NZ) for i in range(NZ)])
-    kept = call(keep_kernel, shape((n_blocks, height, dim), F32), NX * pts, points, *rest, scratch=spare)
+    kept = call(keep_kernel, shape((n_blocks, height, dim), F32), NX * pts, points, *near, *others, scratch=spare)
     send = pl.pallas_call(
         merge_kernel,
         out_shape=shape((n_blocks * N_CENT, height, LANES), BF),

time: 100 us -> 92.3 us (0.923)
  waiting for transfers between devices: 17.8 us -> 11.1 us
  Pallas kernels: 22.8 us -> 26.8 us
  blocking collectives: 34.1 us -> 31.2 us
  starting transfers between devices: 23.2 us -> 20.5 us
    ppermute x8 -> x6, waiting for transfers between devices: 7.3 us -> 0.02 us  [the longest x3 0.01 us: body(): lax.ppermute(own_half, 'x', [(i, (i + k) % NX) for i in range(NX)])]
    ppermute x8 -> x6, starting transfers between devices: 9.49 us -> 6.11 us  [the longest x3 5.04 us: body(): lax.ppermute(own_half, 'x', [(i, (i + k) % NX) for i in range(NX)])]
    pallas_call x3 -> x4, Pallas kernels: 10 us -> 13.3 us  [call(): pl.pallas_call(kernel, out_shape=out_shape, in_specs=[SMEM] + [VMEM] * (3...]
    all_to_all x1, blocking collectives: 34.1 us -> 31.2 us  [body(): got = lax.all_to_all(send, ('zq', *CENT), 0, 0)]
    ppermute x1, waiting for transfers between devices: 3.36 us -> 4.45 us  [body(): lax.ppermute(right, Z, [(i, (i + (1 if i % 2 else -1)) % NZ) for i in ran...]
  transfers between devices with their start and end apart: 11 -> 9, of which waited for: 5 -> 2; matrix products, arithmetic and copies ran while one was open for 0% -> 0% of each run, Pallas kernels for 17% -> 24%
where the time goes in v9:
time: 92.3 us; the launch traced here: 91.9 us
  blocking collectives  31.2 us (34%)
  Pallas kernels  26.8 us (29%)
  starting transfers between devices  20.5 us (22%)
  waiting for transfers between devices  11.1 us (12%)
  local copies, waits for them, and re-layouts  2.16 us (2%)
    all_to_all x1, blocking collectives, body(): got = lax.all_to_all(send, ('zq', *CENT), 0, 0)  31.2 us
    pallas_call x4, Pallas kernels, call(): pl.pallas_call(kernel, out_shape=out_shape, in_specs=[SMEM] + [VMEM] * (3...  13.3 us
    pallas_call x1, Pallas kernels, body(): pl.pallas_call(stats_kernel, grid=(rows // TILE,), out_shape=shape(stats_...  8.48 us
    all_to_all x1, starting transfers between devices, body(): stats = lax.all_to_all(send_stats, ('x', *CENT), 0, 0)  7.94 us
    all_to_all x1, waiting for transfers between devices, body(): stats = lax.all_to_all(send_stats, ('x', *CENT), 0, 0)  6.61 us
    ppermute x3, starting transfers between devices, body(): lax.ppermute(own_half, 'x', [(i, (i + k) % NX) for i in range(NX)])  5.04 us
    ppermute x1, starting transfers between devices, body(): lax.ppermute(right, Z, [(i, (i + (1 if i % 2 else -1)) % NZ) for i in ran...  4.66 us
    ppermute x1, waiting for transfers between devices, body(): lax.ppermute(right, Z, [(i, (i + (1 if i % 2 else -1)) % NZ) for i in ran...  4.45 us
  transfers between devices with their start and end apart: 9, of which 2 were waited for; matrix products, arithmetic and copies ran while one was open for 0% of the time, Pallas kernels for 24%

profile of v9, /device:TPU:1, one launch (start us, length us, event | category | flops | bytes accessed | tf_op | source)
XLA Modules:
  0.0 91.9 jit_solution(9667720324971660718)
XLA Ops:
  0.0 0.1 pad_add_fusion.place
  0.1 1.2 %copy-done = bf16[512,1024]{1,0:T(8,128)(2,1)S(1)} copy-done((bf16[512,1024]{1,0:T(8,128)(2,1)S(1)}, bf16[512,1024]{1,0:T(8,128)(2,1)}, u32[]{:S(2)}) %copy-start) | copy-done | bytes 1048600
  1.3 1.4 %cut.1.after = bf16[256,1024]{1,0:T(8,128)(2,1)} custom-call(s32[3]{0:T(128)S(1)} %pad_add_fusion.place, bf16[512,1024]{1,0:T(8,128)(2,1)S(1)} %copy-done), custom_call_target="tpu_custom_call" | custom-call | flops 1 | bytes 1 | tf_op jit(solution)/shard_map/cut/pallas_call | solution.py:236
  2.7 3.6 %collective-permute-start.2 = (bf16[256,1024]{1,0:T(8,128)(2,1)}, bf16[256,1024]{1,0:T(8,128)(2,1)}, u32[]{:S(2)}, u32[]{:S(2)}) collective-permute-start(bf16[256,1024]{1,0:T(8,128)(2,1)} %cut.1.after), channel_id=1, source_target_pairs={{0,128},{64,192},{128,0},{192,64},{1,129},{65,193},{129,1},{193,65... | collective-permute-start | bytes 1572872 | tf_op jit(solution)/shard_map/ppermute | solution.py:245
  6.3 0.9 collective-permute-start.1
  7.1 0.6 collective-permute-start
  7.7 8.5 %stats.1.after = f32[32,8,128]{2,1,0:T(8,128)} custom-call(bf16[512,1024]{1,0:T(8,128)(2,1)} %own.3, bf16[3200,1024]{1,0:T(8,128)(2,1)} %table.1, bf16[256,1024]{1,0:T(8,128)(2,1)} %cut.1.after), custom_call_target="tpu_custom_call" | custom-call | flops 1 | bytes 1 | tf_op jit(solution)/shard_map/stats/pallas_call | solution.py:248
  16.2 7.9 %all-to-all-start = ((f32[32,8,128]{2,1,0:T(8,128)}), f32[32,8,128]{2,1,0:T(8,128)S(1)}, u32[]{:S(2)}, u32[]{:S(2)}) async-start(f32[32,8,128]{2,1,0:T(8,128)} %stats.1.after), calls=%async_computation | async-start | bytes 262144 | tf_op jit(solution)/shard_map/all_to_all | solution.py:259
  24.2 0.9 %copy-done.2 = f32[32,8,128]{2,1,0:T(8,128)S(1)} copy-done((f32[32,8,128]{2,1,0:T(8,128)S(1)}, f32[32,8,128]{2,1,0:T(8,128)}, u32[]{:S(2)}) %copy-start.2) | copy-done | bytes 131096
  25.1 2.6 %window.1 = (bf16[2,448,1024]{2,1,0:T(8,128)(2,1)S(1)}, f32[2,448,1]{2,1,0:T(8,128)S(1)}) custom-call(s32[3]{0:T(128)S(1)} %pad_add_fusion.place, bf16[3200,1024]{1,0:T(8,128)(2,1)} %table.1, f32[32,8,128]{2,1,0:T(8,128)S(1)} %copy-done.2), custom_call_target="tpu_custom_call" | custom-call | flops 1 | bytes 1 | tf_op jit(solution)/shard_map/window/pallas_call | solution.py:261
  27.7 6.6 %all-to-all-done.stats = f32[32,8,128]{2,1,0:T(8,128)S(1)} async-done(((f32[32,8,128]{2,1,0:T(8,128)}), f32[32,8,128]{2,1,0:T(8,128)S(1)}, u32[]{:S(2)}, u32[]{:S(2)}) %all-to-all-start) | async-done | bytes 131104 | tf_op jit(solution)/shard_map/all_to_all | solution.py:259
  34.3 1.7 %own_kernel.1 = (f32[448,1024]{1,0:T(8,128)S(1)}, f32[448,128]{1,0:T(8,128)S(1)}) custom-call(s32[3]{0:T(128)S(1)} %pad_add_fusion.place, f32[32,8,128]{2,1,0:T(8,128)S(1)} %all-to-all-done.stats, bf16[2,448,1024]{2,1,0:T(8,128)(2,1)S(1)} %get-tuple-element.23.rows, f32[2,448,1]{2,1,0:T(8,128)S(1)} %get-tuple-element.24.norms, bf16[512,1024]{1,0:T(8,128)(2,1)S(1)} %copy-done.1), custom_call_target="tpu_custom_call" | custom-call | flops 1 | bytes 1 | tf_op jit(solution)/shard_map/own_kernel/pallas_call | solution.py:273
  36.0 0.6 collective-permute-start.3
  36.6 0.1 collective-permute-start.4
  36.7 0.4 collective-permute-start.5
  37.1 3.5 %first_kernel.1 = (f32[448,1024]{1,0:T(8,128)S(1)}, f32[448,128]{1,0:T(8,128)S(1)}) custom-call(s32[3]{0:T(128)S(1)} %pad_add_fusion.place, f32[32,8,128]{2,1,0:T(8,128)S(1)} %all-to-all-done.stats, bf16[2,448,1024]{2,1,0:T(8,128)(2,1)S(1)} %get-tuple-element.23.rows, f32[2,448,1]{2,1,0:T(8,128)S(1)} %get-tuple-element.24.norms, ...), custom_call_target="tpu_custom_call" | custom-call | flops 1 | bytes 1 | tf_op jit(solution)/shard_map/first_kernel/pallas_call | solution.py:273
  40.6 2.7 %give_kernel.1 = (bf16[4,104,512]{2,1,0:T(8,128)(2,1)S(1)}, bf16[4,104,512]{2,1,0:T(8,128)(2,1)S(1)}) custom-call(s32[3]{0:T(128)S(1)} %pad_add_fusion.place, f32[32,8,128]{2,1,0:T(8,128)S(1)} %all-to-all-done.stats, bf16[2,448,1024]{2,1,0:T(8,128)(2,1)S(1)} %get-tuple-element.23.rows, f32[2,448,1]{2,1,0:T(8,128)S(1)} %get-tuple-element.24.norms, ...), custom_call_target="tpu_custom_call" | custom-call | flops 1 | bytes 1 | tf_op jit(solution)/shard_map/give_kernel/pallas_call | solution.py:273
  43.3 1.7 %collective-permute-start.6 = (bf16[4,104,512]{2,1,0:T(8,128)(2,1)S(1)}, bf16[4,104,512]{2,1,0:T(8,128)(2,1)S(1)}, u32[]{:S(2)}, u32[]{:S(2)}) collective-permute-start(bf16[4,104,512]{2,1,0:T(8,128)(2,1)S(1)} %get-tuple-element.39), channel_id=1, source_target_pairs={{0,8},{8,0},{16,24},{24,16},{32,40},{40,32},{48,56},{56,48},{1,9},... | collective-permute-start | bytes 1277960 | tf_op jit(solution)/shard_map/ppermute | solution.py:294
  45.1 4.7 %collective-permute-start.7 = (bf16[4,104,512]{2,1,0:T(8,128)(2,1)S(1)}, bf16[4,104,512]{2,1,0:T(8,128)(2,1)S(1)}, u32[]{:S(2)}, u32[]{:S(2)}) collective-permute-start(bf16[4,104,512]{2,1,0:T(8,128)(2,1)S(1)} %get-tuple-element.40), channel_id=1, source_target_pairs={{0,56},{8,16},{16,8},{24,32},{32,24},{40,48},{48,40},{56,0},{1,57}... | collective-permute-start | bytes 1277960 | tf_op jit(solution)/shard_map/ppermute | solution.py:295
  49.7 5.4 %keep_kernel.1.kept = f32[4,104,1024]{2,1,0:T(8,128)S(1)} custom-call(s32[3]{0:T(128)S(1)} %pad_add_fusion.place, f32[32,8,128]{2,1,0:T(8,128)S(1)} %all-to-all-done.stats, bf16[2,448,1024]{2,1,0:T(8,128)(2,1)S(1)} %get-tuple-element.23.rows, f32[2,448,1]{2,1,0:T(8,128)S(1)} %get-tuple-element.24.norms, bf16[512,1024]{1,0:T(8,128)(2,1)S(1)} %copy-done.1, ...), custom_call_target="tpu_custom_call" | custom-call | flops 1 | bytes 1 | tf_op jit(solution)/shard_map/keep_kernel/pallas_call | solution.py:273
  55.2 4.5 %collective-permute-done.7.right = bf16[4,104,512]{2,1,0:T(8,128)(2,1)S(1)} collective-permute-done((bf16[4,104,512]{2,1,0:T(8,128)(2,1)S(1)}, bf16[4,104,512]{2,1,0:T(8,128)(2,1)S(1)}, u32[]{:S(2)}, u32[]{:S(2)}) %collective-permute-start.7) | collective-permute-done | bytes 426016 | tf_op jit(solution)/shard_map/ppermute | solution.py:295
  59.6 0.2 merge.1
  59.8 31.2 %all_to_all.10.got = bf16[32,104,128]{2,1,0:T(8,128)(2,1)S(1)} all-to-all(bf16[32,104,128]{2,1,0:T(8,128)(2,1)S(1)} %merge.1), channel_id=1, replica_groups=mesh['x'=4,'zq'=4,'zp'=2,'y'=4,'core'=2] {'zq','y','core'}, dimensions={0} | all-to-all | bytes 1703936 | tf_op jit(solution)/shard_map/all_to_all | solution.py:305
  91.0 0.9 %final.1 = bf16[800,128]{1,0:T(8,128)(2,1)} custom-call(bf16[32,104,128]{2,1,0:T(8,128)(2,1)S(1)} %all_to_all.10.got), custom_call_target="tpu_custom_call" | custom-call | tf_op jit(solution)/shard_map/final/pallas_call | solution.py:306
  (11 shorter events, 0.0 us)
Async XLA Ops:
  0.1 1.2 %copy-start = (bf16[512,1024]{1,0:T(8,128)(2,1)S(1)}, bf16[512,1024]{1,0:T(8,128)(2,1)}, u32[]{:S(2)}) copy-start(bf16[512,1024]{1,0:T(8,128)(2,1)} %own.3) | copy-start | bytes 3145732
  2.7 33.3 %collective-permute-start.2 = (bf16[256,1024]{1,0:T(8,128)(2,1)}, bf16[256,1024]{1,0:T(8,128)(2,1)}, u32[]{:S(2)}, u32[]{:S(2)}) collective-permute-start(bf16[256,1024]{1,0:T(8,128)(2,1)} %cut.1.after), channel_id=1, source_target_pairs={{0,128},{64,192},{128,0},{192,64},{1,129},{65,193},{129,1},{193,65... | collective-permute-start | bytes 1572872 | tf_op jit(solution)/shard_map/ppermute | solution.py:245
  6.3 29.8 %collective-permute-start.1 = (bf16[256,1024]{1,0:T(8,128)(2,1)}, bf16[256,1024]{1,0:T(8,128)(2,1)}, u32[]{:S(2)}, u32[]{:S(2)}) collective-permute-start(bf16[256,1024]{1,0:T(8,128)(2,1)} %cut.1.after), channel_id=1, source_target_pairs={{0,192},{64,0},{128,64},{192,128},{1,193},{65,1},{129,65},{193,129... | collective-permute-start | bytes 1572872 | tf_op jit(solution)/shard_map/ppermute | solution.py:245
  7.1 28.9 %collective-permute-start = (bf16[256,1024]{1,0:T(8,128)(2,1)}, bf16[256,1024]{1,0:T(8,128)(2,1)}, u32[]{:S(2)}, u32[]{:S(2)}) collective-permute-start(bf16[256,1024]{1,0:T(8,128)(2,1)} %cut.1.after), channel_id=1, source_target_pairs={{0,64},{64,128},{128,192},{192,0},{1,65},{65,129},{129,193},{193,1... | collective-permute-start | bytes 1572872 | tf_op jit(solution)/shard_map/ppermute | solution.py:245
  16.2 18.1 %all-to-all-start = ((f32[32,8,128]{2,1,0:T(8,128)}), f32[32,8,128]{2,1,0:T(8,128)S(1)}, u32[]{:S(2)}, u32[]{:S(2)}) async-start(f32[32,8,128]{2,1,0:T(8,128)} %stats.1.after), calls=%async_computation | async-start | bytes 262144 | tf_op jit(solution)/shard_map/all_to_all | solution.py:259
  24.1 0.9 %copy-start.2 = (f32[32,8,128]{2,1,0:T(8,128)S(1)}, f32[32,8,128]{2,1,0:T(8,128)}, u32[]{:S(2)}) copy-start(f32[32,8,128]{2,1,0:T(8,128)} %stats.1.after) | copy-start | bytes 393220
  25.1 9.2 %copy-start.1 = (bf16[512,1024]{1,0:T(8,128)(2,1)S(1)}, bf16[512,1024]{1,0:T(8,128)(2,1)}, u32[]{:S(2)}) copy-start(bf16[512,1024]{1,0:T(8,128)(2,1)} %own.3) | copy-start | bytes 3145732
  36.0 4.6 %collective-permute-start.3 = (bf16[256,1024]{1,0:T(8,128)(2,1)}, bf16[256,1024]{1,0:T(8,128)(2,1)S(1)}, u32[]{:S(2)}, u32[]{:S(2)}) collective-permute-start(bf16[256,1024]{1,0:T(8,128)(2,1)} %collective-permute-done.up), channel_id=1, source_target_pairs={{0,1},{1,0},{2,3},{3,2},{4,5},{5,4},{6,7},{7,6},{8,9},{9,8},{10,11... | collective-permute-start | bytes 1572872 | tf_op jit(solution)/shard_map/ppermute | solution.py:288
  36.6 4.0 %collective-permute-start.4 = (bf16[256,1024]{1,0:T(8,128)(2,1)}, bf16[256,1024]{1,0:T(8,128)(2,1)S(1)}, u32[]{:S(2)}, u32[]{:S(2)}) collective-permute-start(bf16[256,1024]{1,0:T(8,128)(2,1)} %collective-permute-done.1.down), channel_id=1, source_target_pairs={{0,1},{1,0},{2,3},{3,2},{4,5},{5,4},{6,7},{7,6},{8,9},{9,8},{10,11... | collective-permute-start | bytes 1572872 | tf_op jit(solution)/shard_map/ppermute | solution.py:288
  36.7 3.9 %collective-permute-start.5 = (bf16[256,1024]{1,0:T(8,128)(2,1)}, bf16[256,1024]{1,0:T(8,128)(2,1)S(1)}, u32[]{:S(2)}, u32[]{:S(2)}) collective-permute-start(bf16[256,1024]{1,0:T(8,128)(2,1)} %collective-permute-done.2.far), channel_id=1, source_target_pairs={{0,1},{1,0},{2,3},{3,2},{4,5},{5,4},{6,7},{7,6},{8,9},{9,8},{10,11... | collective-permute-start | bytes 1572872 | tf_op jit(solution)/shard_map/ppermute | solution.py:288
  43.3 11.8 %collective-permute-start.6 = (bf16[4,104,512]{2,1,0:T(8,128)(2,1)S(1)}, bf16[4,104,512]{2,1,0:T(8,128)(2,1)S(1)}, u32[]{:S(2)}, u32[]{:S(2)}) collective-permute-start(bf16[4,104,512]{2,1,0:T(8,128)(2,1)S(1)} %get-tuple-element.39), channel_id=1, source_target_pairs={{0,8},{8,0},{16,24},{24,16},{32,40},{40,32},{48,56},{56,48},{1,9},... | collective-permute-start | bytes 1277960 | tf_op jit(solution)/shard_map/ppermute | solution.py:294
  45.1 14.6 %collective-permute-start.7 = (bf16[4,104,512]{2,1,0:T(8,128)(2,1)S(1)}, bf16[4,104,512]{2,1,0:T(8,128)(2,1)S(1)}, u32[]{:S(2)}, u32[]{:S(2)}) collective-permute-start(bf16[4,104,512]{2,1,0:T(8,128)(2,1)S(1)} %get-tuple-element.40), channel_id=1, source_target_pairs={{0,56},{8,16},{16,8},{24,32},{32,24},{40,48},{48,40},{56,0},{1,57}... | collective-permute-start | bytes 1277960 | tf_op jit(solution)/shard_map/ppermute | solution.py:295

commit v10 on v9

--- a/solution.py
+++ b/solution.py
@@ -21,6 +21,7 @@
 MIB = 2**20
 CHEAP = pl.CostEstimate(flops=1, bytes_accessed=1, transcendentals=0)
 TILE = 640
+LEFT = 640
 SHIFTS = (1, NX - 1, 2)
 
 
@@ -158,13 +159,9 @@
     return [(ref, lse_halves(place, stats, k)[which]) for k, ref in zip(SHIFTS, refs)]
 
 
-def own_kernel(place, stats, rows, norms, own, numer, counts, held):
-    weighted([(own, lse_of(stats, place[2]))], rows, norms, 1 - place[1], held, numer, counts)
-
-
-def first_kernel(place, stats, rows, norms, up, down, far, numer_in, counts_in, numer, counts, held):
-    pieces = half_pieces(place, stats, (up, down, far), 0)
-    weighted(pieces, rows, norms, 1 - place[1], held, numer, counts, (numer_in, counts_in))
+def first_kernel(place, stats, rows, norms, own, up, down, far, numer, counts, held):
+    pieces = [(own, lse_of(stats, place[2]))] + half_pieces(place, stats, (up, down, far), 0)
+    weighted(pieces, rows, norms, 1 - place[1], held, numer, counts)
 
 
 def give_kernel(place, stats, rows, norms, up, down, far, numer_in, counts_in, left, right, held, numer, counts):
@@ -192,20 +189,19 @@
 
 
 def merge_kernel(kept, left, right, send):
-    blocks, height, width = kept.shape
-    at = height - TAIL
+    blocks, height, _ = kept.shape
     for b in range(blocks):
-        for h, got in ((0, left), (1, right)):
-            half = width // 2
-            mine = kept[b, :, h * half : (h + 1) * half]
-            theirs = got[b].astype(F32)
-            values = mine + theirs
+        at = 0
+        for got in (left, right):
+            width = got.shape[2]
+            values = kept[b, :, at : at + width] + got[b].astype(F32)
             tail = values[height - 8 :]
             counts = tail[8 - TAIL : 9 - TAIL, :LANES] + tail[9 - TAIL : 10 - TAIL, :LANES]
             high, low = split(counts)
             values = close(values, high, low).astype(BF)
-            for c in range(half // LANES):
-                send[b * N_CENT + h * (half // LANES) + c] = values[:, c * LANES : (c + 1) * LANES]
+            for c in range(width // LANES):
+                send[b * N_CENT + at // LANES + c] = values[:, c * LANES : (c + 1) * LANES]
+            at += width
 
 
 def final_kernel(got, out, scratch):
@@ -283,13 +279,12 @@
 
     sums = (shape((work, dim), F32), shape((work, LANES), F32))
     spare = [pltpu.VMEM(s.shape, F32) for s in sums]
-    numer = call(own_kernel, sums, pts, points)
-    near, numer = lax.optimization_barrier((near, numer))
+    near, stats = lax.optimization_barrier((near, stats))
     others = [lax.ppermute(a, "core", [(0, 1), (1, 0)]) for a in near]
-    numer = call(first_kernel, sums, 3 * half, *near, *numer)
+    numer = call(first_kernel, sums, pts + 3 * half, points, *near)
     others, numer = lax.optimization_barrier((others, numer))
-    part = shape((n_blocks, height, dim // 2), BF)
-    left, right = call(give_kernel, (part, part), 3 * half, *others, *numer, scratch=spare)
+    parts = tuple(shape((n_blocks, height, width), BF) for width in (LEFT, dim - LEFT))
+    left, right = call(give_kernel, parts, 3 * half, *others, *numer, scratch=spare)
 
     got_left = lax.ppermute(left, Z, [(i, i ^ 1) for i in range(NZ)])
     got_right = lax.ppermute(right, Z, [(i, (i + (1 if i % 2 else -1)) % NZ) for i in range(NZ)])

time: 92.3 us -> 92.8 us (level)
  blocking collectives: 31.2 us -> 51.3 us
  waiting for transfers between devices: 11.1 us -> 3.09 us
  starting transfers between devices: 20.5 us -> 12.6 us
  Pallas kernels: 26.8 us -> 23.2 us
    all_to_all x0 -> x1, blocking collectives: none -> 17.8 us  [body(): stats = lax.all_to_all(send_stats, ('x', *CENT), 0, 0)]
    all_to_all x1 -> x0, starting transfers between devices: 7.94 us -> none  [body(): stats = lax.all_to_all(send_stats, ('x', *CENT), 0, 0)]
    all_to_all x1 -> x0, waiting for transfers between devices: 6.61 us -> none  [body(): stats = lax.all_to_all(send_stats, ('x', *CENT), 0, 0)]
    pallas_call x4 -> x3, Pallas kernels: 13.3 us -> 10.4 us  [call(): pl.pallas_call(kernel, out_shape=out_shape, in_specs=[SMEM] + [VMEM] * (3...]
    all_to_all x1, blocking collectives: 31.2 us -> 33.5 us  [body(): got = lax.all_to_all(send, ('zq', *CENT), 0, 0)]
    ppermute x1, waiting for transfers between devices: 4.45 us -> 3.02 us  [body(): lax.ppermute(right, Z, [(i, (i + (1 if i % 2 else -1)) % NZ) for i in ran...]
    unnamed x6 -> x8, local copies, waits for them, and re-layouts: 2.16 us -> 2.14 us
  transfers between devices with their start and end apart: 9 -> 8, of which waited for: 2 -> 2; matrix products, arithmetic and copies ran while one was open for 0% -> 0% of each run, Pallas kernels for 24% -> 20%
where the time goes in v10:
time: 92.8 us; the launch traced here: 92.5 us
  blocking collectives  51.3 us (55%)
  Pallas kernels  23.2 us (25%)
  starting transfers between devices  12.6 us (14%)
  waiting for transfers between devices  3.09 us (3%)
  local copies, waits for them, and re-layouts  2.14 us (2%)
    all_to_all x1, blocking collectives, body(): got = lax.all_to_all(send, ('zq', *CENT), 0, 0)  33.5 us
    all_to_all x1, blocking collectives, body(): stats = lax.all_to_all(send_stats, ('x', *CENT), 0, 0)  17.8 us
    pallas_call x3, Pallas kernels, call(): pl.pallas_call(kernel, out_shape=out_shape, in_specs=[SMEM] + [VMEM] * (3...  10.4 us
    pallas_call x1, Pallas kernels, body(): pl.pallas_call(stats_kernel, grid=(rows // TILE,), out_shape=shape(stats_...  8.5 us
    ppermute x3, starting transfers between devices, body(): lax.ppermute(own_half, 'x', [(i, (i + k) % NX) for i in range(NX)])  5.13 us
    ppermute x1, starting transfers between devices, body(): lax.ppermute(right, Z, [(i, (i + (1 if i % 2 else -1)) % NZ) for i in ran...  4.67 us
    ppermute x1, waiting for transfers between devices, body(): lax.ppermute(right, Z, [(i, (i + (1 if i % 2 else -1)) % NZ) for i in ran...  3.02 us
    pallas_call x1, Pallas kernels, body(): pl.pallas_call(window_kernel, out_shape=(shape((2, work, dim), BF), shape...  2.55 us
  transfers between devices with their start and end apart: 8, of which 2 were waited for; matrix products, arithmetic and copies ran while one was open for 0% of the time, Pallas kernels for 20%

profile of v10, /device:TPU:1, one launch (start us, length us, event | category | flops | bytes accessed | tf_op | source)
XLA Modules:
  0.0 92.5 jit_solution(16155084988539832208)
XLA Ops:
  0.0 0.1 pad_add_fusion.place
  0.1 1.2 %copy-done = bf16[512,1024]{1,0:T(8,128)(2,1)S(1)} copy-done((bf16[512,1024]{1,0:T(8,128)(2,1)S(1)}, bf16[512,1024]{1,0:T(8,128)(2,1)}, u32[]{:S(2)}) %copy-start) | copy-done | bytes 1048600
  1.3 0.6 cut.1.after
  1.9 3.7 %collective-permute-start.2 = (bf16[256,1024]{1,0:T(8,128)(2,1)S(1)}, bf16[256,1024]{1,0:T(8,128)(2,1)S(1)}, u32[]{:S(2)}, u32[]{:S(2)}) collective-permute-start(bf16[256,1024]{1,0:T(8,128)(2,1)S(1)} %cut.1.after), channel_id=1, source_target_pairs={{0,128},{64,192},{128,0},{192,64},{1,129},{65,193},{129,1},{193,65... | collective-permute-start | bytes 1572872 | tf_op jit(solution)/shard_map/ppermute | solution.py:241
  5.6 0.9 collective-permute-start.1
  6.4 0.6 collective-permute-start
  7.0 8.5 %stats.1.after = f32[32,8,128]{2,1,0:T(8,128)} custom-call(bf16[512,1024]{1,0:T(8,128)(2,1)} %own.3, bf16[3200,1024]{1,0:T(8,128)(2,1)} %table.1, bf16[256,1024]{1,0:T(8,128)(2,1)} %copy-done.2), custom_call_target="tpu_custom_call" | custom-call | flops 1 | bytes 1 | tf_op jit(solution)/shard_map/stats/pallas_call | solution.py:244
  15.5 17.8 %all_to_all.10.stats = f32[32,8,128]{2,1,0:T(8,128)S(1)} all-to-all(f32[32,8,128]{2,1,0:T(8,128)} %stats.1.after), channel_id=1, replica_groups=mesh['x'=4,'zq'=4,'zp'=2,'y'=4,'core'=2] {'x','y','core'}, dimensions={0} | all-to-all | bytes 262144 | tf_op jit(solution)/shard_map/all_to_all | solution.py:255
  33.4 0.0 collective-permute-done.1.down
  33.4 0.6 collective-permute-start.3
  33.9 0.1 collective-permute-start.4
  34.0 0.4 collective-permute-start.5
  34.5 0.9 copy-done.3
  35.4 2.6 %window.1 = (bf16[2,448,1024]{2,1,0:T(8,128)(2,1)S(1)}, f32[2,448,1]{2,1,0:T(8,128)S(1)}) custom-call(s32[3]{0:T(128)S(1)} %pad_add_fusion.place, bf16[3200,1024]{1,0:T(8,128)(2,1)} %table.1, f32[32,8,128]{2,1,0:T(8,128)S(1)} %copy-done.3), custom_call_target="tpu_custom_call" | custom-call | flops 1 | bytes 1 | tf_op jit(solution)/shard_map/window/pallas_call | solution.py:257
  37.9 3.1 %first_kernel.1 = (f32[448,1024]{1,0:T(8,128)S(1)}, f32[448,128]{1,0:T(8,128)S(1)}) custom-call(s32[3]{0:T(128)S(1)} %pad_add_fusion.place, f32[32,8,128]{2,1,0:T(8,128)S(1)} %all_to_all.10.stats, bf16[2,448,1024]{2,1,0:T(8,128)(2,1)S(1)} %get-tuple-element.21.rows, f32[2,448,1]{2,1,0:T(8,128)S(1)} %get-tuple-element.22.norms, ...), custom_call_target="tpu_custom_call" | custom-call | flops 1 | bytes 1 | tf_op jit(solution)/shard_map/first_kernel/pallas_call | solution.py:269
  41.1 2.7 %give_kernel.1 = (bf16[4,104,640]{2,1,0:T(8,128)(2,1)S(1)}, bf16[4,104,384]{2,1,0:T(8,128)(2,1)S(1)}) custom-call(s32[3]{0:T(128)S(1)} %pad_add_fusion.place, f32[32,8,128]{2,1,0:T(8,128)S(1)} %all_to_all.10.stats, bf16[2,448,1024]{2,1,0:T(8,128)(2,1)S(1)} %get-tuple-element.21.rows, f32[2,448,1]{2,1,0:T(8,128)S(1)} %get-tuple-element.22.norms, ...), custom_call_target="tpu_custom_call" | custom-call | flops 1 | bytes 1 | tf_op jit(solution)/shard_map/give_kernel/pallas_call | solution.py:269
  43.8 1.7 %collective-permute-start.6 = (bf16[4,104,640]{2,1,0:T(8,128)(2,1)S(1)}, bf16[4,104,640]{2,1,0:T(8,128)(2,1)S(1)}, u32[]{:S(2)}, u32[]{:S(2)}) collective-permute-start(bf16[4,104,640]{2,1,0:T(8,128)(2,1)S(1)} %get-tuple-element.33), channel_id=1, source_target_pairs={{0,8},{8,0},{16,24},{24,16},{32,40},{40,32},{48,56},{56,48},{1,9},... | collective-permute-start | bytes 1597448 | tf_op jit(solution)/shard_map/ppermute | solution.py:289
  45.5 4.7 %collective-permute-start.7 = (bf16[4,104,384]{2,1,0:T(8,128)(2,1)S(1)}, bf16[4,104,384]{2,1,0:T(8,128)(2,1)S(1)}, u32[]{:S(2)}, u32[]{:S(2)}) collective-permute-start(bf16[4,104,384]{2,1,0:T(8,128)(2,1)S(1)} %get-tuple-element.34), channel_id=1, source_target_pairs={{0,56},{8,16},{16,8},{24,32},{32,24},{40,48},{48,40},{56,0},{1,57}... | collective-permute-start | bytes 958472 | tf_op jit(solution)/shard_map/ppermute | solution.py:290
  50.2 4.6 %keep_kernel.1.kept = f32[4,104,1024]{2,1,0:T(8,128)S(1)} custom-call(s32[3]{0:T(128)S(1)} %pad_add_fusion.place, f32[32,8,128]{2,1,0:T(8,128)S(1)} %all_to_all.10.stats, bf16[2,448,1024]{2,1,0:T(8,128)(2,1)S(1)} %get-tuple-element.21.rows, f32[2,448,1]{2,1,0:T(8,128)S(1)} %get-tuple-element.22.norms, bf16[512,1024]{1,0:T(8,128)(2,1)S(1)} %copy-done.1, ...), custom_call_target="tpu_custom_call" | custom-call | flops 1 | bytes 1 | tf_op jit(solution)/shard_map/keep_kernel/pallas_call | solution.py:269
  54.8 3.0 %collective-permute-done.7.right = bf16[4,104,384]{2,1,0:T(8,128)(2,1)S(1)} collective-permute-done((bf16[4,104,384]{2,1,0:T(8,128)(2,1)S(1)}, bf16[4,104,384]{2,1,0:T(8,128)(2,1)S(1)}, u32[]{:S(2)}, u32[]{:S(2)}) %collective-permute-start.7) | collective-permute-done | bytes 319520 | tf_op jit(solution)/shard_map/ppermute | solution.py:290
  57.8 0.1 collective-permute-done.6.left
  57.9 0.2 merge.1
  58.1 33.5 %all_to_all.11.got = bf16[32,104,128]{2,1,0:T(8,128)(2,1)S(1)} all-to-all(bf16[32,104,128]{2,1,0:T(8,128)(2,1)S(1)} %merge.1), channel_id=1, replica_groups=mesh['x'=4,'zq'=4,'zp'=2,'y'=4,'core'=2] {'zq','y','core'}, dimensions={0} | all-to-all | bytes 1703936 | tf_op jit(solution)/shard_map/all_to_all | solution.py:300
  91.5 0.9 %final.1 = bf16[800,128]{1,0:T(8,128)(2,1)} custom-call(bf16[32,104,128]{2,1,0:T(8,128)(2,1)S(1)} %all_to_all.11.got), custom_call_target="tpu_custom_call" | custom-call | tf_op jit(solution)/shard_map/final/pallas_call | solution.py:301
  (11 shorter events, 0.0 us)
Async XLA Ops:
  0.1 1.2 %copy-start = (bf16[512,1024]{1,0:T(8,128)(2,1)S(1)}, bf16[512,1024]{1,0:T(8,128)(2,1)}, u32[]{:S(2)}) copy-start(bf16[512,1024]{1,0:T(8,128)(2,1)} %own.3) | copy-start | bytes 3145732
  1.9 5.1 %copy-start.2 = (bf16[256,1024]{1,0:T(8,128)(2,1)}, bf16[256,1024]{1,0:T(8,128)(2,1)S(1)}, u32[]{:S(2)}) copy-start(bf16[256,1024]{1,0:T(8,128)(2,1)S(1)} %cut.1.after) | copy-start | bytes 1572868
  1.9 31.5 %collective-permute-start.2 = (bf16[256,1024]{1,0:T(8,128)(2,1)S(1)}, bf16[256,1024]{1,0:T(8,128)(2,1)S(1)}, u32[]{:S(2)}, u32[]{:S(2)}) collective-permute-start(bf16[256,1024]{1,0:T(8,128)(2,1)S(1)} %cut.1.after), channel_id=1, source_target_pairs={{0,128},{64,192},{128,0},{192,64},{1,129},{65,193},{129,1},{193,65... | collective-permute-start | bytes 1572872 | tf_op jit(solution)/shard_map/ppermute | solution.py:241
  5.6 27.8 %collective-permute-start.1 = (bf16[256,1024]{1,0:T(8,128)(2,1)S(1)}, bf16[256,1024]{1,0:T(8,128)(2,1)S(1)}, u32[]{:S(2)}, u32[]{:S(2)}) collective-permute-start(bf16[256,1024]{1,0:T(8,128)(2,1)S(1)} %cut.1.after), channel_id=1, source_target_pairs={{0,192},{64,0},{128,64},{192,128},{1,193},{65,1},{129,65},{193,129... | collective-permute-start | bytes 1572872 | tf_op jit(solution)/shard_map/ppermute | solution.py:241
  6.4 26.9 %collective-permute-start = (bf16[256,1024]{1,0:T(8,128)(2,1)S(1)}, bf16[256,1024]{1,0:T(8,128)(2,1)S(1)}, u32[]{:S(2)}, u32[]{:S(2)}) collective-permute-start(bf16[256,1024]{1,0:T(8,128)(2,1)S(1)} %cut.1.after), channel_id=1, source_target_pairs={{0,64},{64,128},{128,192},{192,0},{1,65},{65,129},{129,193},{193,1... | collective-permute-start | bytes 1572872 | tf_op jit(solution)/shard_map/ppermute | solution.py:241
  33.4 4.6 %copy-start.1 = (bf16[512,1024]{1,0:T(8,128)(2,1)S(1)}, bf16[512,1024]{1,0:T(8,128)(2,1)}, u32[]{:S(2)}) copy-start(bf16[512,1024]{1,0:T(8,128)(2,1)} %own.3) | copy-start | bytes 3145732
  33.4 7.7 %collective-permute-start.3 = (bf16[256,1024]{1,0:T(8,128)(2,1)S(1)}, bf16[256,1024]{1,0:T(8,128)(2,1)S(1)}, u32[]{:S(2)}, u32[]{:S(2)}) collective-permute-start(bf16[256,1024]{1,0:T(8,128)(2,1)S(1)} %collective-permute-done.up), channel_id=1, source_target_pairs={{0,1},{1,0},{2,3},{3,2},{4,5},{5,4},{6,7},{7,6},{8,9},{9,8},{10,11... | collective-permute-start | bytes 1572872 | tf_op jit(solution)/shard_map/ppermute | solution.py:283
  33.9 7.1 %collective-permute-start.4 = (bf16[256,1024]{1,0:T(8,128)(2,1)S(1)}, bf16[256,1024]{1,0:T(8,128)(2,1)S(1)}, u32[]{:S(2)}, u32[]{:S(2)}) collective-permute-start(bf16[256,1024]{1,0:T(8,128)(2,1)S(1)} %collective-permute-done.1.down), channel_id=1, source_target_pairs={{0,1},{1,0},{2,3},{3,2},{4,5},{5,4},{6,7},{7,6},{8,9},{9,8},{10,11... | collective-permute-start | bytes 1572872 | tf_op jit(solution)/shard_map/ppermute | solution.py:283
  34.0 7.1 %collective-permute-start.5 = (bf16[256,1024]{1,0:T(8,128)(2,1)S(1)}, bf16[256,1024]{1,0:T(8,128)(2,1)S(1)}, u32[]{:S(2)}, u32[]{:S(2)}) collective-permute-start(bf16[256,1024]{1,0:T(8,128)(2,1)S(1)} %collective-permute-done.2.far), channel_id=1, source_target_pairs={{0,1},{1,0},{2,3},{3,2},{4,5},{5,4},{6,7},{7,6},{8,9},{9,8},{10,11... | collective-permute-start | bytes 1572872 | tf_op jit(solution)/shard_map/ppermute | solution.py:283
  34.5 0.9 copy-start.3
  43.8 14.1 %collective-permute-start.6 = (bf16[4,104,640]{2,1,0:T(8,128)(2,1)S(1)}, bf16[4,104,640]{2,1,0:T(8,128)(2,1)S(1)}, u32[]{:S(2)}, u32[]{:S(2)}) collective-permute-start(bf16[4,104,640]{2,1,0:T(8,128)(2,1)S(1)} %get-tuple-element.33), channel_id=1, source_target_pairs={{0,8},{8,0},{16,24},{24,16},{32,40},{40,32},{48,56},{56,48},{1,9},... | collective-permute-start | bytes 1597448 | tf_op jit(solution)/shard_map/ppermute | solution.py:289
  45.5 12.3 %collective-permute-start.7 = (bf16[4,104,384]{2,1,0:T(8,128)(2,1)S(1)}, bf16[4,104,384]{2,1,0:T(8,128)(2,1)S(1)}, u32[]{:S(2)}, u32[]{:S(2)}) collective-permute-start(bf16[4,104,384]{2,1,0:T(8,128)(2,1)S(1)} %get-tuple-element.34), channel_id=1, source_target_pairs={{0,56},{8,16},{16,8},{24,32},{32,24},{40,48},{48,40},{56,0},{1,57}... | collective-permute-start | bytes 958472 | tf_op jit(solution)/shard_map/ppermute | solution.py:290

commit v11 on v10

--- a/solution.py
+++ b/solution.py
@@ -38,7 +38,7 @@
     half_out[...] = points[pl.ds(pl.multiple_of(place[0] * half, half), half)]
 
 
-def stats_kernel(points, cents, after, out, top, total):
+def stats_kernel(points, cents, after, out, flag, top, total):
     step = pl.program_id(0)
 
     @pl.when(step == 0)
@@ -66,6 +66,7 @@
         groups = top.shape[1] // LANES
         both = [r[:, g * LANES : (g + 1) * LANES] for r in (top[...], total[...]) for g in range(groups)]
         out[...] = jnp.broadcast_to(jnp.concatenate(both, axis=0)[None], out.shape)
+        flag[...] = jnp.zeros_like(flag)
 
 
 def window_kernel(place, table, after, mine, norms, sems):
@@ -241,12 +242,12 @@
     near = [lax.ppermute(own_half, "x", [(i, (i + k) % NX) for i in range(NX)]) for k in SHIFTS]
 
     stats_shape = (NX * N_CENT, 2 * pts // LANES, LANES)
-    send_stats = pl.pallas_call(
+    send_stats, flag = pl.pallas_call(
         stats_kernel,
         grid=(rows // TILE,),
-        out_shape=shape(stats_shape, F32),
+        out_shape=(shape(stats_shape, F32), shape((8, LANES), F32)),
         in_specs=[pl.BlockSpec((pts, dim), lambda i: (0, 0)), pl.BlockSpec((TILE, dim), lambda i: (i, 0)), ANY],
-        out_specs=pl.BlockSpec(stats_shape, lambda i: (0, 0, 0)),
+        out_specs=(pl.BlockSpec(stats_shape, lambda i: (0, 0, 0)), pl.BlockSpec((8, LANES), lambda i: (0, 0))),
         scratch_shapes=[pltpu.VMEM((1, pts), F32), pltpu.VMEM((1, pts), F32)],
         compiler_params=params(54),
         cost_estimate=CHEAP,
@@ -263,7 +264,7 @@
         compiler_params=params(50),
         cost_estimate=CHEAP,
         name="window",
-    )(place, centroids, send_stats)
+    )(place, centroids, flag)
 
     def call(kernel, out_shape, n_points, *args, scratch=()):
         return pl.pallas_call(
@@ -279,7 +280,7 @@
 
     sums = (shape((work, dim), F32), shape((work, LANES), F32))
     spare = [pltpu.VMEM(s.shape, F32) for s in sums]
-    near, stats = lax.optimization_barrier((near, stats))
+    near, stats, mine, norms = lax.optimization_barrier((near, stats, mine, norms))
     others = [lax.ppermute(a, "core", [(0, 1), (1, 0)]) for a in near]
     numer = call(first_kernel, sums, pts + 3 * half, points, *near)
     others, numer = lax.optimization_barrier((others, numer))

time: 92.8 us -> 91.4 us (0.985)
  blocking collectives: 51.3 us -> 33.8 us
  starting transfers between devices: 12.6 us -> 20.5 us
  waiting for transfers between devices: 3.09 us -> 9.12 us
  Pallas kernels: 23.2 us -> 25.6 us
    all_to_all x1 -> x0, blocking collectives: 17.8 us -> none  [body(): stats = lax.all_to_all(send_stats, ('x', *CENT), 0, 0)]
    all_to_all x0 -> x1, starting transfers between devices: none -> 7.93 us  [body(): stats = lax.all_to_all(send_stats, ('x', *CENT), 0, 0)]
    all_to_all x0 -> x1, waiting for transfers between devices: none -> 6.87 us  [body(): stats = lax.all_to_all(send_stats, ('x', *CENT), 0, 0)]
    pallas_call x3, Pallas kernels: 10.4 us -> 12.1 us  [call(): pl.pallas_call(kernel, out_shape=out_shape, in_specs=[SMEM] + [VMEM] * (3...]
    unnamed x8 -> x6, local copies, waits for them, and re-layouts: 2.14 us -> 1.89 us
  transfers between devices with their start and end apart: 8 -> 9, of which waited for: 2 -> 3; matrix products, arithmetic and copies ran while one was open for 0% -> 0% of each run, Pallas kernels for 20% -> 22%
where the time goes in v11:
time: 91.4 us; the launch traced here: 91 us
  blocking collectives  33.8 us (37%)
  Pallas kernels  25.6 us (28%)
  starting transfers between devices  20.5 us (22%)
  waiting for transfers between devices  9.12 us (10%)
  local copies, waits for them, and re-layouts  1.89 us (2%)
    all_to_all x1, blocking collectives, body(): got = lax.all_to_all(send, ('zq', *CENT), 0, 0)  33.8 us
    pallas_call x3, Pallas kernels, call(): pl.pallas_call(kernel, out_shape=out_shape, in_specs=[SMEM] + [VMEM] * (3...  12.1 us
    pallas_call x1, Pallas kernels, body(): pl.pallas_call(stats_kernel, grid=(rows // TILE,), out_shape=(shape(stats...  8.49 us
    all_to_all x1, starting transfers between devices, body(): stats = lax.all_to_all(send_stats, ('x', *CENT), 0, 0)  7.93 us
    all_to_all x1, waiting for transfers between devices, body(): stats = lax.all_to_all(send_stats, ('x', *CENT), 0, 0)  6.87 us
    ppermute x3, starting transfers between devices, body(): lax.ppermute(own_half, 'x', [(i, (i + k) % NX) for i in range(NX)])  5.04 us
    ppermute x1, starting transfers between devices, body(): lax.ppermute(right, Z, [(i, (i + (1 if i % 2 else -1)) % NZ) for i in ran...  4.67 us
    pallas_call x1, Pallas kernels, body(): pl.pallas_call(window_kernel, out_shape=(shape((2, work, dim), BF), shape...  2.55 us
  transfers between devices with their start and end apart: 9, of which 3 were waited for; matrix products, arithmetic and copies ran while one was open for 0% of the time, Pallas kernels for 22%

profile of v11, /device:TPU:1, one launch (start us, length us, event | category | flops | bytes accessed | tf_op | source)
XLA Modules:
  0.0 91.0 jit_solution(8175888402777120910)
XLA Ops:
  0.0 0.1 pad_add_fusion.place
  0.1 1.2 %copy-done = bf16[512,1024]{1,0:T(8,128)(2,1)S(1)} copy-done((bf16[512,1024]{1,0:T(8,128)(2,1)S(1)}, bf16[512,1024]{1,0:T(8,128)(2,1)}, u32[]{:S(2)}) %copy-start) | copy-done | bytes 1048600
  1.3 1.4 %cut.1.after = bf16[256,1024]{1,0:T(8,128)(2,1)} custom-call(s32[3]{0:T(128)S(1)} %pad_add_fusion.place, bf16[512,1024]{1,0:T(8,128)(2,1)S(1)} %copy-done), custom_call_target="tpu_custom_call" | custom-call | flops 1 | bytes 1 | tf_op jit(solution)/shard_map/cut/pallas_call | solution.py:233
  2.7 3.6 %collective-permute-start.2 = (bf16[256,1024]{1,0:T(8,128)(2,1)}, bf16[256,1024]{1,0:T(8,128)(2,1)}, u32[]{:S(2)}, u32[]{:S(2)}) collective-permute-start(bf16[256,1024]{1,0:T(8,128)(2,1)} %cut.1.after), channel_id=1, source_target_pairs={{0,128},{64,192},{128,0},{192,64},{1,129},{65,193},{129,1},{193,65... | collective-permute-start | bytes 1572872 | tf_op jit(solution)/shard_map/ppermute | solution.py:242
  6.3 0.9 collective-permute-start.1
  7.1 0.6 collective-permute-start
  7.7 8.5 %stats.1 = (f32[32,8,128]{2,1,0:T(8,128)}, f32[8,128]{1,0:T(8,128)}) custom-call(bf16[512,1024]{1,0:T(8,128)(2,1)} %own.3, bf16[3200,1024]{1,0:T(8,128)(2,1)} %table.1, bf16[256,1024]{1,0:T(8,128)(2,1)} %cut.1.after), custom_call_target="tpu_custom_call" | custom-call | flops 1 | bytes 1 | tf_op jit(solution)/shard_map/stats/pallas_call | solution.py:245
  16.2 7.9 %all-to-all-start = ((f32[32,8,128]{2,1,0:T(8,128)}), f32[32,8,128]{2,1,0:T(8,128)S(1)}, u32[]{:S(2)}, u32[]{:S(2)}) async-start(f32[32,8,128]{2,1,0:T(8,128)} %get-tuple-element.24), calls=%async_computation | async-start | bytes 262144 | tf_op jit(solution)/shard_map/all_to_all | solution.py:256
  24.2 0.7 copy-done.2
  24.8 2.6 %window.1 = (bf16[2,448,1024]{2,1,0:T(8,128)(2,1)S(1)}, f32[2,448,1]{2,1,0:T(8,128)S(1)}) custom-call(s32[3]{0:T(128)S(1)} %pad_add_fusion.place, bf16[3200,1024]{1,0:T(8,128)(2,1)} %table.1, f32[8,128]{1,0:T(8,128)S(1)} %copy-done.2), custom_call_target="tpu_custom_call" | custom-call | flops 1 | bytes 1 | tf_op jit(solution)/shard_map/window/pallas_call | solution.py:258
  27.4 6.9 %all-to-all-done.stats = f32[32,8,128]{2,1,0:T(8,128)S(1)} async-done(((f32[32,8,128]{2,1,0:T(8,128)}), f32[32,8,128]{2,1,0:T(8,128)S(1)}, u32[]{:S(2)}, u32[]{:S(2)}) %all-to-all-start) | async-done | bytes 131104 | tf_op jit(solution)/shard_map/all_to_all | solution.py:256
  34.3 0.6 collective-permute-start.3
  34.8 0.1 collective-permute-start.4
  34.9 0.4 collective-permute-start.5
  35.3 4.0 %first_kernel.1 = (f32[448,1024]{1,0:T(8,128)S(1)}, f32[448,128]{1,0:T(8,128)S(1)}) custom-call(s32[3]{0:T(128)S(1)} %pad_add_fusion.place, f32[32,8,128]{2,1,0:T(8,128)S(1)} %all-to-all-done.stats, bf16[2,448,1024]{2,1,0:T(8,128)(2,1)S(1)} %get-tuple-element.29.rows, f32[2,448,1]{2,1,0:T(8,128)S(1)} %get-tuple-element.30.norms, ...), custom_call_target="tpu_custom_call" | custom-call | flops 1 | bytes 1 | tf_op jit(solution)/shard_map/first_kernel/pallas_call | solution.py:270
  39.3 2.7 %give_kernel.1 = (bf16[4,104,640]{2,1,0:T(8,128)(2,1)S(1)}, bf16[4,104,384]{2,1,0:T(8,128)(2,1)S(1)}) custom-call(s32[3]{0:T(128)S(1)} %pad_add_fusion.place, f32[32,8,128]{2,1,0:T(8,128)S(1)} %all-to-all-done.stats, bf16[2,448,1024]{2,1,0:T(8,128)(2,1)S(1)} %get-tuple-element.29.rows, f32[2,448,1]{2,1,0:T(8,128)S(1)} %get-tuple-element.30.norms, ...), custom_call_target="tpu_custom_call" | custom-call | flops 1 | bytes 1 | tf_op jit(solution)/shard_map/give_kernel/pallas_call | solution.py:270
  42.1 1.7 %collective-permute-start.6 = (bf16[4,104,640]{2,1,0:T(8,128)(2,1)S(1)}, bf16[4,104,640]{2,1,0:T(8,128)(2,1)S(1)}, u32[]{:S(2)}, u32[]{:S(2)}) collective-permute-start(bf16[4,104,640]{2,1,0:T(8,128)(2,1)S(1)} %get-tuple-element.41), channel_id=1, source_target_pairs={{0,8},{8,0},{16,24},{24,16},{32,40},{40,32},{48,56},{56,48},{1,9},... | collective-permute-start | bytes 1597448 | tf_op jit(solution)/shard_map/ppermute | solution.py:290
  43.8 4.7 %collective-permute-start.7 = (bf16[4,104,384]{2,1,0:T(8,128)(2,1)S(1)}, bf16[4,104,384]{2,1,0:T(8,128)(2,1)S(1)}, u32[]{:S(2)}, u32[]{:S(2)}) collective-permute-start(bf16[4,104,384]{2,1,0:T(8,128)(2,1)S(1)} %get-tuple-element.42), channel_id=1, source_target_pairs={{0,56},{8,16},{16,8},{24,32},{32,24},{40,48},{48,40},{56,0},{1,57}... | collective-permute-start | bytes 958472 | tf_op jit(solution)/shard_map/ppermute | solution.py:291
  48.5 5.4 %keep_kernel.1.kept = f32[4,104,1024]{2,1,0:T(8,128)S(1)} custom-call(s32[3]{0:T(128)S(1)} %pad_add_fusion.place, f32[32,8,128]{2,1,0:T(8,128)S(1)} %all-to-all-done.stats, bf16[2,448,1024]{2,1,0:T(8,128)(2,1)S(1)} %get-tuple-element.29.rows, f32[2,448,1]{2,1,0:T(8,128)S(1)} %get-tuple-element.30.norms, bf16[512,1024]{1,0:T(8,128)(2,1)S(1)} %copy-done.1, ...), custom_call_target="tpu_custom_call" | custom-call | flops 1 | bytes 1 | tf_op jit(solution)/shard_map/keep_kernel/pallas_call | solution.py:270
  53.9 2.2 %collective-permute-done.7.right = bf16[4,104,384]{2,1,0:T(8,128)(2,1)S(1)} collective-permute-done((bf16[4,104,384]{2,1,0:T(8,128)(2,1)S(1)}, bf16[4,104,384]{2,1,0:T(8,128)(2,1)S(1)}, u32[]{:S(2)}, u32[]{:S(2)}) %collective-permute-start.7) | collective-permute-done | bytes 319520 | tf_op jit(solution)/shard_map/ppermute | solution.py:291
  56.1 0.1 collective-permute-done.6.left
  56.1 0.2 merge.1
  56.3 33.8 %all_to_all.10.got = bf16[32,104,128]{2,1,0:T(8,128)(2,1)S(1)} all-to-all(bf16[32,104,128]{2,1,0:T(8,128)(2,1)S(1)} %merge.1), channel_id=1, replica_groups=mesh['x'=4,'zq'=4,'zp'=2,'y'=4,'core'=2] {'zq','y','core'}, dimensions={0} | all-to-all | bytes 1703936 | tf_op jit(solution)/shard_map/all_to_all | solution.py:301
  90.1 0.9 %final.1 = bf16[800,128]{1,0:T(8,128)(2,1)} custom-call(bf16[32,104,128]{2,1,0:T(8,128)(2,1)S(1)} %all_to_all.10.got), custom_call_target="tpu_custom_call" | custom-call | tf_op jit(solution)/shard_map/final/pallas_call | solution.py:302
  (10 shorter events, 0.0 us)
Async XLA Ops:
  0.1 1.2 %copy-start = (bf16[512,1024]{1,0:T(8,128)(2,1)S(1)}, bf16[512,1024]{1,0:T(8,128)(2,1)}, u32[]{:S(2)}) copy-start(bf16[512,1024]{1,0:T(8,128)(2,1)} %own.3) | copy-start | bytes 3145732
  2.7 31.6 %collective-permute-start.2 = (bf16[256,1024]{1,0:T(8,128)(2,1)}, bf16[256,1024]{1,0:T(8,128)(2,1)}, u32[]{:S(2)}, u32[]{:S(2)}) collective-permute-start(bf16[256,1024]{1,0:T(8,128)(2,1)} %cut.1.after), channel_id=1, source_target_pairs={{0,128},{64,192},{128,0},{192,64},{1,129},{65,193},{129,1},{193,65... | collective-permute-start | bytes 1572872 | tf_op jit(solution)/shard_map/ppermute | solution.py:242
  6.3 28.0 %collective-permute-start.1 = (bf16[256,1024]{1,0:T(8,128)(2,1)}, bf16[256,1024]{1,0:T(8,128)(2,1)}, u32[]{:S(2)}, u32[]{:S(2)}) collective-permute-start(bf16[256,1024]{1,0:T(8,128)(2,1)} %cut.1.after), channel_id=1, source_target_pairs={{0,192},{64,0},{128,64},{192,128},{1,193},{65,1},{129,65},{193,129... | collective-permute-start | bytes 1572872 | tf_op jit(solution)/shard_map/ppermute | solution.py:242
  7.1 27.2 %collective-permute-start = (bf16[256,1024]{1,0:T(8,128)(2,1)}, bf16[256,1024]{1,0:T(8,128)(2,1)}, u32[]{:S(2)}, u32[]{:S(2)}) collective-permute-start(bf16[256,1024]{1,0:T(8,128)(2,1)} %cut.1.after), channel_id=1, source_target_pairs={{0,64},{64,128},{128,192},{192,0},{1,65},{65,129},{129,193},{193,1... | collective-permute-start | bytes 1572872 | tf_op jit(solution)/shard_map/ppermute | solution.py:242
  16.2 18.0 %all-to-all-start = ((f32[32,8,128]{2,1,0:T(8,128)}), f32[32,8,128]{2,1,0:T(8,128)S(1)}, u32[]{:S(2)}, u32[]{:S(2)}) async-start(f32[32,8,128]{2,1,0:T(8,128)} %get-tuple-element.24), calls=%async_computation | async-start | bytes 262144 | tf_op jit(solution)/shard_map/all_to_all | solution.py:256
  24.2 0.7 copy-start.2
  24.8 10.5 %copy-start.1 = (bf16[512,1024]{1,0:T(8,128)(2,1)S(1)}, bf16[512,1024]{1,0:T(8,128)(2,1)}, u32[]{:S(2)}) copy-start(bf16[512,1024]{1,0:T(8,128)(2,1)} %own.3) | copy-start | bytes 3145732
  34.3 5.0 %collective-permute-start.3 = (bf16[256,1024]{1,0:T(8,128)(2,1)}, bf16[256,1024]{1,0:T(8,128)(2,1)S(1)}, u32[]{:S(2)}, u32[]{:S(2)}) collective-permute-start(bf16[256,1024]{1,0:T(8,128)(2,1)} %collective-permute-done.up), channel_id=1, source_target_pairs={{0,1},{1,0},{2,3},{3,2},{4,5},{5,4},{6,7},{7,6},{8,9},{9,8},{10,11... | collective-permute-start | bytes 1572872 | tf_op jit(solution)/shard_map/ppermute | solution.py:284
  34.8 4.5 %collective-permute-start.4 = (bf16[256,1024]{1,0:T(8,128)(2,1)}, bf16[256,1024]{1,0:T(8,128)(2,1)S(1)}, u32[]{:S(2)}, u32[]{:S(2)}) collective-permute-start(bf16[256,1024]{1,0:T(8,128)(2,1)} %collective-permute-done.1.down), channel_id=1, source_target_pairs={{0,1},{1,0},{2,3},{3,2},{4,5},{5,4},{6,7},{7,6},{8,9},{9,8},{10,11... | collective-permute-start | bytes 1572872 | tf_op jit(solution)/shard_map/ppermute | solution.py:284
  34.9 4.4 %collective-permute-start.5 = (bf16[256,1024]{1,0:T(8,128)(2,1)}, bf16[256,1024]{1,0:T(8,128)(2,1)S(1)}, u32[]{:S(2)}, u32[]{:S(2)}) collective-permute-start(bf16[256,1024]{1,0:T(8,128)(2,1)} %collective-permute-done.2.far), channel_id=1, source_target_pairs={{0,1},{1,0},{2,3},{3,2},{4,5},{5,4},{6,7},{7,6},{8,9},{9,8},{10,11... | collective-permute-start | bytes 1572872 | tf_op jit(solution)/shard_map/ppermute | solution.py:284
  42.1 14.1 %collective-permute-start.6 = (bf16[4,104,640]{2,1,0:T(8,128)(2,1)S(1)}, bf16[4,104,640]{2,1,0:T(8,128)(2,1)S(1)}, u32[]{:S(2)}, u32[]{:S(2)}) collective-permute-start(bf16[4,104,640]{2,1,0:T(8,128)(2,1)S(1)} %get-tuple-element.41), channel_id=1, source_target_pairs={{0,8},{8,0},{16,24},{24,16},{32,40},{40,32},{48,56},{56,48},{1,9},... | collective-permute-start | bytes 1597448 | tf_op jit(solution)/shard_map/ppermute | solution.py:290
  43.8 12.3 %collective-permute-start.7 = (bf16[4,104,384]{2,1,0:T(8,128)(2,1)S(1)}, bf16[4,104,384]{2,1,0:T(8,128)(2,1)S(1)}, u32[]{:S(2)}, u32[]{:S(2)}) collective-permute-start(bf16[4,104,384]{2,1,0:T(8,128)(2,1)S(1)} %get-tuple-element.42), channel_id=1, source_target_pairs={{0,56},{8,16},{16,8},{24,32},{32,24},{40,48},{48,40},{56,0},{1,57}... | collective-permute-start | bytes 958472 | tf_op jit(solution)/shard_map/ppermute | solution.py:291

commit v12 on v11

--- a/solution.py
+++ b/solution.py
@@ -20,7 +20,7 @@
 ANY = pl.BlockSpec(memory_space=pl.ANY)
 MIB = 2**20
 CHEAP = pl.CostEstimate(flops=1, bytes_accessed=1, transcendentals=0)
-TILE = 640
+CHUNKS = 5
 LEFT = 640
 SHIFTS = (1, NX - 1, 2)
 
@@ -33,40 +33,28 @@
     return pltpu.CompilerParams(vmem_limit_bytes=mib * MIB)
 
 
-def cut_kernel(place, points, half_out):
+def cut_kernel(place, points, cents, half_out):
     half = half_out.shape[0]
     half_out[...] = points[pl.ds(pl.multiple_of(place[0] * half, half), half)]
 
 
-def stats_kernel(points, cents, after, out, flag, top, total):
-    step = pl.program_id(0)
-
-    @pl.when(step == 0)
-    def _():
-        top[...] = jnp.full_like(top, -jnp.inf)
-        total[...] = jnp.zeros_like(total)
-
-    rows = cents[...]
-    chunk = rows.shape[0] // 2
+def stats_kernel(points, cents, after, out, flag):
+    chunk = cents.shape[0] // CHUNKS
     pts = points[...]
-    tops, totals = [top[...]], [total[...]]
-    for i in range(2):
-        part = rows[i * chunk : (i + 1) * chunk]
-        wide = part.astype(F32)
-        logits = dot_nt(part, pts) - 0.5 * jnp.sum(wide * wide, axis=1, keepdims=True)
-        high = jnp.max(logits, axis=0, keepdims=True)
-        tops.append(high)
-        totals.append(jnp.sum(jnp.exp(logits - high), axis=0, keepdims=True))
-    new = functools.reduce(jnp.maximum, tops)
-    top[...] = new
-    total[...] = sum(s * jnp.exp(t - new) for s, t in zip(totals, tops))
-
-    @pl.when(step == pl.num_programs(0) - 1)
-    def _():
-        groups = top.shape[1] // LANES
-        both = [r[:, g * LANES : (g + 1) * LANES] for r in (top[...], total[...]) for g in range(groups)]
-        out[...] = jnp.broadcast_to(jnp.concatenate(both, axis=0)[None], out.shape)
-        flag[...] = jnp.zeros_like(flag)
+    tops, totals = [], []
+    for i in range(CHUNKS):
+        rows = cents[i * chunk : (i + 1) * chunk]
+        wide = rows.astype(F32)
+        logits = dot_nt(rows, pts) - 0.5 * jnp.sum(wide * wide, axis=1, keepdims=True)
+        top = jnp.max(logits, axis=0, keepdims=True)
+        tops.append(top)
+        totals.append(jnp.sum(jnp.exp(logits - top), axis=0, keepdims=True))
+    top = functools.reduce(jnp.maximum, tops)
+    total = sum(s * jnp.exp(t - top) for s, t in zip(totals, tops))
+    groups = top.shape[1] // LANES
+    both = [r[:, g * LANES : (g + 1) * LANES] for r in (top, total) for g in range(groups)]
+    out[...] = jnp.broadcast_to(jnp.concatenate(both, axis=0)[None], out.shape)
+    flag[...] = jnp.zeros_like(flag)
 
 
 def window_kernel(place, table, after, mine, norms, sems):
@@ -233,23 +221,21 @@
     own_half = pl.pallas_call(
         cut_kernel,
         out_shape=shape((half, dim), BF),
-        in_specs=[SMEM, VMEM],
+        in_specs=[SMEM, VMEM, ANY],
         out_specs=VMEM,
-        compiler_params=params(4),
+        compiler_params=params(50),
         cost_estimate=CHEAP,
         name="cut",
-    )(place, points)
+    )(place, points, centroids)
     near = [lax.ppermute(own_half, "x", [(i, (i + k) % NX) for i in range(NX)]) for k in SHIFTS]
 
     stats_shape = (NX * N_CENT, 2 * pts // LANES, LANES)
     send_stats, flag = pl.pallas_call(
         stats_kernel,
-        grid=(rows // TILE,),
         out_shape=(shape(stats_shape, F32), shape((8, LANES), F32)),
-        in_specs=[pl.BlockSpec((pts, dim), lambda i: (0, 0)), pl.BlockSpec((TILE, dim), lambda i: (i, 0)), ANY],
-        out_specs=(pl.BlockSpec(stats_shape, lambda i: (0, 0, 0)), pl.BlockSpec((8, LANES), lambda i: (0, 0))),
-        scratch_shapes=[pltpu.VMEM((1, pts), F32), pltpu.VMEM((1, pts), F32)],
-        compiler_params=params(54),
+        in_specs=[VMEM, VMEM, ANY],
+        out_specs=(VMEM, VMEM),
+        compiler_params=params(16),
         cost_estimate=CHEAP,
         name="stats",
     )(points, centroids, own_half)

time: 91.4 us -> 91.2 us (level)
  waiting for transfers between devices: 9.12 us -> 12.4 us
  Pallas kernels: 25.6 us -> 23 us
    all_to_all x1, waiting for transfers between devices: 6.87 us -> 10.2 us  [body(): stats = lax.all_to_all(send_stats, ('x', *CENT), 0, 0)]
    pallas_call x1, Pallas kernels: 8.49 us -> 5.85 us  [body(): pl.pallas_call(stats_kernel, out_shape=(shape(stats_shape, F32), shape((8...]
  transfers between devices with their start and end apart: 9 -> 9, of which waited for: 3 -> 3; matrix products, arithmetic and copies ran while one was open for 0% -> 0% of each run, Pallas kernels for 22% -> 20%
where the time goes in v12:
time: 91.2 us; the launch traced here: 91 us
  blocking collectives  33.7 us (37%)
  Pallas kernels  23 us (25%)
  starting transfers between devices  20.4 us (22%)
  waiting for transfers between devices  12.4 us (14%)
  local copies, waits for them, and re-layouts  1.24 us (1%)
    all_to_all x1, blocking collectives, body(): got = lax.all_to_all(send, ('zq', *CENT), 0, 0)  33.7 us
    pallas_call x3, Pallas kernels, call(): pl.pallas_call(kernel, out_shape=out_shape, in_specs=[SMEM] + [VMEM] * (3...  12.1 us
    all_to_all x1, waiting for transfers between devices, body(): stats = lax.all_to_all(send_stats, ('x', *CENT), 0, 0)  10.2 us
    all_to_all x1, starting transfers between devices, body(): stats = lax.all_to_all(send_stats, ('x', *CENT), 0, 0)  7.93 us
    pallas_call x1, Pallas kernels, body(): pl.pallas_call(stats_kernel, out_shape=(shape(stats_shape, F32), shape((8...  5.85 us
    ppermute x3, starting transfers between devices, body(): lax.ppermute(own_half, 'x', [(i, (i + k) % NX) for i in range(NX)])  5.04 us
    ppermute x1, starting transfers between devices, body(): lax.ppermute(right, Z, [(i, (i + (1 if i % 2 else -1)) % NZ) for i in ran...  4.67 us
    pallas_call x1, Pallas kernels, body(): pl.pallas_call(window_kernel, out_shape=(shape((2, work, dim), BF), shape...  2.56 us
  transfers between devices with their start and end apart: 9, of which 3 were waited for; matrix products, arithmetic and copies ran while one was open for 0% of the time, Pallas kernels for 20%

profile of v12, /device:TPU:1, one launch (start us, length us, event | category | flops | bytes accessed | tf_op | source)
XLA Modules:
  0.0 91.0 jit_solution(10514402302012242639)
XLA Ops:
  0.0 0.1 pad_add_fusion.place
  0.1 1.2 %copy-done.1 = bf16[512,1024]{1,0:T(8,128)(2,1)S(1)} copy-done((bf16[512,1024]{1,0:T(8,128)(2,1)S(1)}, bf16[512,1024]{1,0:T(8,128)(2,1)}, u32[]{:S(2)}) %copy-start.1) | copy-done | bytes 1048600
  1.3 1.4 %cut.1.after = bf16[256,1024]{1,0:T(8,128)(2,1)} custom-call(s32[3]{0:T(128)S(1)} %pad_add_fusion.place, bf16[512,1024]{1,0:T(8,128)(2,1)S(1)} %copy-done.1, bf16[3200,1024]{1,0:T(8,128)(2,1)} %table.1), custom_call_target="tpu_custom_call" | custom-call | flops 1 | bytes 1 | tf_op jit(solution)/shard_map/cut/pallas_call | solution.py:221
  2.7 3.6 %collective-permute-start.2 = (bf16[256,1024]{1,0:T(8,128)(2,1)}, bf16[256,1024]{1,0:T(8,128)(2,1)}, u32[]{:S(2)}, u32[]{:S(2)}) collective-permute-start(bf16[256,1024]{1,0:T(8,128)(2,1)} %cut.1.after), channel_id=1, source_target_pairs={{0,128},{64,192},{128,0},{192,64},{1,129},{65,193},{129,1},{193,65... | collective-permute-start | bytes 1572872 | tf_op jit(solution)/shard_map/ppermute | solution.py:230
  6.3 0.9 collective-permute-start.1
  7.1 0.6 collective-permute-start
  7.7 5.9 %stats.1 = (f32[32,8,128]{2,1,0:T(8,128)}, f32[8,128]{1,0:T(8,128)S(1)}) custom-call(bf16[512,1024]{1,0:T(8,128)(2,1)S(1)} %copy-done.1, bf16[3200,1024]{1,0:T(8,128)(2,1)S(1)} %copy-done, bf16[256,1024]{1,0:T(8,128)(2,1)} %cut.1.after), custom_call_target="tpu_custom_call" | custom-call | flops 1 | bytes 1 | tf_op jit(solution)/shard_map/stats/pallas_call | solution.py:233
  13.6 7.9 %all-to-all-start = ((f32[32,8,128]{2,1,0:T(8,128)}), f32[32,8,128]{2,1,0:T(8,128)S(1)}, u32[]{:S(2)}, u32[]{:S(2)}) async-start(f32[32,8,128]{2,1,0:T(8,128)} %get-tuple-element.24), calls=%async_computation | async-start | bytes 262144 | tf_op jit(solution)/shard_map/all_to_all | solution.py:242
  21.5 0.0 copy-start.2
  21.5 2.6 %window.1 = (bf16[2,448,1024]{2,1,0:T(8,128)(2,1)S(1)}, f32[2,448,1]{2,1,0:T(8,128)S(1)}) custom-call(s32[3]{0:T(128)S(1)} %pad_add_fusion.place, bf16[3200,1024]{1,0:T(8,128)(2,1)} %table.1, f32[8,128]{1,0:T(8,128)S(1)} %get-tuple-element.25.after), custom_call_target="tpu_custom_call" | custom-call | flops 1 | bytes 1 | tf_op jit(solution)/shard_map/window/pallas_call | solution.py:244
  24.1 10.2 %all-to-all-done.stats = f32[32,8,128]{2,1,0:T(8,128)S(1)} async-done(((f32[32,8,128]{2,1,0:T(8,128)}), f32[32,8,128]{2,1,0:T(8,128)S(1)}, u32[]{:S(2)}, u32[]{:S(2)}) %all-to-all-start) | async-done | bytes 131104 | tf_op jit(solution)/shard_map/all_to_all | solution.py:242
  34.3 0.6 collective-permute-start.3
  34.8 0.1 collective-permute-start.4
  34.9 0.4 collective-permute-start.5
  35.3 4.0 %first_kernel.1 = (f32[448,1024]{1,0:T(8,128)S(1)}, f32[448,128]{1,0:T(8,128)S(1)}) custom-call(s32[3]{0:T(128)S(1)} %pad_add_fusion.place, f32[32,8,128]{2,1,0:T(8,128)S(1)} %all-to-all-done.stats, bf16[2,448,1024]{2,1,0:T(8,128)(2,1)S(1)} %get-tuple-element.29.rows, f32[2,448,1]{2,1,0:T(8,128)S(1)} %get-tuple-element.30.norms, ...), custom_call_target="tpu_custom_call" | custom-call | flops 1 | bytes 1 | tf_op jit(solution)/shard_map/first_kernel/pallas_call | solution.py:256
  39.3 2.7 %give_kernel.1 = (bf16[4,104,640]{2,1,0:T(8,128)(2,1)S(1)}, bf16[4,104,384]{2,1,0:T(8,128)(2,1)S(1)}) custom-call(s32[3]{0:T(128)S(1)} %pad_add_fusion.place, f32[32,8,128]{2,1,0:T(8,128)S(1)} %all-to-all-done.stats, bf16[2,448,1024]{2,1,0:T(8,128)(2,1)S(1)} %get-tuple-element.29.rows, f32[2,448,1]{2,1,0:T(8,128)S(1)} %get-tuple-element.30.norms, ...), custom_call_target="tpu_custom_call" | custom-call | flops 1 | bytes 1 | tf_op jit(solution)/shard_map/give_kernel/pallas_call | solution.py:256
  42.0 1.7 %collective-permute-start.6 = (bf16[4,104,640]{2,1,0:T(8,128)(2,1)S(1)}, bf16[4,104,640]{2,1,0:T(8,128)(2,1)S(1)}, u32[]{:S(2)}, u32[]{:S(2)}) collective-permute-start(bf16[4,104,640]{2,1,0:T(8,128)(2,1)S(1)} %get-tuple-element.41), channel_id=1, source_target_pairs={{0,8},{8,0},{16,24},{24,16},{32,40},{40,32},{48,56},{56,48},{1,9},... | collective-permute-start | bytes 1597448 | tf_op jit(solution)/shard_map/ppermute | solution.py:276
  43.8 4.7 %collective-permute-start.7 = (bf16[4,104,384]{2,1,0:T(8,128)(2,1)S(1)}, bf16[4,104,384]{2,1,0:T(8,128)(2,1)S(1)}, u32[]{:S(2)}, u32[]{:S(2)}) collective-permute-start(bf16[4,104,384]{2,1,0:T(8,128)(2,1)S(1)} %get-tuple-element.42), channel_id=1, source_target_pairs={{0,56},{8,16},{16,8},{24,32},{32,24},{40,48},{48,40},{56,0},{1,57}... | collective-permute-start | bytes 958472 | tf_op jit(solution)/shard_map/ppermute | solution.py:277
  48.5 5.4 %keep_kernel.1.kept = f32[4,104,1024]{2,1,0:T(8,128)S(1)} custom-call(s32[3]{0:T(128)S(1)} %pad_add_fusion.place, f32[32,8,128]{2,1,0:T(8,128)S(1)} %all-to-all-done.stats, bf16[2,448,1024]{2,1,0:T(8,128)(2,1)S(1)} %get-tuple-element.29.rows, f32[2,448,1]{2,1,0:T(8,128)S(1)} %get-tuple-element.30.norms, bf16[512,1024]{1,0:T(8,128)(2,1)S(1)} %copy-done.2, ...), custom_call_target="tpu_custom_call" | custom-call | flops 1 | bytes 1 | tf_op jit(solution)/shard_map/keep_kernel/pallas_call | solution.py:256
  53.9 2.2 %collective-permute-done.7.right = bf16[4,104,384]{2,1,0:T(8,128)(2,1)S(1)} collective-permute-done((bf16[4,104,384]{2,1,0:T(8,128)(2,1)S(1)}, bf16[4,104,384]{2,1,0:T(8,128)(2,1)S(1)}, u32[]{:S(2)}, u32[]{:S(2)}) %collective-permute-start.7) | collective-permute-done | bytes 319520 | tf_op jit(solution)/shard_map/ppermute | solution.py:277
  56.1 0.1 collective-permute-done.6.left
  56.1 0.2 merge.1
  56.3 33.7 %all_to_all.10.got = bf16[32,104,128]{2,1,0:T(8,128)(2,1)S(1)} all-to-all(bf16[32,104,128]{2,1,0:T(8,128)(2,1)S(1)} %merge.1), channel_id=1, replica_groups=mesh['x'=4,'zq'=4,'zp'=2,'y'=4,'core'=2] {'zq','y','core'}, dimensions={0} | all-to-all | bytes 1703936 | tf_op jit(solution)/shard_map/all_to_all | solution.py:287
  90.0 0.9 %final.1 = bf16[800,128]{1,0:T(8,128)(2,1)} custom-call(bf16[32,104,128]{2,1,0:T(8,128)(2,1)S(1)} %all_to_all.10.got), custom_call_target="tpu_custom_call" | custom-call | tf_op jit(solution)/shard_map/final/pallas_call | solution.py:288
  (10 shorter events, 0.0 us)
Async XLA Ops:
  0.1 1.2 %copy-start.1 = (bf16[512,1024]{1,0:T(8,128)(2,1)S(1)}, bf16[512,1024]{1,0:T(8,128)(2,1)}, u32[]{:S(2)}) copy-start(bf16[512,1024]{1,0:T(8,128)(2,1)} %own.3) | copy-start | bytes 3145732
  1.3 6.4 %copy-start = (bf16[3200,1024]{1,0:T(8,128)(2,1)S(1)}, bf16[3200,1024]{1,0:T(8,128)(2,1)}, u32[]{:S(2)}) copy-start(bf16[3200,1024]{1,0:T(8,128)(2,1)} %table.1) | copy-start | bytes 19660804
  2.7 31.6 %collective-permute-start.2 = (bf16[256,1024]{1,0:T(8,128)(2,1)}, bf16[256,1024]{1,0:T(8,128)(2,1)}, u32[]{:S(2)}, u32[]{:S(2)}) collective-permute-start(bf16[256,1024]{1,0:T(8,128)(2,1)} %cut.1.after), channel_id=1, source_target_pairs={{0,128},{64,192},{128,0},{192,64},{1,129},{65,193},{129,1},{193,65... | collective-permute-start | bytes 1572872 | tf_op jit(solution)/shard_map/ppermute | solution.py:230
  6.3 28.0 %collective-permute-start.1 = (bf16[256,1024]{1,0:T(8,128)(2,1)}, bf16[256,1024]{1,0:T(8,128)(2,1)}, u32[]{:S(2)}, u32[]{:S(2)}) collective-permute-start(bf16[256,1024]{1,0:T(8,128)(2,1)} %cut.1.after), channel_id=1, source_target_pairs={{0,192},{64,0},{128,64},{192,128},{1,193},{65,1},{129,65},{193,129... | collective-permute-start | bytes 1572872 | tf_op jit(solution)/shard_map/ppermute | solution.py:230
  7.1 27.2 %collective-permute-start = (bf16[256,1024]{1,0:T(8,128)(2,1)}, bf16[256,1024]{1,0:T(8,128)(2,1)}, u32[]{:S(2)}, u32[]{:S(2)}) collective-permute-start(bf16[256,1024]{1,0:T(8,128)(2,1)} %cut.1.after), channel_id=1, source_target_pairs={{0,64},{64,128},{128,192},{192,0},{1,65},{65,129},{129,193},{193,1... | collective-permute-start | bytes 1572872 | tf_op jit(solution)/shard_map/ppermute | solution.py:230
  13.6 20.7 %all-to-all-start = ((f32[32,8,128]{2,1,0:T(8,128)}), f32[32,8,128]{2,1,0:T(8,128)S(1)}, u32[]{:S(2)}, u32[]{:S(2)}) async-start(f32[32,8,128]{2,1,0:T(8,128)} %get-tuple-element.24), calls=%async_computation | async-start | bytes 262144 | tf_op jit(solution)/shard_map/all_to_all | solution.py:242
  21.5 13.8 %copy-start.2 = (bf16[512,1024]{1,0:T(8,128)(2,1)S(1)}, bf16[512,1024]{1,0:T(8,128)(2,1)}, u32[]{:S(2)}) copy-start(bf16[512,1024]{1,0:T(8,128)(2,1)} %own.3) | copy-start | bytes 3145732
  34.3 5.0 %collective-permute-start.3 = (bf16[256,1024]{1,0:T(8,128)(2,1)}, bf16[256,1024]{1,0:T(8,128)(2,1)S(1)}, u32[]{:S(2)}, u32[]{:S(2)}) collective-permute-start(bf16[256,1024]{1,0:T(8,128)(2,1)} %collective-permute-done.up), channel_id=1, source_target_pairs={{0,1},{1,0},{2,3},{3,2},{4,5},{5,4},{6,7},{7,6},{8,9},{9,8},{10,11... | collective-permute-start | bytes 1572872 | tf_op jit(solution)/shard_map/ppermute | solution.py:270
  34.8 4.5 %collective-permute-start.4 = (bf16[256,1024]{1,0:T(8,128)(2,1)}, bf16[256,1024]{1,0:T(8,128)(2,1)S(1)}, u32[]{:S(2)}, u32[]{:S(2)}) collective-permute-start(bf16[256,1024]{1,0:T(8,128)(2,1)} %collective-permute-done.1.down), channel_id=1, source_target_pairs={{0,1},{1,0},{2,3},{3,2},{4,5},{5,4},{6,7},{7,6},{8,9},{9,8},{10,11... | collective-permute-start | bytes 1572872 | tf_op jit(solution)/shard_map/ppermute | solution.py:270
  34.9 4.4 %collective-permute-start.5 = (bf16[256,1024]{1,0:T(8,128)(2,1)}, bf16[256,1024]{1,0:T(8,128)(2,1)S(1)}, u32[]{:S(2)}, u32[]{:S(2)}) collective-permute-start(bf16[256,1024]{1,0:T(8,128)(2,1)} %collective-permute-done.2.far), channel_id=1, source_target_pairs={{0,1},{1,0},{2,3},{3,2},{4,5},{5,4},{6,7},{7,6},{8,9},{9,8},{10,11... | collective-permute-start | bytes 1572872 | tf_op jit(solution)/shard_map/ppermute | solution.py:270
  42.0 14.1 %collective-permute-start.6 = (bf16[4,104,640]{2,1,0:T(8,128)(2,1)S(1)}, bf16[4,104,640]{2,1,0:T(8,128)(2,1)S(1)}, u32[]{:S(2)}, u32[]{:S(2)}) collective-permute-start(bf16[4,104,640]{2,1,0:T(8,128)(2,1)S(1)} %get-tuple-element.41), channel_id=1, source_target_pairs={{0,8},{8,0},{16,24},{24,16},{32,40},{40,32},{48,56},{56,48},{1,9},... | collective-permute-start | bytes 1597448 | tf_op jit(solution)/shard_map/ppermute | solution.py:276
  43.8 12.3 %collective-permute-start.7 = (bf16[4,104,384]{2,1,0:T(8,128)(2,1)S(1)}, bf16[4,104,384]{2,1,0:T(8,128)(2,1)S(1)}, u32[]{:S(2)}, u32[]{:S(2)}) collective-permute-start(bf16[4,104,384]{2,1,0:T(8,128)(2,1)S(1)} %get-tuple-element.42), channel_id=1, source_target_pairs={{0,56},{8,16},{16,8},{24,32},{32,24},{40,48},{48,40},{56,0},{1,57}... | collective-permute-start | bytes 958472 | tf_op jit(solution)/shard_map/ppermute | solution.py:277

commit v13 on v12

--- a/solution.py
+++ b/solution.py
@@ -33,9 +33,13 @@
     return pltpu.CompilerParams(vmem_limit_bytes=mib * MIB)
 
 
-def cut_kernel(place, points, cents, half_out):
-    half = half_out.shape[0]
-    half_out[...] = points[pl.ds(pl.multiple_of(place[0] * half, half), half)]
+def cut_kernel(place, points, cents, half_out, held, sems):
+    half = held.shape[0]
+    here = points.at[pl.ds(pl.multiple_of(place[0] * half, half), half)]
+    for i, (source, target) in enumerate(((here, held), (held, half_out))):
+        copy = pltpu.make_async_copy(source, target, sems.at[i])
+        copy.start()
+        copy.wait()
 
 
 def stats_kernel(points, cents, after, out, flag):
@@ -221,9 +225,10 @@
     own_half = pl.pallas_call(
         cut_kernel,
         out_shape=shape((half, dim), BF),
-        in_specs=[SMEM, VMEM, ANY],
-        out_specs=VMEM,
-        compiler_params=params(50),
+        in_specs=[SMEM, ANY, ANY],
+        out_specs=ANY,
+        scratch_shapes=[pltpu.VMEM((half, dim), BF), pltpu.SemaphoreType.DMA((2,))],
+        compiler_params=params(54),
         cost_estimate=CHEAP,
         name="cut",
     )(place, points, centroids)

time: 91.2 us -> 92.3 us (1.012)
  Pallas kernels: 23 us -> 24.4 us
    pallas_call x1, Pallas kernels: 1.37 us -> 2.98 us  [body(): pl.pallas_call(cut_kernel, out_shape=shape((half, dim), BF), in_specs=[SM...]
    all_to_all x1, waiting for transfers between devices: 10.2 us -> 9.24 us  [body(): stats = lax.all_to_all(send_stats, ('x', *CENT), 0, 0)]
  transfers between devices with their start and end apart: 9 -> 9, of which waited for: 3 -> 3; matrix products, arithmetic and copies ran while one was open for 0% -> 0% of each run, Pallas kernels for 20% -> 19%
where the time goes in v13:
time: 92.3 us; the launch traced here: 92 us
  blocking collectives  33.7 us (37%)
  Pallas kernels  24.4 us (26%)
  starting transfers between devices  20.5 us (22%)
  waiting for transfers between devices  11.5 us (12%)
  local copies, waits for them, and re-layouts  1.08 us (1%)
    all_to_all x1, blocking collectives, body(): got = lax.all_to_all(send, ('zq', *CENT), 0, 0)  33.7 us
    pallas_call x3, Pallas kernels, call(): pl.pallas_call(kernel, out_shape=out_shape, in_specs=[SMEM] + [VMEM] * (3...  12 us
    all_to_all x1, waiting for transfers between devices, body(): stats = lax.all_to_all(send_stats, ('x', *CENT), 0, 0)  9.24 us
    all_to_all x1, starting transfers between devices, body(): stats = lax.all_to_all(send_stats, ('x', *CENT), 0, 0)  7.93 us
    pallas_call x1, Pallas kernels, body(): pl.pallas_call(stats_kernel, out_shape=(shape(stats_shape, F32), shape((8...  5.71 us
    ppermute x3, starting transfers between devices, body(): lax.ppermute(own_half, 'x', [(i, (i + k) % NX) for i in range(NX)])  5.13 us
    ppermute x1, starting transfers between devices, body(): lax.ppermute(right, Z, [(i, (i + (1 if i % 2 else -1)) % NZ) for i in ran...  4.67 us
    pallas_call x1, Pallas kernels, body(): pl.pallas_call(cut_kernel, out_shape=shape((half, dim), BF), in_specs=[SM...  2.98 us
  transfers between devices with their start and end apart: 9, of which 3 were waited for; matrix products, arithmetic and copies ran while one was open for 0% of the time, Pallas kernels for 19%

profile of v13, /device:TPU:1, one launch (start us, length us, event | category | flops | bytes accessed | tf_op | source)
XLA Modules:
  0.0 92.0 jit_solution(4727886610042351815)
XLA Ops:
  0.0 0.7 pad_add_fusion.place
  0.7 3.0 %cut.1.after = bf16[256,1024]{1,0:T(8,128)(2,1)} custom-call(s32[3]{0:T(128)} %pad_add_fusion.place, bf16[512,1024]{1,0:T(8,128)(2,1)} %own.3, bf16[3200,1024]{1,0:T(8,128)(2,1)} %table.1), custom_call_target="tpu_custom_call" | custom-call | flops 1 | bytes 1 | tf_op jit(solution)/shard_map/cut/pallas_call | solution.py:225
  3.7 3.7 %collective-permute-start.2 = (bf16[256,1024]{1,0:T(8,128)(2,1)}, bf16[256,1024]{1,0:T(8,128)(2,1)}, u32[]{:S(2)}, u32[]{:S(2)}) collective-permute-start(bf16[256,1024]{1,0:T(8,128)(2,1)} %cut.1.after), channel_id=1, source_target_pairs={{0,128},{64,192},{128,0},{192,64},{1,129},{65,193},{129,1},{193,65... | collective-permute-start | bytes 1572872 | tf_op jit(solution)/shard_map/ppermute | solution.py:235
  7.3 0.9 collective-permute-start.1
  8.2 0.6 collective-permute-start
  8.8 1.1 %copy-done.2 = bf16[256,1024]{1,0:T(8,128)(2,1)S(1)} copy-done((bf16[256,1024]{1,0:T(8,128)(2,1)S(1)}, bf16[256,1024]{1,0:T(8,128)(2,1)}, u32[]{:S(2)}) %copy-start.2) | copy-done | bytes 524312
  9.9 5.7 %stats.1 = (f32[32,8,128]{2,1,0:T(8,128)}, f32[8,128]{1,0:T(8,128)S(1)}) custom-call(bf16[512,1024]{1,0:T(8,128)(2,1)S(1)} %copy-done.1, bf16[3200,1024]{1,0:T(8,128)(2,1)S(1)} %copy-done, bf16[256,1024]{1,0:T(8,128)(2,1)S(1)} %copy-done.2), custom_call_target="tpu_custom_call" | custom-call | flops 1 | bytes 1 | tf_op jit(solution)/shard_map/stats/pallas_call | solution.py:238
  15.6 7.9 %all-to-all-start = ((f32[32,8,128]{2,1,0:T(8,128)}), f32[32,8,128]{2,1,0:T(8,128)S(1)}, u32[]{:S(2)}, u32[]{:S(2)}) async-start(f32[32,8,128]{2,1,0:T(8,128)} %get-tuple-element.24), calls=%async_computation | async-start | bytes 262144 | tf_op jit(solution)/shard_map/all_to_all | solution.py:247
  23.5 2.6 %window.1 = (bf16[2,448,1024]{2,1,0:T(8,128)(2,1)S(1)}, f32[2,448,1]{2,1,0:T(8,128)S(1)}) custom-call(s32[3]{0:T(128)S(1)} %copy-done.3, bf16[3200,1024]{1,0:T(8,128)(2,1)} %table.1, f32[8,128]{1,0:T(8,128)S(1)} %get-tuple-element.25.after), custom_call_target="tpu_custom_call" | custom-call | flops 1 | bytes 1 | tf_op jit(solution)/shard_map/window/pallas_call | solution.py:249
  26.1 9.2 %all-to-all-done.stats = f32[32,8,128]{2,1,0:T(8,128)S(1)} async-done(((f32[32,8,128]{2,1,0:T(8,128)}), f32[32,8,128]{2,1,0:T(8,128)S(1)}, u32[]{:S(2)}, u32[]{:S(2)}) %all-to-all-start) | async-done | bytes 131104 | tf_op jit(solution)/shard_map/all_to_all | solution.py:247
  35.3 0.0 collective-permute-done.2.far
  35.3 0.6 collective-permute-start.3
  35.9 0.1 collective-permute-start.4
  36.0 0.4 collective-permute-start.5
  36.4 4.0 %first_kernel.1 = (f32[448,1024]{1,0:T(8,128)S(1)}, f32[448,128]{1,0:T(8,128)S(1)}) custom-call(s32[3]{0:T(128)S(1)} %copy-done.3, f32[32,8,128]{2,1,0:T(8,128)S(1)} %all-to-all-done.stats, bf16[2,448,1024]{2,1,0:T(8,128)(2,1)S(1)} %get-tuple-element.29.rows, f32[2,448,1]{2,1,0:T(8,128)S(1)} %get-tuple-element.30.norms, bf16[512,1024]{1,0:T(8,128)(2,1)S(1)} %copy-done.1, ...), custom_call_target="tpu_custom_call" | custom-call | flops 1 | bytes 1 | tf_op jit(solution)/shard_map/first_kernel/pallas_call | solution.py:261
  40.4 2.7 %give_kernel.1 = (bf16[4,104,640]{2,1,0:T(8,128)(2,1)S(1)}, bf16[4,104,384]{2,1,0:T(8,128)(2,1)S(1)}) custom-call(s32[3]{0:T(128)S(1)} %copy-done.3, f32[32,8,128]{2,1,0:T(8,128)S(1)} %all-to-all-done.stats, bf16[2,448,1024]{2,1,0:T(8,128)(2,1)S(1)} %get-tuple-element.29.rows, f32[2,448,1]{2,1,0:T(8,128)S(1)} %get-tuple-element.30.norms, ...), custom_call_target="tpu_custom_call" | custom-call | flops 1 | bytes 1 | tf_op jit(solution)/shard_map/give_kernel/pallas_call | solution.py:261
  43.1 1.7 %collective-permute-start.6 = (bf16[4,104,640]{2,1,0:T(8,128)(2,1)S(1)}, bf16[4,104,640]{2,1,0:T(8,128)(2,1)S(1)}, u32[]{:S(2)}, u32[]{:S(2)}) collective-permute-start(bf16[4,104,640]{2,1,0:T(8,128)(2,1)S(1)} %get-tuple-element.41), channel_id=1, source_target_pairs={{0,8},{8,0},{16,24},{24,16},{32,40},{40,32},{48,56},{56,48},{1,9},... | collective-permute-start | bytes 1597448 | tf_op jit(solution)/shard_map/ppermute | solution.py:281
  44.8 4.7 %collective-permute-start.7 = (bf16[4,104,384]{2,1,0:T(8,128)(2,1)S(1)}, bf16[4,104,384]{2,1,0:T(8,128)(2,1)S(1)}, u32[]{:S(2)}, u32[]{:S(2)}) collective-permute-start(bf16[4,104,384]{2,1,0:T(8,128)(2,1)S(1)} %get-tuple-element.42), channel_id=1, source_target_pairs={{0,56},{8,16},{16,8},{24,32},{32,24},{40,48},{48,40},{56,0},{1,57}... | collective-permute-start | bytes 958472 | tf_op jit(solution)/shard_map/ppermute | solution.py:282
  49.5 5.4 %keep_kernel.1.kept = f32[4,104,1024]{2,1,0:T(8,128)S(1)} custom-call(s32[3]{0:T(128)S(1)} %copy-done.3, f32[32,8,128]{2,1,0:T(8,128)S(1)} %all-to-all-done.stats, bf16[2,448,1024]{2,1,0:T(8,128)(2,1)S(1)} %get-tuple-element.29.rows, f32[2,448,1]{2,1,0:T(8,128)S(1)} %get-tuple-element.30.norms, bf16[512,1024]{1,0:T(8,128)(2,1)S(1)} %copy-done.1, ...), custom_call_target="tpu_custom_call" | custom-call | flops 1 | bytes 1 | tf_op jit(solution)/shard_map/keep_kernel/pallas_call | solution.py:261
  54.9 2.2 %collective-permute-done.7.right = bf16[4,104,384]{2,1,0:T(8,128)(2,1)S(1)} collective-permute-done((bf16[4,104,384]{2,1,0:T(8,128)(2,1)S(1)}, bf16[4,104,384]{2,1,0:T(8,128)(2,1)S(1)}, u32[]{:S(2)}, u32[]{:S(2)}) %collective-permute-start.7) | collective-permute-done | bytes 319520 | tf_op jit(solution)/shard_map/ppermute | solution.py:282
  57.1 0.1 collective-permute-done.6.left
  57.2 0.2 merge.1
  57.4 33.7 %all_to_all.10.got = bf16[32,104,128]{2,1,0:T(8,128)(2,1)S(1)} all-to-all(bf16[32,104,128]{2,1,0:T(8,128)(2,1)S(1)} %merge.1), channel_id=1, replica_groups=mesh['x'=4,'zq'=4,'zp'=2,'y'=4,'core'=2] {'zq','y','core'}, dimensions={0} | all-to-all | bytes 1703936 | tf_op jit(solution)/shard_map/all_to_all | solution.py:292
  91.1 0.9 %final.1 = bf16[800,128]{1,0:T(8,128)(2,1)} custom-call(bf16[32,104,128]{2,1,0:T(8,128)(2,1)S(1)} %all_to_all.10.got), custom_call_target="tpu_custom_call" | custom-call | tf_op jit(solution)/shard_map/final/pallas_call | solution.py:293
  (12 shorter events, 0.0 us)
Async XLA Ops:
  0.7 8.1 %copy-start = (bf16[3200,1024]{1,0:T(8,128)(2,1)S(1)}, bf16[3200,1024]{1,0:T(8,128)(2,1)}, u32[]{:S(2)}) copy-start(bf16[3200,1024]{1,0:T(8,128)(2,1)} %table.1) | copy-start | bytes 19660804
  0.7 8.1 %copy-start.1 = (bf16[512,1024]{1,0:T(8,128)(2,1)S(1)}, bf16[512,1024]{1,0:T(8,128)(2,1)}, u32[]{:S(2)}) copy-start(bf16[512,1024]{1,0:T(8,128)(2,1)} %own.3) | copy-start | bytes 3145732
  0.7 22.8 %copy-start.3 = (s32[3]{0:T(128)S(1)}, s32[3]{0:T(128)}, u32[]{:S(2)}) copy-start(s32[3]{0:T(128)} %pad_add_fusion.place) | copy-start | bytes 40
  3.7 31.7 %collective-permute-start.2 = (bf16[256,1024]{1,0:T(8,128)(2,1)}, bf16[256,1024]{1,0:T(8,128)(2,1)}, u32[]{:S(2)}, u32[]{:S(2)}) collective-permute-start(bf16[256,1024]{1,0:T(8,128)(2,1)} %cut.1.after), channel_id=1, source_target_pairs={{0,128},{64,192},{128,0},{192,64},{1,129},{65,193},{129,1},{193,65... | collective-permute-start | bytes 1572872 | tf_op jit(solution)/shard_map/ppermute | solution.py:235
  7.3 28.0 %collective-permute-start.1 = (bf16[256,1024]{1,0:T(8,128)(2,1)}, bf16[256,1024]{1,0:T(8,128)(2,1)}, u32[]{:S(2)}, u32[]{:S(2)}) collective-permute-start(bf16[256,1024]{1,0:T(8,128)(2,1)} %cut.1.after), channel_id=1, source_target_pairs={{0,192},{64,0},{128,64},{192,128},{1,193},{65,1},{129,65},{193,129... | collective-permute-start | bytes 1572872 | tf_op jit(solution)/shard_map/ppermute | solution.py:235
  8.2 27.2 %collective-permute-start = (bf16[256,1024]{1,0:T(8,128)(2,1)}, bf16[256,1024]{1,0:T(8,128)(2,1)}, u32[]{:S(2)}, u32[]{:S(2)}) collective-permute-start(bf16[256,1024]{1,0:T(8,128)(2,1)} %cut.1.after), channel_id=1, source_target_pairs={{0,64},{64,128},{128,192},{192,0},{1,65},{65,129},{129,193},{193,1... | collective-permute-start | bytes 1572872 | tf_op jit(solution)/shard_map/ppermute | solution.py:235
  8.8 1.1 %copy-start.2 = (bf16[256,1024]{1,0:T(8,128)(2,1)S(1)}, bf16[256,1024]{1,0:T(8,128)(2,1)}, u32[]{:S(2)}) copy-start(bf16[256,1024]{1,0:T(8,128)(2,1)} %cut.1.after) | copy-start | bytes 1572868
  15.6 19.8 %all-to-all-start = ((f32[32,8,128]{2,1,0:T(8,128)}), f32[32,8,128]{2,1,0:T(8,128)S(1)}, u32[]{:S(2)}, u32[]{:S(2)}) async-start(f32[32,8,128]{2,1,0:T(8,128)} %get-tuple-element.24), calls=%async_computation | async-start | bytes 262144 | tf_op jit(solution)/shard_map/all_to_all | solution.py:247
  35.3 5.0 %collective-permute-start.3 = (bf16[256,1024]{1,0:T(8,128)(2,1)}, bf16[256,1024]{1,0:T(8,128)(2,1)S(1)}, u32[]{:S(2)}, u32[]{:S(2)}) collective-permute-start(bf16[256,1024]{1,0:T(8,128)(2,1)} %collective-permute-done.up), channel_id=1, source_target_pairs={{0,1},{1,0},{2,3},{3,2},{4,5},{5,4},{6,7},{7,6},{8,9},{9,8},{10,11... | collective-permute-start | bytes 1572872 | tf_op jit(solution)/shard_map/ppermute | solution.py:275
  35.9 4.5 %collective-permute-start.4 = (bf16[256,1024]{1,0:T(8,128)(2,1)}, bf16[256,1024]{1,0:T(8,128)(2,1)S(1)}, u32[]{:S(2)}, u32[]{:S(2)}) collective-permute-start(bf16[256,1024]{1,0:T(8,128)(2,1)} %collective-permute-done.1.down), channel_id=1, source_target_pairs={{0,1},{1,0},{2,3},{3,2},{4,5},{5,4},{6,7},{7,6},{8,9},{9,8},{10,11... | collective-permute-start | bytes 1572872 | tf_op jit(solution)/shard_map/ppermute | solution.py:275
  36.0 4.4 %collective-permute-start.5 = (bf16[256,1024]{1,0:T(8,128)(2,1)}, bf16[256,1024]{1,0:T(8,128)(2,1)S(1)}, u32[]{:S(2)}, u32[]{:S(2)}) collective-permute-start(bf16[256,1024]{1,0:T(8,128)(2,1)} %collective-permute-done.2.far), channel_id=1, source_target_pairs={{0,1},{1,0},{2,3},{3,2},{4,5},{5,4},{6,7},{7,6},{8,9},{9,8},{10,11... | collective-permute-start | bytes 1572872 | tf_op jit(solution)/shard_map/ppermute | solution.py:275
  43.1 14.1 %collective-permute-start.6 = (bf16[4,104,640]{2,1,0:T(8,128)(2,1)S(1)}, bf16[4,104,640]{2,1,0:T(8,128)(2,1)S(1)}, u32[]{:S(2)}, u32[]{:S(2)}) collective-permute-start(bf16[4,104,640]{2,1,0:T(8,128)(2,1)S(1)} %get-tuple-element.41), channel_id=1, source_target_pairs={{0,8},{8,0},{16,24},{24,16},{32,40},{40,32},{48,56},{56,48},{1,9},... | collective-permute-start | bytes 1597448 | tf_op jit(solution)/shard_map/ppermute | solution.py:281
  44.8 12.3 %collective-permute-start.7 = (bf16[4,104,384]{2,1,0:T(8,128)(2,1)S(1)}, bf16[4,104,384]{2,1,0:T(8,128)(2,1)S(1)}, u32[]{:S(2)}, u32[]{:S(2)}) collective-permute-start(bf16[4,104,384]{2,1,0:T(8,128)(2,1)S(1)} %get-tuple-element.42), channel_id=1, source_target_pairs={{0,56},{8,16},{16,8},{24,32},{32,24},{40,48},{48,40},{56,0},{1,57}... | collective-permute-start | bytes 958472 | tf_op jit(solution)/shard_map/ppermute | solution.py:282

commit v14 on v12

--- a/solution.py
+++ b/solution.py
@@ -148,9 +148,30 @@
     return [(ref, lse_halves(place, stats, k)[which]) for k, ref in zip(SHIFTS, refs)]
 
 
-def first_kernel(place, stats, rows, norms, own, up, down, far, numer, counts, held):
-    pieces = [(own, lse_of(stats, place[2]))] + half_pieces(place, stats, (up, down, far), 0)
-    weighted(pieces, rows, norms, 1 - place[1], held, numer, counts)
+def first_kernel(place, stats, rows, norms, own, up, down, far, numer, counts, held, sems):
+    refs = (own, up, down, far)
+    parts = [lse_of(stats, place[2])] + [lse_halves(place, stats, k)[0] for k in SHIFTS]
+    copies, spans, at = [], [], 0
+    for i, ref in enumerate(refs):
+        n = ref.shape[0]
+        copies.append(pltpu.make_async_copy(ref, held.at[pl.ds(at, n)], sems.at[i]))
+        spans.append((at, n))
+        at += n
+    for copy in copies:
+        copy.start()
+    q = 1 - place[1]
+    mine, shift = rows[q], norms[q]
+    some = jnp.zeros(counts.shape, F32)
+    weights = []
+    for copy, (at, n), part in zip(copies, spans, parts):
+        copy.wait()
+        logits = dot_nt(mine, held[at : at + n])
+        for g in range(n // LANES):
+            w = jnp.exp(logits[:, g * LANES : (g + 1) * LANES] - shift - part[g : g + 1]).astype(BF)
+            some += w.astype(F32)
+            weights.append(w)
+    numer[...] = jnp.dot(jnp.concatenate(weights, axis=1), held[...], preferred_element_type=F32)
+    counts[...] = some
 
 
 def give_kernel(place, stats, rows, norms, up, down, far, numer_in, counts_in, left, right, held, numer, counts):
@@ -252,11 +273,11 @@
         name="window",
     )(place, centroids, flag)
 
-    def call(kernel, out_shape, n_points, *args, scratch=()):
+    def call(kernel, out_shape, n_points, *args, scratch=(), place_of=VMEM):
         return pl.pallas_call(
             kernel,
             out_shape=out_shape,
-            in_specs=[SMEM] + [VMEM] * (3 + len(args)),
+            in_specs=[SMEM] + [VMEM] * 3 + [place_of] * len(args),
             out_specs=jax.tree.map(lambda _: VMEM, out_shape),
             scratch_shapes=[pltpu.VMEM((n_points, dim), BF), *scratch],
             compiler_params=params(28),
@@ -268,7 +289,8 @@
     spare = [pltpu.VMEM(s.shape, F32) for s in sums]
     near, stats, mine, norms = lax.optimization_barrier((near, stats, mine, norms))
     others = [lax.ppermute(a, "core", [(0, 1), (1, 0)]) for a in near]
-    numer = call(first_kernel, sums, pts + 3 * half, points, *near)
+    waits = [pltpu.SemaphoreType.DMA((1 + len(near),))]
+    numer = call(first_kernel, sums, pts + 3 * half, points, *near, scratch=waits, place_of=ANY)
     others, numer = lax.optimization_barrier((others, numer))
     parts = tuple(shape((n_blocks, height, width), BF) for width in (LEFT, dim - LEFT))
     left, right = call(give_kernel, parts, 3 * half, *others, *numer, scratch=spare)

time: 91.2 us -> 92 us (level)
    pallas_call x3, Pallas kernels: 12.1 us -> 13.1 us  [call(): pl.pallas_call(kernel, out_shape=out_shape, in_specs=[SMEM] + [VMEM] * 3...]
where the time goes in v14:
time: 92 us; the launch traced here: 91.7 us
  blocking collectives  33.5 us (36%)
  Pallas kernels  23.9 us (26%)
  starting transfers between devices  20.4 us (22%)
  waiting for transfers between devices  12.4 us (13%)
  local copies, waits for them, and re-layouts  1.24 us (1%)
    all_to_all x1, blocking collectives, body(): got = lax.all_to_all(send, ('zq', *CENT), 0, 0)  33.5 us
    pallas_call x3, Pallas kernels, call(): pl.pallas_call(kernel, out_shape=out_shape, in_specs=[SMEM] + [VMEM] * 3...  13.1 us
    all_to_all x1, waiting for transfers between devices, body(): stats = lax.all_to_all(send_stats, ('x', *CENT), 0, 0)  10.2 us
    all_to_all x1, starting transfers between devices, body(): stats = lax.all_to_all(send_stats, ('x', *CENT), 0, 0)  7.93 us
    pallas_call x1, Pallas kernels, body(): pl.pallas_call(stats_kernel, out_shape=(shape(stats_shape, F32), shape((8...  5.85 us
    ppermute x3, starting transfers between devices, body(): lax.ppermute(own_half, 'x', [(i, (i + k) % NX) for i in range(NX)])  5.04 us
    ppermute x1, starting transfers between devices, body(): lax.ppermute(right, Z, [(i, (i + (1 if i % 2 else -1)) % NZ) for i in ran...  4.67 us
    pallas_call x1, Pallas kernels, body(): pl.pallas_call(window_kernel, out_shape=(shape((2, work, dim), BF), shape...  2.56 us
  transfers between devices with their start and end apart: 9, of which 3 were waited for; matrix products, arithmetic and copies ran while one was open for 0% of the time, Pallas kernels for 20%

profile of v14, /device:TPU:1, one launch (start us, length us, event | category | flops | bytes accessed | tf_op | source)
XLA Modules:
  0.0 91.7 jit_solution(3527899797087933744)
XLA Ops:
  0.0 0.1 pad_add_fusion.place
  0.1 1.2 %copy-done.1 = bf16[512,1024]{1,0:T(8,128)(2,1)S(1)} copy-done((bf16[512,1024]{1,0:T(8,128)(2,1)S(1)}, bf16[512,1024]{1,0:T(8,128)(2,1)}, u32[]{:S(2)}) %copy-start.1) | copy-done | bytes 1048600
  1.3 1.4 %cut.1.after = bf16[256,1024]{1,0:T(8,128)(2,1)} custom-call(s32[3]{0:T(128)S(1)} %pad_add_fusion.place, bf16[512,1024]{1,0:T(8,128)(2,1)S(1)} %copy-done.1, bf16[3200,1024]{1,0:T(8,128)(2,1)} %table.1), custom_call_target="tpu_custom_call" | custom-call | flops 1 | bytes 1 | tf_op jit(solution)/shard_map/cut/pallas_call | solution.py:242
  2.7 3.6 %collective-permute-start.2 = (bf16[256,1024]{1,0:T(8,128)(2,1)}, bf16[256,1024]{1,0:T(8,128)(2,1)}, u32[]{:S(2)}, u32[]{:S(2)}) collective-permute-start(bf16[256,1024]{1,0:T(8,128)(2,1)} %cut.1.after), channel_id=1, source_target_pairs={{0,128},{64,192},{128,0},{192,64},{1,129},{65,193},{129,1},{193,65... | collective-permute-start | bytes 1572872 | tf_op jit(solution)/shard_map/ppermute | solution.py:251
  6.3 0.9 collective-permute-start.1
  7.1 0.6 collective-permute-start
  7.7 5.9 %stats.1 = (f32[32,8,128]{2,1,0:T(8,128)}, f32[8,128]{1,0:T(8,128)S(1)}) custom-call(bf16[512,1024]{1,0:T(8,128)(2,1)S(1)} %copy-done.1, bf16[3200,1024]{1,0:T(8,128)(2,1)S(1)} %copy-done, bf16[256,1024]{1,0:T(8,128)(2,1)} %cut.1.after), custom_call_target="tpu_custom_call" | custom-call | flops 1 | bytes 1 | tf_op jit(solution)/shard_map/stats/pallas_call | solution.py:254
  13.6 7.9 %all-to-all-start = ((f32[32,8,128]{2,1,0:T(8,128)}), f32[32,8,128]{2,1,0:T(8,128)S(1)}, u32[]{:S(2)}, u32[]{:S(2)}) async-start(f32[32,8,128]{2,1,0:T(8,128)} %get-tuple-element.24), calls=%async_computation | async-start | bytes 262144 | tf_op jit(solution)/shard_map/all_to_all | solution.py:263
  21.5 0.0 copy-start.2
  21.5 2.6 %window.1 = (bf16[2,448,1024]{2,1,0:T(8,128)(2,1)S(1)}, f32[2,448,1]{2,1,0:T(8,128)S(1)}) custom-call(s32[3]{0:T(128)S(1)} %pad_add_fusion.place, bf16[3200,1024]{1,0:T(8,128)(2,1)} %table.1, f32[8,128]{1,0:T(8,128)S(1)} %get-tuple-element.25.after), custom_call_target="tpu_custom_call" | custom-call | flops 1 | bytes 1 | tf_op jit(solution)/shard_map/window/pallas_call | solution.py:265
  24.1 10.2 %all-to-all-done.stats = f32[32,8,128]{2,1,0:T(8,128)S(1)} async-done(((f32[32,8,128]{2,1,0:T(8,128)}), f32[32,8,128]{2,1,0:T(8,128)S(1)}, u32[]{:S(2)}, u32[]{:S(2)}) %all-to-all-start) | async-done | bytes 131104 | tf_op jit(solution)/shard_map/all_to_all | solution.py:263
  34.3 0.6 collective-permute-start.3
  34.8 0.1 collective-permute-start.4
  34.9 0.4 collective-permute-start.5
  35.3 5.0 %first_kernel.1 = (f32[448,1024]{1,0:T(8,128)S(1)}, f32[448,128]{1,0:T(8,128)S(1)}) custom-call(s32[3]{0:T(128)S(1)} %pad_add_fusion.place, f32[32,8,128]{2,1,0:T(8,128)S(1)} %all-to-all-done.stats, bf16[2,448,1024]{2,1,0:T(8,128)(2,1)S(1)} %get-tuple-element.29.rows, f32[2,448,1]{2,1,0:T(8,128)S(1)} %get-tuple-element.30.norms, ...), custom_call_target="tpu_custom_call" | custom-call | flops 1 | bytes 1 | tf_op jit(solution)/shard_map/first_kernel/pallas_call | solution.py:277
  40.3 2.7 %give_kernel.1 = (bf16[4,104,640]{2,1,0:T(8,128)(2,1)S(1)}, bf16[4,104,384]{2,1,0:T(8,128)(2,1)S(1)}) custom-call(s32[3]{0:T(128)S(1)} %pad_add_fusion.place, f32[32,8,128]{2,1,0:T(8,128)S(1)} %all-to-all-done.stats, bf16[2,448,1024]{2,1,0:T(8,128)(2,1)S(1)} %get-tuple-element.29.rows, f32[2,448,1]{2,1,0:T(8,128)S(1)} %get-tuple-element.30.norms, ...), custom_call_target="tpu_custom_call" | custom-call | flops 1 | bytes 1 | tf_op jit(solution)/shard_map/give_kernel/pallas_call | solution.py:277
  43.0 1.7 %collective-permute-start.6 = (bf16[4,104,640]{2,1,0:T(8,128)(2,1)S(1)}, bf16[4,104,640]{2,1,0:T(8,128)(2,1)S(1)}, u32[]{:S(2)}, u32[]{:S(2)}) collective-permute-start(bf16[4,104,640]{2,1,0:T(8,128)(2,1)S(1)} %get-tuple-element.41), channel_id=1, source_target_pairs={{0,8},{8,0},{16,24},{24,16},{32,40},{40,32},{48,56},{56,48},{1,9},... | collective-permute-start | bytes 1597448 | tf_op jit(solution)/shard_map/ppermute | solution.py:298
  44.8 4.7 %collective-permute-start.7 = (bf16[4,104,384]{2,1,0:T(8,128)(2,1)S(1)}, bf16[4,104,384]{2,1,0:T(8,128)(2,1)S(1)}, u32[]{:S(2)}, u32[]{:S(2)}) collective-permute-start(bf16[4,104,384]{2,1,0:T(8,128)(2,1)S(1)} %get-tuple-element.42), channel_id=1, source_target_pairs={{0,56},{8,16},{16,8},{24,32},{32,24},{40,48},{48,40},{56,0},{1,57}... | collective-permute-start | bytes 958472 | tf_op jit(solution)/shard_map/ppermute | solution.py:299
  49.4 5.4 %keep_kernel.1.kept = f32[4,104,1024]{2,1,0:T(8,128)S(1)} custom-call(s32[3]{0:T(128)S(1)} %pad_add_fusion.place, f32[32,8,128]{2,1,0:T(8,128)S(1)} %all-to-all-done.stats, bf16[2,448,1024]{2,1,0:T(8,128)(2,1)S(1)} %get-tuple-element.29.rows, f32[2,448,1]{2,1,0:T(8,128)S(1)} %get-tuple-element.30.norms, bf16[512,1024]{1,0:T(8,128)(2,1)S(1)} %copy-done.2, ...), custom_call_target="tpu_custom_call" | custom-call | flops 1 | bytes 1 | tf_op jit(solution)/shard_map/keep_kernel/pallas_call | solution.py:277
  54.9 2.2 %collective-permute-done.7.right = bf16[4,104,384]{2,1,0:T(8,128)(2,1)S(1)} collective-permute-done((bf16[4,104,384]{2,1,0:T(8,128)(2,1)S(1)}, bf16[4,104,384]{2,1,0:T(8,128)(2,1)S(1)}, u32[]{:S(2)}, u32[]{:S(2)}) %collective-permute-start.7) | collective-permute-done | bytes 319520 | tf_op jit(solution)/shard_map/ppermute | solution.py:299
  57.1 0.1 collective-permute-done.6.left
  57.1 0.2 merge.1
  57.3 33.5 %all_to_all.10.got = bf16[32,104,128]{2,1,0:T(8,128)(2,1)S(1)} all-to-all(bf16[32,104,128]{2,1,0:T(8,128)(2,1)S(1)} %merge.1), channel_id=1, replica_groups=mesh['x'=4,'zq'=4,'zp'=2,'y'=4,'core'=2] {'zq','y','core'}, dimensions={0} | all-to-all | bytes 1703936 | tf_op jit(solution)/shard_map/all_to_all | solution.py:309
  90.8 0.9 %final.1 = bf16[800,128]{1,0:T(8,128)(2,1)} custom-call(bf16[32,104,128]{2,1,0:T(8,128)(2,1)S(1)} %all_to_all.10.got), custom_call_target="tpu_custom_call" | custom-call | tf_op jit(solution)/shard_map/final/pallas_call | solution.py:310
  (10 shorter events, 0.0 us)
Async XLA Ops:
  0.1 1.2 %copy-start.1 = (bf16[512,1024]{1,0:T(8,128)(2,1)S(1)}, bf16[512,1024]{1,0:T(8,128)(2,1)}, u32[]{:S(2)}) copy-start(bf16[512,1024]{1,0:T(8,128)(2,1)} %own.3) | copy-start | bytes 3145732
  1.3 6.4 %copy-start = (bf16[3200,1024]{1,0:T(8,128)(2,1)S(1)}, bf16[3200,1024]{1,0:T(8,128)(2,1)}, u32[]{:S(2)}) copy-start(bf16[3200,1024]{1,0:T(8,128)(2,1)} %table.1) | copy-start | bytes 19660804
  2.7 31.6 %collective-permute-start.2 = (bf16[256,1024]{1,0:T(8,128)(2,1)}, bf16[256,1024]{1,0:T(8,128)(2,1)}, u32[]{:S(2)}, u32[]{:S(2)}) collective-permute-start(bf16[256,1024]{1,0:T(8,128)(2,1)} %cut.1.after), channel_id=1, source_target_pairs={{0,128},{64,192},{128,0},{192,64},{1,129},{65,193},{129,1},{193,65... | collective-permute-start | bytes 1572872 | tf_op jit(solution)/shard_map/ppermute | solution.py:251
  6.3 28.0 %collective-permute-start.1 = (bf16[256,1024]{1,0:T(8,128)(2,1)}, bf16[256,1024]{1,0:T(8,128)(2,1)}, u32[]{:S(2)}, u32[]{:S(2)}) collective-permute-start(bf16[256,1024]{1,0:T(8,128)(2,1)} %cut.1.after), channel_id=1, source_target_pairs={{0,192},{64,0},{128,64},{192,128},{1,193},{65,1},{129,65},{193,129... | collective-permute-start | bytes 1572872 | tf_op jit(solution)/shard_map/ppermute | solution.py:251
  7.1 27.2 %collective-permute-start = (bf16[256,1024]{1,0:T(8,128)(2,1)}, bf16[256,1024]{1,0:T(8,128)(2,1)}, u32[]{:S(2)}, u32[]{:S(2)}) collective-permute-start(bf16[256,1024]{1,0:T(8,128)(2,1)} %cut.1.after), channel_id=1, source_target_pairs={{0,64},{64,128},{128,192},{192,0},{1,65},{65,129},{129,193},{193,1... | collective-permute-start | bytes 1572872 | tf_op jit(solution)/shard_map/ppermute | solution.py:251
  13.6 20.7 %all-to-all-start = ((f32[32,8,128]{2,1,0:T(8,128)}), f32[32,8,128]{2,1,0:T(8,128)S(1)}, u32[]{:S(2)}, u32[]{:S(2)}) async-start(f32[32,8,128]{2,1,0:T(8,128)} %get-tuple-element.24), calls=%async_computation | async-start | bytes 262144 | tf_op jit(solution)/shard_map/all_to_all | solution.py:263
  21.5 13.8 %copy-start.2 = (bf16[512,1024]{1,0:T(8,128)(2,1)S(1)}, bf16[512,1024]{1,0:T(8,128)(2,1)}, u32[]{:S(2)}) copy-start(bf16[512,1024]{1,0:T(8,128)(2,1)} %own.3) | copy-start | bytes 3145732
  34.3 6.0 %collective-permute-start.3 = (bf16[256,1024]{1,0:T(8,128)(2,1)}, bf16[256,1024]{1,0:T(8,128)(2,1)S(1)}, u32[]{:S(2)}, u32[]{:S(2)}) collective-permute-start(bf16[256,1024]{1,0:T(8,128)(2,1)} %collective-permute-done.up), channel_id=1, source_target_pairs={{0,1},{1,0},{2,3},{3,2},{4,5},{5,4},{6,7},{7,6},{8,9},{9,8},{10,11... | collective-permute-start | bytes 1572872 | tf_op jit(solution)/shard_map/ppermute | solution.py:291
  34.8 5.5 %collective-permute-start.4 = (bf16[256,1024]{1,0:T(8,128)(2,1)}, bf16[256,1024]{1,0:T(8,128)(2,1)S(1)}, u32[]{:S(2)}, u32[]{:S(2)}) collective-permute-start(bf16[256,1024]{1,0:T(8,128)(2,1)} %collective-permute-done.1.down), channel_id=1, source_target_pairs={{0,1},{1,0},{2,3},{3,2},{4,5},{5,4},{6,7},{7,6},{8,9},{9,8},{10,11... | collective-permute-start | bytes 1572872 | tf_op jit(solution)/shard_map/ppermute | solution.py:291
  34.9 5.4 %collective-permute-start.5 = (bf16[256,1024]{1,0:T(8,128)(2,1)}, bf16[256,1024]{1,0:T(8,128)(2,1)S(1)}, u32[]{:S(2)}, u32[]{:S(2)}) collective-permute-start(bf16[256,1024]{1,0:T(8,128)(2,1)} %collective-permute-done.2.far), channel_id=1, source_target_pairs={{0,1},{1,0},{2,3},{3,2},{4,5},{5,4},{6,7},{7,6},{8,9},{9,8},{10,11... | collective-permute-start | bytes 1572872 | tf_op jit(solution)/shard_map/ppermute | solution.py:291
  43.0 14.1 %collective-permute-start.6 = (bf16[4,104,640]{2,1,0:T(8,128)(2,1)S(1)}, bf16[4,104,640]{2,1,0:T(8,128)(2,1)S(1)}, u32[]{:S(2)}, u32[]{:S(2)}) collective-permute-start(bf16[4,104,640]{2,1,0:T(8,128)(2,1)S(1)} %get-tuple-element.41), channel_id=1, source_target_pairs={{0,8},{8,0},{16,24},{24,16},{32,40},{40,32},{48,56},{56,48},{1,9},... | collective-permute-start | bytes 1597448 | tf_op jit(solution)/shard_map/ppermute | solution.py:298
  44.8 12.3 %collective-permute-start.7 = (bf16[4,104,384]{2,1,0:T(8,128)(2,1)S(1)}, bf16[4,104,384]{2,1,0:T(8,128)(2,1)S(1)}, u32[]{:S(2)}, u32[]{:S(2)}) collective-permute-start(bf16[4,104,384]{2,1,0:T(8,128)(2,1)S(1)} %get-tuple-element.42), channel_id=1, source_target_pairs={{0,56},{8,16},{16,8},{24,32},{32,24},{40,48},{48,40},{56,0},{1,57}... | collective-permute-start | bytes 958472 | tf_op jit(solution)/shard_map/ppermute | solution.py:299

commit v15 on v12

--- a/solution.py
+++ b/solution.py
@@ -273,8 +273,8 @@
     parts = tuple(shape((n_blocks, height, width), BF) for width in (LEFT, dim - LEFT))
     left, right = call(give_kernel, parts, 3 * half, *others, *numer, scratch=spare)
 
-    got_left = lax.ppermute(left, Z, [(i, i ^ 1) for i in range(NZ)])
-    got_right = lax.ppermute(right, Z, [(i, (i + (1 if i % 2 else -1)) % NZ) for i in range(NZ)])
+    got_left = lax.ppermute(left, Z, [(i, (i + (1 if i % 2 else -1)) % NZ) for i in range(NZ)])
+    got_right = lax.ppermute(right, Z, [(i, i ^ 1) for i in range(NZ)])
     kept = call(keep_kernel, shape((n_blocks, height, dim), F32), NX * pts, points, *near, *others, scratch=spare)
     send = pl.pallas_call(
         merge_kernel,

time: 91.2 us -> 92.5 us (1.014)
  waiting for transfers between devices: 12.4 us -> 17.1 us
  blocking collectives: 33.7 us -> 31 us
    ppermute x2, waiting for transfers between devices: 2.24 us -> 6.92 us  [the longest x1 3.6 us: body(): lax.ppermute(left, Z, [(i, (i + (1 if i % 2 else -1)) % NZ) for i in rang...]
    all_to_all x1, blocking collectives: 33.7 us -> 31 us  [body(): got = lax.all_to_all(send, ('zq', *CENT), 0, 0)]
  transfers between devices with their start and end apart: 9 -> 9, of which waited for: 3 -> 3; matrix products, arithmetic and copies ran while one was open for 0% -> 0% of each run, Pallas kernels for 20% -> 19%
where the time goes in v15:
time: 92.5 us; the launch traced here: 92.2 us
  blocking collectives  31 us (34%)
  Pallas kernels  23 us (25%)
  starting transfers between devices  19.7 us (21%)
  waiting for transfers between devices  17.1 us (18%)
  local copies, waits for them, and re-layouts  1.24 us (1%)
    all_to_all x1, blocking collectives, body(): got = lax.all_to_all(send, ('zq', *CENT), 0, 0)  31 us
    pallas_call x3, Pallas kernels, call(): pl.pallas_call(kernel, out_shape=out_shape, in_specs=[SMEM] + [VMEM] * (3...  12.1 us
    all_to_all x1, waiting for transfers between devices, body(): stats = lax.all_to_all(send_stats, ('x', *CENT), 0, 0)  10.2 us
    all_to_all x1, starting transfers between devices, body(): stats = lax.all_to_all(send_stats, ('x', *CENT), 0, 0)  7.93 us
    pallas_call x1, Pallas kernels, body(): pl.pallas_call(stats_kernel, out_shape=(shape(stats_shape, F32), shape((8...  5.85 us
    ppermute x1, starting transfers between devices, body(): lax.ppermute(left, Z, [(i, (i + (1 if i % 2 else -1)) % NZ) for i in rang...  5.68 us
    ppermute x3, starting transfers between devices, body(): lax.ppermute(own_half, 'x', [(i, (i + k) % NX) for i in range(NX)])  5.04 us
    ppermute x1, waiting for transfers between devices, body(): lax.ppermute(left, Z, [(i, (i + (1 if i % 2 else -1)) % NZ) for i in rang...  3.6 us
  transfers between devices with their start and end apart: 9, of which 3 were waited for; matrix products, arithmetic and copies ran while one was open for 0% of the time, Pallas kernels for 19%

profile of v15, /device:TPU:1, one launch (start us, length us, event | category | flops | bytes accessed | tf_op | source)
XLA Modules:
  0.0 92.2 jit_solution(11062520389369723564)
XLA Ops:
  0.0 0.1 pad_add_fusion.place
  0.1 1.2 %copy-done.1 = bf16[512,1024]{1,0:T(8,128)(2,1)S(1)} copy-done((bf16[512,1024]{1,0:T(8,128)(2,1)S(1)}, bf16[512,1024]{1,0:T(8,128)(2,1)}, u32[]{:S(2)}) %copy-start.1) | copy-done | bytes 1048600
  1.3 1.4 %cut.1.after = bf16[256,1024]{1,0:T(8,128)(2,1)} custom-call(s32[3]{0:T(128)S(1)} %pad_add_fusion.place, bf16[512,1024]{1,0:T(8,128)(2,1)S(1)} %copy-done.1, bf16[3200,1024]{1,0:T(8,128)(2,1)} %table.1), custom_call_target="tpu_custom_call" | custom-call | flops 1 | bytes 1 | tf_op jit(solution)/shard_map/cut/pallas_call | solution.py:221
  2.7 3.6 %collective-permute-start.2 = (bf16[256,1024]{1,0:T(8,128)(2,1)}, bf16[256,1024]{1,0:T(8,128)(2,1)}, u32[]{:S(2)}, u32[]{:S(2)}) collective-permute-start(bf16[256,1024]{1,0:T(8,128)(2,1)} %cut.1.after), channel_id=1, source_target_pairs={{0,128},{64,192},{128,0},{192,64},{1,129},{65,193},{129,1},{193,65... | collective-permute-start | bytes 1572872 | tf_op jit(solution)/shard_map/ppermute | solution.py:230
  6.3 0.9 collective-permute-start.1
  7.1 0.6 collective-permute-start
  7.7 5.9 %stats.1 = (f32[32,8,128]{2,1,0:T(8,128)}, f32[8,128]{1,0:T(8,128)S(1)}) custom-call(bf16[512,1024]{1,0:T(8,128)(2,1)S(1)} %copy-done.1, bf16[3200,1024]{1,0:T(8,128)(2,1)S(1)} %copy-done, bf16[256,1024]{1,0:T(8,128)(2,1)} %cut.1.after), custom_call_target="tpu_custom_call" | custom-call | flops 1 | bytes 1 | tf_op jit(solution)/shard_map/stats/pallas_call | solution.py:233
  13.6 7.9 %all-to-all-start = ((f32[32,8,128]{2,1,0:T(8,128)}), f32[32,8,128]{2,1,0:T(8,128)S(1)}, u32[]{:S(2)}, u32[]{:S(2)}) async-start(f32[32,8,128]{2,1,0:T(8,128)} %get-tuple-element.24), calls=%async_computation | async-start | bytes 262144 | tf_op jit(solution)/shard_map/all_to_all | solution.py:242
  21.5 0.0 copy-start.2
  21.5 2.6 %window.1 = (bf16[2,448,1024]{2,1,0:T(8,128)(2,1)S(1)}, f32[2,448,1]{2,1,0:T(8,128)S(1)}) custom-call(s32[3]{0:T(128)S(1)} %pad_add_fusion.place, bf16[3200,1024]{1,0:T(8,128)(2,1)} %table.1, f32[8,128]{1,0:T(8,128)S(1)} %get-tuple-element.25.after), custom_call_target="tpu_custom_call" | custom-call | flops 1 | bytes 1 | tf_op jit(solution)/shard_map/window/pallas_call | solution.py:244
  24.1 10.2 %all-to-all-done.stats = f32[32,8,128]{2,1,0:T(8,128)S(1)} async-done(((f32[32,8,128]{2,1,0:T(8,128)}), f32[32,8,128]{2,1,0:T(8,128)S(1)}, u32[]{:S(2)}, u32[]{:S(2)}) %all-to-all-start) | async-done | bytes 131104 | tf_op jit(solution)/shard_map/all_to_all | solution.py:242
  34.3 0.0 collective-permute-done.2.far
  34.3 0.6 collective-permute-start.3
  34.8 0.1 collective-permute-start.4
  34.9 0.4 collective-permute-start.5
  35.3 4.0 %first_kernel.1 = (f32[448,1024]{1,0:T(8,128)S(1)}, f32[448,128]{1,0:T(8,128)S(1)}) custom-call(s32[3]{0:T(128)S(1)} %pad_add_fusion.place, f32[32,8,128]{2,1,0:T(8,128)S(1)} %all-to-all-done.stats, bf16[2,448,1024]{2,1,0:T(8,128)(2,1)S(1)} %get-tuple-element.29.rows, f32[2,448,1]{2,1,0:T(8,128)S(1)} %get-tuple-element.30.norms, ...), custom_call_target="tpu_custom_call" | custom-call | flops 1 | bytes 1 | tf_op jit(solution)/shard_map/first_kernel/pallas_call | solution.py:256
  39.3 2.7 %give_kernel.1 = (bf16[4,104,640]{2,1,0:T(8,128)(2,1)S(1)}, bf16[4,104,384]{2,1,0:T(8,128)(2,1)S(1)}) custom-call(s32[3]{0:T(128)S(1)} %pad_add_fusion.place, f32[32,8,128]{2,1,0:T(8,128)S(1)} %all-to-all-done.stats, bf16[2,448,1024]{2,1,0:T(8,128)(2,1)S(1)} %get-tuple-element.29.rows, f32[2,448,1]{2,1,0:T(8,128)S(1)} %get-tuple-element.30.norms, ...), custom_call_target="tpu_custom_call" | custom-call | flops 1 | bytes 1 | tf_op jit(solution)/shard_map/give_kernel/pallas_call | solution.py:256
  42.0 5.7 %collective-permute-start.6 = (bf16[4,104,640]{2,1,0:T(8,128)(2,1)S(1)}, bf16[4,104,640]{2,1,0:T(8,128)(2,1)S(1)}, u32[]{:S(2)}, u32[]{:S(2)}) collective-permute-start(bf16[4,104,640]{2,1,0:T(8,128)(2,1)S(1)} %get-tuple-element.41), channel_id=1, source_target_pairs={{0,56},{8,16},{16,8},{24,32},{32,24},{40,48},{48,40},{56,0},{1,57}... | collective-permute-start | bytes 1597448 | tf_op jit(solution)/shard_map/ppermute | solution.py:276
  47.7 5.4 %keep_kernel.1.kept = f32[4,104,1024]{2,1,0:T(8,128)S(1)} custom-call(s32[3]{0:T(128)S(1)} %pad_add_fusion.place, f32[32,8,128]{2,1,0:T(8,128)S(1)} %all-to-all-done.stats, bf16[2,448,1024]{2,1,0:T(8,128)(2,1)S(1)} %get-tuple-element.29.rows, f32[2,448,1]{2,1,0:T(8,128)S(1)} %get-tuple-element.30.norms, bf16[512,1024]{1,0:T(8,128)(2,1)S(1)} %copy-done.2, ...), custom_call_target="tpu_custom_call" | custom-call | flops 1 | bytes 1 | tf_op jit(solution)/shard_map/keep_kernel/pallas_call | solution.py:256
  53.2 3.3 %collective-permute-done.7.right = bf16[4,104,384]{2,1,0:T(8,128)(2,1)S(1)} collective-permute-done((bf16[4,104,384]{2,1,0:T(8,128)(2,1)S(1)}, bf16[4,104,384]{2,1,0:T(8,128)(2,1)S(1)}, u32[]{:S(2)}, u32[]{:S(2)}) %collective-permute-start.7) | collective-permute-done | bytes 319520 | tf_op jit(solution)/shard_map/ppermute | solution.py:277
  56.5 3.6 %collective-permute-done.6.left = bf16[4,104,640]{2,1,0:T(8,128)(2,1)S(1)} collective-permute-done((bf16[4,104,640]{2,1,0:T(8,128)(2,1)S(1)}, bf16[4,104,640]{2,1,0:T(8,128)(2,1)S(1)}, u32[]{:S(2)}, u32[]{:S(2)}) %collective-permute-start.6) | collective-permute-done | bytes 532512 | tf_op jit(solution)/shard_map/ppermute | solution.py:276
  60.1 0.2 merge.1
  60.3 31.0 %all_to_all.10.got = bf16[32,104,128]{2,1,0:T(8,128)(2,1)S(1)} all-to-all(bf16[32,104,128]{2,1,0:T(8,128)(2,1)S(1)} %merge.1), channel_id=1, replica_groups=mesh['x'=4,'zq'=4,'zp'=2,'y'=4,'core'=2] {'zq','y','core'}, dimensions={0} | all-to-all | bytes 1703936 | tf_op jit(solution)/shard_map/all_to_all | solution.py:287
  91.3 0.9 %final.1 = bf16[800,128]{1,0:T(8,128)(2,1)} custom-call(bf16[32,104,128]{2,1,0:T(8,128)(2,1)S(1)} %all_to_all.10.got), custom_call_target="tpu_custom_call" | custom-call | tf_op jit(solution)/shard_map/final/pallas_call | solution.py:288
  (10 shorter events, 0.0 us)
Async XLA Ops:
  0.1 1.2 %copy-start.1 = (bf16[512,1024]{1,0:T(8,128)(2,1)S(1)}, bf16[512,1024]{1,0:T(8,128)(2,1)}, u32[]{:S(2)}) copy-start(bf16[512,1024]{1,0:T(8,128)(2,1)} %own.3) | copy-start | bytes 3145732
  1.3 6.4 %copy-start = (bf16[3200,1024]{1,0:T(8,128)(2,1)S(1)}, bf16[3200,1024]{1,0:T(8,128)(2,1)}, u32[]{:S(2)}) copy-start(bf16[3200,1024]{1,0:T(8,128)(2,1)} %table.1) | copy-start | bytes 19660804
  2.7 31.6 %collective-permute-start.2 = (bf16[256,1024]{1,0:T(8,128)(2,1)}, bf16[256,1024]{1,0:T(8,128)(2,1)}, u32[]{:S(2)}, u32[]{:S(2)}) collective-permute-start(bf16[256,1024]{1,0:T(8,128)(2,1)} %cut.1.after), channel_id=1, source_target_pairs={{0,128},{64,192},{128,0},{192,64},{1,129},{65,193},{129,1},{193,65... | collective-permute-start | bytes 1572872 | tf_op jit(solution)/shard_map/ppermute | solution.py:230
  6.3 28.0 %collective-permute-start.1 = (bf16[256,1024]{1,0:T(8,128)(2,1)}, bf16[256,1024]{1,0:T(8,128)(2,1)}, u32[]{:S(2)}, u32[]{:S(2)}) collective-permute-start(bf16[256,1024]{1,0:T(8,128)(2,1)} %cut.1.after), channel_id=1, source_target_pairs={{0,192},{64,0},{128,64},{192,128},{1,193},{65,1},{129,65},{193,129... | collective-permute-start | bytes 1572872 | tf_op jit(solution)/shard_map/ppermute | solution.py:230
  7.1 27.2 %collective-permute-start = (bf16[256,1024]{1,0:T(8,128)(2,1)}, bf16[256,1024]{1,0:T(8,128)(2,1)}, u32[]{:S(2)}, u32[]{:S(2)}) collective-permute-start(bf16[256,1024]{1,0:T(8,128)(2,1)} %cut.1.after), channel_id=1, source_target_pairs={{0,64},{64,128},{128,192},{192,0},{1,65},{65,129},{129,193},{193,1... | collective-permute-start | bytes 1572872 | tf_op jit(solution)/shard_map/ppermute | solution.py:230
  13.6 20.7 %all-to-all-start = ((f32[32,8,128]{2,1,0:T(8,128)}), f32[32,8,128]{2,1,0:T(8,128)S(1)}, u32[]{:S(2)}, u32[]{:S(2)}) async-start(f32[32,8,128]{2,1,0:T(8,128)} %get-tuple-element.24), calls=%async_computation | async-start | bytes 262144 | tf_op jit(solution)/shard_map/all_to_all | solution.py:242
  21.5 13.8 %copy-start.2 = (bf16[512,1024]{1,0:T(8,128)(2,1)S(1)}, bf16[512,1024]{1,0:T(8,128)(2,1)}, u32[]{:S(2)}) copy-start(bf16[512,1024]{1,0:T(8,128)(2,1)} %own.3) | copy-start | bytes 3145732
  34.3 5.0 %collective-permute-start.3 = (bf16[256,1024]{1,0:T(8,128)(2,1)}, bf16[256,1024]{1,0:T(8,128)(2,1)S(1)}, u32[]{:S(2)}, u32[]{:S(2)}) collective-permute-start(bf16[256,1024]{1,0:T(8,128)(2,1)} %collective-permute-done.up), channel_id=1, source_target_pairs={{0,1},{1,0},{2,3},{3,2},{4,5},{5,4},{6,7},{7,6},{8,9},{9,8},{10,11... | collective-permute-start | bytes 1572872 | tf_op jit(solution)/shard_map/ppermute | solution.py:270
  34.8 4.5 %collective-permute-start.4 = (bf16[256,1024]{1,0:T(8,128)(2,1)}, bf16[256,1024]{1,0:T(8,128)(2,1)S(1)}, u32[]{:S(2)}, u32[]{:S(2)}) collective-permute-start(bf16[256,1024]{1,0:T(8,128)(2,1)} %collective-permute-done.1.down), channel_id=1, source_target_pairs={{0,1},{1,0},{2,3},{3,2},{4,5},{5,4},{6,7},{7,6},{8,9},{9,8},{10,11... | collective-permute-start | bytes 1572872 | tf_op jit(solution)/shard_map/ppermute | solution.py:270
  34.9 4.4 %collective-permute-start.5 = (bf16[256,1024]{1,0:T(8,128)(2,1)}, bf16[256,1024]{1,0:T(8,128)(2,1)S(1)}, u32[]{:S(2)}, u32[]{:S(2)}) collective-permute-start(bf16[256,1024]{1,0:T(8,128)(2,1)} %collective-permute-done.2.far), channel_id=1, source_target_pairs={{0,1},{1,0},{2,3},{3,2},{4,5},{5,4},{6,7},{7,6},{8,9},{9,8},{10,11... | collective-permute-start | bytes 1572872 | tf_op jit(solution)/shard_map/ppermute | solution.py:270
  42.0 18.0 %collective-permute-start.6 = (bf16[4,104,640]{2,1,0:T(8,128)(2,1)S(1)}, bf16[4,104,640]{2,1,0:T(8,128)(2,1)S(1)}, u32[]{:S(2)}, u32[]{:S(2)}) collective-permute-start(bf16[4,104,640]{2,1,0:T(8,128)(2,1)S(1)} %get-tuple-element.41), channel_id=1, source_target_pairs={{0,56},{8,16},{16,8},{24,32},{32,24},{40,48},{48,40},{56,0},{1,57}... | collective-permute-start | bytes 1597448 | tf_op jit(solution)/shard_map/ppermute | solution.py:276
  47.7 8.8 %collective-permute-start.7 = (bf16[4,104,384]{2,1,0:T(8,128)(2,1)S(1)}, bf16[4,104,384]{2,1,0:T(8,128)(2,1)S(1)}, u32[]{:S(2)}, u32[]{:S(2)}) collective-permute-start(bf16[4,104,384]{2,1,0:T(8,128)(2,1)S(1)} %get-tuple-element.42), channel_id=1, source_target_pairs={{0,8},{8,0},{16,24},{24,16},{32,40},{40,32},{48,56},{56,48},{1,9},... | collective-permute-start | bytes 958472 | tf_op jit(solution)/shard_map/ppermute | solution.py:277
